TPU v7x, 32 devices: a whole 2x2x4 slice. The times are simulated.
32 devices in a mesh: dp: 2 (over core), blk: 4 (over y, x), hd: 4 (over z).
Axes of the slice: x: 2, y: 2, z: 4, core: 2. Of those that a mesh axis runs over, the one named last changes fastest.
Arguments:
- hidden_in: bfloat16 [2, 2048, 2048], P('dp', ('blk', 'hd')), may hold values from -6 to 6
- gain_attn: bfloat16 [2048], P(('dp', 'blk', 'hd')), may hold values from 0.25 to 1.75
- shift_attn: bfloat16 [2048], P(('dp', 'blk', 'hd')), may hold values from -3 to 3
- gain_mlp: bfloat16 [2048], P(('dp', 'blk', 'hd')), may hold values from 0.25 to 1.75
- shift_mlp: bfloat16 [2048], P(('dp', 'blk', 'hd')), may hold values from -3 to 3
- qkv_weight: bfloat16 [2048, 6144], P(('dp', 'blk', 'hd')), may hold values from -0.125 to 0.125
- qkv_bias: bfloat16 [6144], P(('dp', 'blk', 'hd')), may hold values from -3 to 3
- dense_weight: bfloat16 [2048, 2048], P(('dp', 'blk', 'hd')), may hold values from -1.5 to 1.5
- up_weight: bfloat16 [2048, 8192], P(('dp', 'blk', 'hd')), may hold values from -0.125 to 0.125
- up_bias: bfloat16 [8192], P(('dp', 'blk', 'hd')), may hold values from -3 to 3
- down_weight: bfloat16 [2048, 8192], P(('dp', 'blk', 'hd')), may hold values from -0.0625 to 0.0625
- out_bias: bfloat16 [2048], P(('dp', 'blk', 'hd')), may hold values from -3 to 3
- cotangent: bfloat16 [2, 2048, 2048], P('dp', ('blk', 'hd')), may hold values from -6 to 6
Outputs:
- output: bfloat16 [2, 2048, 2048], P('dp', ('blk', 'hd'))
- grad_hidden: float32 [2, 2048, 2048], P('dp', ('blk', 'hd'))
- grad_gain_attn: float32 [2048], P(('dp', 'blk', 'hd'))
- grad_shift_attn: float32 [2048], P(('dp', 'blk', 'hd'))
- grad_gain_mlp: float32 [2048], P(('dp', 'blk', 'hd'))
- grad_shift_mlp: float32 [2048], P(('dp', 'blk', 'hd'))
- grad_qkv_weight: float32 [2048, 6144], P(('dp', 'blk', 'hd'))
- grad_qkv_bias: float32 [6144], P(('dp', 'blk', 'hd'))
- grad_dense_weight: float32 [2048, 2048], P(('dp', 'blk', 'hd'))
- grad_up_weight: float32 [2048, 8192], P(('dp', 'blk', 'hd'))
- grad_up_bias: float32 [8192], P(('dp', 'blk', 'hd'))
- grad_down_weight: float32 [2048, 8192], P(('dp', 'blk', 'hd'))
- grad_out_bias: float32 [2048], P(('dp', 'blk', 'hd'))
All inputs are finite; a program needn't handle non-finite values.
Results may differ from a plain program's by a relative error of at most 0.011.
Values may be sent and summed in bfloat16 or wider, within the bound.
No kernel may reach another device: no remote copies, remote signals or barrier semaphores. Data moves between devices by JAX's collectives and lax.ppermute only.
A program may use at most 640 MiB of HBM per device.

v0:
```python
import functools

import jax
import jax.numpy as jnp
from jax import lax
from jax.experimental import pallas as pl
from jax.experimental.pallas import tpu as pltpu
from jax.sharding import Mesh, PartitionSpec as P

D = 2048
HEADS = 8
HS = 256
ROT = 64

TP = ("bl", "hd")
RP = ("dp", "bh")
ALL = ("dp", "bh", "bl", "hd")

epsilon = 1e-05
contract_last = (((1,), (1,)), ((), ()))
f32 = jnp.float32
bf16 = jnp.bfloat16


def rotary_tables(positions):
    half_rot = ROT // 2
    frequency = 10000.0 ** (-(2.0 * jnp.arange(half_rot, dtype=f32)) / ROT)
    angles = positions[:, None] * frequency[None, :]
    cosine, sine = jnp.cos(angles), jnp.sin(angles)
    none = jnp.zeros_like(sine)
    rest = jnp.ones((positions.shape[0], 128 - ROT), f32)
    return (
        jnp.concatenate([cosine, cosine, rest], axis=1),
        jnp.concatenate([-sine, none, 0.0 * rest], axis=1),
        jnp.concatenate([none, sine, 0.0 * rest], axis=1),
    )


def mm(a, b):
    return jnp.dot(a, b, preferred_element_type=f32)


def mm_nt(a, b):
    return lax.dot_general(a, b, contract_last, preferred_element_type=f32)


def mm_tn(a, b):
    return lax.dot_general(a, b, (((0,), (0,)), ((), ())), preferred_element_type=f32)


def join(*values):
    return lax.optimization_barrier(values)


def swap(value, axis, distance):
    size = lax.axis_size(axis)
    return lax.ppermute(value, axis, [(i, i ^ distance) for i in range(size)])


def gather_axis(value, axis):
    return [value] + [swap(value, axis, d) for d in range(1, lax.axis_size(axis))]


def gather_start(value):
    size = lax.axis_size("hd")
    return [swap(value, "hd", d) for d in range(1, 3 if size == 4 else size)]


def gather_end(value, near):
    if lax.axis_size("hd") == 4:
        near = [near[0], near[1], swap(near[1], "hd", 1)]
    return [value] + near


def gather_rest(value):
    value = value[None]
    for axis in reversed(RP):
        place, size = lax.axis_index(axis), lax.axis_size(axis)
        bit = 1
        while bit < size:
            other = swap(value, axis, bit)
            upper = (place & bit) != 0
            value = jnp.concatenate(
                [jnp.where(upper, other, value), jnp.where(upper, value, other)], axis=0
            )
            bit *= 2
    return value


def groups():
    size = lax.axis_size("hd")
    part = size // 4
    return [list(range(size - (g + 1) * part, size - g * part)) for g in range(4)]


def send_far(terms, ds):
    return {d: [swap(term[d], "bl", far + 1) for far, term in enumerate(terms)] for d in ds}


def add_far(own, received):
    return {
        d: sum((other.astype(f32) for other in others), own[d])
        for d, others in received.items()
    }


def send_near(blocks, handed):
    four = lax.axis_size("hd") == 4
    out = {}
    for d, block in blocks.items():
        if d == 0:
            continue
        if four and d == 2:
            block = block + handed[3].astype(f32)
        out[d] = swap(block.astype(bf16), "hd", 1 if four and d == 3 else d)
    return out


def add_near(own, received):
    four = lax.axis_size("hd") == 4
    for d, block in received.items():
        if not (four and d == 3):
            own = own + block.astype(f32)
    return own


def spread_group(shard):
    mine = lax.all_to_all(shard, TP, split_axis=0, concat_axis=0, tiled=True)
    return mine.reshape(-1, shard.shape[2])


def spread_rest(mine):
    return lax.all_gather(mine, RP, axis=0, tiled=True)


def pick(value, axis, distance):
    return lax.dynamic_index_in_dim(value, lax.axis_index(axis) ^ distance, 0, keepdims=False)


def collect_dp(partial):
    partial = partial.reshape(lax.axis_size("dp"), -1, partial.shape[1])
    others = [swap(pick(partial, "dp", d), "dp", d) for d in range(1, lax.axis_size("dp"))]
    return pick(partial, "dp", 0), others


def collect_bh(own, others):
    total = sum((other.astype(f32) for other in others), own.astype(f32)).astype(bf16)
    total = total.reshape(lax.axis_size("bh"), -1, own.shape[1])
    others = [swap(pick(total, "bh", d), "bh", d) for d in range(1, lax.axis_size("bh"))]
    return pick(total, "bh", 0), others


def add_others(own, others):
    return sum((other.astype(f32) for other in others), own.astype(f32)).astype(bf16)


def collect_rest(partial):
    return lax.psum_scatter(partial, RP, scatter_dimension=0, tiled=True)


def collect_group(mine):
    mine = mine.reshape(lax.axis_size(TP), -1, mine.shape[1])
    return lax.all_to_all(mine, TP, split_axis=0, concat_axis=0, tiled=True)


TILE = 256
KEYS = 2048


def call(kernel, outs, *ins, scratch=(), grid=(), in_specs=None, out_specs=None):
    vmem = pl.BlockSpec(memory_space=pltpu.VMEM)
    return pl.pallas_call(
        kernel,
        grid=grid,
        out_shape=[jax.ShapeDtypeStruct(shape, dtype) for shape, dtype in outs],
        in_specs=in_specs or [vmem] * len(ins),
        out_specs=out_specs or [vmem] * len(outs),
        scratch_shapes=list(scratch),
        compiler_params=pltpu.CompilerParams(vmem_limit_bytes=58 * 2**20),
        cost_estimate=pl.CostEstimate(flops=1, bytes_accessed=1, transcendentals=0),
    )(*ins)


def tiles(count, step):
    def body(i, _):
        step(pl.ds(pl.multiple_of(i * TILE, TILE), TILE))
        return 0

    lax.fori_loop(0, count // TILE, body, 0)


def turn(value, tables, sign):
    own, above, below = tables
    first = value[:, :128]
    turned = first * own + sign * (
        pltpu.roll(first, 96, 1) * above + pltpu.roll(first, 32, 1) * below
    )
    return jnp.concatenate([turned, value[:, 128:]], axis=1)


def statistics(block):
    average = jnp.mean(block, axis=1, keepdims=True)
    centered = block - average
    return average, lax.rsqrt(jnp.mean(centered * centered, axis=1, keepdims=True) + epsilon)


def project_kernel(count, *refs):
    x_refs, refs = refs[:count], refs[count:]
    vec_ref, w_ref, b_ref, own_ref, above_ref, below_ref, *refs = refs
    attn_ref, mlp_ref, q_ref, kv_ref, average_ref, inverse_ref = refs
    rows = x_refs[0].shape[0]
    for start in range(0, count * rows, TILE):
        for i in range(start // rows, (start + TILE) // rows):
            at = slice(i * rows, (i + 1) * rows)
            block = x_refs[i][...].astype(f32)
            average, inverse = statistics(block)
            average_ref[at, :] = average
            inverse_ref[at, :] = inverse
            normed = (block - average) * inverse
            attn_ref[at, :] = (normed * vec_ref[0:1, :] + vec_ref[1:2, :]).astype(bf16)
            mlp_ref[at, :] = (normed * vec_ref[2:3, :] + vec_ref[3:4, :]).astype(bf16)
        at = slice(start, start + TILE)
        project = mm(attn_ref[at, :], w_ref[:, : 3 * HS]) + b_ref[...]
        tables = own_ref[at, :], above_ref[at, :], below_ref[at, :]
        query = turn(project[:, :HS], tables, 1.0).astype(bf16)
        q_ref[at, :] = (query.astype(f32) * HS**-0.5).astype(bf16)
        kv_ref[at, :HS] = turn(project[:, HS : 2 * HS], tables, 1.0).astype(bf16)
        kv_ref[at, HS:] = project[:, 2 * HS :].astype(bf16)


def cotangent_kernel(count, *refs):
    g_refs, (w_ref, g_ref, out_ref) = refs[:count], refs[count:]
    rows = g_refs[0].shape[0]
    for i in range(count):
        g_ref[i * rows : (i + 1) * rows, :] = g_refs[i][...]

    def step(at):
        out_ref[at, :] = mm(g_ref[at, :], w_ref[:, 3 * HS :]).astype(bf16)

    tiles(g_ref.shape[0], step)


def forward_kernel(mlp_ref, w_ref, b_ref, act_ref, slope_ref):
    def step(at):
        value = mm(mlp_ref[at, :], w_ref[...]) + b_ref[...]
        cdf = 0.5 * (1.0 + lax.erf(value * 0.7071067811865476))
        density = jnp.exp(-0.5 * value * value) * 0.3989422804014327
        act_ref[at, :] = (value * cdf).astype(bf16)
        slope_ref[at, :] = cdf + value * density

    tiles(mlp_ref.shape[0], step)


def backward_kernel(g_ref, w_ref, slope_ref, out_ref, sum_ref):
    sum_ref[...] = jnp.zeros_like(sum_ref)

    def step(at):
        grad = (mm(g_ref[at, :], w_ref[...]) * slope_ref[at, :]).astype(bf16)
        out_ref[at, :] = grad
        sum_ref[...] += jnp.sum(grad.astype(f32), axis=0, keepdims=True)

    tiles(g_ref.shape[0], step)


def output_kernel(att_ref, act_ref, dense_ref, down_ref, *out_refs):
    start = 0
    for out_ref in (out_refs[-1],) + out_refs[:-1]:
        at = slice(start, start + out_ref.shape[0])
        start += out_ref.shape[0]
        term = mm_nt(att_ref[at, :], dense_ref[...]) + mm_nt(act_ref[at, :], down_ref[...])
        out_ref[...] = term.astype(out_ref.dtype)


def output_terms(attended, activated, w_heads, w_down, kinds):
    count, ffl = activated.shape
    return call(
        output_kernel,
        [((rows, D), dtype) for rows, dtype in kinds],
        attended, activated, w_heads, w_down,
        grid=(D // TILE,),
        in_specs=[
            pl.BlockSpec((count, HS), lambda i: (0, 0)),
            pl.BlockSpec((count, ffl), lambda i: (0, 0)),
            pl.BlockSpec((TILE, HS), lambda i: (i, 3)),
            pl.BlockSpec((TILE, ffl), lambda i: (i, 0)),
        ],
        out_specs=[pl.BlockSpec((rows, TILE), lambda i: (0, i)) for rows, _ in kinds],
    )


def turn_back_kernel(count, *refs):
    dq_ref, refs = refs[0], refs[1:]
    term_refs, (own_ref, above_ref, below_ref, out_ref, sum_ref) = refs[:count], refs[count:]
    sum_ref[...] = jnp.zeros_like(sum_ref)

    def step(at):
        tables = own_ref[at, :], above_ref[at, :], below_ref[at, :]
        grad = term_refs[0][at, :].astype(f32)
        for ref in term_refs[1:]:
            grad += ref[at, :].astype(f32)
        grad = grad.astype(bf16)
        out_ref[at, :HS] = turn(dq_ref[at, :].astype(f32), tables, -1.0).astype(bf16)
        out_ref[at, HS : 2 * HS] = turn(grad[:, :HS].astype(f32), tables, -1.0).astype(bf16)
        out_ref[at, 2 * HS :] = grad[:, HS:]
        sum_ref[...] += jnp.sum(out_ref[at, :].astype(f32), axis=0, keepdims=True)

    tiles(dq_ref.shape[0], step)


def input_kernel(count, parts, *refs):
    x_refs, refs = refs[:count], refs[count:]
    average_ref, inverse_ref, gp_ref, gu_ref, heads_ref, up_ref, vec_ref = refs[:7]
    out_refs, sum_ref = refs[7:-1], refs[-1]
    rows = x_refs[0].shape[0]
    sums = [0.0] * 4
    order = (out_refs[-1],) + out_refs[:-1]
    reach = count * rows // parts
    for start in range(0, count * rows, TILE):
        at = slice(start, start + TILE)
        attn = mm_nt(gp_ref[at, :], heads_ref[...])
        mlp = mm_nt(gu_ref[at, :], up_ref[...])
        block = jnp.concatenate(
            [x_refs[i][...].astype(f32) for i in range(start // rows, (start + TILE) // rows)],
            axis=0,
        )
        normed = (block - average_ref[at, :]) * inverse_ref[at, :]
        for i, term in enumerate((attn * normed, attn, mlp * normed, mlp)):
            sums[i] = sums[i] + jnp.sum(term, axis=0, keepdims=True)
        out = attn * vec_ref[0:1, :] + mlp * vec_ref[2:3, :]
        out_ref = order[start // reach]
        out_ref[start % reach : start % reach + TILE, :] = out.astype(out_ref.dtype)
    sum_ref[...] = jnp.concatenate(sums, axis=0)


def input_terms(x_blocks, average, inverse, grad_project, grad_pre_up, w_heads, w_up, vectors, kinds):
    count, ffl = grad_pre_up.shape
    whole = lambda rows, cols: pl.BlockSpec((rows, cols), lambda i: (0, 0))
    return call(
        functools.partial(input_kernel, len(x_blocks), len(kinds)),
        [((rows, D), dtype) for rows, dtype in kinds] + [((4, D), f32)],
        *x_blocks, average, inverse, grad_project, grad_pre_up, w_heads, w_up, vectors,
        grid=(D // TILE,),
        in_specs=[
            *[pl.BlockSpec((block.shape[0], TILE), lambda i: (0, i)) for block in x_blocks],
            whole(count, 1),
            whole(count, 1),
            whole(count, 3 * HS),
            whole(count, ffl),
            pl.BlockSpec((TILE, 3 * HS), lambda i: (i, 0)),
            pl.BlockSpec((TILE, ffl), lambda i: (i, 0)),
            pl.BlockSpec((vectors.shape[0], TILE), lambda i: (0, i)),
        ],
        out_specs=[
            *[pl.BlockSpec((rows, TILE), lambda i: (0, i)) for rows, _ in kinds],
            pl.BlockSpec((4, TILE), lambda i: (0, i)),
        ],
    )


def attention_kernel(q_ref, g_ref, kv_ref, qpos_ref, kpos_ref, o_ref, dq_ref, dkv_ref, sum_ref):
    count, tile = q_ref.shape[0], TILE
    keys = kv_ref[:, :HS]
    values = kv_ref[:, HS:]
    keys_turned = keys.T
    values_turned = values.T
    sum_ref[...] = jnp.zeros_like(sum_ref)

    def step(i, _):
        at = pl.ds(pl.multiple_of(i * tile, tile), tile)
        query = q_ref[at, :]
        grad = g_ref[at, :]
        scores = mm_nt(keys, query)
        scores = jnp.where(kpos_ref[...] <= qpos_ref[:, at], scores, -1e30)
        weights = jnp.exp(scores - jnp.max(scores, axis=0, keepdims=True))
        weights = weights * (1.0 / jnp.sum(weights, axis=0, keepdims=True))
        weights_low = weights.astype(bf16)
        o_ref[at, :] = mm(values_turned, weights_low).T.astype(bf16)
        sum_ref[:, HS:] += mm(weights_low, grad)
        weight_grad = mm_nt(values, grad)
        delta = jnp.sum(weights * weight_grad, axis=0, keepdims=True)
        score_grad = (weights * (weight_grad - delta)).astype(bf16)
        dq_ref[at, :] = (mm(keys_turned, score_grad).T * (HS**-0.5)).astype(bf16)
        sum_ref[:, :HS] += mm(score_grad, query)
        return 0

    lax.fori_loop(0, count // tile, step, 0)
    dkv_ref[...] = sum_ref[...].astype(bf16)


def long_attention_kernel(q_ref, g_ref, kv_ref, qpos_ref, kpos_ref, o_ref, dq_ref, dkv_ref, sum_ref):
    blocks = kv_ref.shape[0] // KEYS
    sum_ref[...] = jnp.zeros_like(sum_ref)

    def step(at):
        query = q_ref[at, :]
        grad = g_ref[at, :]

        def scores_of(j):
            here = pl.ds(pl.multiple_of(j * KEYS, KEYS), KEYS)
            scores = mm_nt(kv_ref[here, :HS], query)
            return here, jnp.where(kpos_ref[here, :] <= qpos_ref[:, at], scores, -1e30)

        def first(j, state):
            top, total = state
            _, scores = scores_of(j)
            higher = jnp.maximum(top, jnp.max(scores, axis=0, keepdims=True))
            now = jnp.sum(jnp.exp(scores - higher), axis=0, keepdims=True)
            return higher, total * jnp.exp(top - higher) + now

        row = (1, TILE)
        top, total = lax.fori_loop(
            0, blocks, first, (jnp.full(row, -1e30, f32), jnp.zeros(row, f32))
        )
        inverse = 1.0 / total

        def second(j, state):
            result, delta = state
            here, scores = scores_of(j)
            weights = jnp.exp(scores - top) * inverse
            values = kv_ref[here, HS:]
            weight_grad = mm_nt(values, grad)
            result = result + mm(values.T, weights.astype(bf16))
            return result, delta + jnp.sum(weights * weight_grad, axis=0, keepdims=True)

        result, delta = lax.fori_loop(
            0, blocks, second, (jnp.zeros((HS, TILE), f32), jnp.zeros(row, f32))
        )
        o_ref[at, :] = result.T.astype(bf16)

        def third(j, result):
            here, scores = scores_of(j)
            weights = jnp.exp(scores - top) * inverse
            weight_grad = mm_nt(kv_ref[here, HS:], grad)
            score_grad = (weights * (weight_grad - delta)).astype(bf16)
            sum_ref[here, HS:] += mm(weights.astype(bf16), grad)
            sum_ref[here, :HS] += mm(score_grad, query)
            return result + mm(kv_ref[here, :HS].T, score_grad)

        result = lax.fori_loop(0, blocks, third, jnp.zeros((HS, TILE), f32))
        dq_ref[at, :] = (result.T * (HS**-0.5)).astype(bf16)

    tiles(q_ref.shape[0], step)
    dkv_ref[...] = sum_ref[...].astype(bf16)


def per_device(
    hidden_in,
    gain_attn,
    shift_attn,
    gain_mlp,
    shift_mlp,
    qkv_weight,
    qkv_bias,
    dense_weight,
    up_weight,
    up_bias,
    down_weight,
    out_bias,
    cotangent,
):
    seq_count, sub_len, _ = hidden_in.shape
    tp, rp = lax.axis_size(TP), lax.axis_size(RP)
    n_dev = lax.axis_size(ALL)
    t = lax.axis_index(TP)
    bh, bh_size, bl_size = lax.axis_index("bh"), lax.axis_size("bh"), lax.axis_size("bl")
    rows = qkv_weight.shape[0]
    ff = up_weight.shape[1]
    ffl = ff // tp
    group_len = sub_len * tp
    reach = lax.axis_size("hd") * sub_len

    x_own = hidden_in.reshape(sub_len, D)
    g_own = cotangent.reshape(sub_len, D)
    smalls = jnp.concatenate(
        [
            vector.reshape(-1, rows)
            for vector in (
                gain_attn, shift_attn, gain_mlp, shift_mlp, out_bias, qkv_bias, up_bias
            )
        ],
        axis=0,
    )
    kinds = smalls.shape[0]
    smalls = gather_rest(smalls).reshape(-1, 4 * HS)
    extra = 8 * -(-smalls.shape[0] // 8)
    smalls = jnp.pad(smalls, ((0, extra - smalls.shape[0]), (0, 0)))
    heads_own = jnp.concatenate(
        [
            qkv_weight.reshape(rows, 3, HEADS, HS).transpose(2, 0, 1, 3).reshape(HEADS, rows, 3 * HS),
            dense_weight.reshape(rows, HEADS, HS).transpose(1, 0, 2),
        ],
        axis=2,
    )
    heads_own = jnp.concatenate(
        [heads_own, jnp.broadcast_to(smalls[None], (tp,) + smalls.shape)], axis=1
    )
    up_own = up_weight.reshape(rows, tp, ffl).transpose(1, 0, 2)
    down_own = down_weight.reshape(rows, tp, ffl).transpose(1, 0, 2)

    x_near = gather_start(x_own)
    x_side = gather_axis(x_own, "bl")
    g_side = gather_axis(g_own, "bl")
    x_near, x_side, g_side, heads_own = join(x_near, x_side, g_side, heads_own)
    m_heads = lax.all_to_all(heads_own, TP, split_axis=0, concat_axis=0, tiled=True)
    x_rows = [x_side] + [gather_axis(block, "bl") for block in x_near[:2]]
    x_near = gather_end(x_own, x_near)
    x_near, x_rows, m_heads, up_own, g_late = join(x_near, x_rows, m_heads, up_own, g_own)
    w_heads = spread_rest(m_heads[:, :rows].reshape(tp * rows, -1))
    x_rows += [gather_axis(block, "bl") for block in x_near[3:]]
    g_first = swap(g_late, "hd", 1)
    m_up = spread_group(up_own)
    smalls = m_heads[:, rows:].reshape(tp, -1)[:, : rp * kinds * rows]
    smalls = smalls.reshape(tp, rp, kinds, rows).transpose(1, 0, 2, 3).reshape(n_dev, kinds, rows)
    smalls = smalls.astype(f32)
    vectors = smalls[:, :5].transpose(1, 0, 2).reshape(5, D)
    nq = qkv_bias.shape[0] // rows
    b_qkv = smalls[:, 5 : 5 + nq].reshape(3, HEADS, HS)
    b_up = smalls[:, 5 + nq :].reshape(tp, ffl)
    b_qkv = lax.dynamic_index_in_dim(b_qkv, t, 1, keepdims=False).reshape(1, 3 * HS)
    b_up = lax.dynamic_index_in_dim(b_up, t, 0, keepdims=True)

    row = jnp.arange(group_len, dtype=jnp.int32)
    inside = ((row // sub_len) ^ t) * sub_len + row % sub_len
    query_places = bh * group_len + inside
    key_places = jnp.concatenate([(bh ^ d) * group_len + inside for d in range(bh_size)])
    tables = rotary_tables(query_places.astype(f32))

    x_rows, g_first, m_up, g_late, down_own, vectors, b_qkv, tables = join(
        x_rows, g_first, m_up, g_late, down_own, vectors, b_qkv, tables
    )
    w_up = spread_rest(m_up)
    x_blocks = [row[far] for far in range(bl_size) for row in x_rows]
    g_rows = [g_side, gather_axis(g_first, "bl")]
    m_down = spread_group(down_own)
    attn_in, mlp_in, query, kv, average, inverse = call(
        functools.partial(project_kernel, tp),
        [
            ((group_len, D), bf16),
            ((group_len, D), bf16),
            ((group_len, HS), bf16),
            ((group_len, 2 * HS), bf16),
            ((group_len, 1), f32),
            ((group_len, 1), f32),
        ],
        *x_blocks, vectors, w_heads, b_qkv, *tables,
    )
    g_rows, m_down, kv, mlp_in, g_late = join(g_rows, m_down, kv, mlp_in, g_late)
    w_down = spread_rest(m_down)
    kv_blocks = gather_axis(kv, "bh")
    hd_size = lax.axis_size("hd")
    g_near = [g_first] + [swap(g_late, "hd", d) for d in range(2, 3 if hd_size == 4 else hd_size)]
    g_near, kv_blocks, mlp_in = join(g_near, kv_blocks, mlp_in)
    g_near = gather_end(g_late, g_near)
    g_rows += [gather_axis(block, "bl") for block in g_near[2:]]
    activated, slope = call(
        forward_kernel, [((group_len, ffl), bf16), ((group_len, ffl), f32)], mlp_in, w_up, b_up
    )
    g_rows, activated, slope = join(g_rows, activated, slope)
    g_blocks = [row[far] for far in range(bl_size) for row in g_rows]
    g_all, grad_att = call(
        functools.partial(cotangent_kernel, tp),
        [((group_len, D), bf16), ((group_len, HS), bf16)],
        *g_blocks, w_heads,
    )
    down_half = collect_dp(mm_tn(g_all, activated).astype(bf16))
    kv_all = jnp.concatenate(kv_blocks, axis=0)
    down_half, grad_att, kv_all = join(down_half, grad_att, kv_all)
    down_mine = collect_bh(*down_half)
    attended, grad_query, grad_kv = call(
        attention_kernel if kv_all.shape[0] <= KEYS else long_attention_kernel,
        [
            ((group_len, HS), bf16),
            ((group_len, HS), bf16),
            ((kv_all.shape[0], 2 * HS), bf16),
        ],
        query, grad_att, kv_all, query_places[None, :], key_places[:, None],
        scratch=[pltpu.VMEM((kv_all.shape[0], 2 * HS), f32)],
    )
    attended, grad_query, grad_kv, down_mine = join(attended, grad_query, grad_kv, down_mine)
    grad_kv = grad_kv.reshape(bh_size, group_len, 2 * HS)
    grad_kv = [grad_kv[0]] + [swap(grad_kv[d], "bh", d) for d in range(1, bh_size)]
    down_grad = collect_group(add_others(*down_mine))
    kinds = [(reach, bf16)] * (bl_size - 1) + [(reach, f32)]
    *out_far, out_own = [
        term.reshape(-1, sub_len, D)
        for term in output_terms(attended, activated, w_heads, w_down, kinds)
    ]
    grad_pre_up, up_bias_term = call(
        backward_kernel, [((group_len, ffl), bf16), ((1, ffl), f32)], g_all, w_down, slope
    )
    up_term = mm_tn(mlp_in, grad_pre_up).astype(bf16)
    grad_kv, down_grad, grad_pre_up, up_term, out_far, out_own = join(
        grad_kv, down_grad, grad_pre_up, up_term, out_far, out_own
    )
    parts = groups()
    up_mine = collect_rest(up_term)
    far = send_far(out_far, parts[0])
    grad_project, qkv_bias_term = call(
        functools.partial(turn_back_kernel, bh_size),
        [((group_len, 3 * HS), bf16), ((1, 3 * HS), f32)],
        grad_query, *grad_kv, *tables,
    )
    qkv_term = mm_tn(attn_in, grad_project).astype(bf16)
    dense_term = mm_tn(g_all, attended).astype(bf16)
    far, qkv_term, dense_term, grad_project, out_far = join(
        far, qkv_term, dense_term, grad_project, out_far
    )
    qkv_half, dense_half = collect_dp(qkv_term), collect_dp(dense_term)
    handed = send_near(add_far(out_own, far), {})
    far = send_far(out_far, parts[1])
    *in_far, in_own, sums = input_terms(
        x_blocks, average, inverse, grad_project, grad_pre_up, w_heads, w_up, vectors, kinds
    )
    in_far = [term.reshape(-1, sub_len, D) for term in in_far]
    in_own = in_own.reshape(-1, sub_len, D)
    qkv_half, dense_half, handed, far, in_far, in_own, out_far = join(
        qkv_half, dense_half, handed, far, in_far, in_own, out_far
    )
    qkv_mine, dense_mine = collect_bh(*qkv_half), collect_bh(*dense_half)
    near = handed | send_near(add_far(out_own, far), handed)
    far = send_far(out_far, parts[2] + parts[3])
    qkv_mine, dense_mine, near, far, in_far = join(qkv_mine, dense_mine, near, far, in_far)
    heads_grad = collect_group(
        jnp.concatenate([add_others(*qkv_mine), add_others(*dense_mine)], axis=1)
    )
    rest = add_far(out_own, far)
    near = near | send_near(rest, {})
    far = send_far(in_far, parts[0] + parts[1])
    projected = rest[0]
    down_grad = down_grad.astype(f32).transpose(1, 0, 2).reshape(rows, ff)
    heads_grad, near, far, in_far, down_grad, up_mine, projected = join(
        heads_grad, near, far, in_far, down_grad, up_mine, projected
    )
    output = (x_own.astype(f32) + add_near(projected, near) + vectors[4:5]).astype(bf16)
    up_grad = collect_group(up_mine)
    upper = add_far(in_own, far)
    handed = send_near({d: upper[d] for d in parts[0]}, {})
    far = send_far(in_far, parts[2] + parts[3])
    heads_grad = heads_grad.astype(f32)
    dense_grad = heads_grad[:, :, 3 * HS :].transpose(1, 0, 2).reshape(rows, D)
    qkv_grad = (
        heads_grad[:, :, : 3 * HS]
        .reshape(tp, rows, 3, HS)
        .transpose(1, 2, 0, 3)
        .reshape(rows, 3 * D)
    )
    sums = jnp.concatenate([sums, jnp.sum(g_own.astype(f32), axis=0, keepdims=True)], axis=0)
    qkv_bias_full = lax.dynamic_update_slice(
        jnp.zeros((3, HEADS, HS), f32), qkv_bias_term.reshape(3, 1, HS), (0, t, 0)
    )
    up_bias_full = lax.dynamic_update_slice(jnp.zeros((tp, ffl), f32), up_bias_term, (t, 0))
    small_terms = jnp.concatenate(
        [
            sums.reshape(5, n_dev, rows).transpose(1, 0, 2),
            qkv_bias_full.reshape(n_dev, nq, rows),
            up_bias_full.reshape(n_dev, -1, rows),
        ],
        axis=1,
    )
    upper = {d: upper[d] for d in parts[1]}
    up_grad, handed, far, output, dense_grad, qkv_grad, small_terms, upper = join(
        up_grad, handed, far, output, dense_grad, qkv_grad, small_terms, upper
    )
    lower = add_far(in_own, far)
    near = handed | send_near(upper | lower, handed)
    small = lax.all_to_all(small_terms, ALL, split_axis=0, concat_axis=0, tiled=True)
    up_grad = up_grad.astype(f32).transpose(1, 0, 2).reshape(rows, ff)
    near, small, up_grad = join(near, small, up_grad)
    grad_normed = add_near(lower[0], near)
    small = jnp.sum(small, axis=0)
    own = x_own.astype(f32)
    own_average, own_inverse = statistics(own)
    own_normed = (own - own_average) * own_inverse
    grad_hidden = g_own.astype(f32) + own_inverse * (
        grad_normed
        - jnp.mean(grad_normed, axis=1, keepdims=True)
        - own_normed * jnp.mean(grad_normed * own_normed, axis=1, keepdims=True)
    )
    return (
        output.reshape(seq_count, sub_len, D),
        grad_hidden.reshape(seq_count, sub_len, D),
        small[0],
        small[1],
        small[2],
        small[3],
        qkv_grad,
        small[5 : 5 + nq].reshape(-1),
        dense_grad,
        up_grad,
        small[5 + nq :].reshape(-1),
        down_grad,
        small[4],
    )


def solution(mesh):
    dp, blk, hd = (mesh.shape[name] for name in ("dp", "blk", "hd"))
    low = HEADS // hd
    inner = Mesh(mesh.devices.reshape(dp, blk // low, low, hd), ALL)
    token = P("dp", ("bh", "bl", "hd"), None)
    vector = P(ALL)
    matrix = P(ALL, None)
    return jax.shard_map(
        per_device,
        mesh=inner,
        in_specs=(
            token, vector, vector, vector, vector, matrix, vector,
            matrix, matrix, vector, matrix, vector, token,
        ),
        out_specs=(
            token, token, vector, vector, vector, vector, matrix, vector,
            matrix, matrix, vector, matrix, vector,
        ),
        check_vma=False,
    )
```

profile of v0, /device:TPU:0, one launch (start us, length us, event | category | flops | bytes accessed | tf_op | source)
XLA Modules:
  0.0 502.1 jit_solution(15509658473984917532)
XLA Ops:
  9.4 3.0 collective-permute-start.4
  14.0 2.6 collective-permute-start.1
  23.7 13.4 %collective-permute-done.refs_1_ = bf16[128,2048]{1,0:T(8,128)(2,1)S(1)} collective-permute-done((bf16[128,2048]{1,0:T(8,128)(2,1)}, bf16[128,2048]{1,0:T(8,128)(2,1)S(1)}, u32[]{:S(2)}, u32[]{:S(2)}) %collective-permute-start) | collective-permute-done | bytes 524320 | tf_op jit(solution)/shard_map/ppermute | solution.py:57
  37.1 2.4 collective-permute-done.1.refs_2_
  41.0 3.6 all-to-all-start
  44.6 1.9 collective-permute-start.6
  48.5 2.3 copy.100
  50.8 24.8 %collective-permute-done.6.refs_3_ = bf16[128,2048]{1,0:T(8,128)(2,1)S(1)} collective-permute-done((bf16[128,2048]{1,0:T(8,128)(2,1)S(1)}, bf16[128,2048]{1,0:T(8,128)(2,1)S(1)}, u32[]{:S(2)}, u32[]{:S(2)}) %collective-permute-start.6) | collective-permute-done | bytes 524320 | tf_op jit(solution)/shard_map/ppermute | solution.py:57
  76.4 4.1 collective-permute-done.8.refs_6_
  81.7 4.5 all-to-all-start.1
  86.3 3.2 multiply_sine_fusion
  89.4 2.4 copy.99
  92.0 2.3 maximum_maximum_fusion.refs_11_.refs_3_
  94.3 2.6 maximum_maximum_fusion.2
  96.9 2.0 collective-permute-start.9
  102.2 12.8 %collective-permute-done.9.refs_7_ = bf16[128,2048]{1,0:T(8,128)(2,1)} collective-permute-done((bf16[128,2048]{1,0:T(8,128)(2,1)S(1)}, bf16[128,2048]{1,0:T(8,128)(2,1)}, u32[]{:S(2)}, u32[]{:S(2)}) %collective-permute-start.9) | collective-permute-done | bytes 524320 | tf_op jit(solution)/shard_map/ppermute | solution.py:57
  114.9 4.9 collective-permute-done.10.refs_1_
  120.8 3.6 all-to-all-start.2
  124.5 1.9 collective-permute-start.11
  126.4 13.3 %shard_map.228 = (bf16[1024,2048]{1,0:T(8,128)(2,1)}, bf16[1024,2048]{1,0:T(8,128)(2,1)}, bf16[1024,256]{1,0:T(8,128)(2,1)}, bf16[1024,512]{1,0:T(8,128)(2,1)}, f32[1024,1]{1,0:T(8,128)}, /*index=5*/f32[1024,1]{1,0:T(8,128)}) custom-call(bf16[128,2048]{1,0:T(8,128)(2,1)} %bitcast.188, bf16[128,2048]{1,0:T(8,128)(2,1)} %copy-done.9, ...), custom_call_target="tpu_custom_call" | custom-call | flops 1 | bytes 1 | tf_op jit(solution)/shard_map/pallas_call | solution.py:172
  139.6 6.3 %collective-permute-done.11.refs_5_ = bf16[128,2048]{1,0:T(8,128)(2,1)S(1)} collective-permute-done((bf16[128,2048]{1,0:T(8,128)(2,1)}, bf16[128,2048]{1,0:T(8,128)(2,1)S(1)}, u32[]{:S(2)}, u32[]{:S(2)}) %collective-permute-start.11) | collective-permute-done | bytes 524320 | tf_op jit(solution)/shard_map/ppermute | solution.py:57
  146.0 4.1 all-to-all-done.2
  151.3 22.5 %collective-permute-done.12.refs_2_ = bf16[128,2048]{1,0:T(8,128)(2,1)S(1)} collective-permute-done((bf16[128,2048]{1,0:T(8,128)(2,1)S(1)}, bf16[128,2048]{1,0:T(8,128)(2,1)S(1)}, u32[]{:S(2)}, u32[]{:S(2)}) %collective-permute-start.12) | collective-permute-done | bytes 524320 | tf_op jit(solution)/shard_map/ppermute | solution.py:57
  176.1 10.7 %collective-permute-done.15.refs_3_ = bf16[128,2048]{1,0:T(8,128)(2,1)S(1)} collective-permute-done((bf16[128,2048]{1,0:T(8,128)(2,1)S(1)}, bf16[128,2048]{1,0:T(8,128)(2,1)S(1)}, u32[]{:S(2)}, u32[]{:S(2)}) %collective-permute-start.15) | collective-permute-done | bytes 524320 | tf_op jit(solution)/shard_map/ppermute | solution.py:57
  186.8 1.9 collective-permute-start.16
  189.5 12.8 %shard_map.229 = (bf16[1024,1024]{1,0:T(8,128)(2,1)}, f32[1024,1024]{1,0:T(8,128)}) custom-call(bf16[1024,2048]{1,0:T(8,128)(2,1)} %get-tuple-element.195.mlp_ref, bf16[2048,1024]{1,0:T(8,128)(2,1)} %all-gather.6.cloned.1.call-done.w_ref.refs_13_, f32[1,1024]{1,0:T(1,128)} %constant_dynamic-slice_fusion.b_ref), custom_call_target="tpu_custom_call" | custom-call | flops 1 | bytes 1 | tf_op jit(solution)/shard_map/pallas_call | solution.py:172
  203.2 7.5 %shard_map.230 = (bf16[1024,2048]{1,0:T(8,128)(2,1)}, bf16[1024,256]{1,0:T(8,128)(2,1)}) custom-call(bf16[128,2048]{1,0:T(8,128)(2,1)} %bitcast.195, bf16[128,2048]{1,0:T(8,128)(2,1)} %collective-permute-done.10.refs_1_, bf16[128,2048]{1,0:T(8,128)(2,1)} %copy-done.22, bf16[128,2048]{1,0:T(8,128)(2,1)} %copy-done.23, ...), custom_call_target="tpu_custom_call" | custom-call | flops 1 | bytes 1 | tf_op jit(solution)/shard_map/pallas_call | solution.py:172
  210.6 7.0 %convolution_convert_fusion.1 = bf16[2048,1024]{1,0:T(8,128)(2,1)S(1)} fusion(bf16[1024,2048]{1,0:T(8,128)(2,1)} %get-tuple-element.207.g_ref, bf16[1024,1024]{1,0:T(8,128)(2,1)S(1)} %copy-done.17), kind=kOutput, calls=%fused_computation.2 | convolution fusion | flops 4297064448 | bytes 10485760 | tf_op jit(solution)/shard_map/dot_general | solution.py:48
  217.7 1.8 dynamic-slice_bitcast_fusion
  219.5 2.7 pad_maximum_fusion.kv_ref
  222.2 1.8 collective-permute-done.17
  224.0 2.5 add_convert_fusion
  230.1 18.1 %shard_map.231 = (bf16[1024,256]{1,0:T(8,128)(2,1)}, bf16[1024,256]{1,0:T(8,128)(2,1)}, bf16[2048,512]{1,0:T(8,128)(2,1)}) custom-call(bf16[1024,256]{1,0:T(8,128)(2,1)} %get-tuple-element.179.q_ref, bf16[1024,256]{1,0:T(8,128)(2,1)} %get-tuple-element.212.g_ref, bf16[2048,512]{1,0:T(8,128)(2,1)} %pad_maximum_fusion.kv_ref, s32[1,1024]{1,0:T(1,128)} %fusion.27.qpos_ref, ...), custom_call_target="tpu_custom_call" | custom-call | flops 1 | bytes 1 | tf_op jit(solution)/shard_map/pallas_call | solution.py:172
  248.2 3.8 collective-permute-done.18
  253.4 4.8 all-to-all-start.3
  258.3 3.0 fusion.38
  262.6 11.2 %shard_map.232 = (bf16[1024,1024]{1,0:T(8,128)(2,1)}, f32[1,1024]{1,0:T(1,128)}) custom-call(bf16[1024,2048]{1,0:T(8,128)(2,1)} %get-tuple-element.207.g_ref, bf16[2048,1024]{1,0:T(8,128)(2,1)} %all-gather.8.cloned.1.call-done.w_ref.down_ref, f32[1024,1024]{1,0:T(8,128)} %get-tuple-element.223.slope_ref), custom_call_target="tpu_custom_call" | custom-call | flops 1 | bytes 1 | tf_op jit(solution)/shard_map/pallas_call | solution.py:172
  273.9 11.8 %shard_map.233 = (bf16[512,2048]{1,0:T(8,128)(2,1)}, f32[512,2048]{1,0:T(8,128)}) custom-call(bf16[1024,256]{1,0:T(8,128)(2,1)} %get-tuple-element.225.att_ref, bf16[1024,1024]{1,0:T(8,128)(2,1)} %get-tuple-element.208.act_ref, bf16[2048,1024]{1,0:T(8,128)(2,1)} %all-gather.4.cloned.1.call-done.refs_9_.refs_8_.dense_ref.refs_12_, ...), custom_call_target="tpu_custom_call" | custom-call | flops 1 | bytes 1 | tf_op jit(solution)/shard_map/pallas_call | solution.py:172
  285.6 8.4 %convolution_convert_fusion = bf16[2048,1024]{1,0:T(8,128)(2,1)} fusion(bf16[1024,2048]{1,0:T(8,128)(2,1)} %get-tuple-element.195.mlp_ref, bf16[1024,1024]{1,0:T(8,128)(2,1)S(1)} %copy-done.8), kind=kOutput, calls=%fused_computation.1 | convolution fusion | flops 4297064448 | bytes 10485760 | tf_op jit(solution)/shard_map/dot_general | solution.py:48
  295.4 3.5 convolution_convert_fusion.3
  300.0 2.0 collective-permute-start.20
  302.1 5.0 %shard_map.234 = (bf16[1024,768]{1,0:T(8,128)(2,1)}, f32[1,768]{1,0:T(1,128)}) custom-call(bf16[1024,256]{1,0:T(8,128)(2,1)} %get-tuple-element.230.refs_0_, bf16[1024,512]{1,0:T(8,128)(2,1)} %get-tuple-element.231.refs_1_, bf16[1024,512]{1,0:T(8,128)(2,1)} %copy-done.20, f32[1024,128]{1,0:T(8,128)} %maximum_maximum_fusion.refs_11_.refs_3_, ...), custom_call_target="tpu_custom_call" | custom-call | flops 1 | bytes 1 | tf_op jit(solution)/shard_map/pallas_call | solution.py:172
  307.1 6.2 %convolution_convert_fusion.2 = bf16[2048,768]{1,0:T(8,128)(2,1)S(1)} fusion(bf16[1024,2048]{1,0:T(8,128)(2,1)} %get-tuple-element.229, bf16[1024,768]{1,0:T(8,128)(2,1)} %get-tuple-element.241.refs_10_), kind=kOutput, calls=%fused_computation.3 | convolution fusion | flops 3222798336 | bytes 8912896 | tf_op jit(solution)/shard_map/dot_general | solution.py:48
  316.9 2.1 fusion.18
  320.3 1.9 slice_bitcast_fusion.7
  323.4 15.0 %shard_map.235 = (bf16[512,2048]{1,0:T(8,128)(2,1)}, f32[512,2048]{1,0:T(8,128)}, f32[4,2048]{1,0:T(4,128)}) custom-call(bf16[128,2048]{1,0:T(8,128)(2,1)} %bitcast.189, bf16[128,2048]{1,0:T(8,128)(2,1)} %copy-done.9, bf16[128,2048]{1,0:T(8,128)(2,1)} %copy-done.10, bf16[128,2048]{1,0:T(8,128)(2,1)} %copy-done.11, ...), custom_call_target="tpu_custom_call" | custom-call | flops 1 | bytes 1 | tf_op jit(solution)/shard_map/pallas_call | solution.py:172
  339.6 1.8 add_convert_fusion.1
  343.9 2.4 collective-permute-start.27
  350.1 16.0 %collective-permute-done.26 = bf16[512,256]{1,0:T(8,128)(2,1)S(1)} collective-permute-done((bf16[512,256]{1,0:T(8,128)(2,1)S(1)}, bf16[512,256]{1,0:T(8,128)(2,1)S(1)}, u32[]{:S(2)}, u32[]{:S(2)}) %collective-permute-start.26) | collective-permute-done | bytes 262176 | tf_op jit(solution)/shard_map/ppermute | solution.py:57
  366.2 3.1 collective-permute-done.27
  372.7 3.6 all-to-all-start.4
  376.5 3.1 bitcast_add_fusion.4
  379.5 1.9 collective-permute-start.30
  385.4 20.4 %collective-permute-done.30 = bf16[128,2048]{1,0:T(8,128)(2,1)S(1)} collective-permute-done((bf16[128,2048]{1,0:T(8,128)(2,1)S(1)}, bf16[128,2048]{1,0:T(8,128)(2,1)S(1)}, u32[]{:S(2)}, u32[]{:S(2)}) %collective-permute-start.30) | collective-permute-done | bytes 524320 | tf_op jit(solution)/shard_map/ppermute | solution.py:57
  406.6 5.8 %collective-permute-done.32 = bf16[128,2048]{1,0:T(8,128)(2,1)} collective-permute-done((bf16[128,2048]{1,0:T(8,128)(2,1)S(1)}, bf16[128,2048]{1,0:T(8,128)(2,1)}, u32[]{:S(2)}, u32[]{:S(2)}) %collective-permute-start.32) | collective-permute-done | bytes 524320 | tf_op jit(solution)/shard_map/ppermute | solution.py:57
  412.4 4.3 all-to-all-start.5
  421.1 2.6 bitcast_add_fusion.2
  423.7 1.9 collective-permute-start.33
  429.6 2.6 reshape.345
  436.1 10.7 %collective-permute-done.33 = bf16[128,2048]{1,0:T(8,128)(2,1)} collective-permute-done((bf16[128,2048]{1,0:T(8,128)(2,1)}, bf16[128,2048]{1,0:T(8,128)(2,1)}, u32[]{:S(2)}, u32[]{:S(2)}) %collective-permute-start.33) | collective-permute-done | bytes 524320 | tf_op jit(solution)/shard_map/ppermute | solution.py:57
  447.3 8.7 %collective-permute-done.35 = bf16[128,2048]{1,0:T(8,128)(2,1)} collective-permute-done((bf16[128,2048]{1,0:T(8,128)(2,1)}, bf16[128,2048]{1,0:T(8,128)(2,1)}, u32[]{:S(2)}, u32[]{:S(2)}) %collective-permute-start.35) | collective-permute-done | bytes 524320 | tf_op jit(solution)/shard_map/ppermute | solution.py:57
  460.6 5.1 %all-to-all-start.6 = ((f32[32,1,768]{2,1,0:T(1,128)}), f32[32,1,768]{2,1,0:T(1,128)S(1)}, u32[]{:S(2)}, u32[]{:S(2)}) async-start(f32[32,1,768]{2,1,0:T(1,128)} %reshape.366), calls=%async_computation.7 | async-start | bytes 196608 | tf_op jit(solution)/shard_map/all_to_all | solution.py:666
  468.6 19.2 %all-to-all-done.6 = f32[32,1,768]{2,1,0:T(1,128)S(1)} async-done(((f32[32,1,768]{2,1,0:T(1,128)}), f32[32,1,768]{2,1,0:T(1,128)S(1)}, u32[]{:S(2)}, u32[]{:S(2)}) %all-to-all-start.6) | async-done | bytes 98336 | tf_op jit(solution)/shard_map/all_to_all | solution.py:666
  490.2 2.2 fusion.36
  (239 shorter events, 81.7 us)
Async XLA Ops:
  9.4 9.2 %collective-permute-start.4 = (bf16[1,12,64]{2,1,0:T(8,128)(2,1)S(1)}, bf16[1,12,64]{2,1,0:T(8,128)(2,1)S(1)}, u32[]{:S(2)}, u32[]{:S(2)}) collective-permute-start(bf16[1,12,64]{2,1,0:T(8,128)(2,1)S(1)} %bitcast.239), channel_id=1, source_target_pairs={{0,8},{8,0},{1,9},{9,1},{2,10},{10,2},{3,11},{11,3},{4,12},{12,4},... | collective-permute-start | bytes 4616 | tf_op jit(solution)/shard_map/ppermute | solution.py:57
  12.4 24.7 %collective-permute-start = (bf16[128,2048]{1,0:T(8,128)(2,1)}, bf16[128,2048]{1,0:T(8,128)(2,1)S(1)}, u32[]{:S(2)}, u32[]{:S(2)}) collective-permute-start(bf16[128,2048]{1,0:T(8,128)(2,1)} %bitcast.185), channel_id=1, source_target_pairs={{0,1},{1,0},{2,3},{3,2},{4,5},{5,4},{6,7},{7,6},{8,9},{9,8},{10,11... | collective-permute-start | bytes 1572872 | tf_op jit(solution)/shard_map/ppermute | solution.py:57
  14.0 25.5 %collective-permute-start.1 = (bf16[128,2048]{1,0:T(8,128)(2,1)}, bf16[128,2048]{1,0:T(8,128)(2,1)S(1)}, u32[]{:S(2)}, u32[]{:S(2)}) collective-permute-start(bf16[128,2048]{1,0:T(8,128)(2,1)} %bitcast.186), channel_id=1, source_target_pairs={{0,2},{1,3},{2,0},{3,1},{4,6},{5,7},{6,4},{7,5},{8,10},{9,11},{10,... | collective-permute-start | bytes 1572872 | tf_op jit(solution)/shard_map/ppermute | solution.py:57
  16.6 22.9 %collective-permute-start.2 = (bf16[128,2048]{1,0:T(8,128)(2,1)}, bf16[128,2048]{1,0:T(8,128)(2,1)}, u32[]{:S(2)}, u32[]{:S(2)}) collective-permute-start(bf16[128,2048]{1,0:T(8,128)(2,1)} %bitcast.187), channel_id=1, source_target_pairs={{0,4},{4,0},{1,5},{5,1},{2,6},{6,2},{3,7},{7,3},{8,12},{12,8},{9,1... | collective-permute-start | bytes 1572872 | tf_op jit(solution)/shard_map/ppermute | solution.py:57
  18.1 22.9 %collective-permute-start.3 = (bf16[128,2048]{1,0:T(8,128)(2,1)}, bf16[128,2048]{1,0:T(8,128)(2,1)}, u32[]{:S(2)}, u32[]{:S(2)}) collective-permute-start(bf16[128,2048]{1,0:T(8,128)(2,1)} %bitcast.194), channel_id=1, source_target_pairs={{0,4},{4,0},{1,5},{5,1},{2,6},{6,2},{3,7},{7,3},{8,12},{12,8},{9,1... | collective-permute-start | bytes 1572872 | tf_op jit(solution)/shard_map/ppermute | solution.py:57
  18.6 3.7 collective-permute-start.5
  37.1 13.7 %copy-start.9 = (bf16[128,2048]{1,0:T(8,128)(2,1)}, bf16[128,2048]{1,0:T(8,128)(2,1)S(1)}, u32[]{:S(2)}) copy-start(bf16[128,2048]{1,0:T(8,128)(2,1)S(1)} %collective-permute-done.refs_1_) | copy-start | bytes 1572868
  39.5 11.3 %copy-start.10 = (bf16[128,2048]{1,0:T(8,128)(2,1)}, bf16[128,2048]{1,0:T(8,128)(2,1)S(1)}, u32[]{:S(2)}) copy-start(bf16[128,2048]{1,0:T(8,128)(2,1)S(1)} %collective-permute-done.1.refs_2_) | copy-start | bytes 1572868
  41.0 39.6 %all-to-all-start = ((bf16[8,72,1024]{2,1,0:T(8,128)(2,1)}), bf16[8,72,1024]{2,1,0:T(8,128)(2,1)S(1)}, u32[]{:S(2)}, u32[]{:S(2)}) async-start(bf16[8,72,1024]{2,1,0:T(8,128)(2,1)} %pad_maximum_fusion.1), calls=%async_computation | async-start | bytes 2359296 | tf_op jit(solution)/shard_map/all_to_all | solution.py:504
  44.5 81.8 %all-gather.4.cloned.1.call-start = ((), (), s32[]{:S(2)}) async-start(), calls=%async_computation.8 | async-start | bytes 5242880 | tf_op jit(solution)/shard_map/all_gather | solution.py:133
  44.6 31.0 %collective-permute-start.6 = (bf16[128,2048]{1,0:T(8,128)(2,1)S(1)}, bf16[128,2048]{1,0:T(8,128)(2,1)S(1)}, u32[]{:S(2)}, u32[]{:S(2)}) collective-permute-start(bf16[128,2048]{1,0:T(8,128)(2,1)S(1)} %collective-permute-done.1.refs_2_), channel_id=1, source_target_pairs={{0,1},{1,0},{2,3},{3,2},{4,5},{5,4},{6,7},{7,6},{8,9},{9,8},{10,11... | collective-permute-start | bytes 1572872 | tf_op jit(solution)/shard_map/ppermute | solution.py:57
  46.5 29.1 %collective-permute-start.7 = (bf16[128,2048]{1,0:T(8,128)(2,1)S(1)}, bf16[128,2048]{1,0:T(8,128)(2,1)S(1)}, u32[]{:S(2)}, u32[]{:S(2)}) collective-permute-start(bf16[128,2048]{1,0:T(8,128)(2,1)S(1)} %collective-permute-done.refs_1_), channel_id=1, source_target_pairs={{0,4},{4,0},{1,5},{5,1},{2,6},{6,2},{3,7},{7,3},{8,12},{12,8},{9,1... | collective-permute-start | bytes 1572872 | tf_op jit(solution)/shard_map/ppermute | solution.py:57
  48.0 32.6 %collective-permute-start.8 = (bf16[128,2048]{1,0:T(8,128)(2,1)S(1)}, bf16[128,2048]{1,0:T(8,128)(2,1)}, u32[]{:S(2)}, u32[]{:S(2)}) collective-permute-start(bf16[128,2048]{1,0:T(8,128)(2,1)S(1)} %collective-permute-done.1.refs_2_), channel_id=1, source_target_pairs={{0,4},{4,0},{1,5},{5,1},{2,6},{6,2},{3,7},{7,3},{8,12},{12,8},{9,1... | collective-permute-start | bytes 1572872 | tf_op jit(solution)/shard_map/ppermute | solution.py:57
  75.5 6.1 %copy-start.11 = (bf16[128,2048]{1,0:T(8,128)(2,1)}, bf16[128,2048]{1,0:T(8,128)(2,1)S(1)}, u32[]{:S(2)}) copy-start(bf16[128,2048]{1,0:T(8,128)(2,1)S(1)} %collective-permute-done.6.refs_3_) | copy-start | bytes 1572868
  81.7 38.1 %all-to-all-start.1 = ((bf16[8,64,1024]{2,1,0:T(8,128)(2,1)}), bf16[8,64,1024]{2,1,0:T(8,128)(2,1)S(1)}, u32[]{:S(2)}, u32[]{:S(2)}) async-start(bf16[8,64,1024]{2,1,0:T(8,128)(2,1)} %bitcast.206), calls=%async_computation.1 | async-start | bytes 2097152 | tf_op jit(solution)/shard_map/all_to_all | solution.py:128
  86.2 103.3 %all-gather.6.cloned.1.call-start = ((), (), s32[]{:S(2)}) async-start(), calls=%async_computation.9 | async-start | bytes 5242880 | tf_op jit(solution)/shard_map/all_gather | solution.py:133
  92.0 6.9 %copy-start.1 = (bf16[1,128,2048]{2,1,0:T(8,128)(2,1)S(1)}, bf16[1,128,2048]{2,1,0:T(8,128)(2,1)}, u32[]{:S(2)}) copy-start(bf16[1,128,2048]{2,1,0:T(8,128)(2,1)} %param.25) | copy-start | bytes 1572868
  96.9 18.0 %collective-permute-start.9 = (bf16[128,2048]{1,0:T(8,128)(2,1)S(1)}, bf16[128,2048]{1,0:T(8,128)(2,1)}, u32[]{:S(2)}, u32[]{:S(2)}) collective-permute-start(bf16[128,2048]{1,0:T(8,128)(2,1)S(1)} %copy-done.12), channel_id=1, source_target_pairs={{0,4},{4,0},{1,5},{5,1},{2,6},{6,2},{3,7},{7,3},{8,12},{12,8},{9,1... | collective-permute-start | bytes 1572872 | tf_op jit(solution)/shard_map/ppermute | solution.py:57
  98.9 21.0 %collective-permute-start.10 = (bf16[128,2048]{1,0:T(8,128)(2,1)S(1)}, bf16[128,2048]{1,0:T(8,128)(2,1)}, u32[]{:S(2)}, u32[]{:S(2)}) collective-permute-start(bf16[128,2048]{1,0:T(8,128)(2,1)S(1)} %bitcast.196), channel_id=1, source_target_pairs={{0,1},{1,0},{2,3},{3,2},{4,5},{5,4},{6,7},{7,6},{8,9},{9,8},{10,11... | collective-permute-start | bytes 1572872 | tf_op jit(solution)/shard_map/ppermute | solution.py:57
  120.8 29.2 %all-to-all-start.2 = ((bf16[8,64,1024]{2,1,0:T(8,128)(2,1)}), bf16[8,64,1024]{2,1,0:T(8,128)(2,1)S(1)}, u32[]{:S(2)}, u32[]{:S(2)}) async-start(bf16[8,64,1024]{2,1,0:T(8,128)(2,1)} %bitcast.207), calls=%async_computation.2 | async-start | bytes 2097152 | tf_op jit(solution)/shard_map/all_to_all | solution.py:128
  124.4 138.2 %all-gather.8.cloned.1.call-start = ((), (), s32[]{:S(2)}) async-start(), calls=%async_computation.10 | async-start | bytes 5242880 | tf_op jit(solution)/shard_map/all_gather | solution.py:133
  124.5 21.5 %collective-permute-start.11 = (bf16[128,2048]{1,0:T(8,128)(2,1)}, bf16[128,2048]{1,0:T(8,128)(2,1)S(1)}, u32[]{:S(2)}, u32[]{:S(2)}) collective-permute-start(bf16[128,2048]{1,0:T(8,128)(2,1)} %collective-permute-done.10.refs_1_), channel_id=1, source_target_pairs={{0,4},{4,0},{1,5},{5,1},{2,6},{6,2},{3,7},{7,3},{8,12},{12,8},{9,1... | collective-permute-start | bytes 1572872 | tf_op jit(solution)/shard_map/ppermute | solution.py:57
  146.0 56.4 %copy-start.21 = (bf16[128,2048]{1,0:T(8,128)(2,1)}, bf16[128,2048]{1,0:T(8,128)(2,1)S(1)}, u32[]{:S(2)}) copy-start(bf16[128,2048]{1,0:T(8,128)(2,1)S(1)} %collective-permute-done.11.refs_5_) | copy-start | bytes 1572868
  150.1 38.7 %copy-start.3 = (bf16[8,64,1024]{2,1,0:T(8,128)(2,1)}, bf16[8,64,1024]{2,1,0:T(8,128)(2,1)S(1)}, u32[]{:S(2)}) copy-start(bf16[8,64,1024]{2,1,0:T(8,128)(2,1)S(1)} %all-to-all-done.2) | copy-start | bytes 3145732
  150.1 23.8 %collective-permute-start.13 = (bf16[1024,512]{1,0:T(8,128)(2,1)}, bf16[1024,512]{1,0:T(8,128)(2,1)}, u32[]{:S(2)}, u32[]{:S(2)}) collective-permute-start(bf16[1024,512]{1,0:T(8,128)(2,1)} %get-tuple-element.210), channel_id=1, source_target_pairs={{0,8},{8,0},{1,9},{9,1},{2,10},{10,2},{3,11},{11,3},{4,12},{12,4},... | collective-permute-start | bytes 3145736 | tf_op jit(solution)/shard_map/ppermute | solution.py:57
  150.7 23.1 %collective-permute-start.12 = (bf16[128,2048]{1,0:T(8,128)(2,1)S(1)}, bf16[128,2048]{1,0:T(8,128)(2,1)S(1)}, u32[]{:S(2)}, u32[]{:S(2)}) collective-permute-start(bf16[128,2048]{1,0:T(8,128)(2,1)S(1)} %bitcast.197), channel_id=1, source_target_pairs={{0,2},{1,3},{2,0},{3,1},{4,6},{5,7},{6,4},{7,5},{8,10},{9,11},{10,... | collective-permute-start | bytes 1572872 | tf_op jit(solution)/shard_map/ppermute | solution.py:57
  173.8 28.5 %copy-start.22 = (bf16[128,2048]{1,0:T(8,128)(2,1)}, bf16[128,2048]{1,0:T(8,128)(2,1)S(1)}, u32[]{:S(2)}) copy-start(bf16[128,2048]{1,0:T(8,128)(2,1)S(1)} %collective-permute-done.12.refs_2_) | copy-start | bytes 1572868
  173.8 13.0 %collective-permute-start.15 = (bf16[128,2048]{1,0:T(8,128)(2,1)S(1)}, bf16[128,2048]{1,0:T(8,128)(2,1)S(1)}, u32[]{:S(2)}, u32[]{:S(2)}) collective-permute-start(bf16[128,2048]{1,0:T(8,128)(2,1)S(1)} %collective-permute-done.12.refs_2_), channel_id=1, source_target_pairs={{0,1},{1,0},{2,3},{3,2},{4,5},{5,4},{6,7},{7,6},{8,9},{9,8},{10,11... | collective-permute-start | bytes 1572872 | tf_op jit(solution)/shard_map/ppermute | solution.py:57
  174.7 27.7 %collective-permute-start.14 = (bf16[128,2048]{1,0:T(8,128)(2,1)S(1)}, bf16[128,2048]{1,0:T(8,128)(2,1)S(1)}, u32[]{:S(2)}, u32[]{:S(2)}) collective-permute-start(bf16[128,2048]{1,0:T(8,128)(2,1)S(1)} %collective-permute-done.12.refs_2_), channel_id=1, source_target_pairs={{0,4},{4,0},{1,5},{5,1},{2,6},{6,2},{3,7},{7,3},{8,12},{12,8},{9,1... | collective-permute-start | bytes 1572872 | tf_op jit(solution)/shard_map/ppermute | solution.py:57
  186.8 15.6 %copy-start.23 = (bf16[128,2048]{1,0:T(8,128)(2,1)}, bf16[128,2048]{1,0:T(8,128)(2,1)S(1)}, u32[]{:S(2)}) copy-start(bf16[128,2048]{1,0:T(8,128)(2,1)S(1)} %collective-permute-done.15.refs_3_) | copy-start | bytes 1572868
  186.8 15.6 %collective-permute-start.16 = (bf16[128,2048]{1,0:T(8,128)(2,1)S(1)}, bf16[128,2048]{1,0:T(8,128)(2,1)}, u32[]{:S(2)}, u32[]{:S(2)}) collective-permute-start(bf16[128,2048]{1,0:T(8,128)(2,1)S(1)} %collective-permute-done.15.refs_3_), channel_id=1, source_target_pairs={{0,4},{4,0},{1,5},{5,1},{2,6},{6,2},{3,7},{7,3},{8,12},{12,8},{9,1... | collective-permute-start | bytes 1572872 | tf_op jit(solution)/shard_map/ppermute | solution.py:57
  203.2 7.5 %copy-start.17 = (bf16[1024,1024]{1,0:T(8,128)(2,1)S(1)}, bf16[1024,1024]{1,0:T(8,128)(2,1)}, u32[]{:S(2)}) copy-start(bf16[1024,1024]{1,0:T(8,128)(2,1)} %get-tuple-element.208.act_ref) | copy-start | bytes 6291460
  219.5 4.5 collective-permute-start.17
  226.7 25.3 %collective-permute-start.18 = (bf16[512,1024]{1,0:T(8,128)(2,1)S(1)}, bf16[512,1024]{1,0:T(8,128)(2,1)S(1)}, u32[]{:S(2)}, u32[]{:S(2)}) collective-permute-start(bf16[512,1024]{1,0:T(8,128)(2,1)S(1)} %get-tuple-element.308), channel_id=1, source_target_pairs={{0,8},{8,0},{1,9},{9,1},{2,10},{10,2},{3,11},{11,3},{4,12},{12,4},... | collective-permute-start | bytes 3145736 | tf_op jit(solution)/shard_map/ppermute | solution.py:57
  253.4 40.6 %all-to-all-start.3 = ((bf16[8,64,1024]{2,1,0:T(8,128)(2,1)}), bf16[8,64,1024]{2,1,0:T(8,128)(2,1)S(1)}, u32[]{:S(2)}, u32[]{:S(2)}) async-start(bf16[8,64,1024]{2,1,0:T(8,128)(2,1)} %bitcast.26), calls=%async_computation.3 | async-start | bytes 2097152 | tf_op jit(solution)/shard_map/all_to_all | solution.py:163
  258.2 154.2 %reduce-scatter.2.cloned.1.call-start = ((), (), s32[]{:S(2)}) async-start(), calls=%async_computation.11 | async-start | bytes 5242880 | tf_op jit(solution)/shard_map/reduce_scatter | solution.py:158
  261.3 32.7 %collective-permute-start.19 = (bf16[1024,512]{1,0:T(8,128)(2,1)}, bf16[1024,512]{1,0:T(8,128)(2,1)S(1)}, u32[]{:S(2)}, u32[]{:S(2)}) collective-permute-start(bf16[1024,512]{1,0:T(8,128)(2,1)} %get-tuple-element.306), channel_id=1, source_target_pairs={{0,8},{8,0},{1,9},{9,1},{2,10},{10,2},{3,11},{11,3},{4,12},{12,4},... | collective-permute-start | bytes 3145736 | tf_op jit(solution)/shard_map/ppermute | solution.py:57
  273.9 11.8 %copy-start.8 = (bf16[1024,1024]{1,0:T(8,128)(2,1)S(1)}, bf16[1024,1024]{1,0:T(8,128)(2,1)}, u32[]{:S(2)}) copy-start(bf16[1024,1024]{1,0:T(8,128)(2,1)} %get-tuple-element.242.refs_11_) | copy-start | bytes 6291460
  300.0 13.3 %collective-permute-start.20 = (bf16[128,2048]{1,0:T(8,128)(2,1)S(1)}, bf16[128,2048]{1,0:T(8,128)(2,1)S(1)}, u32[]{:S(2)}, u32[]{:S(2)}) collective-permute-start(bf16[128,2048]{1,0:T(8,128)(2,1)S(1)} %slice_bitcast_fusion.8), channel_id=1, source_target_pairs={{0,4},{4,0},{1,5},{5,1},{2,6},{6,2},{3,7},{7,3},{8,12},{12,8},{9,1... | collective-permute-start | bytes 1572872 | tf_op jit(solution)/shard_map/ppermute | solution.py:57
  315.5 23.0 %collective-permute-start.21 = (bf16[1024,768]{1,0:T(8,128)(2,1)}, bf16[1024,768]{1,0:T(8,128)(2,1)S(1)}, u32[]{:S(2)}, u32[]{:S(2)}) collective-permute-start(bf16[1024,768]{1,0:T(8,128)(2,1)} %get-tuple-element.298), channel_id=1, source_target_pairs={{0,16},{16,0},{1,17},{17,1},{2,18},{18,2},{3,19},{19,3},{4,20},{20... | collective-permute-start | bytes 4718600 | tf_op jit(solution)/shard_map/ppermute | solution.py:57
  316.3 22.1 %collective-permute-start.22 = (bf16[1024,256]{1,0:T(8,128)(2,1)}, bf16[1024,256]{1,0:T(8,128)(2,1)S(1)}, u32[]{:S(2)}, u32[]{:S(2)}) collective-permute-start(bf16[1024,256]{1,0:T(8,128)(2,1)} %get-tuple-element.312), channel_id=1, source_target_pairs={{0,16},{16,0},{1,17},{17,1},{2,18},{18,2},{3,19},{19,3},{4,20},{20... | collective-permute-start | bytes 1572872 | tf_op jit(solution)/shard_map/ppermute | solution.py:57
  319.0 19.4 %collective-permute-start.23 = (bf16[128,2048]{1,0:T(8,128)(2,1)}, bf16[128,2048]{1,0:T(8,128)(2,1)S(1)}, u32[]{:S(2)}, u32[]{:S(2)}) collective-permute-start(bf16[128,2048]{1,0:T(8,128)(2,1)} %fusion.18), channel_id=1, source_target_pairs={{0,1},{1,0},{2,3},{3,2},{4,5},{5,4},{6,7},{7,6},{8,9},{9,8},{10,11... | collective-permute-start | bytes 1572872 | tf_op jit(solution)/shard_map/ppermute | solution.py:57
  322.1 16.3 %collective-permute-start.24 = (bf16[128,2048]{1,0:T(8,128)(2,1)}, bf16[128,2048]{1,0:T(8,128)(2,1)}, u32[]{:S(2)}, u32[]{:S(2)}) collective-permute-start(bf16[128,2048]{1,0:T(8,128)(2,1)} %slice_bitcast_fusion.7), channel_id=1, source_target_pairs={{0,4},{4,0},{1,5},{5,1},{2,6},{6,2},{3,7},{7,3},{8,12},{12,8},{9,1... | collective-permute-start | bytes 1572872 | tf_op jit(solution)/shard_map/ppermute | solution.py:57
  341.6 29.0 %collective-permute-start.25 = (bf16[512,768]{1,0:T(8,128)(2,1)S(1)}, bf16[512,768]{1,0:T(8,128)(2,1)S(1)}, u32[]{:S(2)}, u32[]{:S(2)}) collective-permute-start(bf16[512,768]{1,0:T(8,128)(2,1)S(1)} %get-tuple-element.310), channel_id=1, source_target_pairs={{0,8},{8,0},{1,9},{9,1},{2,10},{10,2},{3,11},{11,3},{4,12},{12,4},... | collective-permute-start | bytes 2359304 | tf_op jit(solution)/shard_map/ppermute | solution.py:57
  343.9 25.3 %collective-permute-start.27 = (bf16[128,2048]{1,0:T(8,128)(2,1)S(1)}, bf16[128,2048]{1,0:T(8,128)(2,1)S(1)}, u32[]{:S(2)}, u32[]{:S(2)}) collective-permute-start(bf16[128,2048]{1,0:T(8,128)(2,1)S(1)} %fusion.17), channel_id=1, source_target_pairs={{0,2},{1,3},{2,0},{3,1},{4,6},{5,7},{6,4},{7,5},{8,10},{9,11},{10,... | collective-permute-start | bytes 1572872 | tf_op jit(solution)/shard_map/ppermute | solution.py:57
  346.4 22.8 %collective-permute-start.28 = (bf16[128,2048]{1,0:T(8,128)(2,1)S(1)}, bf16[128,2048]{1,0:T(8,128)(2,1)S(1)}, u32[]{:S(2)}, u32[]{:S(2)}) collective-permute-start(bf16[128,2048]{1,0:T(8,128)(2,1)S(1)} %get-tuple-element.305), channel_id=1, source_target_pairs={{0,4},{4,0},{1,5},{5,1},{2,6},{6,2},{3,7},{7,3},{8,12},{12,8},{9,1... | collective-permute-start | bytes 1572872 | tf_op jit(solution)/shard_map/ppermute | solution.py:57
  347.3 23.3 %collective-permute-start.29 = (bf16[128,2048]{1,0:T(8,128)(2,1)S(1)}, bf16[128,2048]{1,0:T(8,128)(2,1)S(1)}, u32[]{:S(2)}, u32[]{:S(2)}) collective-permute-start(bf16[128,2048]{1,0:T(8,128)(2,1)S(1)} %get-tuple-element.304), channel_id=1, source_target_pairs={{0,4},{4,0},{1,5},{5,1},{2,6},{6,2},{3,7},{7,3},{8,12},{12,8},{9,1... | collective-permute-start | bytes 1572872 | tf_op jit(solution)/shard_map/ppermute | solution.py:57
  348.7 17.5 %collective-permute-start.26 = (bf16[512,256]{1,0:T(8,128)(2,1)S(1)}, bf16[512,256]{1,0:T(8,128)(2,1)S(1)}, u32[]{:S(2)}, u32[]{:S(2)}) collective-permute-start(bf16[512,256]{1,0:T(8,128)(2,1)S(1)} %get-tuple-element.318), channel_id=1, source_target_pairs={{0,8},{8,0},{1,9},{9,1},{2,10},{10,2},{3,11},{11,3},{4,12},{12,4},... | collective-permute-start | bytes 786440 | tf_op jit(solution)/shard_map/ppermute | solution.py:57
  372.7 39.7 %all-to-all-start.4 = ((bf16[8,64,1024]{2,1,0:T(8,128)(2,1)}), bf16[8,64,1024]{2,1,0:T(8,128)(2,1)S(1)}, u32[]{:S(2)}, u32[]{:S(2)}) async-start(bf16[8,64,1024]{2,1,0:T(8,128)(2,1)} %bitcast.208), calls=%async_computation.4 | async-start | bytes 2097152 | tf_op jit(solution)/shard_map/all_to_all | solution.py:163
  379.5 26.3 %collective-permute-start.30 = (bf16[128,2048]{1,0:T(8,128)(2,1)S(1)}, bf16[128,2048]{1,0:T(8,128)(2,1)S(1)}, u32[]{:S(2)}, u32[]{:S(2)}) collective-permute-start(bf16[128,2048]{1,0:T(8,128)(2,1)S(1)} %get-tuple-element.295), channel_id=1, source_target_pairs={{0,1},{1,0},{2,3},{3,2},{4,5},{5,4},{6,7},{7,6},{8,9},{9,8},{10,11... | collective-permute-start | bytes 1572872 | tf_op jit(solution)/shard_map/ppermute | solution.py:57
  381.6 24.2 %collective-permute-start.31 = (bf16[128,2048]{1,0:T(8,128)(2,1)S(1)}, bf16[128,2048]{1,0:T(8,128)(2,1)S(1)}, u32[]{:S(2)}, u32[]{:S(2)}) collective-permute-start(bf16[128,2048]{1,0:T(8,128)(2,1)S(1)} %get-tuple-element.303), channel_id=1, source_target_pairs={{0,4},{4,0},{1,5},{5,1},{2,6},{6,2},{3,7},{7,3},{8,12},{12,8},{9,1... | collective-permute-start | bytes 1572872 | tf_op jit(solution)/shard_map/ppermute | solution.py:57
  383.1 29.3 %collective-permute-start.32 = (bf16[128,2048]{1,0:T(8,128)(2,1)S(1)}, bf16[128,2048]{1,0:T(8,128)(2,1)}, u32[]{:S(2)}, u32[]{:S(2)}) collective-permute-start(bf16[128,2048]{1,0:T(8,128)(2,1)S(1)} %get-tuple-element.302), channel_id=1, source_target_pairs={{0,4},{4,0},{1,5},{5,1},{2,6},{6,2},{3,7},{7,3},{8,12},{12,8},{9,1... | collective-permute-start | bytes 1572872 | tf_op jit(solution)/shard_map/ppermute | solution.py:57
  385.4 31.3 %copy-start.2 = (bf16[1,128,2048]{2,1,0:T(8,128)(2,1)S(1)}, bf16[1,128,2048]{2,1,0:T(8,128)(2,1)}, u32[]{:S(2)}) copy-start(bf16[1,128,2048]{2,1,0:T(8,128)(2,1)} %param.25) | copy-start | bytes 1572868
  385.4 32.3 %copy-start.35 = (f32[1,1024]{1,0:T(1,128)S(1)}, f32[1,1024]{1,0:T(1,128)}, u32[]{:S(2)}) copy-start(f32[1,1024]{1,0:T(1,128)} %get-tuple-element.273) | copy-start | bytes 12292
  385.4 32.6 %copy-start.36 = (f32[1,768]{1,0:T(1,128)S(1)}, f32[1,768]{1,0:T(1,128)}, u32[]{:S(2)}) copy-start(f32[1,768]{1,0:T(1,128)} %get-tuple-element.272) | copy-start | bytes 9220
  385.4 32.7 %copy-start.34 = (f32[4,2048]{1,0:T(4,128)S(1)}, f32[4,2048]{1,0:T(4,128)}, u32[]{:S(2)}) copy-start(f32[4,2048]{1,0:T(4,128)} %get-tuple-element.271) | copy-start | bytes 98308
  412.4 43.6 %all-to-all-start.5 = ((bf16[8,64,1024]{2,1,0:T(8,128)(2,1)}), bf16[8,64,1024]{2,1,0:T(8,128)(2,1)}, u32[]{:S(2)}, u32[]{:S(2)}) async-start(bf16[8,64,1024]{2,1,0:T(8,128)(2,1)} %bitcast.227), calls=%async_computation.6 | async-start | bytes 2097152 | tf_op jit(solution)/shard_map/all_to_all | solution.py:163
  423.7 23.1 %collective-permute-start.33 = (bf16[128,2048]{1,0:T(8,128)(2,1)}, bf16[128,2048]{1,0:T(8,128)(2,1)}, u32[]{:S(2)}, u32[]{:S(2)}) collective-permute-start(bf16[128,2048]{1,0:T(8,128)(2,1)} %get-tuple-element.293), channel_id=1, source_target_pairs={{0,1},{1,0},{2,3},{3,2},{4,5},{5,4},{6,7},{7,6},{8,9},{9,8},{10,11... | collective-permute-start | bytes 1572872 | tf_op jit(solution)/shard_map/ppermute | solution.py:57
  426.7 20.6 %collective-permute-start.34 = (bf16[128,2048]{1,0:T(8,128)(2,1)}, bf16[128,2048]{1,0:T(8,128)(2,1)}, u32[]{:S(2)}, u32[]{:S(2)}) collective-permute-start(bf16[128,2048]{1,0:T(8,128)(2,1)} %get-tuple-element.301), channel_id=1, source_target_pairs={{0,4},{4,0},{1,5},{5,1},{2,6},{6,2},{3,7},{7,3},{8,12},{12,8},{9,1... | collective-permute-start | bytes 1572872 | tf_op jit(solution)/shard_map/ppermute | solution.py:57
  428.2 27.7 %collective-permute-start.35 = (bf16[128,2048]{1,0:T(8,128)(2,1)}, bf16[128,2048]{1,0:T(8,128)(2,1)}, u32[]{:S(2)}, u32[]{:S(2)}) collective-permute-start(bf16[128,2048]{1,0:T(8,128)(2,1)} %get-tuple-element.300), channel_id=1, source_target_pairs={{0,4},{4,0},{1,5},{5,1},{2,6},{6,2},{3,7},{7,3},{8,12},{12,8},{9,1... | collective-permute-start | bytes 1572872 | tf_op jit(solution)/shard_map/ppermute | solution.py:57
  434.9 23.6 %copy-start.7 = (f32[128,2048]{1,0:T(8,128)S(1)}, f32[128,2048]{1,0:T(8,128)}, u32[]{:S(2)}) copy-start(f32[128,2048]{1,0:T(8,128)} %get-tuple-element.278) | copy-start | bytes 3145732
  457.5 31.9 %collective-permute-start.36 = (bf16[128,2048]{1,0:T(8,128)(2,1)S(1)}, bf16[128,2048]{1,0:T(8,128)(2,1)}, u32[]{:S(2)}, u32[]{:S(2)}) collective-permute-start(bf16[128,2048]{1,0:T(8,128)(2,1)S(1)} %fusion.11), channel_id=1, source_target_pairs={{0,1},{1,0},{2,3},{3,2},{4,5},{5,4},{6,7},{7,6},{8,9},{9,8},{10,11... | collective-permute-start | bytes 1572872 | tf_op jit(solution)/shard_map/ppermute | solution.py:57
  459.7 29.7 %collective-permute-start.37 = (bf16[128,2048]{1,0:T(8,128)(2,1)S(1)}, bf16[128,2048]{1,0:T(8,128)(2,1)S(1)}, u32[]{:S(2)}, u32[]{:S(2)}) collective-permute-start(bf16[128,2048]{1,0:T(8,128)(2,1)S(1)} %add_convert_fusion.4), channel_id=1, source_target_pairs={{0,2},{1,3},{2,0},{3,1},{4,6},{5,7},{6,4},{7,5},{8,10},{9,11},{10,... | collective-permute-start | bytes 1572872 | tf_op jit(solution)/shard_map/ppermute | solution.py:57
  460.6 27.3 %all-to-all-start.6 = ((f32[32,1,768]{2,1,0:T(1,128)}), f32[32,1,768]{2,1,0:T(1,128)S(1)}, u32[]{:S(2)}, u32[]{:S(2)}) async-start(f32[32,1,768]{2,1,0:T(1,128)} %reshape.366), calls=%async_computation.7 | async-start | bytes 196608 | tf_op jit(solution)/shard_map/all_to_all | solution.py:666
  (22 other events, 47.7 us)
Sparse Core Ops, SparseCore 0:
  81.8 33.5 all-gather.3
  121.0 31.5 all-gather.5
  188.9 35.0 all-gather.7
  295.1 45.0 reduce-scatter.1
where the time goes:
time: 512 us; the launch traced here: 502 us
  waiting for transfers between devices  199 us (39%)
  Pallas kernels  94.7 us (18%)
  starting transfers between devices  77.1 us (15%)
  local copies, waits for them, and re-layouts  51.3 us (10%)
  other arithmetic  40 us (8%)
  matrix products  25.1 us (5%)
  between operations  15 us (3%)
    ppermute x38, waiting for transfers between devices, swap(): return lax.ppermute(value, axis, [(i, i ^ distance) for i in range(size)])  176 us
    pallas_call x8, Pallas kernels, call(): pl.pallas_call(kernel, grid=grid, out_shape=[jax.ShapeDtypeStruct(shape,...  94.7 us
    ppermute x38, starting transfers between devices, swap(): return lax.ppermute(value, axis, [(i, i ^ distance) for i in range(size)])  47.5 us
    dot_general x4, matrix products, mm_tn(): lax.dot_general(a, b, (((0,), (0,)), ((), ())), preferred_element_type=f32)  25.1 us
    all_to_all x1, waiting for transfers between devices, per_device(): lax.all_to_all(small_terms, ALL, split_axis=0, concat_axis=0, tiled=True)  19.2 us
    unnamed x80, local copies, waits for them, and re-layouts  12.8 us
    all_to_all x3, starting transfers between devices, collect_group(): return lax.all_to_all(mine, TP, split_axis=0, concat_axis=0, tiled=True)  12.6 us
  transfers between devices with their start and end apart: 49, of which 22 were waited for; matrix products, arithmetic and copies ran while one was open for 19% of the time, Pallas kernels for 19%

commit v1 on v0

--- a/solution.py
+++ b/solution.py
@@ -44,12 +44,13 @@
     return lax.dot_general(a, b, contract_last, preferred_element_type=f32)
 
 
-def mm_tn(a, b):
-    return lax.dot_general(a, b, (((0,), (0,)), ((), ())), preferred_element_type=f32)
-
-
-def join(*values):
-    return lax.optimization_barrier(values)
+class Order:
+    def __init__(self, token):
+        self.token = token
+
+    def join(self, *values):
+        self.token, values = lax.optimization_barrier((self.token, values))
+        return values
 
 
 def swap(value, axis, distance):
@@ -87,41 +88,10 @@
     return value
 
 
-def groups():
-    size = lax.axis_size("hd")
-    part = size // 4
-    return [list(range(size - (g + 1) * part, size - g * part)) for g in range(4)]
-
-
-def send_far(terms, ds):
-    return {d: [swap(term[d], "bl", far + 1) for far, term in enumerate(terms)] for d in ds}
-
-
-def add_far(own, received):
-    return {
-        d: sum((other.astype(f32) for other in others), own[d])
-        for d, others in received.items()
-    }
-
-
-def send_near(blocks, handed):
-    four = lax.axis_size("hd") == 4
-    out = {}
-    for d, block in blocks.items():
-        if d == 0:
-            continue
-        if four and d == 2:
-            block = block + handed[3].astype(f32)
-        out[d] = swap(block.astype(bf16), "hd", 1 if four and d == 3 else d)
-    return out
-
-
-def add_near(own, received):
-    four = lax.axis_size("hd") == 4
-    for d, block in received.items():
-        if not (four and d == 3):
-            own = own + block.astype(f32)
-    return own
+def hand_on(value, distance):
+    if lax.axis_size("hd") == 4 and distance == 3:
+        distance = 1
+    return swap(value, "hd", distance)
 
 
 def spread_group(shard):
@@ -131,31 +101,6 @@
 
 def spread_rest(mine):
     return lax.all_gather(mine, RP, axis=0, tiled=True)
-
-
-def pick(value, axis, distance):
-    return lax.dynamic_index_in_dim(value, lax.axis_index(axis) ^ distance, 0, keepdims=False)
-
-
-def collect_dp(partial):
-    partial = partial.reshape(lax.axis_size("dp"), -1, partial.shape[1])
-    others = [swap(pick(partial, "dp", d), "dp", d) for d in range(1, lax.axis_size("dp"))]
-    return pick(partial, "dp", 0), others
-
-
-def collect_bh(own, others):
-    total = sum((other.astype(f32) for other in others), own.astype(f32)).astype(bf16)
-    total = total.reshape(lax.axis_size("bh"), -1, own.shape[1])
-    others = [swap(pick(total, "bh", d), "bh", d) for d in range(1, lax.axis_size("bh"))]
-    return pick(total, "bh", 0), others
-
-
-def add_others(own, others):
-    return sum((other.astype(f32) for other in others), own.astype(f32)).astype(bf16)
-
-
-def collect_rest(partial):
-    return lax.psum_scatter(partial, RP, scatter_dimension=0, tiled=True)
 
 
 def collect_group(mine):
@@ -187,6 +132,38 @@
         return 0
 
     lax.fori_loop(0, count // TILE, body, 0)
+
+
+def add_kernel(counts, *refs):
+    start = 0
+    ins = refs[: sum(count for count, _ in counts)]
+    outs = refs[len(ins) :]
+    for count, parts in counts:
+        group, ins = ins[:count], ins[count:]
+        here, outs = outs[:parts], outs[parts:]
+        start = 0
+        for out_ref in here:
+            at = slice(start, start + out_ref.shape[0])
+            start += out_ref.shape[0]
+            total = group[0][at, :].astype(f32)
+            for ref in group[1:]:
+                total += ref[at, :].astype(f32)
+            out_ref[...] = total.astype(out_ref.dtype)
+
+
+def add(*groups):
+    counts, outs, ins = [], [], []
+    for arrays, dtype, parts in groups:
+        rows, cols = arrays[0].shape
+        counts.append((len(arrays), parts))
+        outs += [((rows // parts, cols), dtype)] * parts
+        ins += arrays
+    sums = call(functools.partial(add_kernel, counts), outs, *ins)
+    result = []
+    for _, parts in counts:
+        result.append(list(sums[:parts]))
+        sums = sums[parts:]
+    return result
 
 
 def turn(value, tables, sign):
@@ -220,7 +197,7 @@
             attn_ref[at, :] = (normed * vec_ref[0:1, :] + vec_ref[1:2, :]).astype(bf16)
             mlp_ref[at, :] = (normed * vec_ref[2:3, :] + vec_ref[3:4, :]).astype(bf16)
         at = slice(start, start + TILE)
-        project = mm(attn_ref[at, :], w_ref[:, : 3 * HS]) + b_ref[...]
+        project = mm(attn_ref[at, :], w_ref[...]) + b_ref[...]
         tables = own_ref[at, :], above_ref[at, :], below_ref[at, :]
         query = turn(project[:, :HS], tables, 1.0).astype(bf16)
         q_ref[at, :] = (query.astype(f32) * HS**-0.5).astype(bf16)
@@ -235,7 +212,7 @@
         g_ref[i * rows : (i + 1) * rows, :] = g_refs[i][...]
 
     def step(at):
-        out_ref[at, :] = mm(g_ref[at, :], w_ref[:, 3 * HS :]).astype(bf16)
+        out_ref[at, :] = mm(g_ref[at, :], w_ref[...]).astype(bf16)
 
     tiles(g_ref.shape[0], step)
 
@@ -251,40 +228,117 @@
     tiles(mlp_ref.shape[0], step)
 
 
+def forward(mlp_in, w_up, b_up):
+    count, ffl = mlp_in.shape[0], w_up.shape[1]
+    columns = pl.BlockSpec((count, TILE), lambda i: (0, i))
+    return call(
+        forward_kernel,
+        [((count, ffl), bf16), ((count, ffl), f32)],
+        mlp_in, w_up, b_up,
+        grid=(ffl // TILE,),
+        in_specs=[
+            pl.BlockSpec((count, D), lambda i: (0, 0)),
+            pl.BlockSpec((D, TILE), lambda i: (0, i)),
+            pl.BlockSpec((1, TILE), lambda i: (0, i)),
+        ],
+        out_specs=[columns, columns],
+    )
+
+
 def backward_kernel(g_ref, w_ref, slope_ref, out_ref, sum_ref):
-    sum_ref[...] = jnp.zeros_like(sum_ref)
-
-    def step(at):
-        grad = (mm(g_ref[at, :], w_ref[...]) * slope_ref[at, :]).astype(bf16)
-        out_ref[at, :] = grad
-        sum_ref[...] += jnp.sum(grad.astype(f32), axis=0, keepdims=True)
-
-    tiles(g_ref.shape[0], step)
+    grad = (mm(g_ref[...], w_ref[...]) * slope_ref[...]).astype(bf16)
+    out_ref[...] = grad
+    sum_ref[...] = jnp.sum(grad.astype(f32), axis=0, keepdims=True)
+
+
+def backward(g_all, w_down, slope):
+    count, ffl = slope.shape
+    columns = pl.BlockSpec((count, TILE), lambda i: (0, i))
+    return call(
+        backward_kernel,
+        [((count, ffl), bf16), ((1, ffl), f32)],
+        g_all, w_down, slope,
+        grid=(ffl // TILE,),
+        in_specs=[
+            pl.BlockSpec((count, D), lambda i: (0, 0)),
+            pl.BlockSpec((D, TILE), lambda i: (0, i)),
+            columns,
+        ],
+        out_specs=[columns, pl.BlockSpec((1, TILE), lambda i: (0, i))],
+    )
+
+
+def weight_kernel(steps, place_ref, *refs):
+    pairs, (far_ref, own_ref) = refs[:-2], refs[-2:]
+
+    def store(out_ref):
+        start = 0
+        for lhs_ref, rhs_ref in zip(pairs[::2], pairs[1::2]):
+            cols = slice(start, start + rhs_ref.shape[1])
+            start += rhs_ref.shape[1]
+            out_ref[:, cols] = mm(lhs_ref[...].T, rhs_ref[...]).astype(bf16)
+
+    pl.when(pl.program_id(0) < steps)(lambda: store(far_ref))
+    pl.when(pl.program_id(0) >= steps)(lambda: store(own_ref))
+
+
+def weight_terms(*pairs):
+    bh = lax.axis_size("bh")
+    part = D // (2 * bh)
+    tile = min(2 * TILE, part)
+    per = part // tile
+    steps = bh * per
+    place = jnp.stack([lax.axis_index("dp"), lax.axis_index("bh")]).astype(jnp.int32)
+
+    def lhs_at(i, place_ref):
+        core = place_ref[0] ^ jnp.where(i < steps, 1, 0)
+        block = place_ref[1] ^ (i % steps // per)
+        return (0, (core * bh + block) * per + i % per)
+
+    count = pairs[0].shape[0]
+    cols = sum(rhs.shape[1] for rhs in pairs[1::2])
+    specs = []
+    for rhs in pairs[1::2]:
+        specs.append(pl.BlockSpec((count, tile), lhs_at))
+        specs.append(pl.BlockSpec(rhs.shape, lambda i, place_ref: (0, 0)))
+    return pl.pallas_call(
+        functools.partial(weight_kernel, steps),
+        grid_spec=pltpu.PrefetchScalarGridSpec(
+            num_scalar_prefetch=1,
+            grid=(2 * steps,),
+            in_specs=specs,
+            out_specs=[
+                pl.BlockSpec((tile, cols), lambda i, place_ref: (jnp.minimum(i, steps - 1), 0)),
+                pl.BlockSpec((tile, cols), lambda i, place_ref: (jnp.maximum(i - steps, 0), 0)),
+            ],
+        ),
+        out_shape=[jax.ShapeDtypeStruct((D // 2, cols), bf16)] * 2,
+        compiler_params=pltpu.CompilerParams(vmem_limit_bytes=58 * 2**20),
+        cost_estimate=pl.CostEstimate(flops=1, bytes_accessed=1, transcendentals=0),
+    )(place, *pairs)
 
 
 def output_kernel(att_ref, act_ref, dense_ref, down_ref, *out_refs):
-    start = 0
-    for out_ref in (out_refs[-1],) + out_refs[:-1]:
-        at = slice(start, start + out_ref.shape[0])
-        start += out_ref.shape[0]
-        term = mm_nt(att_ref[at, :], dense_ref[...]) + mm_nt(act_ref[at, :], down_ref[...])
-        out_ref[...] = term.astype(out_ref.dtype)
-
-
-def output_terms(attended, activated, w_heads, w_down, kinds):
-    count, ffl = activated.shape
+    term = mm_nt(att_ref[...], dense_ref[...]) + mm_nt(act_ref[...], down_ref[...])
+    rows = out_refs[0].shape[0]
+    for i, out_ref in enumerate(out_refs):
+        out_ref[...] = term[i * rows : (i + 1) * rows].astype(out_ref.dtype)
+
+
+def output_terms(attended, activated, w_heads, w_down, part, count, rows, dtype):
+    ffl, wide = activated.shape[1], 4 * TILE if count * rows <= 512 else 2 * TILE
     return call(
         output_kernel,
-        [((rows, D), dtype) for rows, dtype in kinds],
+        [((rows, D), dtype)] * count,
         attended, activated, w_heads, w_down,
-        grid=(D // TILE,),
+        grid=(D // wide,),
         in_specs=[
-            pl.BlockSpec((count, HS), lambda i: (0, 0)),
-            pl.BlockSpec((count, ffl), lambda i: (0, 0)),
-            pl.BlockSpec((TILE, HS), lambda i: (i, 3)),
-            pl.BlockSpec((TILE, ffl), lambda i: (i, 0)),
+            pl.BlockSpec((count * rows, HS), lambda i: (part, 0)),
+            pl.BlockSpec((count * rows, ffl), lambda i: (part, 0)),
+            pl.BlockSpec((wide, HS), lambda i: (i, 3)),
+            pl.BlockSpec((wide, ffl), lambda i: (i, 0)),
         ],
-        out_specs=[pl.BlockSpec((rows, TILE), lambda i: (0, i)) for rows, _ in kinds],
+        out_specs=[pl.BlockSpec((rows, wide), lambda i: (0, i))] * count,
     )
 
 
@@ -307,14 +361,12 @@
     tiles(dq_ref.shape[0], step)
 
 
-def input_kernel(count, parts, *refs):
+def input_kernel(count, *refs):
     x_refs, refs = refs[:count], refs[count:]
     average_ref, inverse_ref, gp_ref, gu_ref, heads_ref, up_ref, vec_ref = refs[:7]
     out_refs, sum_ref = refs[7:-1], refs[-1]
     rows = x_refs[0].shape[0]
     sums = [0.0] * 4
-    order = (out_refs[-1],) + out_refs[:-1]
-    reach = count * rows // parts
     for start in range(0, count * rows, TILE):
         at = slice(start, start + TILE)
         attn = mm_nt(gp_ref[at, :], heads_ref[...])
@@ -327,21 +379,23 @@
         for i, term in enumerate((attn * normed, attn, mlp * normed, mlp)):
             sums[i] = sums[i] + jnp.sum(term, axis=0, keepdims=True)
         out = attn * vec_ref[0:1, :] + mlp * vec_ref[2:3, :]
-        out_ref = order[start // reach]
-        out_ref[start % reach : start % reach + TILE, :] = out.astype(out_ref.dtype)
+        for i in range(0, TILE, rows):
+            out_ref = out_refs[(start + i) // rows]
+            out_ref[...] = out[i : i + rows].astype(out_ref.dtype)
     sum_ref[...] = jnp.concatenate(sums, axis=0)
 
 
-def input_terms(x_blocks, average, inverse, grad_project, grad_pre_up, w_heads, w_up, vectors, kinds):
+def input_terms(x_blocks, average, inverse, grad_project, grad_pre_up, w_heads, w_up, vectors, own):
     count, ffl = grad_pre_up.shape
     whole = lambda rows, cols: pl.BlockSpec((rows, cols), lambda i: (0, 0))
-    return call(
-        functools.partial(input_kernel, len(x_blocks), len(kinds)),
-        [((rows, D), dtype) for rows, dtype in kinds] + [((4, D), f32)],
+    block = pl.BlockSpec((x_blocks[0].shape[0], TILE), lambda i: (0, i))
+    *terms, sums = call(
+        functools.partial(input_kernel, len(x_blocks)),
+        [(x.shape, f32 if i < own else bf16) for i, x in enumerate(x_blocks)] + [((4, D), f32)],
         *x_blocks, average, inverse, grad_project, grad_pre_up, w_heads, w_up, vectors,
         grid=(D // TILE,),
         in_specs=[
-            *[pl.BlockSpec((block.shape[0], TILE), lambda i: (0, i)) for block in x_blocks],
+            *[block] * len(x_blocks),
             whole(count, 1),
             whole(count, 1),
             whole(count, 3 * HS),
@@ -350,23 +404,21 @@
             pl.BlockSpec((TILE, ffl), lambda i: (i, 0)),
             pl.BlockSpec((vectors.shape[0], TILE), lambda i: (0, i)),
         ],
-        out_specs=[
-            *[pl.BlockSpec((rows, TILE), lambda i: (0, i)) for rows, _ in kinds],
-            pl.BlockSpec((4, TILE), lambda i: (0, i)),
-        ],
-    )
-
-
-def attention_kernel(q_ref, g_ref, kv_ref, qpos_ref, kpos_ref, o_ref, dq_ref, dkv_ref, sum_ref):
-    count, tile = q_ref.shape[0], TILE
-    keys = kv_ref[:, :HS]
-    values = kv_ref[:, HS:]
+        out_specs=[*[block] * len(x_blocks), pl.BlockSpec((4, TILE), lambda i: (0, i))],
+    )
+    return terms, sums
+
+
+def attention_kernel(count, q_ref, g_ref, qpos_ref, kpos_ref, *refs):
+    kv_refs, (o_ref, dq_ref), refs = refs[:count], refs[count : count + 2], refs[count + 2 :]
+    dkv_refs, sum_ref = refs[:-1], refs[-1]
+    keys = jnp.concatenate([ref[:, :HS] for ref in kv_refs], axis=0)
+    values = jnp.concatenate([ref[:, HS:] for ref in kv_refs], axis=0)
     keys_turned = keys.T
     values_turned = values.T
     sum_ref[...] = jnp.zeros_like(sum_ref)
 
-    def step(i, _):
-        at = pl.ds(pl.multiple_of(i * tile, tile), tile)
+    def step(at):
         query = q_ref[at, :]
         grad = g_ref[at, :]
         scores = mm_nt(keys, query)
@@ -381,10 +433,12 @@
         score_grad = (weights * (weight_grad - delta)).astype(bf16)
         dq_ref[at, :] = (mm(keys_turned, score_grad).T * (HS**-0.5)).astype(bf16)
         sum_ref[:, :HS] += mm(score_grad, query)
-        return 0
-
-    lax.fori_loop(0, count // tile, step, 0)
-    dkv_ref[...] = sum_ref[...].astype(bf16)
+
+    tiles(q_ref.shape[0], step)
+    start = 0
+    for ref in dkv_refs:
+        ref[...] = sum_ref[start : start + ref.shape[0], :].astype(bf16)
+        start += ref.shape[0]
 
 
 def long_attention_kernel(q_ref, g_ref, kv_ref, qpos_ref, kpos_ref, o_ref, dq_ref, dkv_ref, sum_ref):
@@ -441,6 +495,26 @@
 
     tiles(q_ref.shape[0], step)
     dkv_ref[...] = sum_ref[...].astype(bf16)
+
+
+def attention(query, grad, kv_blocks, qpos, kpos):
+    count, total = len(kv_blocks), kpos.shape[0]
+    low = (query.shape, bf16)
+    scratch = [pltpu.VMEM((total, 2 * HS), f32)]
+    if total <= KEYS:
+        attended, grad_query, *grad_kv = call(
+            functools.partial(attention_kernel, count),
+            [low, low] + [(block.shape, bf16) for block in kv_blocks],
+            query, grad, qpos, kpos, *kv_blocks,
+            scratch=scratch,
+        )
+        return attended, grad_query, grad_kv
+    kv_all = jnp.concatenate(kv_blocks, axis=0)
+    attended, grad_query, grad_kv = call(
+        long_attention_kernel, [low, low, (kv_all.shape, bf16)], query, grad, kv_all, qpos, kpos,
+        scratch=scratch,
+    )
+    return attended, grad_query, jnp.split(grad_kv, count, axis=0)
 
 
 def per_device(
@@ -467,9 +541,10 @@
     ff = up_weight.shape[1]
     ffl = ff // tp
     group_len = sub_len * tp
-    reach = lax.axis_size("hd") * sub_len
-
+
+    vmem = pl.BlockSpec(memory_space=pltpu.VMEM)
     x_own = hidden_in.reshape(sub_len, D)
+    join = Order(out_bias).join
     g_own = cotangent.reshape(sub_len, D)
     smalls = jnp.concatenate(
         [
@@ -504,7 +579,14 @@
     m_heads = lax.all_to_all(heads_own, TP, split_axis=0, concat_axis=0, tiled=True)
     x_rows = [x_side] + [gather_axis(block, "bl") for block in x_near[:2]]
     x_near = gather_end(x_own, x_near)
-    x_near, x_rows, m_heads, up_own, g_late = join(x_near, x_rows, m_heads, up_own, g_own)
+    row = jnp.arange(group_len, dtype=jnp.int32)
+    inside = ((row // sub_len) ^ t) * sub_len + row % sub_len
+    query_places = bh * group_len + inside
+    key_places = jnp.concatenate([(bh ^ d) * group_len + inside for d in range(bh_size)])
+    tables = rotary_tables(query_places.astype(f32))
+    x_near, x_rows, m_heads, up_own, g_late, tables, query_places, key_places = join(
+        x_near, x_rows, m_heads, up_own, g_own, tables, query_places[None, :], key_places[:, None]
+    )
     w_heads = spread_rest(m_heads[:, :rows].reshape(tp * rows, -1))
     x_rows += [gather_axis(block, "bl") for block in x_near[3:]]
     g_first = swap(g_late, "hd", 1)
@@ -519,19 +601,15 @@
     b_qkv = lax.dynamic_index_in_dim(b_qkv, t, 1, keepdims=False).reshape(1, 3 * HS)
     b_up = lax.dynamic_index_in_dim(b_up, t, 0, keepdims=True)
 
-    row = jnp.arange(group_len, dtype=jnp.int32)
-    inside = ((row // sub_len) ^ t) * sub_len + row % sub_len
-    query_places = bh * group_len + inside
-    key_places = jnp.concatenate([(bh ^ d) * group_len + inside for d in range(bh_size)])
-    tables = rotary_tables(query_places.astype(f32))
-
-    x_rows, g_first, m_up, g_late, down_own, vectors, b_qkv, tables = join(
-        x_rows, g_first, m_up, g_late, down_own, vectors, b_qkv, tables
+    x_rows, g_first, m_up, g_late, down_own, vectors, b_qkv, b_up = join(
+        x_rows, g_first, m_up, g_late, down_own, vectors, b_qkv, b_up
     )
     w_up = spread_rest(m_up)
     x_blocks = [row[far] for far in range(bl_size) for row in x_rows]
     g_rows = [g_side, gather_axis(g_first, "bl")]
-    m_down = spread_group(down_own)
+    hd_size = lax.axis_size("hd")
+    four = hd_size == 4
+    g_near = [g_first] + [swap(g_late, "hd", d) for d in range(2, 3 if hd_size == 4 else hd_size)]
     attn_in, mlp_in, query, kv, average, inverse = call(
         functools.partial(project_kernel, tp),
         [
@@ -543,107 +621,109 @@
             ((group_len, 1), f32),
         ],
         *x_blocks, vectors, w_heads, b_qkv, *tables,
-    )
-    g_rows, m_down, kv, mlp_in, g_late = join(g_rows, m_down, kv, mlp_in, g_late)
+        grid=(1,),
+        in_specs=[vmem] * (tp + 1) + [pl.BlockSpec((D, 3 * HS), lambda i: (0, 0))] + [vmem] * 4,
+    )
+    g_rows, g_near, kv, mlp_in, g_late, down_own = join(
+        g_rows, g_near, kv, mlp_in, g_late, down_own
+    )
+    g_near = gather_end(g_late, g_near)
+    g_rows += [gather_axis(block, "bl") for block in g_near[2:3]]
+    g_rows, g_near, kv, down_own, mlp_in = join(g_rows, g_near, kv, down_own, mlp_in)
+    g_rows += [gather_axis(block, "bl") for block in g_near[3:]]
+    kv_blocks = gather_axis(kv, "bh")
+    m_down = spread_group(down_own)
+    activated, slope = forward(mlp_in, w_up, b_up)
+    g_rows, kv_blocks, m_down, activated, slope = join(g_rows, kv_blocks, m_down, activated, slope)
     w_down = spread_rest(m_down)
-    kv_blocks = gather_axis(kv, "bh")
-    hd_size = lax.axis_size("hd")
-    g_near = [g_first] + [swap(g_late, "hd", d) for d in range(2, 3 if hd_size == 4 else hd_size)]
-    g_near, kv_blocks, mlp_in = join(g_near, kv_blocks, mlp_in)
-    g_near = gather_end(g_late, g_near)
-    g_rows += [gather_axis(block, "bl") for block in g_near[2:]]
-    activated, slope = call(
-        forward_kernel, [((group_len, ffl), bf16), ((group_len, ffl), f32)], mlp_in, w_up, b_up
-    )
-    g_rows, activated, slope = join(g_rows, activated, slope)
     g_blocks = [row[far] for far in range(bl_size) for row in g_rows]
     g_all, grad_att = call(
         functools.partial(cotangent_kernel, tp),
         [((group_len, D), bf16), ((group_len, HS), bf16)],
         *g_blocks, w_heads,
-    )
-    down_half = collect_dp(mm_tn(g_all, activated).astype(bf16))
-    kv_all = jnp.concatenate(kv_blocks, axis=0)
-    down_half, grad_att, kv_all = join(down_half, grad_att, kv_all)
-    down_mine = collect_bh(*down_half)
-    attended, grad_query, grad_kv = call(
-        attention_kernel if kv_all.shape[0] <= KEYS else long_attention_kernel,
-        [
-            ((group_len, HS), bf16),
-            ((group_len, HS), bf16),
-            ((kv_all.shape[0], 2 * HS), bf16),
-        ],
-        query, grad_att, kv_all, query_places[None, :], key_places[:, None],
-        scratch=[pltpu.VMEM((kv_all.shape[0], 2 * HS), f32)],
-    )
-    attended, grad_query, grad_kv, down_mine = join(attended, grad_query, grad_kv, down_mine)
-    grad_kv = grad_kv.reshape(bh_size, group_len, 2 * HS)
-    grad_kv = [grad_kv[0]] + [swap(grad_kv[d], "bh", d) for d in range(1, bh_size)]
-    down_grad = collect_group(add_others(*down_mine))
-    kinds = [(reach, bf16)] * (bl_size - 1) + [(reach, f32)]
-    *out_far, out_own = [
-        term.reshape(-1, sub_len, D)
-        for term in output_terms(attended, activated, w_heads, w_down, kinds)
+        grid=(1,),
+        in_specs=[vmem] * tp + [pl.BlockSpec((D, HS), lambda i: (0, 3))],
+    )
+    down_far, down_own = weight_terms(g_all, activated)
+    down_far, down_own, grad_att = join(down_far, down_own, grad_att)
+    down_far = swap(down_far, "dp", 1)
+    down_far, grad_att = join(down_far, grad_att)
+    ((down_mine),) = add(([down_far, down_own], bf16, bh_size))
+    down_mine, grad_att = join(down_mine, grad_att)
+    down_others = [swap(down_mine[d], "bh", d) for d in range(1, bh_size)]
+    attended, grad_query, grad_kv = attention(
+        query, grad_att, kv_blocks, query_places, key_places
+    )
+    hd_terms = (hd_size, sub_len)
+    out_far = [
+        output_terms(attended, activated, w_heads, w_down, far, *hd_terms, bf16)
+        for far in range(1, bl_size)
     ]
-    grad_pre_up, up_bias_term = call(
-        backward_kernel, [((group_len, ffl), bf16), ((1, ffl), f32)], g_all, w_down, slope
-    )
-    up_term = mm_tn(mlp_in, grad_pre_up).astype(bf16)
-    grad_kv, down_grad, grad_pre_up, up_term, out_far, out_own = join(
-        grad_kv, down_grad, grad_pre_up, up_term, out_far, out_own
-    )
-    parts = groups()
-    up_mine = collect_rest(up_term)
-    far = send_far(out_far, parts[0])
+    down_others, out_far, attended, grad_kv, slope = join(
+        down_others, out_far, attended, grad_kv, slope
+    )
+    part = hd_size // 4
+    parts = [range(hd_size - (g + 1) * part, hd_size - g * part) for g in range(4)]
+
+    def over_bl(terms, ds):
+        return {d: [swap(term[d], "bl", f + 1) for f, term in enumerate(terms)] for d in ds}
+
+    def sums_of(own, received, ds, handed=()):
+        return [
+            ([own[d], *received[d], *(handed if d == 2 else ())], f32 if d == 0 else bf16, 1)
+            for d in ds
+        ]
+
+    ((down_last,),) = add(([down_mine[0], *down_others], bf16, 1))
+    down_last, attended, slope = join(down_last, attended, slope)
+    kv_others = [swap(grad_kv[d], "bh", d) for d in range(1, bh_size)]
+    down_grad = collect_group(down_last)
+    received = over_bl(out_far, parts[0])
+    grad_pre_up, up_bias_term = backward(g_all, w_down, slope)
+    out_own = output_terms(attended, activated, w_heads, w_down, 0, *hd_terms, f32)
+    up_far, up_own = weight_terms(mlp_in, grad_pre_up)
+    kv_others, down_grad, received, grad_pre_up, out_own, up_far, up_own, out_far = join(
+        kv_others, down_grad, received, grad_pre_up, out_own, up_far, up_own, out_far
+    )
+    out = dict(zip(parts[0], add(*sums_of(out_own, received, parts[0]))))
+    out, kv_others, up_far = join(out, kv_others, up_far)
+    out_near = {d: hand_on(out[d][0], d) for d in parts[0]}
+    received = over_bl(out_far, [*parts[1], *parts[2]])
+    up_far = swap(up_far, "dp", 1)
     grad_project, qkv_bias_term = call(
         functools.partial(turn_back_kernel, bh_size),
         [((group_len, 3 * HS), bf16), ((1, 3 * HS), f32)],
-        grad_query, *grad_kv, *tables,
-    )
-    qkv_term = mm_tn(attn_in, grad_project).astype(bf16)
-    dense_term = mm_tn(g_all, attended).astype(bf16)
-    far, qkv_term, dense_term, grad_project, out_far = join(
-        far, qkv_term, dense_term, grad_project, out_far
-    )
-    qkv_half, dense_half = collect_dp(qkv_term), collect_dp(dense_term)
-    handed = send_near(add_far(out_own, far), {})
-    far = send_far(out_far, parts[1])
-    *in_far, in_own, sums = input_terms(
-        x_blocks, average, inverse, grad_project, grad_pre_up, w_heads, w_up, vectors, kinds
-    )
-    in_far = [term.reshape(-1, sub_len, D) for term in in_far]
-    in_own = in_own.reshape(-1, sub_len, D)
-    qkv_half, dense_half, handed, far, in_far, in_own, out_far = join(
-        qkv_half, dense_half, handed, far, in_far, in_own, out_far
-    )
-    qkv_mine, dense_mine = collect_bh(*qkv_half), collect_bh(*dense_half)
-    near = handed | send_near(add_far(out_own, far), handed)
-    far = send_far(out_far, parts[2] + parts[3])
-    qkv_mine, dense_mine, near, far, in_far = join(qkv_mine, dense_mine, near, far, in_far)
-    heads_grad = collect_group(
-        jnp.concatenate([add_others(*qkv_mine), add_others(*dense_mine)], axis=1)
-    )
-    rest = add_far(out_own, far)
-    near = near | send_near(rest, {})
-    far = send_far(in_far, parts[0] + parts[1])
-    projected = rest[0]
-    down_grad = down_grad.astype(f32).transpose(1, 0, 2).reshape(rows, ff)
-    heads_grad, near, far, in_far, down_grad, up_mine, projected = join(
-        heads_grad, near, far, in_far, down_grad, up_mine, projected
-    )
-    output = (x_own.astype(f32) + add_near(projected, near) + vectors[4:5]).astype(bf16)
-    up_grad = collect_group(up_mine)
-    upper = add_far(in_own, far)
-    handed = send_near({d: upper[d] for d in parts[0]}, {})
-    far = send_far(in_far, parts[2] + parts[3])
-    heads_grad = heads_grad.astype(f32)
-    dense_grad = heads_grad[:, :, 3 * HS :].transpose(1, 0, 2).reshape(rows, D)
-    qkv_grad = (
-        heads_grad[:, :, : 3 * HS]
-        .reshape(tp, rows, 3, HS)
-        .transpose(1, 2, 0, 3)
-        .reshape(rows, 3 * D)
-    )
+        grad_query, grad_kv[0], *kv_others, *tables,
+    )
+    heads_far, heads_own = weight_terms(attn_in, grad_project, g_all, attended)
+    out_near, received, up_far, grad_project, heads_far, heads_own, out_far = join(
+        out_near, received, up_far, grad_project, heads_far, heads_own, out_far
+    )
+    middle = [*parts[1], *parts[2]]
+    up_mine, *out = add(
+        ([up_far, up_own], bf16, bh_size),
+        *sums_of(out_own, received, middle, [out_near[3]] if four else []),
+    )
+    up_mine, out, grad_project, heads_far = join(up_mine, out, grad_project, heads_far)
+    out_near |= {d: hand_on(term, d) for d, (term,) in zip(middle, out)}
+    received = over_bl(out_far, parts[3])
+    up_others = [swap(up_mine[d], "bh", d) for d in range(1, bh_size)]
+    heads_far = swap(heads_far, "dp", 1)
+    in_terms, sums = input_terms(
+        x_blocks, average, inverse, grad_project, grad_pre_up, w_heads, w_up, vectors, hd_size
+    )
+    out_near, received, up_others, heads_far, in_terms = join(
+        out_near, received, up_others, heads_far, in_terms
+    )
+    in_own = in_terms[:hd_size]
+    in_far = [in_terms[f * hd_size : (f + 1) * hd_size] for f in range(1, bl_size)]
+    (up_last,), heads_mine = add(
+        ([up_mine[0], *up_others], bf16, 1), ([heads_far, heads_own], bf16, bh_size)
+    )
+    up_last, heads_mine, in_far = join(up_last, heads_mine, in_far)
+    up_grad = collect_group(up_last)
+    heads_others = [swap(heads_mine[d], "bh", d) for d in range(1, bh_size)]
+    received_in = over_bl(in_far, parts[0])
     sums = jnp.concatenate([sums, jnp.sum(g_own.astype(f32), axis=0, keepdims=True)], axis=0)
     qkv_bias_full = lax.dynamic_update_slice(
         jnp.zeros((3, HEADS, HS), f32), qkv_bias_term.reshape(3, 1, HS), (0, t, 0)
@@ -657,17 +737,48 @@
         ],
         axis=1,
     )
-    upper = {d: upper[d] for d in parts[1]}
-    up_grad, handed, far, output, dense_grad, qkv_grad, small_terms, upper = join(
-        up_grad, handed, far, output, dense_grad, qkv_grad, small_terms, upper
-    )
-    lower = add_far(in_own, far)
-    near = handed | send_near(upper | lower, handed)
+    up_grad, heads_others, received_in, small_terms, in_far, in_own = join(
+        up_grad, heads_others, received_in, small_terms, in_far, in_own
+    )
+    (heads_last,), *ins = add(
+        ([heads_mine[0], *heads_others], bf16, 1), *sums_of(in_own, received_in, parts[0])
+    )
+    heads_last, ins, in_far = join(heads_last, ins, in_far)
+    heads_grad = collect_group(heads_last)
+    in_near = {d: hand_on(term, d) for d, (term,) in zip(parts[0], ins)}
+    received_in = over_bl(in_far, middle)
+    down_grad = down_grad.astype(f32).transpose(1, 0, 2).reshape(rows, ff)
+    up_grad = up_grad.astype(f32).transpose(1, 0, 2).reshape(rows, ff)
+    heads_grad, in_near, received_in, down_grad, up_grad, in_far, in_own, small_terms = join(
+        heads_grad, in_near, received_in, down_grad, up_grad, in_far, in_own, small_terms
+    )
+    ins = add(*sums_of(in_own, received_in, middle, [in_near[3]] if four else []))
+    ins, in_far, small_terms, heads_grad = join(ins, in_far, small_terms, heads_grad)
+    in_near |= {d: hand_on(term, d) for d, (term,) in zip(middle, ins)}
+    received_in = over_bl(in_far, parts[3])
     small = lax.all_to_all(small_terms, ALL, split_axis=0, concat_axis=0, tiled=True)
-    up_grad = up_grad.astype(f32).transpose(1, 0, 2).reshape(rows, ff)
-    near, small, up_grad = join(near, small, up_grad)
-    grad_normed = add_near(lower[0], near)
+    heads_grad = heads_grad.astype(f32)
+    dense_grad = heads_grad[:, :, 3 * HS :].transpose(1, 0, 2).reshape(rows, D)
+    qkv_grad = (
+        heads_grad[:, :, : 3 * HS]
+        .reshape(tp, rows, 3, HS)
+        .transpose(1, 2, 0, 3)
+        .reshape(rows, 3 * D)
+    )
+
+    def total(own, received, near):
+        rest = {d: sum((x.astype(f32) for x in received[d]), own[d]) for d in received}
+        near = near | {d: hand_on(rest[d].astype(bf16), d) for d in rest if d}
+        straight = [d for d in range(1, hd_size) if not (four and d == 3)]
+        return sum((near[d].astype(f32) for d in straight), rest[0])
+
+    projected = total(out_own, received, out_near)
+    output = (x_own.astype(f32) + projected + vectors[4:5]).astype(bf16)
+    in_near, received_in, small, dense_grad, qkv_grad, output, in_own = join(
+        in_near, received_in, small, dense_grad, qkv_grad, output, in_own
+    )
     small = jnp.sum(small, axis=0)
+    grad_normed = total(in_own, received_in, in_near)
     own = x_own.astype(f32)
     own_average, own_inverse = statistics(own)
     own_normed = (own - own_average) * own_inverse

time: 512 us -> 477 us (0.932)
  Pallas kernels: 94.7 us -> 145 us
  waiting for transfers between devices: 199 us -> 173 us
  other arithmetic: 40 us -> 14.7 us
  matrix products: 25.1 us -> 0 us
  local copies, waits for them, and re-layouts: 51.3 us -> 42.2 us
    pallas_call x0 -> x3, Pallas kernels: none -> 29.2 us  [weight_terms(): pl.pallas_call(functools.partial(weight_kernel, steps), grid_spec=pltpu.P...]
    dot_general x4 -> x0, matrix products: 25.1 us -> none  [mm_tn(): lax.dot_general(a, b, (((0,), (0,)), ((), ())), preferred_element_type=f32)]
    pallas_call x8 -> x16, Pallas kernels: 94.7 us -> 116 us  [call(): pl.pallas_call(kernel, grid=grid, out_shape=[jax.ShapeDtypeStruct(shape,...]
    ppermute x38, waiting for transfers between devices: 176 us -> 160 us  [swap(): return lax.ppermute(value, axis, [(i, i ^ distance) for i in range(size)])]
    convert_element_type x10 -> x0, other arithmetic: 12.5 us -> none  [the longest x4 6.34 us: send_near(): out[d] = swap(block.astype(bf16), 'hd', 1 if four and d == 3 else d)]
    all_to_all x1, waiting for transfers between devices: 19.2 us -> 9.76 us  [per_device(): lax.all_to_all(small_terms, ALL, split_axis=0, concat_axis=0, tiled=True)]
    squeeze x11 -> x0, local copies, waits for them, and re-layouts: 8.56 us -> none  [the longest x6 4.33 us: pick(): lax.dynamic_index_in_dim(value, lax.axis_index(axis) ^ distance, 0, keepd...]
    add x2 -> x0, other arithmetic: 5.67 us -> none  [add_far(): sum((other.astype(f32) for other in others), own[d])]
  transfers between devices with their start and end apart: 49 -> 48, of which waited for: 22 -> 22; matrix products, arithmetic and copies ran while one was open for 19% -> 8% of each run, Pallas kernels for 19% -> 26%
where the time goes in v1:
time: 477 us; the launch traced here: 471 us
  waiting for transfers between devices  173 us (36%)
  Pallas kernels  145 us (30%)
  starting transfers between devices  80.6 us (17%)
  local copies, waits for them, and re-layouts  42.2 us (9%)
  other arithmetic  14.7 us (3%)
  between operations  14.7 us (3%)
    ppermute x38, waiting for transfers between devices, swap(): return lax.ppermute(value, axis, [(i, i ^ distance) for i in range(size)])  160 us
    pallas_call x16, Pallas kernels, call(): pl.pallas_call(kernel, grid=grid, out_shape=[jax.ShapeDtypeStruct(shape,...  116 us
    ppermute x38, starting transfers between devices, swap(): return lax.ppermute(value, axis, [(i, i ^ distance) for i in range(size)])  46.5 us
    pallas_call x3, Pallas kernels, weight_terms(): pl.pallas_call(functools.partial(weight_kernel, steps), grid_spec=pltpu.P...  29.2 us
    unnamed x92, local copies, waits for them, and re-layouts  16.7 us
    all_to_all x3, starting transfers between devices, collect_group(): return lax.all_to_all(mine, TP, split_axis=0, concat_axis=0, tiled=True)  15.9 us
    all_to_all x2, starting transfers between devices, spread_group(): mine = lax.all_to_all(shard, TP, split_axis=0, concat_axis=0, tiled=True)  10.7 us
    all_to_all x1, waiting for transfers between devices, per_device(): lax.all_to_all(small_terms, ALL, split_axis=0, concat_axis=0, tiled=True)  9.76 us
  transfers between devices with their start and end apart: 48, of which 22 were waited for; matrix products, arithmetic and copies ran while one was open for 8% of the time, Pallas kernels for 26%

profile of v1, /device:TPU:0, one launch (start us, length us, event | category | flops | bytes accessed | tf_op | source)
XLA Modules:
  0.0 470.6 jit_solution(4890901312961955389)
XLA Ops:
  9.4 3.0 collective-permute-start.4
  12.4 1.6 collective-permute-start
  14.0 2.6 collective-permute-start.1
  16.6 1.5 collective-permute-start.2
  23.7 13.4 %collective-permute-done.refs_1_ = bf16[128,2048]{1,0:T(8,128)(2,1)S(1)} collective-permute-done((bf16[128,2048]{1,0:T(8,128)(2,1)}, bf16[128,2048]{1,0:T(8,128)(2,1)S(1)}, u32[]{:S(2)}, u32[]{:S(2)}) %collective-permute-start) | collective-permute-done | bytes 524320 | tf_op jit(solution)/shard_map/ppermute | solution.py:58
  37.1 2.4 collective-permute-done.1.refs_2_
  41.0 3.6 all-to-all-start
  44.7 1.9 multiply_sine_fusion
  46.6 1.9 collective-permute-start.6
  54.7 20.8 %collective-permute-done.6.refs_3_ = bf16[128,2048]{1,0:T(8,128)(2,1)S(1)} collective-permute-done((bf16[128,2048]{1,0:T(8,128)(2,1)S(1)}, bf16[128,2048]{1,0:T(8,128)(2,1)S(1)}, u32[]{:S(2)}, u32[]{:S(2)}) %collective-permute-start.6) | collective-permute-done | bytes 524320 | tf_op jit(solution)/shard_map/ppermute | solution.py:58
  76.4 5.1 %collective-permute-done.7.refs_5_ = bf16[128,2048]{1,0:T(8,128)(2,1)} collective-permute-done((bf16[128,2048]{1,0:T(8,128)(2,1)S(1)}, bf16[128,2048]{1,0:T(8,128)(2,1)}, u32[]{:S(2)}, u32[]{:S(2)}) %collective-permute-start.7) | collective-permute-done | bytes 524320 | tf_op jit(solution)/shard_map/ppermute | solution.py:58
  82.6 3.8 all-to-all-start.1
  86.9 2.4 copy.89
  89.4 2.0 collective-permute-start.10
  95.4 20.6 %collective-permute-done.10.refs_1_ = bf16[128,2048]{1,0:T(8,128)(2,1)} collective-permute-done((bf16[128,2048]{1,0:T(8,128)(2,1)S(1)}, bf16[128,2048]{1,0:T(8,128)(2,1)}, u32[]{:S(2)}, u32[]{:S(2)}) %collective-permute-start.10) | collective-permute-done | bytes 524320 | tf_op jit(solution)/shard_map/ppermute | solution.py:58
  118.5 2.4 collective-permute-start.12
  120.9 13.1 %shard_map.228 = (bf16[1024,2048]{1,0:T(8,128)(2,1)}, bf16[1024,2048]{1,0:T(8,128)(2,1)}, bf16[1024,256]{1,0:T(8,128)(2,1)}, bf16[1024,512]{1,0:T(8,128)(2,1)}, f32[1024,1]{1,0:T(8,128)}, /*index=5*/f32[1024,1]{1,0:T(8,128)}) custom-call(bf16[128,2048]{1,0:T(8,128)(2,1)} %bitcast.99, bf16[128,2048]{1,0:T(8,128)(2,1)} %copy-done.8, ...), custom_call_target="tpu_custom_call" | custom-call | flops 1 | bytes 1 | tf_op jit(solution)/shard_map/pallas_call | solution.py:117
  134.0 7.9 %collective-permute-done.12.refs_2_ = bf16[128,2048]{1,0:T(8,128)(2,1)S(1)} collective-permute-done((bf16[128,2048]{1,0:T(8,128)(2,1)S(1)}, bf16[128,2048]{1,0:T(8,128)(2,1)S(1)}, u32[]{:S(2)}, u32[]{:S(2)}) %collective-permute-start.12) | collective-permute-done | bytes 524320 | tf_op jit(solution)/shard_map/ppermute | solution.py:58
  143.1 10.7 %collective-permute-done.13.refs_6_ = bf16[128,2048]{1,0:T(8,128)(2,1)S(1)} collective-permute-done((bf16[128,2048]{1,0:T(8,128)(2,1)S(1)}, bf16[128,2048]{1,0:T(8,128)(2,1)S(1)}, u32[]{:S(2)}, u32[]{:S(2)}) %collective-permute-start.13) | collective-permute-done | bytes 524320 | tf_op jit(solution)/shard_map/ppermute | solution.py:58
  155.0 6.9 %all-to-all-start.2 = ((bf16[8,64,1024]{2,1,0:T(8,128)(2,1)}), bf16[8,64,1024]{2,1,0:T(8,128)(2,1)S(1)}, u32[]{:S(2)}, u32[]{:S(2)}) async-start(bf16[8,64,1024]{2,1,0:T(8,128)(2,1)} %bitcast.89), calls=%async_computation.2 | async-start | bytes 2097152 | tf_op jit(solution)/shard_map/all_to_all | solution.py:98
  162.7 2.0 collective-permute-start.15
  164.7 11.9 %shard_map.229 = (bf16[1024,1024]{1,0:T(8,128)(2,1)}, f32[1024,1024]{1,0:T(8,128)}) custom-call(bf16[1024,2048]{1,0:T(8,128)(2,1)} %get-tuple-element.309.mlp_ref.refs_0_, bf16[2048,1024]{1,0:T(8,128)(2,1)} %all-gather.6.cloned.1.call-done.w_ref.refs_13_, f32[1,1024]{1,0:T(1,128)} %constant_dynamic-slice_fusion.b_ref), custom_call_target="tpu_custom_call" | custom-call | flops 1 | bytes 1 | tf_op jit(solution)/shard_map/pallas_call | solution.py:117
  176.6 7.0 %collective-permute-done.15.refs_7_ = bf16[128,2048]{1,0:T(8,128)(2,1)} collective-permute-done((bf16[128,2048]{1,0:T(8,128)(2,1)}, bf16[128,2048]{1,0:T(8,128)(2,1)}, u32[]{:S(2)}, u32[]{:S(2)}) %collective-permute-start.15) | collective-permute-done | bytes 524320 | tf_op jit(solution)/shard_map/ppermute | solution.py:58
  183.6 2.2 collective-permute-done.16.refs_1_
  185.9 1.7 all-to-all-done.2
  189.2 6.3 %shard_map.230 = (bf16[1024,2048]{1,0:T(8,128)(2,1)}, bf16[1024,256]{1,0:T(8,128)(2,1)}) custom-call(bf16[128,2048]{1,0:T(8,128)(2,1)} %bitcast.104, bf16[128,2048]{1,0:T(8,128)(2,1)} %collective-permute-done.10.refs_1_, bf16[128,2048]{1,0:T(8,128)(2,1)} %copy-done.25, bf16[128,2048]{1,0:T(8,128)(2,1)} %collective-permute-done.14.refs_3_, ...), custom_call_target="tpu_custom_call" | custom-call | flops 1 | bytes 1 | tf_op jit(solution)/shard_map/pallas_call | solution.py:117
  195.5 9.6 %shard_map.231 = (bf16[1024,1024]{1,0:T(8,128)(2,1)}, bf16[1024,1024]{1,0:T(8,128)(2,1)}) custom-call(s32[2]{0:T(128)} %pad_add_fusion.1.place_ref, bf16[1024,2048]{1,0:T(8,128)(2,1)} %get-tuple-element.323.refs_0_.g_ref.refs_2_, bf16[1024,1024]{1,0:T(8,128)(2,1)} %get-tuple-element.324.refs_1_.act_ref), custom_call_target="tpu_custom_call" | custom-call | flops 1 | bytes 1 | tf_op jit(solution)/shard_map/pallas_call | solution.py:304
  205.1 4.4 collective-permute-done.17.refs_0_
  210.8 3.8 shard_map.232
  217.2 18.2 %shard_map.233 = (bf16[1024,256]{1,0:T(8,128)(2,1)}, bf16[1024,256]{1,0:T(8,128)(2,1)}, bf16[1024,512]{1,0:T(8,128)(2,1)}, bf16[1024,512]{1,0:T(8,128)(2,1)}) custom-call(bf16[1024,256]{1,0:T(8,128)(2,1)} %get-tuple-element.337.q_ref, bf16[1024,256]{1,0:T(8,128)(2,1)} %get-tuple-element.338.g_ref, s32[1,1024]{1,0:T(1,128)} %fusion.19.qpos_ref, ...), custom_call_target="tpu_custom_call" | custom-call | flops 1 | bytes 1 | tf_op jit(solution)/shard_map/pallas_call | solution.py:117
  235.4 6.1 %shard_map.234 = (bf16[128,2048]{1,0:T(8,128)(2,1)}, bf16[128,2048]{1,0:T(8,128)(2,1)}, bf16[128,2048]{1,0:T(8,128)(2,1)}, bf16[128,2048]{1,0:T(8,128)(2,1)}) custom-call(bf16[1024,256]{1,0:T(8,128)(2,1)} %get-tuple-element.361.att_ref.refs_3_, bf16[1024,1024]{1,0:T(8,128)(2,1)} %get-tuple-element.324.refs_1_.act_ref, ...), custom_call_target="tpu_custom_call" | custom-call | flops 1 | bytes 1 | tf_op jit(solution)/shard_map/pallas_call | solution.py:117
  243.5 2.8 shard_map.235
  246.3 5.8 %all-to-all-start.3 = ((bf16[8,64,1024]{2,1,0:T(8,128)(2,1)}), bf16[8,64,1024]{2,1,0:T(8,128)(2,1)S(1)}, u32[]{:S(2)}, u32[]{:S(2)}) async-start(bf16[8,64,1024]{2,1,0:T(8,128)(2,1)} %bitcast.107), calls=%async_computation.3 | async-start | bytes 2097152 | tf_op jit(solution)/shard_map/all_to_all | solution.py:108
  252.7 2.0 collective-permute-start.20
  254.7 9.3 %shard_map.236 = (bf16[1024,1024]{1,0:T(8,128)(2,1)}, f32[1,1024]{1,0:T(1,128)}) custom-call(bf16[1024,2048]{1,0:T(8,128)(2,1)} %get-tuple-element.323.refs_0_.g_ref.refs_2_, bf16[2048,1024]{1,0:T(8,128)(2,1)} %all-gather.8.cloned.1.call-done.down_ref.w_ref, f32[1024,1024]{1,0:T(8,128)} %get-tuple-element.359.slope_ref), custom_call_target="tpu_custom_call" | custom-call | flops 1 | bytes 1 | tf_op jit(solution)/shard_map/pallas_call | solution.py:117
  264.0 9.5 %shard_map.238 = (bf16[1024,1024]{1,0:T(8,128)(2,1)}, bf16[1024,1024]{1,0:T(8,128)(2,1)}) custom-call(s32[2]{0:T(128)} %pad_add_fusion.1.place_ref, bf16[1024,2048]{1,0:T(8,128)(2,1)} %get-tuple-element.309.mlp_ref.refs_0_, bf16[1024,1024]{1,0:T(8,128)(2,1)} %get-tuple-element.409.refs_1_.refs_11_), custom_call_target="tpu_custom_call" | custom-call | flops 1 | bytes 1 | tf_op jit(solution)/shard_map/pallas_call | solution.py:304
  273.5 6.5 %shard_map.237 = (f32[128,2048]{1,0:T(8,128)}, f32[128,2048]{1,0:T(8,128)}, f32[128,2048]{1,0:T(8,128)}, f32[128,2048]{1,0:T(8,128)}) custom-call(bf16[1024,256]{1,0:T(8,128)(2,1)} %get-tuple-element.361.att_ref.refs_3_, bf16[1024,1024]{1,0:T(8,128)(2,1)} %get-tuple-element.324.refs_1_.act_ref, ...), custom_call_target="tpu_custom_call" | custom-call | flops 1 | bytes 1 | tf_op jit(solution)/shard_map/pallas_call | solution.py:117
  280.8 2.2 shard_map.239
  286.6 4.4 shard_map.240
  290.9 10.1 %shard_map.241 = (bf16[1024,1024]{1,0:T(8,128)(2,1)}, bf16[1024,1024]{1,0:T(8,128)(2,1)}) custom-call(s32[2]{0:T(128)} %pad_add_fusion.1.place_ref, bf16[1024,2048]{1,0:T(8,128)(2,1)} %get-tuple-element.383.refs_0_, bf16[1024,768]{1,0:T(8,128)(2,1)} %get-tuple-element.408.refs_1_.refs_10_, bf16[1024,2048]{1,0:T(8,128)(2,1)} %get-tuple-element.323.refs_0_.g_ref.refs_2_, ...), custom_call_target="tpu_custom_call" | custom-call | flops 1 | bytes 1 | tf_op jit(solution)/shard_map/pallas_call | solution.py:304
  301.1 9.0 %collective-permute-done.23.refs_3_ = bf16[128,2048]{1,0:T(8,128)(2,1)S(1)} collective-permute-done((bf16[128,2048]{1,0:T(8,128)(2,1)}, bf16[128,2048]{1,0:T(8,128)(2,1)S(1)}, u32[]{:S(2)}, u32[]{:S(2)}) %collective-permute-start.23) | collective-permute-done | bytes 524320 | tf_op jit(solution)/shard_map/ppermute | solution.py:58
  311.5 5.1 %shard_map.242 = (bf16[512,1024]{1,0:T(8,128)(2,1)}, bf16[512,1024]{1,0:T(8,128)(2,1)}, bf16[128,2048]{1,0:T(8,128)(2,1)}, bf16[128,2048]{1,0:T(8,128)(2,1)}) custom-call(bf16[1024,1024]{1,0:T(8,128)(2,1)} %copy-done.15, bf16[1024,1024]{1,0:T(8,128)(2,1)} %get-tuple-element.388.refs_1_, f32[128,2048]{1,0:T(8,128)} %get-tuple-element.389.refs_2_, ...), custom_call_target="tpu_custom_call" | custom-call | flops 1 | bytes 1 | tf_op jit(solution)/shard_map/pallas_call | solution.py:117
  318.7 2.4 collective-permute-start.26
  321.6 14.6 %shard_map.243 = (f32[128,2048]{1,0:T(8,128)}, f32[128,2048]{1,0:T(8,128)}, f32[128,2048]{1,0:T(8,128)}, f32[128,2048]{1,0:T(8,128)}, bf16[128,2048]{1,0:T(8,128...) custom-call(bf16[128,2048]{1,0:T(8,128)(2,1)} %bitcast.100, ...), custom_call_target="tpu_custom_call" | custom-call | flops 1 | bytes 1 | tf_op jit(solution)/shard_map/pallas_call | solution.py:117
  336.2 7.4 %collective-permute-done.25 = bf16[128,2048]{1,0:T(8,128)(2,1)S(1)} collective-permute-done((bf16[128,2048]{1,0:T(8,128)(2,1)}, bf16[128,2048]{1,0:T(8,128)(2,1)S(1)}, u32[]{:S(2)}, u32[]{:S(2)}) %collective-permute-start.25) | collective-permute-done | bytes 524320 | tf_op jit(solution)/shard_map/ppermute | solution.py:58
  345.5 4.8 %shard_map.244 = (bf16[512,1024]{1,0:T(8,128)(2,1)}, bf16[512,1024]{1,0:T(8,128)(2,1)}, bf16[512,1024]{1,0:T(8,128)(2,1)}) custom-call(bf16[512,1024]{1,0:T(8,128)(2,1)} %get-tuple-element.400.refs_0_, bf16[512,1024]{1,0:T(8,128)(2,1)} %copy-done.22, bf16[1024,1024]{1,0:T(8,128)(2,1)} %copy-done.7, bf16[1024,1024]{1,0:T(8,128)(2,1)} %get-tuple-element.420.refs_3_), custom_call_target="tpu_custom_call" | custom-call | flops 1 | bytes 1 | tf_op jit(solution)/shard_map/pallas_call | solution.py:117
  350.3 5.9 %all-to-all-start.4 = ((bf16[8,64,1024]{2,1,0:T(8,128)(2,1)}), bf16[8,64,1024]{2,1,0:T(8,128)(2,1)S(1)}, u32[]{:S(2)}, u32[]{:S(2)}) async-start(bf16[8,64,1024]{2,1,0:T(8,128)(2,1)} %bitcast.121), calls=%async_computation.4 | async-start | bytes 2097152 | tf_op jit(solution)/shard_map/all_to_all | solution.py:108
  356.8 2.0 collective-permute-start.31
  359.6 18.4 %collective-permute-done.31.refs_3_ = bf16[128,2048]{1,0:T(8,128)(2,1)} collective-permute-done((bf16[128,2048]{1,0:T(8,128)(2,1)}, bf16[128,2048]{1,0:T(8,128)(2,1)}, u32[]{:S(2)}, u32[]{:S(2)}) %collective-permute-start.31) | collective-permute-done | bytes 524320 | tf_op jit(solution)/shard_map/ppermute | solution.py:58
  378.0 2.4 collective-permute-done.30.refs_1_
  380.4 1.7 all-to-all-done.4
  382.1 3.8 shard_map.245
  385.9 4.3 all-to-all-start.5
  391.2 2.1 collective-permute-start.32
  398.9 20.2 %collective-permute-done.32.refs_2_ = bf16[128,2048]{1,0:T(8,128)(2,1)S(1)} collective-permute-done((bf16[128,2048]{1,0:T(8,128)(2,1)}, bf16[128,2048]{1,0:T(8,128)(2,1)S(1)}, u32[]{:S(2)}, u32[]{:S(2)}) %collective-permute-start.32) | collective-permute-done | bytes 524320 | tf_op jit(solution)/shard_map/ppermute | solution.py:58
  420.7 5.0 %collective-permute-done.34.refs_1_ = bf16[128,2048]{1,0:T(8,128)(2,1)} collective-permute-done((bf16[128,2048]{1,0:T(8,128)(2,1)}, bf16[128,2048]{1,0:T(8,128)(2,1)}, u32[]{:S(2)}, u32[]{:S(2)}) %collective-permute-start.34) | collective-permute-done | bytes 524320 | tf_op jit(solution)/shard_map/ppermute | solution.py:58
  425.7 3.2 shard_map.246
  429.7 2.3 collective-permute-start.36
  434.9 1.6 convert_element_type.61
  436.5 2.6 reshape.305
  440.0 1.6 copy.83
  442.4 3.0 all-to-all-start.6
  447.4 9.8 %all-to-all-done.6 = f32[32,1,768]{2,1,0:T(1,128)S(1)} async-done(((f32[32,1,768]{2,1,0:T(1,128)}), f32[32,1,768]{2,1,0:T(1,128)S(1)}, u32[]{:S(2)}, u32[]{:S(2)}) %all-to-all-start.6) | async-done | bytes 98336 | tf_op jit(solution)/shard_map/all_to_all | solution.py:759
  459.3 1.8 fusion.28
  (230 shorter events, 67.6 us)
Async XLA Ops:
  9.4 9.2 %collective-permute-start.4 = (bf16[1,12,64]{2,1,0:T(8,128)(2,1)S(1)}, bf16[1,12,64]{2,1,0:T(8,128)(2,1)S(1)}, u32[]{:S(2)}, u32[]{:S(2)}) collective-permute-start(bf16[1,12,64]{2,1,0:T(8,128)(2,1)S(1)} %bitcast.133), channel_id=1, source_target_pairs={{0,8},{8,0},{1,9},{9,1},{2,10},{10,2},{3,11},{11,3},{4,12},{12,4},... | collective-permute-start | bytes 4616 | tf_op jit(solution)/shard_map/ppermute | solution.py:58
  12.4 24.7 %collective-permute-start = (bf16[128,2048]{1,0:T(8,128)(2,1)}, bf16[128,2048]{1,0:T(8,128)(2,1)S(1)}, u32[]{:S(2)}, u32[]{:S(2)}) collective-permute-start(bf16[128,2048]{1,0:T(8,128)(2,1)} %bitcast.96), channel_id=1, source_target_pairs={{0,1},{1,0},{2,3},{3,2},{4,5},{5,4},{6,7},{7,6},{8,9},{9,8},{10,11... | collective-permute-start | bytes 1572872 | tf_op jit(solution)/shard_map/ppermute | solution.py:58
  14.0 25.5 %collective-permute-start.1 = (bf16[128,2048]{1,0:T(8,128)(2,1)}, bf16[128,2048]{1,0:T(8,128)(2,1)S(1)}, u32[]{:S(2)}, u32[]{:S(2)}) collective-permute-start(bf16[128,2048]{1,0:T(8,128)(2,1)} %bitcast.97), channel_id=1, source_target_pairs={{0,2},{1,3},{2,0},{3,1},{4,6},{5,7},{6,4},{7,5},{8,10},{9,11},{10,... | collective-permute-start | bytes 1572872 | tf_op jit(solution)/shard_map/ppermute | solution.py:58
  16.6 22.9 %collective-permute-start.2 = (bf16[128,2048]{1,0:T(8,128)(2,1)}, bf16[128,2048]{1,0:T(8,128)(2,1)S(1)}, u32[]{:S(2)}, u32[]{:S(2)}) collective-permute-start(bf16[128,2048]{1,0:T(8,128)(2,1)} %bitcast.98), channel_id=1, source_target_pairs={{0,4},{4,0},{1,5},{5,1},{2,6},{6,2},{3,7},{7,3},{8,12},{12,8},{9,1... | collective-permute-start | bytes 1572872 | tf_op jit(solution)/shard_map/ppermute | solution.py:58
  18.1 22.9 %collective-permute-start.3 = (bf16[128,2048]{1,0:T(8,128)(2,1)}, bf16[128,2048]{1,0:T(8,128)(2,1)}, u32[]{:S(2)}, u32[]{:S(2)}) collective-permute-start(bf16[128,2048]{1,0:T(8,128)(2,1)} %bitcast.103), channel_id=1, source_target_pairs={{0,4},{4,0},{1,5},{5,1},{2,6},{6,2},{3,7},{7,3},{8,12},{12,8},{9,1... | collective-permute-start | bytes 1572872 | tf_op jit(solution)/shard_map/ppermute | solution.py:58
  18.6 3.7 collective-permute-start.5
  37.1 15.2 %copy-start.8 = (bf16[128,2048]{1,0:T(8,128)(2,1)}, bf16[128,2048]{1,0:T(8,128)(2,1)S(1)}, u32[]{:S(2)}) copy-start(bf16[128,2048]{1,0:T(8,128)(2,1)S(1)} %collective-permute-done.refs_1_) | copy-start | bytes 1572868
  39.5 12.8 %copy-start.9 = (bf16[128,2048]{1,0:T(8,128)(2,1)}, bf16[128,2048]{1,0:T(8,128)(2,1)S(1)}, u32[]{:S(2)}) copy-start(bf16[128,2048]{1,0:T(8,128)(2,1)S(1)} %collective-permute-done.1.refs_2_) | copy-start | bytes 1572868
  39.5 12.8 %copy-start.10 = (bf16[128,2048]{1,0:T(8,128)(2,1)}, bf16[128,2048]{1,0:T(8,128)(2,1)S(1)}, u32[]{:S(2)}) copy-start(bf16[128,2048]{1,0:T(8,128)(2,1)S(1)} %collective-permute-done.2.refs_4_) | copy-start | bytes 1572868
  41.0 40.5 %all-to-all-start = ((bf16[8,72,1024]{2,1,0:T(8,128)(2,1)}), bf16[8,72,1024]{2,1,0:T(8,128)(2,1)S(1)}, u32[]{:S(2)}, u32[]{:S(2)}) async-start(bf16[8,72,1024]{2,1,0:T(8,128)(2,1)} %pad_maximum_fusion), calls=%async_computation | async-start | bytes 2359296 | tf_op jit(solution)/shard_map/all_to_all | solution.py:579
  44.5 76.4 %all-gather.4.cloned.1.call-start = ((), (), s32[]{:S(2)}) async-start(), calls=%async_computation.7 | async-start | bytes 5242880 | tf_op jit(solution)/shard_map/all_gather | solution.py:103
  46.6 29.0 %collective-permute-start.6 = (bf16[128,2048]{1,0:T(8,128)(2,1)S(1)}, bf16[128,2048]{1,0:T(8,128)(2,1)S(1)}, u32[]{:S(2)}, u32[]{:S(2)}) collective-permute-start(bf16[128,2048]{1,0:T(8,128)(2,1)S(1)} %collective-permute-done.1.refs_2_), channel_id=1, source_target_pairs={{0,1},{1,0},{2,3},{3,2},{4,5},{5,4},{6,7},{7,6},{8,9},{9,8},{10,11... | collective-permute-start | bytes 1572872 | tf_op jit(solution)/shard_map/ppermute | solution.py:58
  48.5 27.1 %collective-permute-start.8 = (bf16[128,2048]{1,0:T(8,128)(2,1)S(1)}, bf16[128,2048]{1,0:T(8,128)(2,1)S(1)}, u32[]{:S(2)}, u32[]{:S(2)}) collective-permute-start(bf16[128,2048]{1,0:T(8,128)(2,1)S(1)} %collective-permute-done.1.refs_2_), channel_id=1, source_target_pairs={{0,4},{4,0},{1,5},{5,1},{2,6},{6,2},{3,7},{7,3},{8,12},{12,8},{9,1... | collective-permute-start | bytes 1572872 | tf_op jit(solution)/shard_map/ppermute | solution.py:58
  50.0 31.5 %collective-permute-start.7 = (bf16[128,2048]{1,0:T(8,128)(2,1)S(1)}, bf16[128,2048]{1,0:T(8,128)(2,1)}, u32[]{:S(2)}, u32[]{:S(2)}) collective-permute-start(bf16[128,2048]{1,0:T(8,128)(2,1)S(1)} %collective-permute-done.refs_1_), channel_id=1, source_target_pairs={{0,4},{4,0},{1,5},{5,1},{2,6},{6,2},{3,7},{7,3},{8,12},{12,8},{9,1... | collective-permute-start | bytes 1572872 | tf_op jit(solution)/shard_map/ppermute | solution.py:58
  82.6 33.4 %all-to-all-start.1 = ((bf16[8,64,1024]{2,1,0:T(8,128)(2,1)}), bf16[8,64,1024]{2,1,0:T(8,128)(2,1)S(1)}, u32[]{:S(2)}, u32[]{:S(2)}) async-start(bf16[8,64,1024]{2,1,0:T(8,128)(2,1)} %bitcast.110), calls=%async_computation.1 | async-start | bytes 2097152 | tf_op jit(solution)/shard_map/all_to_all | solution.py:98
  86.4 78.4 %all-gather.6.cloned.1.call-start = ((), (), s32[]{:S(2)}) async-start(), calls=%async_computation.8 | async-start | bytes 5242880 | tf_op jit(solution)/shard_map/all_gather | solution.py:103
  89.4 26.6 %collective-permute-start.10 = (bf16[128,2048]{1,0:T(8,128)(2,1)S(1)}, bf16[128,2048]{1,0:T(8,128)(2,1)}, u32[]{:S(2)}, u32[]{:S(2)}) collective-permute-start(bf16[128,2048]{1,0:T(8,128)(2,1)S(1)} %bitcast.105), channel_id=1, source_target_pairs={{0,1},{1,0},{2,3},{3,2},{4,5},{5,4},{6,7},{7,6},{8,9},{9,8},{10,11... | collective-permute-start | bytes 1572872 | tf_op jit(solution)/shard_map/ppermute | solution.py:58
  91.5 24.5 %collective-permute-start.9 = (bf16[128,2048]{1,0:T(8,128)(2,1)}, bf16[128,2048]{1,0:T(8,128)(2,1)S(1)}, u32[]{:S(2)}, u32[]{:S(2)}) collective-permute-start(bf16[128,2048]{1,0:T(8,128)(2,1)} %copy-done.11), channel_id=1, source_target_pairs={{0,4},{4,0},{1,5},{5,1},{2,6},{6,2},{3,7},{7,3},{8,12},{12,8},{9,1... | collective-permute-start | bytes 1572872 | tf_op jit(solution)/shard_map/ppermute | solution.py:58
  117.0 17.0 %collective-permute-start.11 = (bf16[128,2048]{1,0:T(8,128)(2,1)}, bf16[128,2048]{1,0:T(8,128)(2,1)S(1)}, u32[]{:S(2)}, u32[]{:S(2)}) collective-permute-start(bf16[128,2048]{1,0:T(8,128)(2,1)} %collective-permute-done.10.refs_1_), channel_id=1, source_target_pairs={{0,4},{4,0},{1,5},{5,1},{2,6},{6,2},{3,7},{7,3},{8,12},{12,8},{9,1... | collective-permute-start | bytes 1572872 | tf_op jit(solution)/shard_map/ppermute | solution.py:58
  118.5 23.4 %collective-permute-start.12 = (bf16[128,2048]{1,0:T(8,128)(2,1)S(1)}, bf16[128,2048]{1,0:T(8,128)(2,1)S(1)}, u32[]{:S(2)}, u32[]{:S(2)}) collective-permute-start(bf16[128,2048]{1,0:T(8,128)(2,1)S(1)} %bitcast.106), channel_id=1, source_target_pairs={{0,2},{1,3},{2,0},{3,1},{4,6},{5,7},{6,4},{7,5},{8,10},{9,11},{10,... | collective-permute-start | bytes 1572872 | tf_op jit(solution)/shard_map/ppermute | solution.py:58
  134.0 28.1 %copy-start.16 = (bf16[1024,512]{1,0:T(8,128)(2,1)S(1)}, bf16[1024,512]{1,0:T(8,128)(2,1)}, u32[]{:S(2)}) copy-start(bf16[1024,512]{1,0:T(8,128)(2,1)} %get-tuple-element.341.refs_0_) | copy-start | bytes 3145732
  134.0 21.0 %copy-start.24 = (bf16[128,2048]{1,0:T(8,128)(2,1)}, bf16[128,2048]{1,0:T(8,128)(2,1)S(1)}, u32[]{:S(2)}) copy-start(bf16[128,2048]{1,0:T(8,128)(2,1)S(1)} %collective-permute-done.11.refs_5_) | copy-start | bytes 1572868
  142.0 20.0 %copy-start.25 = (bf16[128,2048]{1,0:T(8,128)(2,1)}, bf16[128,2048]{1,0:T(8,128)(2,1)S(1)}, u32[]{:S(2)}) copy-start(bf16[128,2048]{1,0:T(8,128)(2,1)S(1)} %collective-permute-done.12.refs_2_) | copy-start | bytes 1572868
  142.0 11.8 %collective-permute-start.13 = (bf16[128,2048]{1,0:T(8,128)(2,1)S(1)}, bf16[128,2048]{1,0:T(8,128)(2,1)S(1)}, u32[]{:S(2)}, u32[]{:S(2)}) collective-permute-start(bf16[128,2048]{1,0:T(8,128)(2,1)S(1)} %collective-permute-done.12.refs_2_), channel_id=1, source_target_pairs={{0,4},{4,0},{1,5},{5,1},{2,6},{6,2},{3,7},{7,3},{8,12},{12,8},{9,1... | collective-permute-start | bytes 1572872 | tf_op jit(solution)/shard_map/ppermute | solution.py:58
  142.5 12.5 %collective-permute-start.14 = (bf16[128,2048]{1,0:T(8,128)(2,1)S(1)}, bf16[128,2048]{1,0:T(8,128)(2,1)}, u32[]{:S(2)}, u32[]{:S(2)}) collective-permute-start(bf16[128,2048]{1,0:T(8,128)(2,1)S(1)} %collective-permute-done.12.refs_2_), channel_id=1, source_target_pairs={{0,1},{1,0},{2,3},{3,2},{4,5},{5,4},{6,7},{7,6},{8,9},{9,8},{10,11... | collective-permute-start | bytes 1572872 | tf_op jit(solution)/shard_map/ppermute | solution.py:58
  155.0 32.6 %all-to-all-start.2 = ((bf16[8,64,1024]{2,1,0:T(8,128)(2,1)}), bf16[8,64,1024]{2,1,0:T(8,128)(2,1)S(1)}, u32[]{:S(2)}, u32[]{:S(2)}) async-start(bf16[8,64,1024]{2,1,0:T(8,128)(2,1)} %bitcast.89), calls=%async_computation.2 | async-start | bytes 2097152 | tf_op jit(solution)/shard_map/all_to_all | solution.py:98
  161.9 73.5 %all-gather.8.cloned.1.call-start = ((), (), s32[]{:S(2)}) async-start(), calls=%async_computation.9 | async-start | bytes 5242880 | tf_op jit(solution)/shard_map/all_gather | solution.py:103
  162.2 23.7 %collective-permute-start.16 = (bf16[1024,512]{1,0:T(8,128)(2,1)S(1)}, bf16[1024,512]{1,0:T(8,128)(2,1)S(1)}, u32[]{:S(2)}, u32[]{:S(2)}) collective-permute-start(bf16[1024,512]{1,0:T(8,128)(2,1)S(1)} %copy-done.16), channel_id=1, source_target_pairs={{0,8},{8,0},{1,9},{9,1},{2,10},{10,2},{3,11},{11,3},{4,12},{12,4},... | collective-permute-start | bytes 3145736 | tf_op jit(solution)/shard_map/ppermute | solution.py:58
  162.7 20.9 %collective-permute-start.15 = (bf16[128,2048]{1,0:T(8,128)(2,1)}, bf16[128,2048]{1,0:T(8,128)(2,1)}, u32[]{:S(2)}, u32[]{:S(2)}) collective-permute-start(bf16[128,2048]{1,0:T(8,128)(2,1)} %collective-permute-done.14.refs_3_), channel_id=1, source_target_pairs={{0,4},{4,0},{1,5},{5,1},{2,6},{6,2},{3,7},{7,3},{8,12},{12,8},{9,1... | collective-permute-start | bytes 1572872 | tf_op jit(solution)/shard_map/ppermute | solution.py:58
  185.9 19.2 %copy-start.17 = (bf16[1024,512]{1,0:T(8,128)(2,1)}, bf16[1024,512]{1,0:T(8,128)(2,1)S(1)}, u32[]{:S(2)}) copy-start(bf16[1024,512]{1,0:T(8,128)(2,1)S(1)} %collective-permute-done.16.refs_1_) | copy-start | bytes 3145732
  205.1 4.4 collective-permute-start.17
  214.6 28.0 %collective-permute-start.18 = (bf16[512,1024]{1,0:T(8,128)(2,1)}, bf16[512,1024]{1,0:T(8,128)(2,1)S(1)}, u32[]{:S(2)}, u32[]{:S(2)}) collective-permute-start(bf16[512,1024]{1,0:T(8,128)(2,1)} %get-tuple-element.336), channel_id=1, source_target_pairs={{0,8},{8,0},{1,9},{9,1},{2,10},{10,2},{3,11},{11,3},{4,12},{12,4},... | collective-permute-start | bytes 3145736 | tf_op jit(solution)/shard_map/ppermute | solution.py:58
  243.5 9.2 %copy-start.42 = (bf16[128,2048]{1,0:T(8,128)(2,1)S(1)}, bf16[128,2048]{1,0:T(8,128)(2,1)}, u32[]{:S(2)}) copy-start(bf16[128,2048]{1,0:T(8,128)(2,1)} %get-tuple-element.358) | copy-start | bytes 1572868
  246.3 33.7 %all-to-all-start.3 = ((bf16[8,64,1024]{2,1,0:T(8,128)(2,1)}), bf16[8,64,1024]{2,1,0:T(8,128)(2,1)S(1)}, u32[]{:S(2)}, u32[]{:S(2)}) async-start(bf16[8,64,1024]{2,1,0:T(8,128)(2,1)} %bitcast.107), calls=%async_computation.3 | async-start | bytes 2097152 | tf_op jit(solution)/shard_map/all_to_all | solution.py:108
  252.1 27.9 %collective-permute-start.19 = (bf16[1024,512]{1,0:T(8,128)(2,1)}, bf16[1024,512]{1,0:T(8,128)(2,1)S(1)}, u32[]{:S(2)}, u32[]{:S(2)}) collective-permute-start(bf16[1024,512]{1,0:T(8,128)(2,1)} %get-tuple-element.352), channel_id=1, source_target_pairs={{0,8},{8,0},{1,9},{9,1},{2,10},{10,2},{3,11},{11,3},{4,12},{12,4},... | collective-permute-start | bytes 3145736 | tf_op jit(solution)/shard_map/ppermute | solution.py:58
  252.7 27.3 %collective-permute-start.20 = (bf16[128,2048]{1,0:T(8,128)(2,1)S(1)}, bf16[128,2048]{1,0:T(8,128)(2,1)S(1)}, u32[]{:S(2)}, u32[]{:S(2)}) collective-permute-start(bf16[128,2048]{1,0:T(8,128)(2,1)S(1)} %copy-done.42), channel_id=1, source_target_pairs={{0,4},{4,0},{1,5},{5,1},{2,6},{6,2},{3,7},{7,3},{8,12},{12,8},{9,1... | collective-permute-start | bytes 1572872 | tf_op jit(solution)/shard_map/ppermute | solution.py:58
  283.1 27.0 %collective-permute-start.24 = (bf16[1024,1024]{1,0:T(8,128)(2,1)}, bf16[1024,1024]{1,0:T(8,128)(2,1)S(1)}, u32[]{:S(2)}, u32[]{:S(2)}) collective-permute-start(bf16[1024,1024]{1,0:T(8,128)(2,1)} %get-tuple-element.378), channel_id=1, source_target_pairs={{0,16},{16,0},{1,17},{17,1},{2,18},{18,2},{3,19},{19,3},{4,20},{20... | collective-permute-start | bytes 6291464 | tf_op jit(solution)/shard_map/ppermute | solution.py:58
  283.1 18.0 %collective-permute-start.21 = (bf16[128,2048]{1,0:T(8,128)(2,1)}, bf16[128,2048]{1,0:T(8,128)(2,1)S(1)}, u32[]{:S(2)}, u32[]{:S(2)}) collective-permute-start(bf16[128,2048]{1,0:T(8,128)(2,1)} %shard_map.239), channel_id=1, source_target_pairs={{0,1},{1,0},{2,3},{3,2},{4,5},{5,4},{6,7},{7,6},{8,9},{9,8},{10,11... | collective-permute-start | bytes 1572872 | tf_op jit(solution)/shard_map/ppermute | solution.py:58
  284.5 16.5 %collective-permute-start.22 = (bf16[128,2048]{1,0:T(8,128)(2,1)}, bf16[128,2048]{1,0:T(8,128)(2,1)S(1)}, u32[]{:S(2)}, u32[]{:S(2)}) collective-permute-start(bf16[128,2048]{1,0:T(8,128)(2,1)} %get-tuple-element.376), channel_id=1, source_target_pairs={{0,4},{4,0},{1,5},{5,1},{2,6},{6,2},{3,7},{7,3},{8,12},{12,8},{9,1... | collective-permute-start | bytes 1572872 | tf_op jit(solution)/shard_map/ppermute | solution.py:58
  285.1 24.9 %collective-permute-start.23 = (bf16[128,2048]{1,0:T(8,128)(2,1)}, bf16[128,2048]{1,0:T(8,128)(2,1)S(1)}, u32[]{:S(2)}, u32[]{:S(2)}) collective-permute-start(bf16[128,2048]{1,0:T(8,128)(2,1)} %get-tuple-element.377), channel_id=1, source_target_pairs={{0,4},{4,0},{1,5},{5,1},{2,6},{6,2},{3,7},{7,3},{8,12},{12,8},{9,1... | collective-permute-start | bytes 1572872 | tf_op jit(solution)/shard_map/ppermute | solution.py:58
  301.0 9.0 %copy-start.36 = (bf16[128,2048]{1,0:T(8,128)(2,1)}, bf16[128,2048]{1,0:T(8,128)(2,1)S(1)}, u32[]{:S(2)}) copy-start(bf16[128,2048]{1,0:T(8,128)(2,1)S(1)} %collective-permute-done.21.refs_4_) | copy-start | bytes 1572868
  301.1 9.0 %copy-start.37 = (bf16[128,2048]{1,0:T(8,128)(2,1)}, bf16[128,2048]{1,0:T(8,128)(2,1)S(1)}, u32[]{:S(2)}) copy-start(bf16[128,2048]{1,0:T(8,128)(2,1)S(1)} %collective-permute-done.22.refs_6_) | copy-start | bytes 1572868
  316.7 27.0 %collective-permute-start.29 = (bf16[1024,1024]{1,0:T(8,128)(2,1)}, bf16[1024,1024]{1,0:T(8,128)(2,1)S(1)}, u32[]{:S(2)}, u32[]{:S(2)}) collective-permute-start(bf16[1024,1024]{1,0:T(8,128)(2,1)} %get-tuple-element.405), channel_id=1, source_target_pairs={{0,16},{16,0},{1,17},{17,1},{2,18},{18,2},{3,19},{19,3},{4,20},{20... | collective-permute-start | bytes 6291464 | tf_op jit(solution)/shard_map/ppermute | solution.py:58
  316.7 27.0 %collective-permute-start.28 = (bf16[512,1024]{1,0:T(8,128)(2,1)}, bf16[512,1024]{1,0:T(8,128)(2,1)S(1)}, u32[]{:S(2)}, u32[]{:S(2)}) collective-permute-start(bf16[512,1024]{1,0:T(8,128)(2,1)} %get-tuple-element.404), channel_id=1, source_target_pairs={{0,8},{8,0},{1,9},{9,1},{2,10},{10,2},{3,11},{11,3},{4,12},{12,4},... | collective-permute-start | bytes 3145736 | tf_op jit(solution)/shard_map/ppermute | solution.py:58
  318.1 25.5 %collective-permute-start.25 = (bf16[128,2048]{1,0:T(8,128)(2,1)}, bf16[128,2048]{1,0:T(8,128)(2,1)S(1)}, u32[]{:S(2)}, u32[]{:S(2)}) collective-permute-start(bf16[128,2048]{1,0:T(8,128)(2,1)} %get-tuple-element.401), channel_id=1, source_target_pairs={{0,1},{1,0},{2,3},{3,2},{4,5},{5,4},{6,7},{7,6},{8,9},{9,8},{10,11... | collective-permute-start | bytes 1572872 | tf_op jit(solution)/shard_map/ppermute | solution.py:58
  318.7 24.9 %collective-permute-start.26 = (bf16[128,2048]{1,0:T(8,128)(2,1)}, bf16[128,2048]{1,0:T(8,128)(2,1)S(1)}, u32[]{:S(2)}, u32[]{:S(2)}) collective-permute-start(bf16[128,2048]{1,0:T(8,128)(2,1)} %get-tuple-element.402), channel_id=1, source_target_pairs={{0,2},{1,3},{2,0},{3,1},{4,6},{5,7},{6,4},{7,5},{8,10},{9,11},{10,... | collective-permute-start | bytes 1572872 | tf_op jit(solution)/shard_map/ppermute | solution.py:58
  321.1 22.6 %collective-permute-start.27 = (bf16[128,2048]{1,0:T(8,128)(2,1)}, bf16[128,2048]{1,0:T(8,128)(2,1)S(1)}, u32[]{:S(2)}, u32[]{:S(2)}) collective-permute-start(bf16[128,2048]{1,0:T(8,128)(2,1)} %get-tuple-element.403), channel_id=1, source_target_pairs={{0,4},{4,0},{1,5},{5,1},{2,6},{6,2},{3,7},{7,3},{8,12},{12,8},{9,1... | collective-permute-start | bytes 1572872 | tf_op jit(solution)/shard_map/ppermute | solution.py:58
  350.3 8.7 %copy-start.40 = (f32[1,1024]{1,0:T(1,128)S(1)}, f32[1,1024]{1,0:T(1,128)}, u32[]{:S(2)}) copy-start(f32[1,1024]{1,0:T(1,128)} %get-tuple-element.434) | copy-start | bytes 12292
  350.3 8.9 %copy-start.41 = (f32[1,768]{1,0:T(1,128)S(1)}, f32[1,768]{1,0:T(1,128)}, u32[]{:S(2)}) copy-start(f32[1,768]{1,0:T(1,128)} %get-tuple-element.433) | copy-start | bytes 9220
  350.3 9.1 %copy-start.39 = (f32[4,2048]{1,0:T(4,128)S(1)}, f32[4,2048]{1,0:T(4,128)}, u32[]{:S(2)}) copy-start(f32[4,2048]{1,0:T(4,128)} %get-tuple-element.432) | copy-start | bytes 98308
  350.3 31.8 %all-to-all-start.4 = ((bf16[8,64,1024]{2,1,0:T(8,128)(2,1)}), bf16[8,64,1024]{2,1,0:T(8,128)(2,1)S(1)}, u32[]{:S(2)}, u32[]{:S(2)}) async-start(bf16[8,64,1024]{2,1,0:T(8,128)(2,1)} %bitcast.121), calls=%async_computation.4 | async-start | bytes 2097152 | tf_op jit(solution)/shard_map/all_to_all | solution.py:108
  356.2 24.2 %collective-permute-start.30 = (bf16[512,1024]{1,0:T(8,128)(2,1)}, bf16[512,1024]{1,0:T(8,128)(2,1)}, u32[]{:S(2)}, u32[]{:S(2)}) collective-permute-start(bf16[512,1024]{1,0:T(8,128)(2,1)} %get-tuple-element.430), channel_id=1, source_target_pairs={{0,8},{8,0},{1,9},{9,1},{2,10},{10,2},{3,11},{11,3},{4,12},{12,4},... | collective-permute-start | bytes 3145736 | tf_op jit(solution)/shard_map/ppermute | solution.py:58
  356.8 21.2 %collective-permute-start.31 = (bf16[128,2048]{1,0:T(8,128)(2,1)}, bf16[128,2048]{1,0:T(8,128)(2,1)}, u32[]{:S(2)}, u32[]{:S(2)}) collective-permute-start(bf16[128,2048]{1,0:T(8,128)(2,1)} %get-tuple-element.431), channel_id=1, source_target_pairs={{0,4},{4,0},{1,5},{5,1},{2,6},{6,2},{3,7},{7,3},{8,12},{12,8},{9,1... | collective-permute-start | bytes 1572872 | tf_op jit(solution)/shard_map/ppermute | solution.py:58
  359.6 30.6 %copy-start = (bf16[1,128,2048]{2,1,0:T(8,128)(2,1)S(1)}, bf16[1,128,2048]{2,1,0:T(8,128)(2,1)}, u32[]{:S(2)}) copy-start(bf16[1,128,2048]{2,1,0:T(8,128)(2,1)} %param.13) | copy-start | bytes 1572868
  385.9 39.9 %all-to-all-start.5 = ((bf16[8,64,1024]{2,1,0:T(8,128)(2,1)}), bf16[8,64,1024]{2,1,0:T(8,128)(2,1)S(1)}, u32[]{:S(2)}, u32[]{:S(2)}) async-start(bf16[8,64,1024]{2,1,0:T(8,128)(2,1)} %bitcast.122), calls=%async_computation.5 | async-start | bytes 2097152 | tf_op jit(solution)/shard_map/all_to_all | solution.py:108
  391.2 27.9 %collective-permute-start.32 = (bf16[128,2048]{1,0:T(8,128)(2,1)}, bf16[128,2048]{1,0:T(8,128)(2,1)S(1)}, u32[]{:S(2)}, u32[]{:S(2)}) collective-permute-start(bf16[128,2048]{1,0:T(8,128)(2,1)} %get-tuple-element.451), channel_id=1, source_target_pairs={{0,1},{1,0},{2,3},{3,2},{4,5},{5,4},{6,7},{7,6},{8,9},{9,8},{10,11... | collective-permute-start | bytes 1572872 | tf_op jit(solution)/shard_map/ppermute | solution.py:58
  393.3 25.8 %collective-permute-start.33 = (bf16[128,2048]{1,0:T(8,128)(2,1)}, bf16[128,2048]{1,0:T(8,128)(2,1)S(1)}, u32[]{:S(2)}, u32[]{:S(2)}) collective-permute-start(bf16[128,2048]{1,0:T(8,128)(2,1)} %get-tuple-element.452), channel_id=1, source_target_pairs={{0,4},{4,0},{1,5},{5,1},{2,6},{6,2},{3,7},{7,3},{8,12},{12,8},{9,1... | collective-permute-start | bytes 1572872 | tf_op jit(solution)/shard_map/ppermute | solution.py:58
  394.8 30.9 %collective-permute-start.34 = (bf16[128,2048]{1,0:T(8,128)(2,1)}, bf16[128,2048]{1,0:T(8,128)(2,1)}, u32[]{:S(2)}, u32[]{:S(2)}) collective-permute-start(bf16[128,2048]{1,0:T(8,128)(2,1)} %get-tuple-element.453), channel_id=1, source_target_pairs={{0,4},{4,0},{1,5},{5,1},{2,6},{6,2},{3,7},{7,3},{8,12},{12,8},{9,1... | collective-permute-start | bytes 1572872 | tf_op jit(solution)/shard_map/ppermute | solution.py:58
  398.9 33.3 %copy-start.20 = (f32[128,2048]{1,0:T(8,128)S(1)}, f32[128,2048]{1,0:T(8,128)}, u32[]{:S(2)}) copy-start(f32[128,2048]{1,0:T(8,128)} %get-tuple-element.476) | copy-start | bytes 3145732
  429.0 29.6 %collective-permute-start.35 = (bf16[128,2048]{1,0:T(8,128)(2,1)}, bf16[128,2048]{1,0:T(8,128)(2,1)}, u32[]{:S(2)}, u32[]{:S(2)}) collective-permute-start(bf16[128,2048]{1,0:T(8,128)(2,1)} %get-tuple-element.471), channel_id=1, source_target_pairs={{0,1},{1,0},{2,3},{3,2},{4,5},{5,4},{6,7},{7,6},{8,9},{9,8},{10,11... | collective-permute-start | bytes 1572872 | tf_op jit(solution)/shard_map/ppermute | solution.py:58
  429.7 29.0 %collective-permute-start.36 = (bf16[128,2048]{1,0:T(8,128)(2,1)}, bf16[128,2048]{1,0:T(8,128)(2,1)}, u32[]{:S(2)}, u32[]{:S(2)}) collective-permute-start(bf16[128,2048]{1,0:T(8,128)(2,1)} %get-tuple-element.472), channel_id=1, source_target_pairs={{0,2},{1,3},{2,0},{3,1},{4,6},{5,7},{6,4},{7,5},{8,10},{9,11},{10,... | collective-permute-start | bytes 1572872 | tf_op jit(solution)/shard_map/ppermute | solution.py:58
  431.9 26.7 %collective-permute-start.37 = (bf16[128,2048]{1,0:T(8,128)(2,1)}, bf16[128,2048]{1,0:T(8,128)(2,1)}, u32[]{:S(2)}, u32[]{:S(2)}) collective-permute-start(bf16[128,2048]{1,0:T(8,128)(2,1)} %get-tuple-element.473), channel_id=1, source_target_pairs={{0,4},{4,0},{1,5},{5,1},{2,6},{6,2},{3,7},{7,3},{8,12},{12,8},{9,1... | collective-permute-start | bytes 1572872 | tf_op jit(solution)/shard_map/ppermute | solution.py:58
  441.6 17.6 %copy-start.21 = (f32[128,2048]{1,0:T(8,128)S(1)}, f32[128,2048]{1,0:T(8,128)}, u32[]{:S(2)}) copy-start(f32[128,2048]{1,0:T(8,128)} %get-tuple-element.482) | copy-start | bytes 3145732
  442.4 14.7 %all-to-all-start.6 = ((f32[32,1,768]{2,1,0:T(1,128)}), f32[32,1,768]{2,1,0:T(1,128)S(1)}, u32[]{:S(2)}, u32[]{:S(2)}) async-start(f32[32,1,768]{2,1,0:T(1,128)} %reshape.321), calls=%async_computation.6 | async-start | bytes 196608 | tf_op jit(solution)/shard_map/all_to_all | solution.py:759
  (27 other events, 93.1 us)
Sparse Core Ops, SparseCore 0:
  82.7 32.6 all-gather.3
  117.5 34.4 all-gather.5
  188.7 35.4 all-gather.7

commit v2 on v1

--- a/solution.py
+++ b/solution.py
@@ -74,18 +74,15 @@
 
 
 def gather_rest(value):
-    value = value[None]
-    for axis in reversed(RP):
-        place, size = lax.axis_index(axis), lax.axis_size(axis)
-        bit = 1
-        while bit < size:
-            other = swap(value, axis, bit)
-            upper = (place & bit) != 0
-            value = jnp.concatenate(
-                [jnp.where(upper, other, value), jnp.where(upper, value, other)], axis=0
-            )
-            bit *= 2
-    return value
+    place, size = lax.axis_index(RP), lax.axis_size(RP)
+    blocks = jnp.stack([value] + [swap(value, RP, d) for d in range(1, size)])
+    bit = 1
+    while bit < size:
+        pairs = blocks.reshape((size // (2 * bit), 2, bit) + value.shape)
+        turned = jnp.stack([pairs[:, 1], pairs[:, 0]], axis=1).reshape(blocks.shape)
+        blocks = jnp.where((place & bit) != 0, turned, blocks)
+        bit *= 2
+    return blocks
 
 
 def hand_on(value, distance):
@@ -101,6 +98,10 @@
 
 def spread_rest(mine):
     return lax.all_gather(mine, RP, axis=0, tiled=True)
+
+
+def collect_rest(terms):
+    return lax.psum_scatter(terms, RP, scatter_dimension=0, tiled=True)
 
 
 def collect_group(mine):
@@ -134,36 +135,11 @@
     lax.fori_loop(0, count // TILE, body, 0)
 
 
-def add_kernel(counts, *refs):
-    start = 0
-    ins = refs[: sum(count for count, _ in counts)]
-    outs = refs[len(ins) :]
-    for count, parts in counts:
-        group, ins = ins[:count], ins[count:]
-        here, outs = outs[:parts], outs[parts:]
-        start = 0
-        for out_ref in here:
-            at = slice(start, start + out_ref.shape[0])
-            start += out_ref.shape[0]
-            total = group[0][at, :].astype(f32)
-            for ref in group[1:]:
-                total += ref[at, :].astype(f32)
-            out_ref[...] = total.astype(out_ref.dtype)
-
-
 def add(*groups):
-    counts, outs, ins = [], [], []
-    for arrays, dtype, parts in groups:
-        rows, cols = arrays[0].shape
-        counts.append((len(arrays), parts))
-        outs += [((rows // parts, cols), dtype)] * parts
-        ins += arrays
-    sums = call(functools.partial(add_kernel, counts), outs, *ins)
-    result = []
-    for _, parts in counts:
-        result.append(list(sums[:parts]))
-        sums = sums[parts:]
-    return result
+    return [
+        [sum((x.astype(f32) for x in arrays[1:]), arrays[0].astype(f32)).astype(dtype)]
+        for arrays, dtype, _ in groups
+    ]
 
 
 def turn(value, tables, sign):
@@ -268,54 +244,70 @@
     )
 
 
-def weight_kernel(steps, place_ref, *refs):
-    pairs, (far_ref, own_ref) = refs[:-2], refs[-2:]
-
-    def store(out_ref):
-        start = 0
-        for lhs_ref, rhs_ref in zip(pairs[::2], pairs[1::2]):
-            cols = slice(start, start + rhs_ref.shape[1])
-            start += rhs_ref.shape[1]
-            out_ref[:, cols] = mm(lhs_ref[...].T, rhs_ref[...]).astype(bf16)
-
-    pl.when(pl.program_id(0) < steps)(lambda: store(far_ref))
-    pl.when(pl.program_id(0) >= steps)(lambda: store(own_ref))
+def weight_kernel(*refs):
+    pairs, out_ref = refs[:-1], refs[-1]
+    start = 0
+    for lhs_ref, rhs_ref in zip(pairs[::2], pairs[1::2]):
+        cols = slice(start, start + rhs_ref.shape[1])
+        start += rhs_ref.shape[1]
+        out_ref[:, cols] = mm(lhs_ref[...].T, rhs_ref[...]).astype(bf16)
 
 
 def weight_terms(*pairs):
+    count = pairs[0].shape[0]
+    cols = sum(rhs.shape[1] for rhs in pairs[1::2])
+    specs = []
+    for rhs in pairs[1::2]:
+        specs.append(pl.BlockSpec((count, 2 * TILE), lambda i: (0, i)))
+        specs.append(pl.BlockSpec(rhs.shape, lambda i: (0, 0)))
+    return call(
+        weight_kernel,
+        [((D, cols), bf16)],
+        *pairs,
+        grid=(D // (2 * TILE),),
+        in_specs=specs,
+        out_specs=[pl.BlockSpec((2 * TILE, cols), lambda i: (i, 0))],
+    )[0]
+
+
+def weight_half_kernel(per, place_ref, lhs_ref, rhs_ref, *out_refs):
+    term = mm(lhs_ref[...].T, rhs_ref[...]).astype(bf16)
+    for d, out_ref in enumerate(out_refs):
+
+        @pl.when(pl.program_id(0) // per == d)
+        def _(out_ref=out_ref):
+            out_ref[...] = term
+
+
+def weight_half(lhs, rhs, other):
     bh = lax.axis_size("bh")
     part = D // (2 * bh)
     tile = min(2 * TILE, part)
     per = part // tile
-    steps = bh * per
-    place = jnp.stack([lax.axis_index("dp"), lax.axis_index("bh")]).astype(jnp.int32)
+    place = jnp.stack([lax.axis_index("dp") ^ other, lax.axis_index("bh")]).astype(jnp.int32)
+    count, cols = rhs.shape
 
     def lhs_at(i, place_ref):
-        core = place_ref[0] ^ jnp.where(i < steps, 1, 0)
-        block = place_ref[1] ^ (i % steps // per)
-        return (0, (core * bh + block) * per + i % per)
-
-    count = pairs[0].shape[0]
-    cols = sum(rhs.shape[1] for rhs in pairs[1::2])
-    specs = []
-    for rhs in pairs[1::2]:
-        specs.append(pl.BlockSpec((count, tile), lhs_at))
-        specs.append(pl.BlockSpec(rhs.shape, lambda i, place_ref: (0, 0)))
+        return (0, (place_ref[0] * bh + (place_ref[1] ^ (i // per))) * per + i % per)
+
+    def out_at(d):
+        return lambda i, place_ref: (jnp.clip(i - d * per, 0, per - 1), 0)
+
     return pl.pallas_call(
-        functools.partial(weight_kernel, steps),
+        functools.partial(weight_half_kernel, per),
         grid_spec=pltpu.PrefetchScalarGridSpec(
             num_scalar_prefetch=1,
-            grid=(2 * steps,),
-            in_specs=specs,
-            out_specs=[
-                pl.BlockSpec((tile, cols), lambda i, place_ref: (jnp.minimum(i, steps - 1), 0)),
-                pl.BlockSpec((tile, cols), lambda i, place_ref: (jnp.maximum(i - steps, 0), 0)),
+            grid=(bh * per,),
+            in_specs=[
+                pl.BlockSpec((count, tile), lhs_at),
+                pl.BlockSpec((count, cols), lambda i, place_ref: (0, 0)),
             ],
+            out_specs=[pl.BlockSpec((tile, cols), out_at(d)) for d in range(bh)],
         ),
-        out_shape=[jax.ShapeDtypeStruct((D // 2, cols), bf16)] * 2,
+        out_shape=[jax.ShapeDtypeStruct((part, cols), bf16)] * bh,
         compiler_params=pltpu.CompilerParams(vmem_limit_bytes=58 * 2**20),
         cost_estimate=pl.CostEstimate(flops=1, bytes_accessed=1, transcendentals=0),
-    )(place, *pairs)
+    )(place, lhs, rhs)
 
 
 def output_kernel(att_ref, act_ref, dense_ref, down_ref, *out_refs):
@@ -409,50 +401,60 @@
     return terms, sums
 
 
-def attention_kernel(count, q_ref, g_ref, qpos_ref, kpos_ref, *refs):
+def places(block, start, shape, dim, sizes, t):
+    rows, tp = sizes
+    index = start + lax.broadcasted_iota(jnp.int32, shape, dim)
+    device = index // rows
+    block = block ^ (device // tp)
+    return (block * tp + (t ^ (device % tp))) * rows + index % rows
+
+
+def attention_kernel(count, sizes, place_ref, q_ref, g_ref, *refs):
     kv_refs, (o_ref, dq_ref), refs = refs[:count], refs[count : count + 2], refs[count + 2 :]
     dkv_refs, sum_ref = refs[:-1], refs[-1]
+    t, block, tile = place_ref[0], place_ref[1], 2 * TILE
     keys = jnp.concatenate([ref[:, :HS] for ref in kv_refs], axis=0)
     values = jnp.concatenate([ref[:, HS:] for ref in kv_refs], axis=0)
     keys_turned = keys.T
     values_turned = values.T
+    key_places = places(block, 0, (keys.shape[0], 1), 0, sizes, t)
     sum_ref[...] = jnp.zeros_like(sum_ref)
-
-    def step(at):
+    for start in range(0, q_ref.shape[0], tile):
+        at = slice(start, start + tile)
         query = q_ref[at, :]
         grad = g_ref[at, :]
-        scores = mm_nt(keys, query)
-        scores = jnp.where(kpos_ref[...] <= qpos_ref[:, at], scores, -1e30)
+        visible = key_places <= places(block, start, (1, tile), 1, sizes, t)
+        scores = jnp.where(visible, mm_nt(keys, query), -1e30)
         weights = jnp.exp(scores - jnp.max(scores, axis=0, keepdims=True))
         weights = weights * (1.0 / jnp.sum(weights, axis=0, keepdims=True))
         weights_low = weights.astype(bf16)
-        o_ref[at, :] = mm(values_turned, weights_low).T.astype(bf16)
+        result = mm(values_turned, weights_low)
+        o_ref[at, :] = result.T.astype(bf16)
         sum_ref[:, HS:] += mm(weights_low, grad)
-        weight_grad = mm_nt(values, grad)
-        delta = jnp.sum(weights * weight_grad, axis=0, keepdims=True)
-        score_grad = (weights * (weight_grad - delta)).astype(bf16)
+        delta = jnp.sum(result * grad.T.astype(f32), axis=0, keepdims=True)
+        score_grad = (weights * (mm_nt(values, grad) - delta)).astype(bf16)
         dq_ref[at, :] = (mm(keys_turned, score_grad).T * (HS**-0.5)).astype(bf16)
         sum_ref[:, :HS] += mm(score_grad, query)
-
-    tiles(q_ref.shape[0], step)
     start = 0
     for ref in dkv_refs:
         ref[...] = sum_ref[start : start + ref.shape[0], :].astype(bf16)
         start += ref.shape[0]
 
 
-def long_attention_kernel(q_ref, g_ref, kv_ref, qpos_ref, kpos_ref, o_ref, dq_ref, dkv_ref, sum_ref):
+def long_attention_kernel(sizes, place_ref, q_ref, g_ref, kv_ref, o_ref, dq_ref, dkv_ref, sum_ref):
     blocks = kv_ref.shape[0] // KEYS
+    t, block = place_ref[0], place_ref[1]
     sum_ref[...] = jnp.zeros_like(sum_ref)
 
     def step(at):
         query = q_ref[at, :]
         grad = g_ref[at, :]
+        query_places = places(block, at.start, (1, TILE), 1, sizes, t)
 
         def scores_of(j):
             here = pl.ds(pl.multiple_of(j * KEYS, KEYS), KEYS)
-            scores = mm_nt(kv_ref[here, :HS], query)
-            return here, jnp.where(kpos_ref[here, :] <= qpos_ref[:, at], scores, -1e30)
+            visible = places(block, j * KEYS, (KEYS, 1), 0, sizes, t) <= query_places
+            return here, jnp.where(visible, mm_nt(kv_ref[here, :HS], query), -1e30)
 
         def first(j, state):
             top, total = state
@@ -467,19 +469,14 @@
         )
         inverse = 1.0 / total
 
-        def second(j, state):
-            result, delta = state
+        def second(j, result):
             here, scores = scores_of(j)
             weights = jnp.exp(scores - top) * inverse
-            values = kv_ref[here, HS:]
-            weight_grad = mm_nt(values, grad)
-            result = result + mm(values.T, weights.astype(bf16))
-            return result, delta + jnp.sum(weights * weight_grad, axis=0, keepdims=True)
-
-        result, delta = lax.fori_loop(
-            0, blocks, second, (jnp.zeros((HS, TILE), f32), jnp.zeros(row, f32))
-        )
+            return result + mm(kv_ref[here, HS:].T, weights.astype(bf16))
+
+        result = lax.fori_loop(0, blocks, second, jnp.zeros((HS, TILE), f32))
         o_ref[at, :] = result.T.astype(bf16)
+        delta = jnp.sum(result * grad.T.astype(f32), axis=0, keepdims=True)
 
         def third(j, result):
             here, scores = scores_of(j)
@@ -497,22 +494,29 @@
     dkv_ref[...] = sum_ref[...].astype(bf16)
 
 
-def attention(query, grad, kv_blocks, qpos, kpos):
-    count, total = len(kv_blocks), kpos.shape[0]
+def attention(query, grad, kv_blocks, sizes):
+    place = jnp.stack([lax.axis_index(TP), lax.axis_index("bh")]).astype(jnp.int32)
+    count, total = len(kv_blocks), sum(block.shape[0] for block in kv_blocks)
     low = (query.shape, bf16)
     scratch = [pltpu.VMEM((total, 2 * HS), f32)]
+    vmem = pl.BlockSpec(memory_space=pltpu.VMEM)
+    smem = pl.BlockSpec(memory_space=pltpu.SMEM)
     if total <= KEYS:
         attended, grad_query, *grad_kv = call(
-            functools.partial(attention_kernel, count),
+            functools.partial(attention_kernel, count, sizes),
             [low, low] + [(block.shape, bf16) for block in kv_blocks],
-            query, grad, qpos, kpos, *kv_blocks,
+            place, query, grad, *kv_blocks,
             scratch=scratch,
+            in_specs=[smem] + [vmem] * (2 + count),
         )
         return attended, grad_query, grad_kv
     kv_all = jnp.concatenate(kv_blocks, axis=0)
     attended, grad_query, grad_kv = call(
-        long_attention_kernel, [low, low, (kv_all.shape, bf16)], query, grad, kv_all, qpos, kpos,
+        functools.partial(long_attention_kernel, sizes),
+        [low, low, (kv_all.shape, bf16)],
+        place, query, grad, kv_all,
         scratch=scratch,
+        in_specs=[smem] + [vmem] * 3,
     )
     return attended, grad_query, jnp.split(grad_kv, count, axis=0)
 
@@ -556,9 +560,8 @@
         axis=0,
     )
     kinds = smalls.shape[0]
-    smalls = gather_rest(smalls).reshape(-1, 4 * HS)
-    extra = 8 * -(-smalls.shape[0] // 8)
-    smalls = jnp.pad(smalls, ((0, extra - smalls.shape[0]), (0, 0)))
+    count = kinds * rows
+    smalls = jnp.pad(smalls.reshape(1, count), ((0, 7), (0, 4 * HS - count)))
     heads_own = jnp.concatenate(
         [
             qkv_weight.reshape(rows, 3, HEADS, HS).transpose(2, 0, 1, 3).reshape(HEADS, rows, 3 * HS),
@@ -582,18 +585,15 @@
     row = jnp.arange(group_len, dtype=jnp.int32)
     inside = ((row // sub_len) ^ t) * sub_len + row % sub_len
     query_places = bh * group_len + inside
-    key_places = jnp.concatenate([(bh ^ d) * group_len + inside for d in range(bh_size)])
     tables = rotary_tables(query_places.astype(f32))
-    x_near, x_rows, m_heads, up_own, g_late, tables, query_places, key_places = join(
-        x_near, x_rows, m_heads, up_own, g_own, tables, query_places[None, :], key_places[:, None]
+    x_near, x_rows, m_heads, up_own, g_late, tables = join(
+        x_near, x_rows, m_heads, up_own, g_own, tables
     )
     w_heads = spread_rest(m_heads[:, :rows].reshape(tp * rows, -1))
     x_rows += [gather_axis(block, "bl") for block in x_near[3:]]
     g_first = swap(g_late, "hd", 1)
     m_up = spread_group(up_own)
-    smalls = m_heads[:, rows:].reshape(tp, -1)[:, : rp * kinds * rows]
-    smalls = smalls.reshape(tp, rp, kinds, rows).transpose(1, 0, 2, 3).reshape(n_dev, kinds, rows)
-    smalls = smalls.astype(f32)
+    smalls = gather_rest(m_heads[:, rows, :count]).reshape(n_dev, kinds, rows).astype(f32)
     vectors = smalls[:, :5].transpose(1, 0, 2).reshape(5, D)
     nq = qkv_bias.shape[0] // rows
     b_qkv = smalls[:, 5 : 5 + nq].reshape(3, HEADS, HS)
@@ -644,23 +644,23 @@
         grid=(1,),
         in_specs=[vmem] * tp + [pl.BlockSpec((D, HS), lambda i: (0, 3))],
     )
-    down_far, down_own = weight_terms(g_all, activated)
+    down_far = weight_half(g_all, activated, 1)
+    down_far, grad_att, g_all = join(down_far, grad_att, g_all)
+    down_far = [swap(terms, "dp", 1) for terms in reversed(down_far)][::-1]
+    down_own = weight_half(g_all, activated, 0)
     down_far, down_own, grad_att = join(down_far, down_own, grad_att)
-    down_far = swap(down_far, "dp", 1)
-    down_far, grad_att = join(down_far, grad_att)
-    ((down_mine),) = add(([down_far, down_own], bf16, bh_size))
-    down_mine, grad_att = join(down_mine, grad_att)
-    down_others = [swap(down_mine[d], "bh", d) for d in range(1, bh_size)]
-    attended, grad_query, grad_kv = attention(
-        query, grad_att, kv_blocks, query_places, key_places
-    )
+    down_sent = add(*[([down_far[d], down_own[d]], bf16, 1) for d in range(1, bh_size)])
+    down_sent, grad_att = join(down_sent, grad_att)
+    down_others = [swap(sent[0], "bh", d + 1) for d, sent in enumerate(down_sent)]
+    attended, grad_query, grad_kv = attention(query, grad_att, kv_blocks, (sub_len, tp))
     hd_terms = (hd_size, sub_len)
     out_far = [
         output_terms(attended, activated, w_heads, w_down, far, *hd_terms, bf16)
         for far in range(1, bl_size)
     ]
-    down_others, out_far, attended, grad_kv, slope = join(
-        down_others, out_far, attended, grad_kv, slope
+    out_own = output_terms(attended, activated, w_heads, w_down, 0, *hd_terms, f32)
+    down_others, out_far, attended, grad_kv, slope, out_own = join(
+        down_others, out_far, attended, grad_kv, slope, out_own
     )
     part = hd_size // 4
     parts = [range(hd_size - (g + 1) * part, hd_size - g * part) for g in range(4)]
@@ -674,56 +674,50 @@
             for d in ds
         ]
 
-    ((down_last,),) = add(([down_mine[0], *down_others], bf16, 1))
+    ((down_last,),) = add(([down_far[0], down_own[0], *down_others], bf16, 1))
     down_last, attended, slope = join(down_last, attended, slope)
     kv_others = [swap(grad_kv[d], "bh", d) for d in range(1, bh_size)]
     down_grad = collect_group(down_last)
     received = over_bl(out_far, parts[0])
     grad_pre_up, up_bias_term = backward(g_all, w_down, slope)
-    out_own = output_terms(attended, activated, w_heads, w_down, 0, *hd_terms, f32)
-    up_far, up_own = weight_terms(mlp_in, grad_pre_up)
-    kv_others, down_grad, received, grad_pre_up, out_own, up_far, up_own, out_far = join(
-        kv_others, down_grad, received, grad_pre_up, out_own, up_far, up_own, out_far
-    )
+    up_terms = weight_terms(mlp_in, grad_pre_up)
+    kv_others, down_grad, received, grad_pre_up, out_far, up_terms = join(
+        kv_others, down_grad, received, grad_pre_up, out_far, up_terms
+    )
+    up_mine = collect_rest(up_terms)
     out = dict(zip(parts[0], add(*sums_of(out_own, received, parts[0]))))
-    out, kv_others, up_far = join(out, kv_others, up_far)
+    out, kv_others = join(out, kv_others)
     out_near = {d: hand_on(out[d][0], d) for d in parts[0]}
-    received = over_bl(out_far, [*parts[1], *parts[2]])
-    up_far = swap(up_far, "dp", 1)
+    middle = [*parts[1], *parts[2]]
+    received = over_bl(out_far, middle)
     grad_project, qkv_bias_term = call(
         functools.partial(turn_back_kernel, bh_size),
         [((group_len, 3 * HS), bf16), ((1, 3 * HS), f32)],
         grad_query, grad_kv[0], *kv_others, *tables,
     )
-    heads_far, heads_own = weight_terms(attn_in, grad_project, g_all, attended)
-    out_near, received, up_far, grad_project, heads_far, heads_own, out_far = join(
-        out_near, received, up_far, grad_project, heads_far, heads_own, out_far
-    )
-    middle = [*parts[1], *parts[2]]
-    up_mine, *out = add(
-        ([up_far, up_own], bf16, bh_size),
-        *sums_of(out_own, received, middle, [out_near[3]] if four else []),
-    )
-    up_mine, out, grad_project, heads_far = join(up_mine, out, grad_project, heads_far)
+    in_terms, sums = input_terms(
+        x_blocks, average, inverse, grad_project, grad_pre_up, w_heads, w_up, vectors, hd_size
+    )
+    in_own = in_terms[:hd_size]
+    in_far = [in_terms[f * hd_size : (f + 1) * hd_size] for f in range(1, bl_size)]
+    out_near, received, out_far, in_far, grad_project = join(
+        out_near, received, out_far, in_far, grad_project
+    )
+    out = add(*sums_of(out_own, received, middle, [out_near[3]] if four else []))
+    out, in_far, grad_project = join(out, in_far, grad_project)
     out_near |= {d: hand_on(term, d) for d, (term,) in zip(middle, out)}
     received = over_bl(out_far, parts[3])
-    up_others = [swap(up_mine[d], "bh", d) for d in range(1, bh_size)]
-    heads_far = swap(heads_far, "dp", 1)
-    in_terms, sums = input_terms(
-        x_blocks, average, inverse, grad_project, grad_pre_up, w_heads, w_up, vectors, hd_size
-    )
-    out_near, received, up_others, heads_far, in_terms = join(
-        out_near, received, up_others, heads_far, in_terms
-    )
-    in_own = in_terms[:hd_size]
-    in_far = [in_terms[f * hd_size : (f + 1) * hd_size] for f in range(1, bl_size)]
-    (up_last,), heads_mine = add(
-        ([up_mine[0], *up_others], bf16, 1), ([heads_far, heads_own], bf16, bh_size)
-    )
-    up_last, heads_mine, in_far = join(up_last, heads_mine, in_far)
-    up_grad = collect_group(up_last)
-    heads_others = [swap(heads_mine[d], "bh", d) for d in range(1, bh_size)]
     received_in = over_bl(in_far, parts[0])
+    heads_terms = weight_terms(attn_in, grad_project, g_all, attended)
+    out_near, received, received_in, heads_terms, up_mine, in_far = join(
+        out_near, received, received_in, heads_terms, up_mine, in_far
+    )
+    heads_mine = collect_rest(heads_terms)
+    ins = add(*sums_of(in_own, received_in, parts[0]))
+    ins, up_mine, in_far = join(ins, up_mine, in_far)
+    up_grad = collect_group(up_mine)
+    in_near = {d: hand_on(term, d) for d, (term,) in zip(parts[0], ins)}
+    received_in = over_bl(in_far, middle)
     sums = jnp.concatenate([sums, jnp.sum(g_own.astype(f32), axis=0, keepdims=True)], axis=0)
     qkv_bias_full = lax.dynamic_update_slice(
         jnp.zeros((3, HEADS, HS), f32), qkv_bias_term.reshape(3, 1, HS), (0, t, 0)
@@ -737,25 +731,19 @@
         ],
         axis=1,
     )
-    up_grad, heads_others, received_in, small_terms, in_far, in_own = join(
-        up_grad, heads_others, received_in, small_terms, in_far, in_own
-    )
-    (heads_last,), *ins = add(
-        ([heads_mine[0], *heads_others], bf16, 1), *sums_of(in_own, received_in, parts[0])
-    )
-    heads_last, ins, in_far = join(heads_last, ins, in_far)
-    heads_grad = collect_group(heads_last)
-    in_near = {d: hand_on(term, d) for d, (term,) in zip(parts[0], ins)}
-    received_in = over_bl(in_far, middle)
+    up_grad, in_near, received_in, small_terms, in_far = join(
+        up_grad, in_near, received_in, small_terms, in_far
+    )
+    ins = add(*sums_of(in_own, received_in, middle, [in_near[3]] if four else []))
+    ins, in_far, heads_mine, small_terms = join(ins, in_far, heads_mine, small_terms)
+    heads_grad = collect_group(heads_mine)
+    received_in = over_bl(in_far, parts[3])
     down_grad = down_grad.astype(f32).transpose(1, 0, 2).reshape(rows, ff)
     up_grad = up_grad.astype(f32).transpose(1, 0, 2).reshape(rows, ff)
-    heads_grad, in_near, received_in, down_grad, up_grad, in_far, in_own, small_terms = join(
-        heads_grad, in_near, received_in, down_grad, up_grad, in_far, in_own, small_terms
-    )
-    ins = add(*sums_of(in_own, received_in, middle, [in_near[3]] if four else []))
-    ins, in_far, small_terms, heads_grad = join(ins, in_far, small_terms, heads_grad)
+    heads_grad, received_in, down_grad, up_grad, ins, small_terms = join(
+        heads_grad, received_in, down_grad, up_grad, ins, small_terms
+    )
     in_near |= {d: hand_on(term, d) for d, (term,) in zip(middle, ins)}
-    received_in = over_bl(in_far, parts[3])
     small = lax.all_to_all(small_terms, ALL, split_axis=0, concat_axis=0, tiled=True)
     heads_grad = heads_grad.astype(f32)
     dense_grad = heads_grad[:, :, 3 * HS :].transpose(1, 0, 2).reshape(rows, D)

time: 477 us -> 449 us (0.941)
  Pallas kernels: 145 us -> 119 us
  other arithmetic: 14.7 us -> 28.2 us
  local copies, waits for them, and re-layouts: 42.2 us -> 32.9 us
  starting transfers between devices: 80.6 us -> 74 us
    pallas_call x3 -> x2, Pallas kernels: 29.2 us -> 14.3 us  [weight_half(): pl.pallas_call(functools.partial(weight_half_kernel, per), grid_spec=pltp...]
    pallas_call x16 -> x11, Pallas kernels: 116 us -> 105 us  [call(): pl.pallas_call(kernel, grid=grid, out_shape=[jax.ShapeDtypeStruct(shape,...]
    convert_element_type x1 -> x9, other arithmetic: 0.01 us -> 11.2 us  [the longest x8 11.2 us: add(): sum((x.astype(f32) for x in arrays[1:]), arrays[0].astype(f32))]
    unnamed x92 -> x71, local copies, waits for them, and re-layouts: 16.7 us -> 7.81 us
    ppermute x38 -> x36, waiting for transfers between devices: 160 us -> 156 us  [swap(): return lax.ppermute(value, axis, [(i, i ^ distance) for i in range(size)])]
    ppermute x38 -> x36, starting transfers between devices: 46.5 us -> 45.1 us  [swap(): return lax.ppermute(value, axis, [(i, i ^ distance) for i in range(size)])]
  transfers between devices with their start and end apart: 48 -> 48, of which waited for: 22 -> 26; matrix products, arithmetic and copies ran while one was open for 8% -> 11% of each run, Pallas kernels for 26% -> 27%
where the time goes in v2:
time: 449 us; the launch traced here: 443 us
  waiting for transfers between devices  175 us (39%)
  Pallas kernels  119 us (27%)
  starting transfers between devices  74 us (16%)
  local copies, waits for them, and re-layouts  32.9 us (7%)
  other arithmetic  28.2 us (6%)
  between operations  14.7 us (3%)
    ppermute x36, waiting for transfers between devices, swap(): return lax.ppermute(value, axis, [(i, i ^ distance) for i in range(size)])  156 us
    pallas_call x11, Pallas kernels, call(): pl.pallas_call(kernel, grid=grid, out_shape=[jax.ShapeDtypeStruct(shape,...  105 us
    ppermute x36, starting transfers between devices, swap(): return lax.ppermute(value, axis, [(i, i ^ distance) for i in range(size)])  45.1 us
    pallas_call x2, Pallas kernels, weight_half(): pl.pallas_call(functools.partial(weight_half_kernel, per), grid_spec=pltp...  14.3 us
    all_to_all x3, starting transfers between devices, collect_group(): return lax.all_to_all(mine, TP, split_axis=0, concat_axis=0, tiled=True)  13.7 us
    convert_element_type x8, other arithmetic, add(): sum((x.astype(f32) for x in arrays[1:]), arrays[0].astype(f32))  11.2 us
    all_to_all x1, waiting for transfers between devices, per_device(): lax.all_to_all(small_terms, ALL, split_axis=0, concat_axis=0, tiled=True)  9.15 us
  transfers between devices with their start and end apart: 48, of which 26 were waited for; matrix products, arithmetic and copies ran while one was open for 11% of the time, Pallas kernels for 27%

profile of v2, /device:TPU:0, one launch (start us, length us, event | category | flops | bytes accessed | tf_op | source)
XLA Modules:
  0.0 443.4 jit_solution(3924659040416574932)
XLA Ops:
  7.2 3.1 collective-permute-start
  10.3 2.6 collective-permute-start.1
  17.2 1.7 copy.87
  21.6 2.1 pad_maximum_fusion
  23.7 9.8 %collective-permute-done.refs_1_ = bf16[128,2048]{1,0:T(8,128)(2,1)S(1)} collective-permute-done((bf16[128,2048]{1,0:T(8,128)(2,1)}, bf16[128,2048]{1,0:T(8,128)(2,1)S(1)}, u32[]{:S(2)}, u32[]{:S(2)}) %collective-permute-start) | collective-permute-done | bytes 524320 | tf_op jit(solution)/shard_map/ppermute | solution.py:58
  33.5 2.5 collective-permute-done.1.refs_2_
  37.5 3.6 all-to-all-start
  41.2 1.9 collective-permute-start.4
  45.1 1.9 multiply_sine_fusion
  50.6 21.7 %collective-permute-done.4.refs_3_ = bf16[128,2048]{1,0:T(8,128)(2,1)S(1)} collective-permute-done((bf16[128,2048]{1,0:T(8,128)(2,1)S(1)}, bf16[128,2048]{1,0:T(8,128)(2,1)S(1)}, u32[]{:S(2)}, u32[]{:S(2)}) %collective-permute-start.4) | collective-permute-done | bytes 524320 | tf_op jit(solution)/shard_map/ppermute | solution.py:58
  72.4 4.9 %collective-permute-done.5.refs_5_ = bf16[128,2048]{1,0:T(8,128)(2,1)S(1)} collective-permute-done((bf16[128,2048]{1,0:T(8,128)(2,1)S(1)}, bf16[128,2048]{1,0:T(8,128)(2,1)S(1)}, u32[]{:S(2)}, u32[]{:S(2)}) %collective-permute-start.5) | collective-permute-done | bytes 524320 | tf_op jit(solution)/shard_map/ppermute | solution.py:58
  79.2 4.7 %all-to-all-start.1 = ((bf16[8,64,1024]{2,1,0:T(8,128)(2,1)}), bf16[8,64,1024]{2,1,0:T(8,128)(2,1)S(1)}, u32[]{:S(2)}, u32[]{:S(2)}) async-start(bf16[8,64,1024]{2,1,0:T(8,128)(2,1)} %bitcast.118), calls=%async_computation.1 | async-start | bytes 2097152 | tf_op jit(solution)/shard_map/all_to_all | solution.py:95
  86.3 2.4 copy.84
  88.7 2.0 collective-permute-start.7
  95.0 12.8 %collective-permute-done.7.refs_7_ = bf16[128,2048]{1,0:T(8,128)(2,1)S(1)} collective-permute-done((bf16[128,2048]{1,0:T(8,128)(2,1)S(1)}, bf16[128,2048]{1,0:T(8,128)(2,1)S(1)}, u32[]{:S(2)}, u32[]{:S(2)}) %collective-permute-start.7) | collective-permute-done | bytes 524320 | tf_op jit(solution)/shard_map/ppermute | solution.py:58
  107.8 6.7 %collective-permute-done.8.refs_1_ = bf16[128,2048]{1,0:T(8,128)(2,1)} collective-permute-done((bf16[128,2048]{1,0:T(8,128)(2,1)S(1)}, bf16[128,2048]{1,0:T(8,128)(2,1)}, u32[]{:S(2)}, u32[]{:S(2)}) %collective-permute-start.8) | collective-permute-done | bytes 524320 | tf_op jit(solution)/shard_map/ppermute | solution.py:58
  116.3 2.4 collective-permute-start.13
  118.7 12.8 %shard_map.228 = (bf16[1024,2048]{1,0:T(8,128)(2,1)}, bf16[1024,2048]{1,0:T(8,128)(2,1)}, bf16[1024,256]{1,0:T(8,128)(2,1)}, bf16[1024,512]{1,0:T(8,128)(2,1)}, f32[1024,1]{1,0:T(8,128)}, /*index=5*/f32[1024,1]{1,0:T(8,128)}) custom-call(bf16[128,2048]{1,0:T(8,128)(2,1)} %bitcast.108, bf16[128,2048]{1,0:T(8,128)(2,1)} %copy-done.7, ...), custom_call_target="tpu_custom_call" | custom-call | flops 1 | bytes 1 | tf_op jit(solution)/shard_map/pallas_call | solution.py:118
  131.5 9.8 %collective-permute-done.13.refs_2_ = bf16[128,2048]{1,0:T(8,128)(2,1)S(1)} collective-permute-done((bf16[128,2048]{1,0:T(8,128)(2,1)S(1)}, bf16[128,2048]{1,0:T(8,128)(2,1)S(1)}, u32[]{:S(2)}, u32[]{:S(2)}) %collective-permute-start.13) | collective-permute-done | bytes 524320 | tf_op jit(solution)/shard_map/ppermute | solution.py:58
  142.1 12.6 %collective-permute-done.14.refs_6_ = bf16[128,2048]{1,0:T(8,128)(2,1)S(1)} collective-permute-done((bf16[128,2048]{1,0:T(8,128)(2,1)S(1)}, bf16[128,2048]{1,0:T(8,128)(2,1)S(1)}, u32[]{:S(2)}, u32[]{:S(2)}) %collective-permute-start.14) | collective-permute-done | bytes 524320 | tf_op jit(solution)/shard_map/ppermute | solution.py:58
  155.8 3.9 all-to-all-start.2
  161.3 2.0 collective-permute-start.16
  163.3 12.0 %shard_map.229 = (bf16[1024,1024]{1,0:T(8,128)(2,1)}, f32[1024,1024]{1,0:T(8,128)}) custom-call(bf16[1024,2048]{1,0:T(8,128)(2,1)} %get-tuple-element.277.mlp_ref.refs_0_, bf16[2048,1024]{1,0:T(8,128)(2,1)} %all-gather.6.cloned.1.call-done.w_ref.refs_13_, f32[1,1024]{1,0:T(1,128)} %constant_dynamic-slice_fusion.b_ref), custom_call_target="tpu_custom_call" | custom-call | flops 1 | bytes 1 | tf_op jit(solution)/shard_map/pallas_call | solution.py:118
  175.3 6.1 %collective-permute-done.16.refs_7_ = bf16[128,2048]{1,0:T(8,128)(2,1)} collective-permute-done((bf16[128,2048]{1,0:T(8,128)(2,1)}, bf16[128,2048]{1,0:T(8,128)(2,1)}, u32[]{:S(2)}, u32[]{:S(2)}) %collective-permute-start.16) | collective-permute-done | bytes 524320 | tf_op jit(solution)/shard_map/ppermute | solution.py:58
  181.4 2.0 collective-permute-done.17.refs_1_
  183.5 1.9 all-to-all-done.2
  187.0 6.3 %shard_map.230 = (bf16[1024,2048]{1,0:T(8,128)(2,1)}, bf16[1024,256]{1,0:T(8,128)(2,1)}) custom-call(bf16[128,2048]{1,0:T(8,128)(2,1)} %bitcast.113, bf16[128,2048]{1,0:T(8,128)(2,1)} %collective-permute-done.8.refs_1_, bf16[128,2048]{1,0:T(8,128)(2,1)} %copy-done.26, bf16[128,2048]{1,0:T(8,128)(2,1)} %collective-permute-done.15.refs_3_, ...), custom_call_target="tpu_custom_call" | custom-call | flops 1 | bytes 1 | tf_op jit(solution)/shard_map/pallas_call | solution.py:118
  193.3 7.4 %shard_map.231 = (bf16[512,1024]{1,0:T(8,128)(2,1)}, bf16[512,1024]{1,0:T(8,128)(2,1)}) custom-call(s32[2]{0:T(128)} %get-tuple-element.443.place_ref, bf16[1024,2048]{1,0:T(8,128)(2,1)} %get-tuple-element.298.lhs_ref.g_ref.refs_2_, bf16[1024,1024]{1,0:T(8,128)(2,1)} %get-tuple-element.292.rhs_ref.act_ref), custom_call_target="tpu_custom_call" | custom-call | flops 1 | bytes 1 | tf_op jit(solution)/shard_map/pallas_call | solution.py:296
  201.7 6.9 %shard_map.232 = (bf16[512,1024]{1,0:T(8,128)(2,1)}, bf16[512,1024]{1,0:T(8,128)(2,1)}) custom-call(s32[2]{0:T(128)} %pad_add_fusion.2.place_ref, bf16[1024,2048]{1,0:T(8,128)(2,1)} %get-tuple-element.298.lhs_ref.g_ref.refs_2_, bf16[1024,1024]{1,0:T(8,128)(2,1)} %get-tuple-element.292.rhs_ref.act_ref), custom_call_target="tpu_custom_call" | custom-call | flops 1 | bytes 1 | tf_op jit(solution)/shard_map/pallas_call | solution.py:296
  208.7 1.6 add_convert_fusion.1
  211.9 12.7 %shard_map.233 = (bf16[1024,256]{1,0:T(8,128)(2,1)}, bf16[1024,256]{1,0:T(8,128)(2,1)}, bf16[1024,512]{1,0:T(8,128)(2,1)}, bf16[1024,512]{1,0:T(8,128)(2,1)}) custom-call(s32[2]{0:T(128)} %get-tuple-element.442.place_ref, bf16[1024,256]{1,0:T(8,128)(2,1)} %get-tuple-element.249.q_ref, bf16[1024,256]{1,0:T(8,128)(2,1)} %get-tuple-element.305.g_ref, ...), custom_call_target="tpu_custom_call" | custom-call | flops 1 | bytes 1 | tf_op jit(solution)/shard_map/pallas_call | solution.py:118
  226.0 6.2 %shard_map.234 = (bf16[128,2048]{1,0:T(8,128)(2,1)}, bf16[128,2048]{1,0:T(8,128)(2,1)}, bf16[128,2048]{1,0:T(8,128)(2,1)}, bf16[128,2048]{1,0:T(8,128)(2,1)}) custom-call(bf16[1024,256]{1,0:T(8,128)(2,1)} %get-tuple-element.369.att_ref.refs_3_, bf16[1024,1024]{1,0:T(8,128)(2,1)} %get-tuple-element.292.rhs_ref.act_ref, ...), custom_call_target="tpu_custom_call" | custom-call | flops 1 | bytes 1 | tf_op jit(solution)/shard_map/pallas_call | solution.py:118
  232.1 6.9 %shard_map.235 = (f32[128,2048]{1,0:T(8,128)}, f32[128,2048]{1,0:T(8,128)}, f32[128,2048]{1,0:T(8,128)}, f32[128,2048]{1,0:T(8,128)}) custom-call(bf16[1024,256]{1,0:T(8,128)(2,1)} %get-tuple-element.369.att_ref.refs_3_, bf16[1024,1024]{1,0:T(8,128)(2,1)} %get-tuple-element.292.rhs_ref.act_ref, ...), custom_call_target="tpu_custom_call" | custom-call | flops 1 | bytes 1 | tf_op jit(solution)/shard_map/pallas_call | solution.py:118
  239.0 2.1 collective-permute-done.20
  242.8 5.6 %all-to-all-start.3 = ((bf16[8,64,1024]{2,1,0:T(8,128)(2,1)}), bf16[8,64,1024]{2,1,0:T(8,128)(2,1)S(1)}, u32[]{:S(2)}, u32[]{:S(2)}) async-start(bf16[8,64,1024]{2,1,0:T(8,128)(2,1)} %bitcast.26), calls=%async_computation.3 | async-start | bytes 2097152 | tf_op jit(solution)/shard_map/all_to_all | solution.py:109
  249.1 1.9 collective-permute-start.22
  251.0 9.3 %shard_map.236 = (bf16[1024,1024]{1,0:T(8,128)(2,1)}, f32[1,1024]{1,0:T(1,128)}) custom-call(bf16[1024,2048]{1,0:T(8,128)(2,1)} %get-tuple-element.298.lhs_ref.g_ref.refs_2_, bf16[2048,1024]{1,0:T(8,128)(2,1)} %all-gather.8.cloned.1.call-done.down_ref.w_ref, f32[1024,1024]{1,0:T(8,128)} %get-tuple-element.333.slope_ref), custom_call_target="tpu_custom_call" | custom-call | flops 1 | bytes 1 | tf_op jit(solution)/shard_map/pallas_call | solution.py:118
  260.3 8.6 %shard_map.237 = bf16[2048,1024]{1,0:T(8,128)(2,1)} custom-call(bf16[1024,2048]{1,0:T(8,128)(2,1)} %get-tuple-element.277.mlp_ref.refs_0_, bf16[1024,1024]{1,0:T(8,128)(2,1)} %get-tuple-element.342.refs_1_.refs_11_), custom_call_target="tpu_custom_call" | custom-call | flops 1 | bytes 1 | tf_op jit(solution)/shard_map/pallas_call | solution.py:118
  269.1 4.7 %collective-permute-done.21.refs_2_ = bf16[1024,512]{1,0:T(8,128)(2,1)} collective-permute-done((bf16[1024,512]{1,0:T(8,128)(2,1)}, bf16[1024,512]{1,0:T(8,128)(2,1)}, u32[]{:S(2)}, u32[]{:S(2)}) %collective-permute-start.21) | collective-permute-done | bytes 1048608 | tf_op jit(solution)/shard_map/ppermute | solution.py:58
  277.7 4.9 %shard_map.238 = (bf16[1024,768]{1,0:T(8,128)(2,1)}, f32[1,768]{1,0:T(1,128)}) custom-call(bf16[1024,256]{1,0:T(8,128)(2,1)} %get-tuple-element.308.refs_0_, bf16[1024,512]{1,0:T(8,128)(2,1)} %get-tuple-element.323.refs_1_, bf16[1024,512]{1,0:T(8,128)(2,1)} %collective-permute-done.21.refs_2_, f32[1024,128]{1,0:T(8,128)} %maximum_maximum_fusion.refs_11_.refs_3_, ...), custom_call_target="tpu_custom_call" | custom-call | flops 1 | bytes 1 | tf_op jit(solution)/shard_map/pallas_call | solution.py:118
  282.6 15.6 %shard_map.239 = (f32[128,2048]{1,0:T(8,128)}, f32[128,2048]{1,0:T(8,128)}, f32[128,2048]{1,0:T(8,128)}, f32[128,2048]{1,0:T(8,128)}, bf16[128,2048]{1,0:T(8,128...) custom-call(bf16[128,2048]{1,0:T(8,128)(2,1)} %bitcast.109, ...), custom_call_target="tpu_custom_call" | custom-call | flops 1 | bytes 1 | tf_op jit(solution)/shard_map/pallas_call | solution.py:118
  298.3 1.7 collective-permute-done.25
  301.0 1.7 collective-permute-start.26
  306.3 9.3 %shard_map.240 = bf16[2048,1024]{1,0:T(8,128)(2,1)} custom-call(bf16[1024,2048]{1,0:T(8,128)(2,1)} %get-tuple-element.367.refs_0_, bf16[1024,768]{1,0:T(8,128)(2,1)} %get-tuple-element.368.refs_10_.refs_1_, bf16[1024,2048]{1,0:T(8,128)(2,1)} %get-tuple-element.298.lhs_ref.g_ref.refs_2_, bf16[1024,256]{1,0:T(8,128)(2,1)} %get-tuple-element.369.att_ref.refs_3_), custom_call_target="tpu_custom_call" | custom-call | flops 1 | bytes 1 | tf_op jit(solution)/shard_map/pallas_call | solution.py:118
  315.6 8.9 %collective-permute-done.26 = bf16[128,2048]{1,0:T(8,128)(2,1)S(1)} collective-permute-done((bf16[128,2048]{1,0:T(8,128)(2,1)}, bf16[128,2048]{1,0:T(8,128)(2,1)S(1)}, u32[]{:S(2)}, u32[]{:S(2)}) %collective-permute-start.26) | collective-permute-done | bytes 524320 | tf_op jit(solution)/shard_map/ppermute | solution.py:58
  324.5 3.2 collective-permute-done.29
  327.8 2.0 add_convert_fusion.4
  329.8 3.6 all-to-all-start.4
  333.4 1.9 collective-permute-start.30
  338.2 23.1 %collective-permute-done.30 = bf16[128,2048]{1,0:T(8,128)(2,1)S(1)} collective-permute-done((bf16[128,2048]{1,0:T(8,128)(2,1)}, bf16[128,2048]{1,0:T(8,128)(2,1)S(1)}, u32[]{:S(2)}, u32[]{:S(2)}) %collective-permute-start.30) | collective-permute-done | bytes 524320 | tf_op jit(solution)/shard_map/ppermute | solution.py:58
  361.3 5.8 %collective-permute-done.32 = bf16[128,2048]{1,0:T(8,128)(2,1)} collective-permute-done((bf16[128,2048]{1,0:T(8,128)(2,1)}, bf16[128,2048]{1,0:T(8,128)(2,1)}, u32[]{:S(2)}, u32[]{:S(2)}) %collective-permute-start.32) | collective-permute-done | bytes 524320 | tf_op jit(solution)/shard_map/ppermute | solution.py:58
  367.1 2.7 add_convert_fusion.2
  369.9 2.1 add_convert_fusion.3
  372.0 4.5 %all-to-all-start.5 = ((bf16[8,64,1024]{2,1,0:T(8,128)(2,1)}), bf16[8,64,1024]{2,1,0:T(8,128)(2,1)S(1)}, u32[]{:S(2)}, u32[]{:S(2)}) async-start(bf16[8,64,1024]{2,1,0:T(8,128)(2,1)} %bitcast.129), calls=%async_computation.7 | async-start | bytes 2097152 | tf_op jit(solution)/shard_map/all_to_all | solution.py:109
  377.4 2.1 collective-permute-start.33
  383.1 15.1 %collective-permute-done.33 = bf16[128,2048]{1,0:T(8,128)(2,1)} collective-permute-done((bf16[128,2048]{1,0:T(8,128)(2,1)}, bf16[128,2048]{1,0:T(8,128)(2,1)}, u32[]{:S(2)}, u32[]{:S(2)}) %collective-permute-start.33) | collective-permute-done | bytes 524320 | tf_op jit(solution)/shard_map/ppermute | solution.py:58
  398.2 4.2 all-to-all-done.5
  402.5 2.1 collective-permute-start.35
  404.6 2.7 fusion.7
  411.0 2.8 all-to-all-start.6
  415.7 2.6 reshape.271
  419.3 1.6 copy.77
  420.9 9.2 %all-to-all-done.6 = f32[32,1,768]{2,1,0:T(1,128)S(1)} async-done(((f32[32,1,768]{2,1,0:T(1,128)}), f32[32,1,768]{2,1,0:T(1,128)S(1)}, u32[]{:S(2)}, u32[]{:S(2)}) %all-to-all-start.6) | async-done | bytes 98336 | tf_op jit(solution)/shard_map/all_to_all | solution.py:747
  432.1 1.8 fusion.24
  (213 shorter events, 63.4 us)
Async XLA Ops:
  7.2 26.3 %collective-permute-start = (bf16[128,2048]{1,0:T(8,128)(2,1)}, bf16[128,2048]{1,0:T(8,128)(2,1)S(1)}, u32[]{:S(2)}, u32[]{:S(2)}) collective-permute-start(bf16[128,2048]{1,0:T(8,128)(2,1)} %bitcast.105), channel_id=1, source_target_pairs={{0,1},{1,0},{2,3},{3,2},{4,5},{5,4},{6,7},{7,6},{8,9},{9,8},{10,11... | collective-permute-start | bytes 1572872 | tf_op jit(solution)/shard_map/ppermute | solution.py:58
  10.3 25.8 %collective-permute-start.1 = (bf16[128,2048]{1,0:T(8,128)(2,1)}, bf16[128,2048]{1,0:T(8,128)(2,1)S(1)}, u32[]{:S(2)}, u32[]{:S(2)}) collective-permute-start(bf16[128,2048]{1,0:T(8,128)(2,1)} %bitcast.106), channel_id=1, source_target_pairs={{0,2},{1,3},{2,0},{3,1},{4,6},{5,7},{6,4},{7,5},{8,10},{9,11},{10,... | collective-permute-start | bytes 1572872 | tf_op jit(solution)/shard_map/ppermute | solution.py:58
  12.9 23.2 %collective-permute-start.2 = (bf16[128,2048]{1,0:T(8,128)(2,1)}, bf16[128,2048]{1,0:T(8,128)(2,1)S(1)}, u32[]{:S(2)}, u32[]{:S(2)}) collective-permute-start(bf16[128,2048]{1,0:T(8,128)(2,1)} %bitcast.107), channel_id=1, source_target_pairs={{0,4},{4,0},{1,5},{5,1},{2,6},{6,2},{3,7},{7,3},{8,12},{12,8},{9,1... | collective-permute-start | bytes 1572872 | tf_op jit(solution)/shard_map/ppermute | solution.py:58
  14.3 23.2 %collective-permute-start.3 = (bf16[128,2048]{1,0:T(8,128)(2,1)}, bf16[128,2048]{1,0:T(8,128)(2,1)}, u32[]{:S(2)}, u32[]{:S(2)}) collective-permute-start(bf16[128,2048]{1,0:T(8,128)(2,1)} %bitcast.112), channel_id=1, source_target_pairs={{0,4},{4,0},{1,5},{5,1},{2,6},{6,2},{3,7},{7,3},{8,12},{12,8},{9,1... | collective-permute-start | bytes 1572872 | tf_op jit(solution)/shard_map/ppermute | solution.py:58
  33.5 14.6 %copy-start.7 = (bf16[128,2048]{1,0:T(8,128)(2,1)}, bf16[128,2048]{1,0:T(8,128)(2,1)S(1)}, u32[]{:S(2)}) copy-start(bf16[128,2048]{1,0:T(8,128)(2,1)S(1)} %collective-permute-done.refs_1_) | copy-start | bytes 1572868
  36.1 12.1 %copy-start.8 = (bf16[128,2048]{1,0:T(8,128)(2,1)}, bf16[128,2048]{1,0:T(8,128)(2,1)S(1)}, u32[]{:S(2)}) copy-start(bf16[128,2048]{1,0:T(8,128)(2,1)S(1)} %collective-permute-done.1.refs_2_) | copy-start | bytes 1572868
  36.1 12.1 %copy-start.9 = (bf16[128,2048]{1,0:T(8,128)(2,1)}, bf16[128,2048]{1,0:T(8,128)(2,1)S(1)}, u32[]{:S(2)}) copy-start(bf16[128,2048]{1,0:T(8,128)(2,1)S(1)} %collective-permute-done.2.refs_4_) | copy-start | bytes 1572868
  37.5 40.6 %all-to-all-start = ((bf16[8,72,1024]{2,1,0:T(8,128)(2,1)}), bf16[8,72,1024]{2,1,0:T(8,128)(2,1)S(1)}, u32[]{:S(2)}, u32[]{:S(2)}) async-start(bf16[8,72,1024]{2,1,0:T(8,128)(2,1)} %pad_maximum_fusion), calls=%async_computation | async-start | bytes 2359296 | tf_op jit(solution)/shard_map/all_to_all | solution.py:582
  41.1 77.6 %all-gather.4.cloned.1.call-start = ((), (), s32[]{:S(2)}) async-start(), calls=%async_computation.9 | async-start | bytes 5242880 | tf_op jit(solution)/shard_map/all_gather | solution.py:100
  41.2 31.2 %collective-permute-start.4 = (bf16[128,2048]{1,0:T(8,128)(2,1)S(1)}, bf16[128,2048]{1,0:T(8,128)(2,1)S(1)}, u32[]{:S(2)}, u32[]{:S(2)}) collective-permute-start(bf16[128,2048]{1,0:T(8,128)(2,1)S(1)} %collective-permute-done.1.refs_2_), channel_id=1, source_target_pairs={{0,1},{1,0},{2,3},{3,2},{4,5},{5,4},{6,7},{7,6},{8,9},{9,8},{10,11... | collective-permute-start | bytes 1572872 | tf_op jit(solution)/shard_map/ppermute | solution.py:58
  43.1 35.0 %collective-permute-start.6 = (bf16[128,2048]{1,0:T(8,128)(2,1)S(1)}, bf16[128,2048]{1,0:T(8,128)(2,1)}, u32[]{:S(2)}, u32[]{:S(2)}) collective-permute-start(bf16[128,2048]{1,0:T(8,128)(2,1)S(1)} %collective-permute-done.1.refs_2_), channel_id=1, source_target_pairs={{0,4},{4,0},{1,5},{5,1},{2,6},{6,2},{3,7},{7,3},{8,12},{12,8},{9,1... | collective-permute-start | bytes 1572872 | tf_op jit(solution)/shard_map/ppermute | solution.py:58
  44.6 32.7 %collective-permute-start.5 = (bf16[128,2048]{1,0:T(8,128)(2,1)S(1)}, bf16[128,2048]{1,0:T(8,128)(2,1)S(1)}, u32[]{:S(2)}, u32[]{:S(2)}) collective-permute-start(bf16[128,2048]{1,0:T(8,128)(2,1)S(1)} %collective-permute-done.refs_1_), channel_id=1, source_target_pairs={{0,4},{4,0},{1,5},{5,1},{2,6},{6,2},{3,7},{7,3},{8,12},{12,8},{9,1... | collective-permute-start | bytes 1572872 | tf_op jit(solution)/shard_map/ppermute | solution.py:58
  79.2 11.5 %copy-start.1 = (bf16[1,128,2048]{2,1,0:T(8,128)(2,1)S(1)}, bf16[1,128,2048]{2,1,0:T(8,128)(2,1)}, u32[]{:S(2)}) copy-start(bf16[1,128,2048]{2,1,0:T(8,128)(2,1)} %param.25) | copy-start | bytes 1572868
  79.2 35.2 %all-to-all-start.1 = ((bf16[8,64,1024]{2,1,0:T(8,128)(2,1)}), bf16[8,64,1024]{2,1,0:T(8,128)(2,1)S(1)}, u32[]{:S(2)}, u32[]{:S(2)}) async-start(bf16[8,64,1024]{2,1,0:T(8,128)(2,1)} %bitcast.118), calls=%async_computation.1 | async-start | bytes 2097152 | tf_op jit(solution)/shard_map/all_to_all | solution.py:95
  83.9 79.5 %all-gather.6.cloned.1.call-start = ((), (), s32[]{:S(2)}) async-start(), calls=%async_computation.10 | async-start | bytes 5242880 | tf_op jit(solution)/shard_map/all_gather | solution.py:100
  84.1 8.0 %collective-permute-start.11 = (bf16[8,768]{1,0:T(8,128)(2,1)S(1)}, bf16[8,768]{1,0:T(8,128)(2,1)S(1)}, u32[]{:S(2)}, u32[]{:S(2)}) collective-permute-start(bf16[8,768]{1,0:T(8,128)(2,1)S(1)} %bitcast.136), channel_id=1, source_target_pairs={{0,24},{8,16},{16,8},{24,0},{1,25},{9,17},{17,9},{25,1},{2,26},{10... | collective-permute-start | bytes 36872 | tf_op jit(solution)/shard_map/ppermute | solution.py:58
  84.2 7.9 %collective-permute-start.10 = (bf16[8,768]{1,0:T(8,128)(2,1)S(1)}, bf16[8,768]{1,0:T(8,128)(2,1)S(1)}, u32[]{:S(2)}, u32[]{:S(2)}) collective-permute-start(bf16[8,768]{1,0:T(8,128)(2,1)S(1)} %bitcast.137), channel_id=1, source_target_pairs={{0,16},{8,24},{16,0},{24,8},{1,17},{9,25},{17,1},{25,9},{2,18},{10... | collective-permute-start | bytes 36872 | tf_op jit(solution)/shard_map/ppermute | solution.py:58
  85.8 6.3 %collective-permute-start.9 = (bf16[8,768]{1,0:T(8,128)(2,1)S(1)}, bf16[8,768]{1,0:T(8,128)(2,1)S(1)}, u32[]{:S(2)}, u32[]{:S(2)}) collective-permute-start(bf16[8,768]{1,0:T(8,128)(2,1)S(1)} %bitcast.138), channel_id=1, source_target_pairs={{0,8},{8,0},{16,24},{24,16},{1,9},{9,1},{17,25},{25,17},{2,10},{10... | collective-permute-start | bytes 36872 | tf_op jit(solution)/shard_map/ppermute | solution.py:58
  88.7 19.0 %collective-permute-start.7 = (bf16[128,2048]{1,0:T(8,128)(2,1)S(1)}, bf16[128,2048]{1,0:T(8,128)(2,1)S(1)}, u32[]{:S(2)}, u32[]{:S(2)}) collective-permute-start(bf16[128,2048]{1,0:T(8,128)(2,1)S(1)} %copy-done.11), channel_id=1, source_target_pairs={{0,4},{4,0},{1,5},{5,1},{2,6},{6,2},{3,7},{7,3},{8,12},{12,8},{9,1... | collective-permute-start | bytes 1572872 | tf_op jit(solution)/shard_map/ppermute | solution.py:58
  90.7 23.7 %collective-permute-start.8 = (bf16[128,2048]{1,0:T(8,128)(2,1)S(1)}, bf16[128,2048]{1,0:T(8,128)(2,1)}, u32[]{:S(2)}, u32[]{:S(2)}) collective-permute-start(bf16[128,2048]{1,0:T(8,128)(2,1)S(1)} %bitcast.114), channel_id=1, source_target_pairs={{0,1},{1,0},{2,3},{3,2},{4,5},{5,4},{6,7},{7,6},{8,9},{9,8},{10,11... | collective-permute-start | bytes 1572872 | tf_op jit(solution)/shard_map/ppermute | solution.py:58
  107.7 10.9 %copy-start.13 = (bf16[128,2048]{1,0:T(8,128)(2,1)}, bf16[128,2048]{1,0:T(8,128)(2,1)S(1)}, u32[]{:S(2)}) copy-start(bf16[128,2048]{1,0:T(8,128)(2,1)S(1)} %collective-permute-done.7.refs_7_) | copy-start | bytes 1572868
  115.4 16.1 %collective-permute-start.12 = (bf16[128,2048]{1,0:T(8,128)(2,1)}, bf16[128,2048]{1,0:T(8,128)(2,1)S(1)}, u32[]{:S(2)}, u32[]{:S(2)}) collective-permute-start(bf16[128,2048]{1,0:T(8,128)(2,1)} %collective-permute-done.8.refs_1_), channel_id=1, source_target_pairs={{0,4},{4,0},{1,5},{5,1},{2,6},{6,2},{3,7},{7,3},{8,12},{12,8},{9,1... | collective-permute-start | bytes 1572872 | tf_op jit(solution)/shard_map/ppermute | solution.py:58
  116.3 25.0 %collective-permute-start.13 = (bf16[128,2048]{1,0:T(8,128)(2,1)S(1)}, bf16[128,2048]{1,0:T(8,128)(2,1)S(1)}, u32[]{:S(2)}, u32[]{:S(2)}) collective-permute-start(bf16[128,2048]{1,0:T(8,128)(2,1)S(1)} %bitcast.115), channel_id=1, source_target_pairs={{0,2},{1,3},{2,0},{3,1},{4,6},{5,7},{6,4},{7,5},{8,10},{9,11},{10,... | collective-permute-start | bytes 1572872 | tf_op jit(solution)/shard_map/ppermute | solution.py:58
  131.5 28.3 %copy-start.16 = (bf16[1024,512]{1,0:T(8,128)(2,1)S(1)}, bf16[1024,512]{1,0:T(8,128)(2,1)}, u32[]{:S(2)}) copy-start(bf16[1024,512]{1,0:T(8,128)(2,1)} %get-tuple-element.306.refs_0_) | copy-start | bytes 3145732
  131.5 24.3 %copy-start.25 = (bf16[128,2048]{1,0:T(8,128)(2,1)}, bf16[128,2048]{1,0:T(8,128)(2,1)S(1)}, u32[]{:S(2)}) copy-start(bf16[128,2048]{1,0:T(8,128)(2,1)S(1)} %collective-permute-done.12.refs_5_) | copy-start | bytes 1572868
  141.3 18.4 %copy-start.26 = (bf16[128,2048]{1,0:T(8,128)(2,1)}, bf16[128,2048]{1,0:T(8,128)(2,1)S(1)}, u32[]{:S(2)}) copy-start(bf16[128,2048]{1,0:T(8,128)(2,1)S(1)} %collective-permute-done.13.refs_2_) | copy-start | bytes 1572868
  141.3 13.4 %collective-permute-start.14 = (bf16[128,2048]{1,0:T(8,128)(2,1)S(1)}, bf16[128,2048]{1,0:T(8,128)(2,1)S(1)}, u32[]{:S(2)}, u32[]{:S(2)}) collective-permute-start(bf16[128,2048]{1,0:T(8,128)(2,1)S(1)} %collective-permute-done.13.refs_2_), channel_id=1, source_target_pairs={{0,4},{4,0},{1,5},{5,1},{2,6},{6,2},{3,7},{7,3},{8,12},{12,8},{9,1... | collective-permute-start | bytes 1572872 | tf_op jit(solution)/shard_map/ppermute | solution.py:58
  142.1 13.7 %collective-permute-start.15 = (bf16[128,2048]{1,0:T(8,128)(2,1)S(1)}, bf16[128,2048]{1,0:T(8,128)(2,1)}, u32[]{:S(2)}, u32[]{:S(2)}) collective-permute-start(bf16[128,2048]{1,0:T(8,128)(2,1)S(1)} %collective-permute-done.13.refs_2_), channel_id=1, source_target_pairs={{0,1},{1,0},{2,3},{3,2},{4,5},{5,4},{6,7},{7,6},{8,9},{9,8},{10,11... | collective-permute-start | bytes 1572872 | tf_op jit(solution)/shard_map/ppermute | solution.py:58
  155.8 29.6 %all-to-all-start.2 = ((bf16[8,64,1024]{2,1,0:T(8,128)(2,1)}), bf16[8,64,1024]{2,1,0:T(8,128)(2,1)S(1)}, u32[]{:S(2)}, u32[]{:S(2)}) async-start(bf16[8,64,1024]{2,1,0:T(8,128)(2,1)} %bitcast.98), calls=%async_computation.2 | async-start | bytes 2097152 | tf_op jit(solution)/shard_map/all_to_all | solution.py:95
  159.7 66.3 %all-gather.8.cloned.1.call-start = ((), (), s32[]{:S(2)}) async-start(), calls=%async_computation.11 | async-start | bytes 5242880 | tf_op jit(solution)/shard_map/all_gather | solution.py:100
  159.8 23.7 %collective-permute-start.17 = (bf16[1024,512]{1,0:T(8,128)(2,1)S(1)}, bf16[1024,512]{1,0:T(8,128)(2,1)S(1)}, u32[]{:S(2)}, u32[]{:S(2)}) collective-permute-start(bf16[1024,512]{1,0:T(8,128)(2,1)S(1)} %copy-done.16), channel_id=1, source_target_pairs={{0,8},{8,0},{1,9},{9,1},{2,10},{10,2},{3,11},{11,3},{4,12},{12,4},... | collective-permute-start | bytes 3145736 | tf_op jit(solution)/shard_map/ppermute | solution.py:58
  161.3 20.1 %collective-permute-start.16 = (bf16[128,2048]{1,0:T(8,128)(2,1)}, bf16[128,2048]{1,0:T(8,128)(2,1)}, u32[]{:S(2)}, u32[]{:S(2)}) collective-permute-start(bf16[128,2048]{1,0:T(8,128)(2,1)} %collective-permute-done.15.refs_3_), channel_id=1, source_target_pairs={{0,4},{4,0},{1,5},{5,1},{2,6},{6,2},{3,7},{7,3},{8,12},{12,8},{9,1... | collective-permute-start | bytes 1572872 | tf_op jit(solution)/shard_map/ppermute | solution.py:58
  183.5 17.2 %copy-start.19 = (bf16[1024,512]{1,0:T(8,128)(2,1)}, bf16[1024,512]{1,0:T(8,128)(2,1)S(1)}, u32[]{:S(2)}) copy-start(bf16[1024,512]{1,0:T(8,128)(2,1)S(1)} %collective-permute-done.17.refs_1_) | copy-start | bytes 3145732
  200.6 8.0 %collective-permute-start.18 = (bf16[512,1024]{1,0:T(8,128)(2,1)}, bf16[512,1024]{1,0:T(8,128)(2,1)S(1)}, u32[]{:S(2)}, u32[]{:S(2)}) collective-permute-start(bf16[512,1024]{1,0:T(8,128)(2,1)} %get-tuple-element.296), channel_id=1, source_target_pairs={{0,16},{16,0},{1,17},{17,1},{2,18},{18,2},{3,19},{19,3},{4,20},{20... | collective-permute-start | bytes 3145736 | tf_op jit(solution)/shard_map/ppermute | solution.py:58
  200.7 8.0 %collective-permute-start.19 = (bf16[512,1024]{1,0:T(8,128)(2,1)}, bf16[512,1024]{1,0:T(8,128)(2,1)S(1)}, u32[]{:S(2)}, u32[]{:S(2)}) collective-permute-start(bf16[512,1024]{1,0:T(8,128)(2,1)} %get-tuple-element.297), channel_id=1, source_target_pairs={{0,16},{16,0},{1,17},{17,1},{2,18},{18,2},{3,19},{19,3},{4,20},{20... | collective-permute-start | bytes 3145736 | tf_op jit(solution)/shard_map/ppermute | solution.py:58
  210.3 30.9 %collective-permute-start.20 = (bf16[512,1024]{1,0:T(8,128)(2,1)S(1)}, bf16[512,1024]{1,0:T(8,128)(2,1)S(1)}, u32[]{:S(2)}, u32[]{:S(2)}) collective-permute-start(bf16[512,1024]{1,0:T(8,128)(2,1)S(1)} %add_convert_fusion.1), channel_id=1, source_target_pairs={{0,8},{8,0},{1,9},{9,1},{2,10},{10,2},{3,11},{11,3},{4,12},{12,4},... | collective-permute-start | bytes 3145736 | tf_op jit(solution)/shard_map/ppermute | solution.py:58
  242.8 32.5 %all-to-all-start.3 = ((bf16[8,64,1024]{2,1,0:T(8,128)(2,1)}), bf16[8,64,1024]{2,1,0:T(8,128)(2,1)S(1)}, u32[]{:S(2)}, u32[]{:S(2)}) async-start(bf16[8,64,1024]{2,1,0:T(8,128)(2,1)} %bitcast.26), calls=%async_computation.3 | async-start | bytes 2097152 | tf_op jit(solution)/shard_map/all_to_all | solution.py:109
  248.4 79.3 %reduce-scatter.3.cloned.1.call-start = ((), (), s32[]{:S(2)}) async-start(), calls=%async_computation.12 | async-start | bytes 5242880 | tf_op jit(solution)/shard_map/reduce_scatter | solution.py:104
  248.5 25.3 %collective-permute-start.21 = (bf16[1024,512]{1,0:T(8,128)(2,1)}, bf16[1024,512]{1,0:T(8,128)(2,1)}, u32[]{:S(2)}, u32[]{:S(2)}) collective-permute-start(bf16[1024,512]{1,0:T(8,128)(2,1)} %get-tuple-element.325), channel_id=1, source_target_pairs={{0,8},{8,0},{1,9},{9,1},{2,10},{10,2},{3,11},{11,3},{4,12},{12,4},... | collective-permute-start | bytes 3145736 | tf_op jit(solution)/shard_map/ppermute | solution.py:58
  249.1 20.0 %collective-permute-start.22 = (bf16[128,2048]{1,0:T(8,128)(2,1)S(1)}, bf16[128,2048]{1,0:T(8,128)(2,1)S(1)}, u32[]{:S(2)}, u32[]{:S(2)}) collective-permute-start(bf16[128,2048]{1,0:T(8,128)(2,1)S(1)} %copy-done.32), channel_id=1, source_target_pairs={{0,4},{4,0},{1,5},{5,1},{2,6},{6,2},{3,7},{7,3},{8,12},{12,8},{9,1... | collective-permute-start | bytes 1572872 | tf_op jit(solution)/shard_map/ppermute | solution.py:58
  275.4 96.6 %reduce-scatter.5.cloned.1.call-start = ((), (), s32[]{:S(2)}) async-start(), calls=%async_computation.13 | async-start | bytes 5242880 | tf_op jit(solution)/shard_map/reduce_scatter | solution.py:104
  275.5 22.7 %collective-permute-start.23 = (bf16[128,2048]{1,0:T(8,128)(2,1)S(1)}, bf16[128,2048]{1,0:T(8,128)(2,1)S(1)}, u32[]{:S(2)}, u32[]{:S(2)}) collective-permute-start(bf16[128,2048]{1,0:T(8,128)(2,1)S(1)} %add_convert_fusion.7), channel_id=1, source_target_pairs={{0,1},{1,0},{2,3},{3,2},{4,5},{5,4},{6,7},{7,6},{8,9},{9,8},{10,11... | collective-permute-start | bytes 1572872 | tf_op jit(solution)/shard_map/ppermute | solution.py:58
  275.7 22.6 %collective-permute-start.24 = (bf16[128,2048]{1,0:T(8,128)(2,1)}, bf16[128,2048]{1,0:T(8,128)(2,1)S(1)}, u32[]{:S(2)}, u32[]{:S(2)}) collective-permute-start(bf16[128,2048]{1,0:T(8,128)(2,1)} %get-tuple-element.347), channel_id=1, source_target_pairs={{0,4},{4,0},{1,5},{5,1},{2,6},{6,2},{3,7},{7,3},{8,12},{12,8},{9,1... | collective-permute-start | bytes 1572872 | tf_op jit(solution)/shard_map/ppermute | solution.py:58
  277.1 22.8 %collective-permute-start.25 = (bf16[128,2048]{1,0:T(8,128)(2,1)}, bf16[128,2048]{1,0:T(8,128)(2,1)S(1)}, u32[]{:S(2)}, u32[]{:S(2)}) collective-permute-start(bf16[128,2048]{1,0:T(8,128)(2,1)} %get-tuple-element.348), channel_id=1, source_target_pairs={{0,4},{4,0},{1,5},{5,1},{2,6},{6,2},{3,7},{7,3},{8,12},{12,8},{9,1... | collective-permute-start | bytes 1572872 | tf_op jit(solution)/shard_map/ppermute | solution.py:58
  282.6 17.3 %copy-start.18 = (f32[128,2048]{1,0:T(8,128)S(1)}, f32[128,2048]{1,0:T(8,128)}, u32[]{:S(2)}) copy-start(f32[128,2048]{1,0:T(8,128)} %get-tuple-element.356) | copy-start | bytes 3145732
  301.0 23.5 %collective-permute-start.26 = (bf16[128,2048]{1,0:T(8,128)(2,1)}, bf16[128,2048]{1,0:T(8,128)(2,1)S(1)}, u32[]{:S(2)}, u32[]{:S(2)}) collective-permute-start(bf16[128,2048]{1,0:T(8,128)(2,1)} %add_convert_fusion.5), channel_id=1, source_target_pairs={{0,1},{1,0},{2,3},{3,2},{4,5},{5,4},{6,7},{7,6},{8,9},{9,8},{10,11... | collective-permute-start | bytes 1572872 | tf_op jit(solution)/shard_map/ppermute | solution.py:58
  302.7 21.8 %collective-permute-start.27 = (bf16[128,2048]{1,0:T(8,128)(2,1)S(1)}, bf16[128,2048]{1,0:T(8,128)(2,1)}, u32[]{:S(2)}, u32[]{:S(2)}) collective-permute-start(bf16[128,2048]{1,0:T(8,128)(2,1)S(1)} %add_convert_fusion.6), channel_id=1, source_target_pairs={{0,2},{1,3},{2,0},{3,1},{4,6},{5,7},{6,4},{7,5},{8,10},{9,11},{10,... | collective-permute-start | bytes 1572872 | tf_op jit(solution)/shard_map/ppermute | solution.py:58
  304.3 20.2 %collective-permute-start.28 = (bf16[128,2048]{1,0:T(8,128)(2,1)}, bf16[128,2048]{1,0:T(8,128)(2,1)}, u32[]{:S(2)}, u32[]{:S(2)}) collective-permute-start(bf16[128,2048]{1,0:T(8,128)(2,1)} %get-tuple-element.365), channel_id=1, source_target_pairs={{0,4},{4,0},{1,5},{5,1},{2,6},{6,2},{3,7},{7,3},{8,12},{12,8},{9,1... | collective-permute-start | bytes 1572872 | tf_op jit(solution)/shard_map/ppermute | solution.py:58
  305.2 22.6 %collective-permute-start.29 = (bf16[128,2048]{1,0:T(8,128)(2,1)}, bf16[128,2048]{1,0:T(8,128)(2,1)}, u32[]{:S(2)}, u32[]{:S(2)}) collective-permute-start(bf16[128,2048]{1,0:T(8,128)(2,1)} %get-tuple-element.366), channel_id=1, source_target_pairs={{0,4},{4,0},{1,5},{5,1},{2,6},{6,2},{3,7},{7,3},{8,12},{12,8},{9,1... | collective-permute-start | bytes 1572872 | tf_op jit(solution)/shard_map/ppermute | solution.py:58
  315.6 12.2 %copy-start.20 = (f32[128,2048]{1,0:T(8,128)S(1)}, f32[128,2048]{1,0:T(8,128)}, u32[]{:S(2)}) copy-start(f32[128,2048]{1,0:T(8,128)} %get-tuple-element.344) | copy-start | bytes 3145732
  327.8 9.7 %copy-start.30 = (f32[1,1024]{1,0:T(1,128)S(1)}, f32[1,1024]{1,0:T(1,128)}, u32[]{:S(2)}) copy-start(f32[1,1024]{1,0:T(1,128)} %get-tuple-element.385) | copy-start | bytes 12292
  327.8 9.9 %copy-start.31 = (f32[1,768]{1,0:T(1,128)S(1)}, f32[1,768]{1,0:T(1,128)}, u32[]{:S(2)}) copy-start(f32[1,768]{1,0:T(1,128)} %get-tuple-element.384) | copy-start | bytes 9220
  327.8 10.1 %copy-start.29 = (f32[4,2048]{1,0:T(4,128)S(1)}, f32[4,2048]{1,0:T(4,128)}, u32[]{:S(2)}) copy-start(f32[4,2048]{1,0:T(4,128)} %get-tuple-element.383) | copy-start | bytes 98308
  329.8 37.3 %all-to-all-start.4 = ((bf16[8,64,1024]{2,1,0:T(8,128)(2,1)}), bf16[8,64,1024]{2,1,0:T(8,128)(2,1)S(1)}, u32[]{:S(2)}, u32[]{:S(2)}) async-start(bf16[8,64,1024]{2,1,0:T(8,128)(2,1)} %bitcast.128), calls=%async_computation.5 | async-start | bytes 2097152 | tf_op jit(solution)/shard_map/all_to_all | solution.py:109
  333.4 27.9 %collective-permute-start.30 = (bf16[128,2048]{1,0:T(8,128)(2,1)}, bf16[128,2048]{1,0:T(8,128)(2,1)S(1)}, u32[]{:S(2)}, u32[]{:S(2)}) collective-permute-start(bf16[128,2048]{1,0:T(8,128)(2,1)} %add_convert_fusion.4), channel_id=1, source_target_pairs={{0,1},{1,0},{2,3},{3,2},{4,5},{5,4},{6,7},{7,6},{8,9},{9,8},{10,11... | collective-permute-start | bytes 1572872 | tf_op jit(solution)/shard_map/ppermute | solution.py:58
  335.3 26.0 %collective-permute-start.31 = (bf16[128,2048]{1,0:T(8,128)(2,1)}, bf16[128,2048]{1,0:T(8,128)(2,1)}, u32[]{:S(2)}, u32[]{:S(2)}) collective-permute-start(bf16[128,2048]{1,0:T(8,128)(2,1)} %get-tuple-element.381), channel_id=1, source_target_pairs={{0,4},{4,0},{1,5},{5,1},{2,6},{6,2},{3,7},{7,3},{8,12},{12,8},{9,1... | collective-permute-start | bytes 1572872 | tf_op jit(solution)/shard_map/ppermute | solution.py:58
  336.8 30.4 %collective-permute-start.32 = (bf16[128,2048]{1,0:T(8,128)(2,1)}, bf16[128,2048]{1,0:T(8,128)(2,1)}, u32[]{:S(2)}, u32[]{:S(2)}) collective-permute-start(bf16[128,2048]{1,0:T(8,128)(2,1)} %get-tuple-element.382), channel_id=1, source_target_pairs={{0,4},{4,0},{1,5},{5,1},{2,6},{6,2},{3,7},{7,3},{8,12},{12,8},{9,1... | collective-permute-start | bytes 1572872 | tf_op jit(solution)/shard_map/ppermute | solution.py:58
  372.0 30.5 %all-to-all-start.5 = ((bf16[8,64,1024]{2,1,0:T(8,128)(2,1)}), bf16[8,64,1024]{2,1,0:T(8,128)(2,1)S(1)}, u32[]{:S(2)}, u32[]{:S(2)}) async-start(bf16[8,64,1024]{2,1,0:T(8,128)(2,1)} %bitcast.129), calls=%async_computation.7 | async-start | bytes 2097152 | tf_op jit(solution)/shard_map/all_to_all | solution.py:109
  377.4 20.8 %collective-permute-start.33 = (bf16[128,2048]{1,0:T(8,128)(2,1)}, bf16[128,2048]{1,0:T(8,128)(2,1)}, u32[]{:S(2)}, u32[]{:S(2)}) collective-permute-start(bf16[128,2048]{1,0:T(8,128)(2,1)} %get-tuple-element.395), channel_id=1, source_target_pairs={{0,4},{4,0},{1,5},{5,1},{2,6},{6,2},{3,7},{7,3},{8,12},{12,8},{9,1... | collective-permute-start | bytes 1572872 | tf_op jit(solution)/shard_map/ppermute | solution.py:58
  381.6 23.0 %copy-start.22 = (f32[128,2048]{1,0:T(8,128)S(1)}, f32[128,2048]{1,0:T(8,128)}, u32[]{:S(2)}) copy-start(f32[128,2048]{1,0:T(8,128)} %get-tuple-element.406) | copy-start | bytes 3145732
  402.5 29.1 %collective-permute-start.34 = (bf16[128,2048]{1,0:T(8,128)(2,1)}, bf16[128,2048]{1,0:T(8,128)(2,1)}, u32[]{:S(2)}, u32[]{:S(2)}) collective-permute-start(bf16[128,2048]{1,0:T(8,128)(2,1)} %add_convert_fusion.2), channel_id=1, source_target_pairs={{0,1},{1,0},{2,3},{3,2},{4,5},{5,4},{6,7},{7,6},{8,9},{9,8},{10,11... | collective-permute-start | bytes 1572872 | tf_op jit(solution)/shard_map/ppermute | solution.py:58
  402.5 29.1 %collective-permute-start.35 = (bf16[128,2048]{1,0:T(8,128)(2,1)}, bf16[128,2048]{1,0:T(8,128)(2,1)}, u32[]{:S(2)}, u32[]{:S(2)}) collective-permute-start(bf16[128,2048]{1,0:T(8,128)(2,1)} %add_convert_fusion.3), channel_id=1, source_target_pairs={{0,2},{1,3},{2,0},{3,1},{4,6},{5,7},{6,4},{7,5},{8,10},{9,11},{10,... | collective-permute-start | bytes 1572872 | tf_op jit(solution)/shard_map/ppermute | solution.py:58
  411.0 19.1 %all-to-all-start.6 = ((f32[32,1,768]{2,1,0:T(1,128)}), f32[32,1,768]{2,1,0:T(1,128)S(1)}, u32[]{:S(2)}, u32[]{:S(2)}) async-start(f32[32,1,768]{2,1,0:T(1,128)} %reshape.285), calls=%async_computation.8 | async-start | bytes 196608 | tf_op jit(solution)/shard_map/all_to_all | solution.py:747
  419.2 12.9 %copy-start.23 = (f32[128,2048]{1,0:T(8,128)S(1)}, f32[128,2048]{1,0:T(8,128)}, u32[]{:S(2)}) copy-start(f32[128,2048]{1,0:T(8,128)} %get-tuple-element.412) | copy-start | bytes 3145732
  (17 other events, 72.0 us)
Sparse Core Ops, SparseCore 0:
  79.3 34.4 all-gather.3
  115.9 34.6 all-gather.5
  186.5 39.4 all-gather.7
  275.5 43.0 reduce-scatter.2
  327.9 42.4 reduce-scatter.4

commit v3 on v2

--- a/solution.py
+++ b/solution.py
@@ -89,6 +89,12 @@
     if lax.axis_size("hd") == 4 and distance == 3:
         distance = 1
     return swap(value, "hd", distance)
+
+
+def exchange(terms, axis, dim):
+    place, size = lax.axis_index(axis), lax.axis_size(axis)
+    pick = lambda d: lax.dynamic_index_in_dim(terms, place ^ d, dim, keepdims=False)
+    return [pick(0)] + [swap(pick(d), axis, d) for d in range(1, size)]
 
 
 def spread_group(shard):
@@ -586,8 +592,8 @@
     inside = ((row // sub_len) ^ t) * sub_len + row % sub_len
     query_places = bh * group_len + inside
     tables = rotary_tables(query_places.astype(f32))
-    x_near, x_rows, m_heads, up_own, g_late, tables = join(
-        x_near, x_rows, m_heads, up_own, g_own, tables
+    x_near, x_rows, m_heads, up_own, g_late, tables, down_own = join(
+        x_near, x_rows, m_heads, up_own, g_own, tables, down_own
     )
     w_heads = spread_rest(m_heads[:, :rows].reshape(tp * rows, -1))
     x_rows += [gather_axis(block, "bl") for block in x_near[3:]]
@@ -629,7 +635,7 @@
     )
     g_near = gather_end(g_late, g_near)
     g_rows += [gather_axis(block, "bl") for block in g_near[2:3]]
-    g_rows, g_near, kv, down_own, mlp_in = join(g_rows, g_near, kv, down_own, mlp_in)
+    g_rows, g_near, down_own, mlp_in = join(g_rows, g_near, down_own, mlp_in)
     g_rows += [gather_axis(block, "bl") for block in g_near[3:]]
     kv_blocks = gather_axis(kv, "bh")
     m_down = spread_group(down_own)
@@ -659,8 +665,8 @@
         for far in range(1, bl_size)
     ]
     out_own = output_terms(attended, activated, w_heads, w_down, 0, *hd_terms, f32)
-    down_others, out_far, attended, grad_kv, slope, out_own = join(
-        down_others, out_far, attended, grad_kv, slope, out_own
+    down_others, out_far, attended, slope, out_own = join(
+        down_others, out_far, attended, slope, out_own
     )
     part = hd_size // 4
     parts = [range(hd_size - (g + 1) * part, hd_size - g * part) for g in range(4)]
@@ -709,15 +715,6 @@
     received = over_bl(out_far, parts[3])
     received_in = over_bl(in_far, parts[0])
     heads_terms = weight_terms(attn_in, grad_project, g_all, attended)
-    out_near, received, received_in, heads_terms, up_mine, in_far = join(
-        out_near, received, received_in, heads_terms, up_mine, in_far
-    )
-    heads_mine = collect_rest(heads_terms)
-    ins = add(*sums_of(in_own, received_in, parts[0]))
-    ins, up_mine, in_far = join(ins, up_mine, in_far)
-    up_grad = collect_group(up_mine)
-    in_near = {d: hand_on(term, d) for d, (term,) in zip(parts[0], ins)}
-    received_in = over_bl(in_far, middle)
     sums = jnp.concatenate([sums, jnp.sum(g_own.astype(f32), axis=0, keepdims=True)], axis=0)
     qkv_bias_full = lax.dynamic_update_slice(
         jnp.zeros((3, HEADS, HS), f32), qkv_bias_term.reshape(3, 1, HS), (0, t, 0)
@@ -731,20 +728,31 @@
         ],
         axis=1,
     )
-    up_grad, in_near, received_in, small_terms, in_far = join(
-        up_grad, in_near, received_in, small_terms, in_far
+    out_near, received, received_in, heads_terms, up_mine, in_far, small = join(
+        out_near, received, received_in, heads_terms, up_mine, in_far, small_terms
+    )
+    heads_mine = collect_rest(heads_terms)
+    ins = add(*sums_of(in_own, received_in, parts[0]))
+    ins, up_mine, in_far = join(ins, up_mine, in_far)
+    up_grad = collect_group(up_mine)
+    in_near = {d: hand_on(term, d) for d, (term,) in zip(parts[0], ins)}
+    received_in = over_bl(in_far, middle)
+    small = exchange(small.reshape(rp, bl_size, hd_size, kinds, rows), RP, 0)
+    up_grad, in_near, received_in, small, in_far = join(
+        up_grad, in_near, received_in, small, in_far
     )
     ins = add(*sums_of(in_own, received_in, middle, [in_near[3]] if four else []))
-    ins, in_far, heads_mine, small_terms = join(ins, in_far, heads_mine, small_terms)
+    in_far, heads_mine, small = join(in_far, heads_mine, small)
     heads_grad = collect_group(heads_mine)
     received_in = over_bl(in_far, parts[3])
     down_grad = down_grad.astype(f32).transpose(1, 0, 2).reshape(rows, ff)
     up_grad = up_grad.astype(f32).transpose(1, 0, 2).reshape(rows, ff)
-    heads_grad, received_in, down_grad, up_grad, ins, small_terms = join(
-        heads_grad, received_in, down_grad, up_grad, ins, small_terms
+    small = exchange(sum(small[1:], small[0]), "hd", 1)
+    heads_grad, received_in, down_grad, up_grad, ins, small = join(
+        heads_grad, received_in, down_grad, up_grad, ins, small
     )
     in_near |= {d: hand_on(term, d) for d, (term,) in zip(middle, ins)}
-    small = lax.all_to_all(small_terms, ALL, split_axis=0, concat_axis=0, tiled=True)
+    small = exchange(sum(small[1:], small[0]), "bl", 0)
     heads_grad = heads_grad.astype(f32)
     dense_grad = heads_grad[:, :, 3 * HS :].transpose(1, 0, 2).reshape(rows, D)
     qkv_grad = (
@@ -765,7 +773,7 @@
     in_near, received_in, small, dense_grad, qkv_grad, output, in_own = join(
         in_near, received_in, small, dense_grad, qkv_grad, output, in_own
     )
-    small = jnp.sum(small, axis=0)
+    small = sum(small[1:], small[0])
     grad_normed = total(in_own, received_in, in_near)
     own = x_own.astype(f32)
     own_average, own_inverse = statistics(own)

time: 449 us -> 445 us (level)
  starting transfers between devices: 74 us -> 80.5 us
    all_to_all x1 -> x0, waiting for transfers between devices: 9.15 us -> none  [per_device(): lax.all_to_all(small_terms, ALL, split_axis=0, concat_axis=0, tiled=True)]
    ppermute x36 -> x43, starting transfers between devices: 45.1 us -> 52.3 us  [swap(): return lax.ppermute(value, axis, [(i, i ^ distance) for i in range(size)])]
    ppermute x36 -> x43, waiting for transfers between devices: 156 us -> 161 us  [swap(): return lax.ppermute(value, axis, [(i, i ^ distance) for i in range(size)])]
  transfers between devices with their start and end apart: 48 -> 54, of which waited for: 26 -> 28; matrix products, arithmetic and copies ran while one was open for 11% -> 10% of each run, Pallas kernels for 27% -> 27%
where the time goes in v3:
time: 445 us; the launch traced here: 440 us
  waiting for transfers between devices  171 us (38%)
  Pallas kernels  118 us (27%)
  starting transfers between devices  80.5 us (18%)
  local copies, waits for them, and re-layouts  30.1 us (7%)
  other arithmetic  25.8 us (6%)
  between operations  14.7 us (3%)
    ppermute x43, waiting for transfers between devices, swap(): return lax.ppermute(value, axis, [(i, i ^ distance) for i in range(size)])  161 us
    pallas_call x11, Pallas kernels, call(): pl.pallas_call(kernel, grid=grid, out_shape=[jax.ShapeDtypeStruct(shape,...  103 us
    ppermute x43, starting transfers between devices, swap(): return lax.ppermute(value, axis, [(i, i ^ distance) for i in range(size)])  52.3 us
    all_to_all x3, starting transfers between devices, collect_group(): return lax.all_to_all(mine, TP, split_axis=0, concat_axis=0, tiled=True)  15.1 us
    pallas_call x2, Pallas kernels, weight_half(): pl.pallas_call(functools.partial(weight_half_kernel, per), grid_spec=pltp...  14.3 us
    convert_element_type x8, other arithmetic, add(): sum((x.astype(f32) for x in arrays[1:]), arrays[0].astype(f32))  12 us
  transfers between devices with their start and end apart: 54, of which 28 were waited for; matrix products, arithmetic and copies ran while one was open for 10% of the time, Pallas kernels for 27%

profile of v3, /device:TPU:0, one launch (start us, length us, event | category | flops | bytes accessed | tf_op | source)
XLA Modules:
  0.0 439.5 jit_solution(330548239152125023)
XLA Ops:
  7.2 3.1 collective-permute-start
  10.3 2.6 collective-permute-start.1
  22.0 11.5 %collective-permute-done.refs_1_ = bf16[128,2048]{1,0:T(8,128)(2,1)S(1)} collective-permute-done((bf16[128,2048]{1,0:T(8,128)(2,1)}, bf16[128,2048]{1,0:T(8,128)(2,1)S(1)}, u32[]{:S(2)}, u32[]{:S(2)}) %collective-permute-start) | collective-permute-done | bytes 524320 | tf_op jit(solution)/shard_map/ppermute | solution.py:58
  33.5 2.5 collective-permute-done.1.refs_2_
  37.5 4.0 all-to-all-start
  41.8 1.9 multiply_sine_fusion
  45.0 2.0 collective-permute-start.4
  51.6 20.8 %collective-permute-done.4.refs_3_ = bf16[128,2048]{1,0:T(8,128)(2,1)S(1)} collective-permute-done((bf16[128,2048]{1,0:T(8,128)(2,1)S(1)}, bf16[128,2048]{1,0:T(8,128)(2,1)S(1)}, u32[]{:S(2)}, u32[]{:S(2)}) %collective-permute-start.4) | collective-permute-done | bytes 524320 | tf_op jit(solution)/shard_map/ppermute | solution.py:58
  72.3 5.8 %collective-permute-done.5.refs_5_ = bf16[128,2048]{1,0:T(8,128)(2,1)S(1)} collective-permute-done((bf16[128,2048]{1,0:T(8,128)(2,1)S(1)}, bf16[128,2048]{1,0:T(8,128)(2,1)S(1)}, u32[]{:S(2)}, u32[]{:S(2)}) %collective-permute-start.5) | collective-permute-done | bytes 524320 | tf_op jit(solution)/shard_map/ppermute | solution.py:58
  80.1 3.8 all-to-all-start.1
  84.2 1.6 collective-permute-start.10
  86.4 2.0 collective-permute-start.7
  93.3 13.6 %collective-permute-done.7.refs_7_ = bf16[128,2048]{1,0:T(8,128)(2,1)S(1)} collective-permute-done((bf16[128,2048]{1,0:T(8,128)(2,1)S(1)}, bf16[128,2048]{1,0:T(8,128)(2,1)S(1)}, u32[]{:S(2)}, u32[]{:S(2)}) %collective-permute-start.7) | collective-permute-done | bytes 524320 | tf_op jit(solution)/shard_map/ppermute | solution.py:58
  106.9 6.7 %collective-permute-done.8.refs_1_ = bf16[128,2048]{1,0:T(8,128)(2,1)S(1)} collective-permute-done((bf16[128,2048]{1,0:T(8,128)(2,1)S(1)}, bf16[128,2048]{1,0:T(8,128)(2,1)S(1)}, u32[]{:S(2)}, u32[]{:S(2)}) %collective-permute-start.8) | collective-permute-done | bytes 524320 | tf_op jit(solution)/shard_map/ppermute | solution.py:58
  116.1 2.4 collective-permute-start.13
  118.5 12.7 %shard_map.228 = (bf16[1024,2048]{1,0:T(8,128)(2,1)}, bf16[1024,2048]{1,0:T(8,128)(2,1)}, bf16[1024,256]{1,0:T(8,128)(2,1)}, bf16[1024,512]{1,0:T(8,128)(2,1)}, f32[1024,1]{1,0:T(8,128)}, /*index=5*/f32[1024,1]{1,0:T(8,128)}) custom-call(bf16[128,2048]{1,0:T(8,128)(2,1)} %bitcast.145, bf16[128,2048]{1,0:T(8,128)(2,1)} %copy-done.5, ...), custom_call_target="tpu_custom_call" | custom-call | flops 1 | bytes 1 | tf_op jit(solution)/shard_map/pallas_call | solution.py:124
  131.2 9.1 %collective-permute-done.13.refs_2_ = bf16[128,2048]{1,0:T(8,128)(2,1)} collective-permute-done((bf16[128,2048]{1,0:T(8,128)(2,1)S(1)}, bf16[128,2048]{1,0:T(8,128)(2,1)}, u32[]{:S(2)}, u32[]{:S(2)}) %collective-permute-start.13) | collective-permute-done | bytes 524320 | tf_op jit(solution)/shard_map/ppermute | solution.py:58
  141.6 11.8 %collective-permute-done.14.refs_6_ = bf16[128,2048]{1,0:T(8,128)(2,1)S(1)} collective-permute-done((bf16[128,2048]{1,0:T(8,128)(2,1)}, bf16[128,2048]{1,0:T(8,128)(2,1)S(1)}, u32[]{:S(2)}, u32[]{:S(2)}) %collective-permute-start.14) | collective-permute-done | bytes 524320 | tf_op jit(solution)/shard_map/ppermute | solution.py:58
  155.0 5.0 %all-to-all-start.2 = ((bf16[8,64,1024]{2,1,0:T(8,128)(2,1)}), bf16[8,64,1024]{2,1,0:T(8,128)(2,1)S(1)}, u32[]{:S(2)}, u32[]{:S(2)}) async-start(bf16[8,64,1024]{2,1,0:T(8,128)(2,1)} %get-tuple-element.283), calls=%async_computation.2 | async-start | bytes 2097152 | tf_op jit(solution)/shard_map/all_to_all | solution.py:101
  160.0 1.6 collective-permute-start.17
  161.6 2.0 collective-permute-start.16
  163.6 11.9 %shard_map.229 = (bf16[1024,1024]{1,0:T(8,128)(2,1)}, f32[1024,1024]{1,0:T(8,128)}) custom-call(bf16[1024,2048]{1,0:T(8,128)(2,1)} %get-tuple-element.284.mlp_ref.refs_0_, bf16[2048,1024]{1,0:T(8,128)(2,1)} %all-gather.6.cloned.1.call-done.w_ref.refs_13_, f32[1,1024]{1,0:T(1,128)} %constant_dynamic-slice_fusion.10.b_ref), custom_call_target="tpu_custom_call" | custom-call | flops 1 | bytes 1 | tf_op jit(solution)/shard_map/pallas_call | solution.py:124
  175.5 8.2 %collective-permute-done.17.refs_1_ = bf16[1024,512]{1,0:T(8,128)(2,1)S(1)} collective-permute-done((bf16[1024,512]{1,0:T(8,128)(2,1)S(1)}, bf16[1024,512]{1,0:T(8,128)(2,1)S(1)}, u32[]{:S(2)}, u32[]{:S(2)}) %collective-permute-start.17) | collective-permute-done | bytes 1048608 | tf_op jit(solution)/shard_map/ppermute | solution.py:58
  183.7 1.9 all-to-all-done.2
  187.2 6.3 %shard_map.230 = (bf16[1024,2048]{1,0:T(8,128)(2,1)}, bf16[1024,256]{1,0:T(8,128)(2,1)}) custom-call(bf16[128,2048]{1,0:T(8,128)(2,1)} %bitcast.150, bf16[128,2048]{1,0:T(8,128)(2,1)} %copy-done.25, bf16[128,2048]{1,0:T(8,128)(2,1)} %collective-permute-done.13.refs_2_, bf16[128,2048]{1,0:T(8,128)(2,1)} %collective-permute-done.15.refs_3_, ...), custom_call_target="tpu_custom_call" | custom-call | flops 1 | bytes 1 | tf_op jit(solution)/shard_map/pallas_call | solution.py:124
  193.5 7.3 %shard_map.231 = (bf16[512,1024]{1,0:T(8,128)(2,1)}, bf16[512,1024]{1,0:T(8,128)(2,1)}) custom-call(s32[2]{0:T(128)} %get-tuple-element.467.place_ref, bf16[1024,2048]{1,0:T(8,128)(2,1)} %get-tuple-element.305.lhs_ref.g_ref.refs_2_, bf16[1024,1024]{1,0:T(8,128)(2,1)} %get-tuple-element.299.rhs_ref.act_ref), custom_call_target="tpu_custom_call" | custom-call | flops 1 | bytes 1 | tf_op jit(solution)/shard_map/pallas_call | solution.py:302
  201.9 6.9 %shard_map.232 = (bf16[512,1024]{1,0:T(8,128)(2,1)}, bf16[512,1024]{1,0:T(8,128)(2,1)}) custom-call(s32[2]{0:T(128)} %pad_add_fusion.2.place_ref, bf16[1024,2048]{1,0:T(8,128)(2,1)} %get-tuple-element.305.lhs_ref.g_ref.refs_2_, bf16[1024,1024]{1,0:T(8,128)(2,1)} %get-tuple-element.299.rhs_ref.act_ref), custom_call_target="tpu_custom_call" | custom-call | flops 1 | bytes 1 | tf_op jit(solution)/shard_map/pallas_call | solution.py:302
  208.9 1.6 add_convert_fusion.1
  212.1 12.7 %shard_map.233 = (bf16[1024,256]{1,0:T(8,128)(2,1)}, bf16[1024,256]{1,0:T(8,128)(2,1)}, bf16[1024,512]{1,0:T(8,128)(2,1)}, bf16[1024,512]{1,0:T(8,128)(2,1)}) custom-call(s32[2]{0:T(128)} %get-tuple-element.466.place_ref, bf16[1024,256]{1,0:T(8,128)(2,1)} %get-tuple-element.257.q_ref, bf16[1024,256]{1,0:T(8,128)(2,1)} %get-tuple-element.312.g_ref, ...), custom_call_target="tpu_custom_call" | custom-call | flops 1 | bytes 1 | tf_op jit(solution)/shard_map/pallas_call | solution.py:124
  226.3 6.2 %shard_map.234 = (bf16[128,2048]{1,0:T(8,128)(2,1)}, bf16[128,2048]{1,0:T(8,128)(2,1)}, bf16[128,2048]{1,0:T(8,128)(2,1)}, bf16[128,2048]{1,0:T(8,128)(2,1)}) custom-call(bf16[1024,256]{1,0:T(8,128)(2,1)} %get-tuple-element.373.att_ref.refs_3_, bf16[1024,1024]{1,0:T(8,128)(2,1)} %get-tuple-element.299.rhs_ref.act_ref, ...), custom_call_target="tpu_custom_call" | custom-call | flops 1 | bytes 1 | tf_op jit(solution)/shard_map/pallas_call | solution.py:124
  232.4 6.9 %shard_map.235 = (f32[128,2048]{1,0:T(8,128)}, f32[128,2048]{1,0:T(8,128)}, f32[128,2048]{1,0:T(8,128)}, f32[128,2048]{1,0:T(8,128)}) custom-call(bf16[1024,256]{1,0:T(8,128)(2,1)} %get-tuple-element.373.att_ref.refs_3_, bf16[1024,1024]{1,0:T(8,128)(2,1)} %get-tuple-element.299.rhs_ref.act_ref, ...), custom_call_target="tpu_custom_call" | custom-call | flops 1 | bytes 1 | tf_op jit(solution)/shard_map/pallas_call | solution.py:124
  239.3 2.1 collective-permute-done.20
  241.4 1.6 add_convert_fusion
  243.0 5.5 %all-to-all-start.3 = ((bf16[8,64,1024]{2,1,0:T(8,128)(2,1)}), bf16[8,64,1024]{2,1,0:T(8,128)(2,1)S(1)}, u32[]{:S(2)}, u32[]{:S(2)}) async-start(bf16[8,64,1024]{2,1,0:T(8,128)(2,1)} %bitcast.26), calls=%async_computation.3 | async-start | bytes 2097152 | tf_op jit(solution)/shard_map/all_to_all | solution.py:115
  249.2 1.9 collective-permute-start.22
  251.1 9.3 %shard_map.236 = (bf16[1024,1024]{1,0:T(8,128)(2,1)}, f32[1,1024]{1,0:T(1,128)}) custom-call(bf16[1024,2048]{1,0:T(8,128)(2,1)} %get-tuple-element.305.lhs_ref.g_ref.refs_2_, bf16[2048,1024]{1,0:T(8,128)(2,1)} %all-gather.8.cloned.1.call-done.down_ref.w_ref, f32[1024,1024]{1,0:T(8,128)} %get-tuple-element.338.slope_ref), custom_call_target="tpu_custom_call" | custom-call | flops 1 | bytes 1 | tf_op jit(solution)/shard_map/pallas_call | solution.py:124
  260.4 8.5 %shard_map.237 = bf16[2048,1024]{1,0:T(8,128)(2,1)} custom-call(bf16[1024,2048]{1,0:T(8,128)(2,1)} %get-tuple-element.284.mlp_ref.refs_0_, bf16[1024,1024]{1,0:T(8,128)(2,1)} %get-tuple-element.347.refs_1_.refs_11_), custom_call_target="tpu_custom_call" | custom-call | flops 1 | bytes 1 | tf_op jit(solution)/shard_map/pallas_call | solution.py:124
  268.9 4.9 %collective-permute-done.21.refs_2_ = bf16[1024,512]{1,0:T(8,128)(2,1)S(1)} collective-permute-done((bf16[1024,512]{1,0:T(8,128)(2,1)}, bf16[1024,512]{1,0:T(8,128)(2,1)S(1)}, u32[]{:S(2)}, u32[]{:S(2)}) %collective-permute-start.21) | collective-permute-done | bytes 1048608 | tf_op jit(solution)/shard_map/ppermute | solution.py:58
  273.8 1.7 all-to-all-done.3
  279.8 4.5 %shard_map.238 = (bf16[1024,768]{1,0:T(8,128)(2,1)}, f32[1,768]{1,0:T(1,128)}) custom-call(bf16[1024,256]{1,0:T(8,128)(2,1)} %get-tuple-element.315.refs_0_, bf16[1024,512]{1,0:T(8,128)(2,1)} %get-tuple-element.316.refs_1_, bf16[1024,512]{1,0:T(8,128)(2,1)} %copy-done.23, f32[1024,128]{1,0:T(8,128)} %maximum_maximum_fusion.refs_11_.refs_3_, ...), custom_call_target="tpu_custom_call" | custom-call | flops 1 | bytes 1 | tf_op jit(solution)/shard_map/pallas_call | solution.py:124
  284.2 15.2 %shard_map.239 = (f32[128,2048]{1,0:T(8,128)}, f32[128,2048]{1,0:T(8,128)}, f32[128,2048]{1,0:T(8,128)}, f32[128,2048]{1,0:T(8,128)}, bf16[128,2048]{1,0:T(8,128...) custom-call(bf16[128,2048]{1,0:T(8,128)(2,1)} %bitcast.146, ...), custom_call_target="tpu_custom_call" | custom-call | flops 1 | bytes 1 | tf_op jit(solution)/shard_map/pallas_call | solution.py:124
  299.5 1.8 collective-permute-done.25
  308.2 9.2 %shard_map.240 = bf16[2048,1024]{1,0:T(8,128)(2,1)} custom-call(bf16[1024,2048]{1,0:T(8,128)(2,1)} %get-tuple-element.371.refs_0_, bf16[1024,768]{1,0:T(8,128)(2,1)} %get-tuple-element.372.refs_10_.refs_1_, bf16[1024,2048]{1,0:T(8,128)(2,1)} %get-tuple-element.305.lhs_ref.g_ref.refs_2_, bf16[1024,256]{1,0:T(8,128)(2,1)} %get-tuple-element.373.att_ref.refs_3_), custom_call_target="tpu_custom_call" | custom-call | flops 1 | bytes 1 | tf_op jit(solution)/shard_map/pallas_call | solution.py:124
  317.4 8.2 %collective-permute-done.26 = bf16[128,2048]{1,0:T(8,128)(2,1)} collective-permute-done((bf16[128,2048]{1,0:T(8,128)(2,1)}, bf16[128,2048]{1,0:T(8,128)(2,1)}, u32[]{:S(2)}, u32[]{:S(2)}) %collective-permute-start.26) | collective-permute-done | bytes 524320 | tf_op jit(solution)/shard_map/ppermute | solution.py:58
  325.6 2.5 collective-permute-done.29
  328.1 2.0 add_convert_fusion.4
  330.1 3.9 all-to-all-start.4
  335.0 2.1 collective-permute-start.30
  341.1 2.2 collective-permute-done.33
  343.4 2.7 fusion.7
  346.9 13.9 %collective-permute-done.30 = bf16[128,2048]{1,0:T(8,128)(2,1)S(1)} collective-permute-done((bf16[128,2048]{1,0:T(8,128)(2,1)}, bf16[128,2048]{1,0:T(8,128)(2,1)S(1)}, u32[]{:S(2)}, u32[]{:S(2)}) %collective-permute-start.30) | collective-permute-done | bytes 524320 | tf_op jit(solution)/shard_map/ppermute | solution.py:58
  362.3 5.1 %collective-permute-done.32 = bf16[128,2048]{1,0:T(8,128)(2,1)} collective-permute-done((bf16[128,2048]{1,0:T(8,128)(2,1)}, bf16[128,2048]{1,0:T(8,128)(2,1)}, u32[]{:S(2)}, u32[]{:S(2)}) %collective-permute-start.32) | collective-permute-done | bytes 524320 | tf_op jit(solution)/shard_map/ppermute | solution.py:58
  367.4 3.7 reduce-scatter.5.cloned.1.call-done
  371.1 5.7 %all-to-all-start.5 = ((bf16[8,64,1024]{2,1,0:T(8,128)(2,1)}), bf16[8,64,1024]{2,1,0:T(8,128)(2,1)S(1)}, u32[]{:S(2)}, u32[]{:S(2)}) async-start(bf16[8,64,1024]{2,1,0:T(8,128)(2,1)} %bitcast.163), calls=%async_computation.7 | async-start | bytes 2097152 | tf_op jit(solution)/shard_map/all_to_all | solution.py:115
  376.9 2.4 add_convert_fusion.2
  379.3 2.0 add_convert_fusion.3
  381.3 2.0 collective-permute-start.36
  385.0 2.4 collective-permute-start.38
  389.6 4.8 %collective-permute-done.37 = f32[2,12,64]{2,0,1:T(2,128)S(1)} collective-permute-done((f32[2,12,64]{2,0,1:T(2,128)S(1)}, f32[2,12,64]{2,0,1:T(2,128)S(1)}, u32[]{:S(2)}, u32[]{:S(2)}) %collective-permute-start.37) | collective-permute-done | bytes 6176 | tf_op jit(solution)/shard_map/ppermute | solution.py:58
  394.4 9.0 %collective-permute-done.38 = f32[2,12,64]{2,0,1:T(2,128)S(1)} collective-permute-done((f32[2,12,64]{2,0,1:T(2,128)S(1)}, f32[2,12,64]{2,0,1:T(2,128)S(1)}, u32[]{:S(2)}, u32[]{:S(2)}) %collective-permute-start.38) | collective-permute-done | bytes 6176 | tf_op jit(solution)/shard_map/ppermute | solution.py:58
  409.6 2.6 reshape.275
  413.1 1.6 copy.76
  414.7 12.9 %collective-permute-done.40 = bf16[128,2048]{1,0:T(8,128)(2,1)} collective-permute-done((bf16[128,2048]{1,0:T(8,128)(2,1)}, bf16[128,2048]{1,0:T(8,128)(2,1)}, u32[]{:S(2)}, u32[]{:S(2)}) %collective-permute-start.40) | collective-permute-done | bytes 524320 | tf_op jit(solution)/shard_map/ppermute | solution.py:58
  428.2 1.9 fusion.24
  (244 shorter events, 68.6 us)
Async XLA Ops:
  7.2 26.3 %collective-permute-start = (bf16[128,2048]{1,0:T(8,128)(2,1)}, bf16[128,2048]{1,0:T(8,128)(2,1)S(1)}, u32[]{:S(2)}, u32[]{:S(2)}) collective-permute-start(bf16[128,2048]{1,0:T(8,128)(2,1)} %bitcast.142), channel_id=1, source_target_pairs={{0,1},{1,0},{2,3},{3,2},{4,5},{5,4},{6,7},{7,6},{8,9},{9,8},{10,11... | collective-permute-start | bytes 1572872 | tf_op jit(solution)/shard_map/ppermute | solution.py:58
  10.3 25.8 %collective-permute-start.1 = (bf16[128,2048]{1,0:T(8,128)(2,1)}, bf16[128,2048]{1,0:T(8,128)(2,1)S(1)}, u32[]{:S(2)}, u32[]{:S(2)}) collective-permute-start(bf16[128,2048]{1,0:T(8,128)(2,1)} %bitcast.143), channel_id=1, source_target_pairs={{0,2},{1,3},{2,0},{3,1},{4,6},{5,7},{6,4},{7,5},{8,10},{9,11},{10,... | collective-permute-start | bytes 1572872 | tf_op jit(solution)/shard_map/ppermute | solution.py:58
  12.9 23.2 %collective-permute-start.2 = (bf16[128,2048]{1,0:T(8,128)(2,1)}, bf16[128,2048]{1,0:T(8,128)(2,1)}, u32[]{:S(2)}, u32[]{:S(2)}) collective-permute-start(bf16[128,2048]{1,0:T(8,128)(2,1)} %bitcast.144), channel_id=1, source_target_pairs={{0,4},{4,0},{1,5},{5,1},{2,6},{6,2},{3,7},{7,3},{8,12},{12,8},{9,1... | collective-permute-start | bytes 1572872 | tf_op jit(solution)/shard_map/ppermute | solution.py:58
  14.3 23.2 %collective-permute-start.3 = (bf16[128,2048]{1,0:T(8,128)(2,1)}, bf16[128,2048]{1,0:T(8,128)(2,1)}, u32[]{:S(2)}, u32[]{:S(2)}) collective-permute-start(bf16[128,2048]{1,0:T(8,128)(2,1)} %bitcast.149), channel_id=1, source_target_pairs={{0,4},{4,0},{1,5},{5,1},{2,6},{6,2},{3,7},{7,3},{8,12},{12,8},{9,1... | collective-permute-start | bytes 1572872 | tf_op jit(solution)/shard_map/ppermute | solution.py:58
  33.5 14.9 %copy-start.5 = (bf16[128,2048]{1,0:T(8,128)(2,1)}, bf16[128,2048]{1,0:T(8,128)(2,1)S(1)}, u32[]{:S(2)}) copy-start(bf16[128,2048]{1,0:T(8,128)(2,1)S(1)} %collective-permute-done.refs_1_) | copy-start | bytes 1572868
  37.5 41.5 %all-to-all-start = ((bf16[8,72,1024]{2,1,0:T(8,128)(2,1)}), bf16[8,72,1024]{2,1,0:T(8,128)(2,1)S(1)}, u32[]{:S(2)}, u32[]{:S(2)}) async-start(bf16[8,72,1024]{2,1,0:T(8,128)(2,1)} %pad_maximum_fusion), calls=%async_computation | async-start | bytes 2359296 | tf_op jit(solution)/shard_map/all_to_all | solution.py:588
  41.5 77.0 %all-gather.4.cloned.1.call-start = ((), (), s32[]{:S(2)}) async-start(), calls=%async_computation.8 | async-start | bytes 5242880 | tf_op jit(solution)/shard_map/all_gather | solution.py:106
  45.0 27.3 %collective-permute-start.4 = (bf16[128,2048]{1,0:T(8,128)(2,1)S(1)}, bf16[128,2048]{1,0:T(8,128)(2,1)S(1)}, u32[]{:S(2)}, u32[]{:S(2)}) collective-permute-start(bf16[128,2048]{1,0:T(8,128)(2,1)S(1)} %copy-done.7), channel_id=1, source_target_pairs={{0,1},{1,0},{2,3},{3,2},{4,5},{5,4},{6,7},{7,6},{8,9},{9,8},{10,11... | collective-permute-start | bytes 1572872 | tf_op jit(solution)/shard_map/ppermute | solution.py:58
  47.0 32.0 %collective-permute-start.6 = (bf16[128,2048]{1,0:T(8,128)(2,1)S(1)}, bf16[128,2048]{1,0:T(8,128)(2,1)}, u32[]{:S(2)}, u32[]{:S(2)}) collective-permute-start(bf16[128,2048]{1,0:T(8,128)(2,1)S(1)} %copy-done.7), channel_id=1, source_target_pairs={{0,4},{4,0},{1,5},{5,1},{2,6},{6,2},{3,7},{7,3},{8,12},{12,8},{9,1... | collective-permute-start | bytes 1572872 | tf_op jit(solution)/shard_map/ppermute | solution.py:58
  48.5 29.7 %collective-permute-start.5 = (bf16[128,2048]{1,0:T(8,128)(2,1)S(1)}, bf16[128,2048]{1,0:T(8,128)(2,1)S(1)}, u32[]{:S(2)}, u32[]{:S(2)}) collective-permute-start(bf16[128,2048]{1,0:T(8,128)(2,1)S(1)} %collective-permute-done.refs_1_), channel_id=1, source_target_pairs={{0,4},{4,0},{1,5},{5,1},{2,6},{6,2},{3,7},{7,3},{8,12},{12,8},{9,1... | collective-permute-start | bytes 1572872 | tf_op jit(solution)/shard_map/ppermute | solution.py:58
  80.1 33.4 %all-to-all-start.1 = ((bf16[8,64,1024]{2,1,0:T(8,128)(2,1)}), bf16[8,64,1024]{2,1,0:T(8,128)(2,1)S(1)}, u32[]{:S(2)}, u32[]{:S(2)}) async-start(bf16[8,64,1024]{2,1,0:T(8,128)(2,1)} %get-tuple-element.239), calls=%async_computation.1 | async-start | bytes 2097152 | tf_op jit(solution)/shard_map/all_to_all | solution.py:101
  83.9 79.7 %all-gather.6.cloned.1.call-start = ((), (), s32[]{:S(2)}) async-start(), calls=%async_computation.9 | async-start | bytes 5242880 | tf_op jit(solution)/shard_map/all_gather | solution.py:106
  84.2 5.7 %collective-permute-start.11 = (bf16[8,768]{1,0:T(8,128)(2,1)S(1)}, bf16[8,768]{1,0:T(8,128)(2,1)S(1)}, u32[]{:S(2)}, u32[]{:S(2)}) collective-permute-start(bf16[8,768]{1,0:T(8,128)(2,1)S(1)} %bitcast.178), channel_id=1, source_target_pairs={{0,24},{8,16},{16,8},{24,0},{1,25},{9,17},{17,9},{25,1},{2,26},{10... | collective-permute-start | bytes 36872 | tf_op jit(solution)/shard_map/ppermute | solution.py:58
  84.2 5.6 %collective-permute-start.10 = (bf16[8,768]{1,0:T(8,128)(2,1)S(1)}, bf16[8,768]{1,0:T(8,128)(2,1)S(1)}, u32[]{:S(2)}, u32[]{:S(2)}) collective-permute-start(bf16[8,768]{1,0:T(8,128)(2,1)S(1)} %bitcast.179), channel_id=1, source_target_pairs={{0,16},{8,24},{16,0},{24,8},{1,17},{9,25},{17,1},{25,9},{2,18},{10... | collective-permute-start | bytes 36872 | tf_op jit(solution)/shard_map/ppermute | solution.py:58
  85.9 4.0 collective-permute-start.9
  86.4 20.5 %collective-permute-start.7 = (bf16[128,2048]{1,0:T(8,128)(2,1)S(1)}, bf16[128,2048]{1,0:T(8,128)(2,1)S(1)}, u32[]{:S(2)}, u32[]{:S(2)}) collective-permute-start(bf16[128,2048]{1,0:T(8,128)(2,1)S(1)} %copy-done.9), channel_id=1, source_target_pairs={{0,4},{4,0},{1,5},{5,1},{2,6},{6,2},{3,7},{7,3},{8,12},{12,8},{9,1... | collective-permute-start | bytes 1572872 | tf_op jit(solution)/shard_map/ppermute | solution.py:58
  88.4 25.2 %collective-permute-start.8 = (bf16[128,2048]{1,0:T(8,128)(2,1)S(1)}, bf16[128,2048]{1,0:T(8,128)(2,1)S(1)}, u32[]{:S(2)}, u32[]{:S(2)}) collective-permute-start(bf16[128,2048]{1,0:T(8,128)(2,1)S(1)} %bitcast.151), channel_id=1, source_target_pairs={{0,1},{1,0},{2,3},{3,2},{4,5},{5,4},{6,7},{7,6},{8,9},{9,8},{10,11... | collective-permute-start | bytes 1572872 | tf_op jit(solution)/shard_map/ppermute | solution.py:58
  106.9 11.6 %copy-start.11 = (bf16[128,2048]{1,0:T(8,128)(2,1)}, bf16[128,2048]{1,0:T(8,128)(2,1)S(1)}, u32[]{:S(2)}) copy-start(bf16[128,2048]{1,0:T(8,128)(2,1)S(1)} %collective-permute-done.7.refs_7_) | copy-start | bytes 1572868
  113.5 41.4 %copy-start.25 = (bf16[128,2048]{1,0:T(8,128)(2,1)}, bf16[128,2048]{1,0:T(8,128)(2,1)S(1)}, u32[]{:S(2)}) copy-start(bf16[128,2048]{1,0:T(8,128)(2,1)S(1)} %collective-permute-done.8.refs_1_) | copy-start | bytes 1572868
  114.6 16.6 %collective-permute-start.12 = (bf16[128,2048]{1,0:T(8,128)(2,1)S(1)}, bf16[128,2048]{1,0:T(8,128)(2,1)S(1)}, u32[]{:S(2)}, u32[]{:S(2)}) collective-permute-start(bf16[128,2048]{1,0:T(8,128)(2,1)S(1)} %collective-permute-done.8.refs_1_), channel_id=1, source_target_pairs={{0,4},{4,0},{1,5},{5,1},{2,6},{6,2},{3,7},{7,3},{8,12},{12,8},{9,1... | collective-permute-start | bytes 1572872 | tf_op jit(solution)/shard_map/ppermute | solution.py:58
  116.1 24.3 %collective-permute-start.13 = (bf16[128,2048]{1,0:T(8,128)(2,1)S(1)}, bf16[128,2048]{1,0:T(8,128)(2,1)}, u32[]{:S(2)}, u32[]{:S(2)}) collective-permute-start(bf16[128,2048]{1,0:T(8,128)(2,1)S(1)} %bitcast.152), channel_id=1, source_target_pairs={{0,2},{1,3},{2,0},{3,1},{4,6},{5,7},{6,4},{7,5},{8,10},{9,11},{10,... | collective-permute-start | bytes 1572872 | tf_op jit(solution)/shard_map/ppermute | solution.py:58
  131.2 28.8 %copy-start.13 = (bf16[1024,512]{1,0:T(8,128)(2,1)S(1)}, bf16[1024,512]{1,0:T(8,128)(2,1)}, u32[]{:S(2)}) copy-start(bf16[1024,512]{1,0:T(8,128)(2,1)} %get-tuple-element.313.refs_0_) | copy-start | bytes 3145732
  131.2 23.7 %copy-start.28 = (bf16[128,2048]{1,0:T(8,128)(2,1)}, bf16[128,2048]{1,0:T(8,128)(2,1)S(1)}, u32[]{:S(2)}) copy-start(bf16[128,2048]{1,0:T(8,128)(2,1)S(1)} %collective-permute-done.12.refs_5_) | copy-start | bytes 1572868
  140.4 13.0 %collective-permute-start.14 = (bf16[128,2048]{1,0:T(8,128)(2,1)}, bf16[128,2048]{1,0:T(8,128)(2,1)S(1)}, u32[]{:S(2)}, u32[]{:S(2)}) collective-permute-start(bf16[128,2048]{1,0:T(8,128)(2,1)} %collective-permute-done.13.refs_2_), channel_id=1, source_target_pairs={{0,4},{4,0},{1,5},{5,1},{2,6},{6,2},{3,7},{7,3},{8,12},{12,8},{9,1... | collective-permute-start | bytes 1572872 | tf_op jit(solution)/shard_map/ppermute | solution.py:58
  141.6 13.4 %collective-permute-start.15 = (bf16[128,2048]{1,0:T(8,128)(2,1)}, bf16[128,2048]{1,0:T(8,128)(2,1)}, u32[]{:S(2)}, u32[]{:S(2)}) collective-permute-start(bf16[128,2048]{1,0:T(8,128)(2,1)} %collective-permute-done.13.refs_2_), channel_id=1, source_target_pairs={{0,1},{1,0},{2,3},{3,2},{4,5},{5,4},{6,7},{7,6},{8,9},{9,8},{10,11... | collective-permute-start | bytes 1572872 | tf_op jit(solution)/shard_map/ppermute | solution.py:58
  155.0 30.6 %all-to-all-start.2 = ((bf16[8,64,1024]{2,1,0:T(8,128)(2,1)}), bf16[8,64,1024]{2,1,0:T(8,128)(2,1)S(1)}, u32[]{:S(2)}, u32[]{:S(2)}) async-start(bf16[8,64,1024]{2,1,0:T(8,128)(2,1)} %get-tuple-element.283), calls=%async_computation.2 | async-start | bytes 2097152 | tf_op jit(solution)/shard_map/all_to_all | solution.py:101
  159.9 66.3 %all-gather.8.cloned.1.call-start = ((), (), s32[]{:S(2)}) async-start(), calls=%async_computation.10 | async-start | bytes 5242880 | tf_op jit(solution)/shard_map/all_gather | solution.py:106
  160.0 23.7 %collective-permute-start.17 = (bf16[1024,512]{1,0:T(8,128)(2,1)S(1)}, bf16[1024,512]{1,0:T(8,128)(2,1)S(1)}, u32[]{:S(2)}, u32[]{:S(2)}) collective-permute-start(bf16[1024,512]{1,0:T(8,128)(2,1)S(1)} %copy-done.13), channel_id=1, source_target_pairs={{0,8},{8,0},{1,9},{9,1},{2,10},{10,2},{3,11},{11,3},{4,12},{12,4},... | collective-permute-start | bytes 3145736 | tf_op jit(solution)/shard_map/ppermute | solution.py:58
  161.6 22.1 %collective-permute-start.16 = (bf16[128,2048]{1,0:T(8,128)(2,1)}, bf16[128,2048]{1,0:T(8,128)(2,1)}, u32[]{:S(2)}, u32[]{:S(2)}) collective-permute-start(bf16[128,2048]{1,0:T(8,128)(2,1)} %collective-permute-done.15.refs_3_), channel_id=1, source_target_pairs={{0,4},{4,0},{1,5},{5,1},{2,6},{6,2},{3,7},{7,3},{8,12},{12,8},{9,1... | collective-permute-start | bytes 1572872 | tf_op jit(solution)/shard_map/ppermute | solution.py:58
  183.7 17.1 %copy-start.17 = (bf16[1024,512]{1,0:T(8,128)(2,1)}, bf16[1024,512]{1,0:T(8,128)(2,1)S(1)}, u32[]{:S(2)}) copy-start(bf16[1024,512]{1,0:T(8,128)(2,1)S(1)} %collective-permute-done.17.refs_1_) | copy-start | bytes 3145732
  200.8 8.0 %collective-permute-start.18 = (bf16[512,1024]{1,0:T(8,128)(2,1)}, bf16[512,1024]{1,0:T(8,128)(2,1)S(1)}, u32[]{:S(2)}, u32[]{:S(2)}) collective-permute-start(bf16[512,1024]{1,0:T(8,128)(2,1)} %get-tuple-element.303), channel_id=1, source_target_pairs={{0,16},{16,0},{1,17},{17,1},{2,18},{18,2},{3,19},{19,3},{4,20},{20... | collective-permute-start | bytes 3145736 | tf_op jit(solution)/shard_map/ppermute | solution.py:58
  200.8 8.0 %collective-permute-start.19 = (bf16[512,1024]{1,0:T(8,128)(2,1)}, bf16[512,1024]{1,0:T(8,128)(2,1)S(1)}, u32[]{:S(2)}, u32[]{:S(2)}) collective-permute-start(bf16[512,1024]{1,0:T(8,128)(2,1)} %get-tuple-element.304), channel_id=1, source_target_pairs={{0,16},{16,0},{1,17},{17,1},{2,18},{18,2},{3,19},{19,3},{4,20},{20... | collective-permute-start | bytes 3145736 | tf_op jit(solution)/shard_map/ppermute | solution.py:58
  210.5 30.9 %collective-permute-start.20 = (bf16[512,1024]{1,0:T(8,128)(2,1)S(1)}, bf16[512,1024]{1,0:T(8,128)(2,1)S(1)}, u32[]{:S(2)}, u32[]{:S(2)}) collective-permute-start(bf16[512,1024]{1,0:T(8,128)(2,1)S(1)} %add_convert_fusion.1), channel_id=1, source_target_pairs={{0,8},{8,0},{1,9},{9,1},{2,10},{10,2},{3,11},{11,3},{4,12},{12,4},... | collective-permute-start | bytes 3145736 | tf_op jit(solution)/shard_map/ppermute | solution.py:58
  232.4 9.0 %copy-start.24 = (bf16[512,1024]{1,0:T(8,128)(2,1)S(1)}, bf16[512,1024]{1,0:T(8,128)(2,1)}, u32[]{:S(2)}) copy-start(bf16[512,1024]{1,0:T(8,128)(2,1)} %get-tuple-element.332) | copy-start | bytes 3145732
  243.0 32.5 %all-to-all-start.3 = ((bf16[8,64,1024]{2,1,0:T(8,128)(2,1)}), bf16[8,64,1024]{2,1,0:T(8,128)(2,1)S(1)}, u32[]{:S(2)}, u32[]{:S(2)}) async-start(bf16[8,64,1024]{2,1,0:T(8,128)(2,1)} %bitcast.26), calls=%async_computation.3 | async-start | bytes 2097152 | tf_op jit(solution)/shard_map/all_to_all | solution.py:115
  248.5 79.5 %reduce-scatter.3.cloned.1.call-start = ((), (), s32[]{:S(2)}) async-start(), calls=%async_computation.11 | async-start | bytes 5242880 | tf_op jit(solution)/shard_map/reduce_scatter | solution.py:110
  248.6 25.2 %collective-permute-start.21 = (bf16[1024,512]{1,0:T(8,128)(2,1)}, bf16[1024,512]{1,0:T(8,128)(2,1)S(1)}, u32[]{:S(2)}, u32[]{:S(2)}) collective-permute-start(bf16[1024,512]{1,0:T(8,128)(2,1)} %get-tuple-element.330), channel_id=1, source_target_pairs={{0,8},{8,0},{1,9},{9,1},{2,10},{10,2},{3,11},{11,3},{4,12},{12,4},... | collective-permute-start | bytes 3145736 | tf_op jit(solution)/shard_map/ppermute | solution.py:58
  249.2 24.6 %collective-permute-start.22 = (bf16[128,2048]{1,0:T(8,128)(2,1)}, bf16[128,2048]{1,0:T(8,128)(2,1)}, u32[]{:S(2)}, u32[]{:S(2)}) collective-permute-start(bf16[128,2048]{1,0:T(8,128)(2,1)} %get-tuple-element.337), channel_id=1, source_target_pairs={{0,4},{4,0},{1,5},{5,1},{2,6},{6,2},{3,7},{7,3},{8,12},{12,8},{9,1... | collective-permute-start | bytes 1572872 | tf_op jit(solution)/shard_map/ppermute | solution.py:58
  275.5 95.6 %reduce-scatter.5.cloned.1.call-start = ((), (), s32[]{:S(2)}) async-start(), calls=%async_computation.12 | async-start | bytes 5242880 | tf_op jit(solution)/shard_map/reduce_scatter | solution.py:110
  276.8 22.6 %collective-permute-start.23 = (bf16[128,2048]{1,0:T(8,128)(2,1)S(1)}, bf16[128,2048]{1,0:T(8,128)(2,1)S(1)}, u32[]{:S(2)}, u32[]{:S(2)}) collective-permute-start(bf16[128,2048]{1,0:T(8,128)(2,1)S(1)} %add_convert_fusion.7), channel_id=1, source_target_pairs={{0,1},{1,0},{2,3},{3,2},{4,5},{5,4},{6,7},{7,6},{8,9},{9,8},{10,11... | collective-permute-start | bytes 1572872 | tf_op jit(solution)/shard_map/ppermute | solution.py:58
  277.7 21.7 %collective-permute-start.24 = (bf16[128,2048]{1,0:T(8,128)(2,1)S(1)}, bf16[128,2048]{1,0:T(8,128)(2,1)S(1)}, u32[]{:S(2)}, u32[]{:S(2)}) collective-permute-start(bf16[128,2048]{1,0:T(8,128)(2,1)S(1)} %copy-done.36), channel_id=1, source_target_pairs={{0,4},{4,0},{1,5},{5,1},{2,6},{6,2},{3,7},{7,3},{8,12},{12,8},{9,1... | collective-permute-start | bytes 1572872 | tf_op jit(solution)/shard_map/ppermute | solution.py:58
  279.2 22.1 %collective-permute-start.25 = (bf16[128,2048]{1,0:T(8,128)(2,1)S(1)}, bf16[128,2048]{1,0:T(8,128)(2,1)S(1)}, u32[]{:S(2)}, u32[]{:S(2)}) collective-permute-start(bf16[128,2048]{1,0:T(8,128)(2,1)S(1)} %copy-done.35), channel_id=1, source_target_pairs={{0,4},{4,0},{1,5},{5,1},{2,6},{6,2},{3,7},{7,3},{8,12},{12,8},{9,1... | collective-permute-start | bytes 1572872 | tf_op jit(solution)/shard_map/ppermute | solution.py:58
  284.2 17.1 %copy-start.16 = (f32[128,2048]{1,0:T(8,128)S(1)}, f32[128,2048]{1,0:T(8,128)}, u32[]{:S(2)}) copy-start(f32[128,2048]{1,0:T(8,128)} %get-tuple-element.360) | copy-start | bytes 3145732
  302.4 23.1 %collective-permute-start.26 = (bf16[128,2048]{1,0:T(8,128)(2,1)}, bf16[128,2048]{1,0:T(8,128)(2,1)}, u32[]{:S(2)}, u32[]{:S(2)}) collective-permute-start(bf16[128,2048]{1,0:T(8,128)(2,1)} %add_convert_fusion.5), channel_id=1, source_target_pairs={{0,1},{1,0},{2,3},{3,2},{4,5},{5,4},{6,7},{7,6},{8,9},{9,8},{10,11... | collective-permute-start | bytes 1572872 | tf_op jit(solution)/shard_map/ppermute | solution.py:58
  303.9 21.7 %collective-permute-start.27 = (bf16[128,2048]{1,0:T(8,128)(2,1)S(1)}, bf16[128,2048]{1,0:T(8,128)(2,1)}, u32[]{:S(2)}, u32[]{:S(2)}) collective-permute-start(bf16[128,2048]{1,0:T(8,128)(2,1)S(1)} %add_convert_fusion.6), channel_id=1, source_target_pairs={{0,2},{1,3},{2,0},{3,1},{4,6},{5,7},{6,4},{7,5},{8,10},{9,11},{10,... | collective-permute-start | bytes 1572872 | tf_op jit(solution)/shard_map/ppermute | solution.py:58
  305.4 20.2 %collective-permute-start.28 = (bf16[128,2048]{1,0:T(8,128)(2,1)}, bf16[128,2048]{1,0:T(8,128)(2,1)}, u32[]{:S(2)}, u32[]{:S(2)}) collective-permute-start(bf16[128,2048]{1,0:T(8,128)(2,1)} %get-tuple-element.369), channel_id=1, source_target_pairs={{0,4},{4,0},{1,5},{5,1},{2,6},{6,2},{3,7},{7,3},{8,12},{12,8},{9,1... | collective-permute-start | bytes 1572872 | tf_op jit(solution)/shard_map/ppermute | solution.py:58
  306.9 21.2 %collective-permute-start.29 = (bf16[128,2048]{1,0:T(8,128)(2,1)}, bf16[128,2048]{1,0:T(8,128)(2,1)}, u32[]{:S(2)}, u32[]{:S(2)}) collective-permute-start(bf16[128,2048]{1,0:T(8,128)(2,1)} %get-tuple-element.370), channel_id=1, source_target_pairs={{0,4},{4,0},{1,5},{5,1},{2,6},{6,2},{3,7},{7,3},{8,12},{12,8},{9,1... | collective-permute-start | bytes 1572872 | tf_op jit(solution)/shard_map/ppermute | solution.py:58
  317.4 10.7 %copy-start.14 = (f32[128,2048]{1,0:T(8,128)S(1)}, f32[128,2048]{1,0:T(8,128)}, u32[]{:S(2)}) copy-start(f32[128,2048]{1,0:T(8,128)} %get-tuple-element.348) | copy-start | bytes 3145732
  330.1 37.3 %all-to-all-start.4 = ((bf16[8,64,1024]{2,1,0:T(8,128)(2,1)}), bf16[8,64,1024]{2,1,0:T(8,128)(2,1)S(1)}, u32[]{:S(2)}, u32[]{:S(2)}) async-start(bf16[8,64,1024]{2,1,0:T(8,128)(2,1)} %bitcast.162), calls=%async_computation.5 | async-start | bytes 2097152 | tf_op jit(solution)/shard_map/all_to_all | solution.py:115
  335.0 25.7 %collective-permute-start.30 = (bf16[128,2048]{1,0:T(8,128)(2,1)}, bf16[128,2048]{1,0:T(8,128)(2,1)S(1)}, u32[]{:S(2)}, u32[]{:S(2)}) collective-permute-start(bf16[128,2048]{1,0:T(8,128)(2,1)} %add_convert_fusion.4), channel_id=1, source_target_pairs={{0,1},{1,0},{2,3},{3,2},{4,5},{5,4},{6,7},{7,6},{8,9},{9,8},{10,11... | collective-permute-start | bytes 1572872 | tf_op jit(solution)/shard_map/ppermute | solution.py:58
  337.1 23.6 %collective-permute-start.31 = (bf16[128,2048]{1,0:T(8,128)(2,1)}, bf16[128,2048]{1,0:T(8,128)(2,1)S(1)}, u32[]{:S(2)}, u32[]{:S(2)}) collective-permute-start(bf16[128,2048]{1,0:T(8,128)(2,1)} %get-tuple-element.388), channel_id=1, source_target_pairs={{0,4},{4,0},{1,5},{5,1},{2,6},{6,2},{3,7},{7,3},{8,12},{12,8},{9,1... | collective-permute-start | bytes 1572872 | tf_op jit(solution)/shard_map/ppermute | solution.py:58
  338.6 28.8 %collective-permute-start.32 = (bf16[128,2048]{1,0:T(8,128)(2,1)}, bf16[128,2048]{1,0:T(8,128)(2,1)}, u32[]{:S(2)}, u32[]{:S(2)}) collective-permute-start(bf16[128,2048]{1,0:T(8,128)(2,1)} %get-tuple-element.389), channel_id=1, source_target_pairs={{0,4},{4,0},{1,5},{5,1},{2,6},{6,2},{3,7},{7,3},{8,12},{12,8},{9,1... | collective-permute-start | bytes 1572872 | tf_op jit(solution)/shard_map/ppermute | solution.py:58
  339.2 4.2 collective-permute-start.33
  341.0 5.1 %collective-permute-start.34 = (f32[2,4,12,64]{3,1,2,0:T(4,128)S(1)}, f32[2,4,12,64]{3,1,2,0:T(4,128)S(1)}, u32[]{:S(2)}, u32[]{:S(2)}) collective-permute-start(f32[2,4,12,64]{3,1,2,0:T(4,128)S(1)} %bitcast.175), channel_id=1, source_target_pairs={{0,16},{8,24},{16,0},{24,8},{1,17},{9,25},{17,1},{25,9},{2,18},{10... | collective-permute-start | bytes 73736 | tf_op jit(solution)/shard_map/ppermute | solution.py:58
  343.4 3.5 collective-permute-start.35
  371.1 33.1 %all-to-all-start.5 = ((bf16[8,64,1024]{2,1,0:T(8,128)(2,1)}), bf16[8,64,1024]{2,1,0:T(8,128)(2,1)S(1)}, u32[]{:S(2)}, u32[]{:S(2)}) async-start(bf16[8,64,1024]{2,1,0:T(8,128)(2,1)} %bitcast.163), calls=%async_computation.7 | async-start | bytes 2097152 | tf_op jit(solution)/shard_map/all_to_all | solution.py:115
  381.3 22.1 %collective-permute-start.36 = (bf16[128,2048]{1,0:T(8,128)(2,1)S(1)}, bf16[128,2048]{1,0:T(8,128)(2,1)}, u32[]{:S(2)}, u32[]{:S(2)}) collective-permute-start(bf16[128,2048]{1,0:T(8,128)(2,1)S(1)} %copy-done.34), channel_id=1, source_target_pairs={{0,4},{4,0},{1,5},{5,1},{2,6},{6,2},{3,7},{7,3},{8,12},{12,8},{9,1... | collective-permute-start | bytes 1572872 | tf_op jit(solution)/shard_map/ppermute | solution.py:58
  383.5 10.9 %collective-permute-start.37 = (f32[2,12,64]{2,0,1:T(2,128)S(1)}, f32[2,12,64]{2,0,1:T(2,128)S(1)}, u32[]{:S(2)}, u32[]{:S(2)}) collective-permute-start(f32[2,12,64]{2,0,1:T(2,128)S(1)} %bitcast.193), channel_id=1, source_target_pairs={{0,1},{1,0},{2,3},{3,2},{4,5},{5,4},{6,7},{7,6},{8,9},{9,8},{10,11... | collective-permute-start | bytes 18440 | tf_op jit(solution)/shard_map/ppermute | solution.py:58
  385.0 18.4 %collective-permute-start.38 = (f32[2,12,64]{2,0,1:T(2,128)S(1)}, f32[2,12,64]{2,0,1:T(2,128)S(1)}, u32[]{:S(2)}, u32[]{:S(2)}) collective-permute-start(f32[2,12,64]{2,0,1:T(2,128)S(1)} %bitcast.194), channel_id=1, source_target_pairs={{0,2},{1,3},{2,0},{3,1},{4,6},{5,7},{6,4},{7,5},{8,10},{9,11},{10,... | collective-permute-start | bytes 18440 | tf_op jit(solution)/shard_map/ppermute | solution.py:58
  387.4 16.1 %collective-permute-start.39 = (f32[2,12,64]{2,0,1:T(2,128)S(1)}, f32[2,12,64]{2,0,1:T(2,128)S(1)}, u32[]{:S(2)}, u32[]{:S(2)}) collective-permute-start(f32[2,12,64]{2,0,1:T(2,128)S(1)} %bitcast.195), channel_id=1, source_target_pairs={{0,3},{1,2},{2,1},{3,0},{4,7},{5,6},{6,5},{7,4},{8,11},{9,10},{10,... | collective-permute-start | bytes 18440 | tf_op jit(solution)/shard_map/ppermute | solution.py:58
  404.2 23.5 %collective-permute-start.40 = (bf16[128,2048]{1,0:T(8,128)(2,1)}, bf16[128,2048]{1,0:T(8,128)(2,1)}, u32[]{:S(2)}, u32[]{:S(2)}) collective-permute-start(bf16[128,2048]{1,0:T(8,128)(2,1)} %add_convert_fusion.2), channel_id=1, source_target_pairs={{0,1},{1,0},{2,3},{3,2},{4,5},{5,4},{6,7},{7,6},{8,9},{9,8},{10,11... | collective-permute-start | bytes 1572872 | tf_op jit(solution)/shard_map/ppermute | solution.py:58
  404.2 23.5 %collective-permute-start.41 = (bf16[128,2048]{1,0:T(8,128)(2,1)}, bf16[128,2048]{1,0:T(8,128)(2,1)}, u32[]{:S(2)}, u32[]{:S(2)}) collective-permute-start(bf16[128,2048]{1,0:T(8,128)(2,1)} %add_convert_fusion.3), channel_id=1, source_target_pairs={{0,2},{1,3},{2,0},{3,1},{4,6},{5,7},{6,4},{7,5},{8,10},{9,11},{10,... | collective-permute-start | bytes 1572872 | tf_op jit(solution)/shard_map/ppermute | solution.py:58
  405.6 9.2 %collective-permute-start.42 = (f32[12,64]{1,0:T(8,128)S(1)}, f32[12,64]{1,0:T(8,128)S(1)}, u32[]{:S(2)}, u32[]{:S(2)}) collective-permute-start(f32[12,64]{1,0:T(8,128)S(1)} %bitcast.199), channel_id=1, source_target_pairs={{0,4},{4,0},{1,5},{5,1},{2,6},{6,2},{3,7},{7,3},{8,12},{12,8},{9,1... | collective-permute-start | bytes 9224 | tf_op jit(solution)/shard_map/ppermute | solution.py:58
  413.1 15.1 %copy-start.21 = (f32[128,2048]{1,0:T(8,128)S(1)}, f32[128,2048]{1,0:T(8,128)}, u32[]{:S(2)}) copy-start(f32[128,2048]{1,0:T(8,128)} %get-tuple-element.425) | copy-start | bytes 3145732
  (27 other events, 107.9 us)
Sparse Core Ops, SparseCore 0:
  80.2 33.5 all-gather.3
  116.0 34.6 all-gather.5
  186.7 39.4 all-gather.7
  275.6 42.9 reduce-scatter.2
  328.2 42.8 reduce-scatter.4

commit v4 on v3

--- a/solution.py
+++ b/solution.py
@@ -584,19 +584,24 @@
     x_near = gather_start(x_own)
     x_side = gather_axis(x_own, "bl")
     g_side = gather_axis(g_own, "bl")
-    x_near, x_side, g_side, heads_own = join(x_near, x_side, g_side, heads_own)
+    x_near, x_side, g_side, heads_own, up_own, down_own = join(
+        x_near, x_side, g_side, heads_own, up_own, down_own
+    )
     m_heads = lax.all_to_all(heads_own, TP, split_axis=0, concat_axis=0, tiled=True)
-    x_rows = [x_side] + [gather_axis(block, "bl") for block in x_near[:2]]
+    x_rows = [x_side, gather_axis(x_near[0], "bl")]
+    x_second = x_near[1]
+    x_left = gather_axis(x_second[: sub_len // 2], "bl")[1:]
     x_near = gather_end(x_own, x_near)
     row = jnp.arange(group_len, dtype=jnp.int32)
     inside = ((row // sub_len) ^ t) * sub_len + row % sub_len
     query_places = bh * group_len + inside
     tables = rotary_tables(query_places.astype(f32))
-    x_near, x_rows, m_heads, up_own, g_late, tables, down_own = join(
-        x_near, x_rows, m_heads, up_own, g_own, tables, down_own
-    )
+    x_near, x_rows, x_left, m_heads, up_own, g_late, tables, down_own, x_second = join(
+        x_near, x_rows, x_left, m_heads, up_own, g_own, tables, down_own, x_second
+    )
+    x_right = gather_axis(x_second[sub_len // 2 :], "bl")[1:]
     w_heads = spread_rest(m_heads[:, :rows].reshape(tp * rows, -1))
-    x_rows += [gather_axis(block, "bl") for block in x_near[3:]]
+    x_rows += [None] + [gather_axis(block, "bl") for block in x_near[3:]]
     g_first = swap(g_late, "hd", 1)
     m_up = spread_group(up_own)
     smalls = gather_rest(m_heads[:, rows, :count]).reshape(n_dev, kinds, rows).astype(f32)
@@ -607,9 +612,12 @@
     b_qkv = lax.dynamic_index_in_dim(b_qkv, t, 1, keepdims=False).reshape(1, 3 * HS)
     b_up = lax.dynamic_index_in_dim(b_up, t, 0, keepdims=True)
 
-    x_rows, g_first, m_up, g_late, down_own, vectors, b_qkv, b_up = join(
-        x_rows, g_first, m_up, g_late, down_own, vectors, b_qkv, b_up
-    )
+    x_rows, x_right, g_first, m_up, g_late, down_own, vectors, b_qkv, b_up = join(
+        x_rows, x_right, g_first, m_up, g_late, down_own, vectors, b_qkv, b_up
+    )
+    x_rows[2] = [x_second] + [
+        jnp.concatenate(halves, axis=0) for halves in zip(x_left, x_right)
+    ]
     w_up = spread_rest(m_up)
     x_blocks = [row[far] for far in range(bl_size) for row in x_rows]
     g_rows = [g_side, gather_axis(g_first, "bl")]

time: 445 us -> 441 us (level)
  waiting for transfers between devices: 171 us -> 163 us
    ppermute x43 -> x44, waiting for transfers between devices: 161 us -> 154 us  [swap(): return lax.ppermute(value, axis, [(i, i ^ distance) for i in range(size)])]
    ppermute x43 -> x44, starting transfers between devices: 52.3 us -> 52.9 us  [swap(): return lax.ppermute(value, axis, [(i, i ^ distance) for i in range(size)])]
  transfers between devices with their start and end apart: 54 -> 55, of which waited for: 28 -> 27; matrix products, arithmetic and copies ran while one was open for 10% -> 10% of each run, Pallas kernels for 27% -> 27%
where the time goes in v4:
time: 441 us; the launch traced here: 436 us
  waiting for transfers between devices  163 us (37%)
  Pallas kernels  118 us (27%)
  starting transfers between devices  82.1 us (19%)
  local copies, waits for them, and re-layouts  31.5 us (7%)
  other arithmetic  25.8 us (6%)
  between operations  14.8 us (3%)
    ppermute x44, waiting for transfers between devices, swap(): return lax.ppermute(value, axis, [(i, i ^ distance) for i in range(size)])  154 us
    pallas_call x11, Pallas kernels, call(): pl.pallas_call(kernel, grid=grid, out_shape=[jax.ShapeDtypeStruct(shape,...  104 us
    ppermute x44, starting transfers between devices, swap(): return lax.ppermute(value, axis, [(i, i ^ distance) for i in range(size)])  52.9 us
    all_to_all x3, starting transfers between devices, collect_group(): return lax.all_to_all(mine, TP, split_axis=0, concat_axis=0, tiled=True)  15.1 us
    pallas_call x2, Pallas kernels, weight_half(): pl.pallas_call(functools.partial(weight_half_kernel, per), grid_spec=pltp...  14.3 us
    convert_element_type x8, other arithmetic, add(): sum((x.astype(f32) for x in arrays[1:]), arrays[0].astype(f32))  12 us
    all_to_all x2, starting transfers between devices, spread_group(): mine = lax.all_to_all(shard, TP, split_axis=0, concat_axis=0, tiled=True)  10.2 us
  transfers between devices with their start and end apart: 55, of which 27 were waited for; matrix products, arithmetic and copies ran while one was open for 10% of the time, Pallas kernels for 27%

profile of v4, /device:TPU:0, one launch (start us, length us, event | category | flops | bytes accessed | tf_op | source)
XLA Modules:
  0.0 435.9 jit_solution(10739056539508156020)
XLA Ops:
  7.2 3.1 collective-permute-start
  10.3 2.6 collective-permute-start.1
  24.3 9.2 %collective-permute-done.refs_1_ = bf16[128,2048]{1,0:T(8,128)(2,1)S(1)} collective-permute-done((bf16[128,2048]{1,0:T(8,128)(2,1)}, bf16[128,2048]{1,0:T(8,128)(2,1)S(1)}, u32[]{:S(2)}, u32[]{:S(2)}) %collective-permute-start) | collective-permute-done | bytes 524320 | tf_op jit(solution)/shard_map/ppermute | solution.py:58
  33.5 2.5 collective-permute-done.1.refs_2_
  37.5 3.6 all-to-all-start
  41.2 1.9 collective-permute-start.4
  44.6 1.9 multiply_sine_fusion
  49.7 22.0 %collective-permute-done.6 = bf16[64,2048]{1,0:T(8,128)(2,1)S(1)} collective-permute-done((bf16[64,2048]{1,0:T(8,128)(2,1)S(1)}, bf16[64,2048]{1,0:T(8,128)(2,1)S(1)}, u32[]{:S(2)}, u32[]{:S(2)}) %collective-permute-start.6) | collective-permute-done | bytes 262176 | tf_op jit(solution)/shard_map/ppermute | solution.py:58
  74.2 4.8 %all-to-all-start.1 = ((bf16[8,64,1024]{2,1,0:T(8,128)(2,1)}), bf16[8,64,1024]{2,1,0:T(8,128)(2,1)}, u32[]{:S(2)}, u32[]{:S(2)}) async-start(bf16[8,64,1024]{2,1,0:T(8,128)(2,1)} %get-tuple-element.241), calls=%async_computation.1 | async-start | bytes 2097152 | tf_op jit(solution)/shard_map/all_to_all | solution.py:101
  81.5 2.0 collective-permute-start.7
  83.6 2.0 collective-permute-start.9
  88.4 21.2 %collective-permute-done.8 = bf16[64,2048]{1,0:T(8,128)(2,1)S(1)} collective-permute-done((bf16[64,2048]{1,0:T(8,128)(2,1)S(1)}, bf16[64,2048]{1,0:T(8,128)(2,1)S(1)}, u32[]{:S(2)}, u32[]{:S(2)}) %collective-permute-start.8) | collective-permute-done | bytes 262176 | tf_op jit(solution)/shard_map/ppermute | solution.py:58
  111.2 2.4 collective-permute-start.14
  115.4 13.4 %shard_map.228 = (bf16[1024,2048]{1,0:T(8,128)(2,1)}, bf16[1024,2048]{1,0:T(8,128)(2,1)}, bf16[1024,256]{1,0:T(8,128)(2,1)}, bf16[1024,512]{1,0:T(8,128)(2,1)}, f32[1024,1]{1,0:T(8,128)}, /*index=5*/f32[1024,1]{1,0:T(8,128)}) custom-call(bf16[128,2048]{1,0:T(8,128)(2,1)} %bitcast.145, bf16[128,2048]{1,0:T(8,128)(2,1)} %copy-done.6, ...), custom_call_target="tpu_custom_call" | custom-call | flops 1 | bytes 1 | tf_op jit(solution)/shard_map/pallas_call | solution.py:124
  128.9 7.6 %collective-permute-done.14.refs_2_ = bf16[128,2048]{1,0:T(8,128)(2,1)} collective-permute-done((bf16[128,2048]{1,0:T(8,128)(2,1)S(1)}, bf16[128,2048]{1,0:T(8,128)(2,1)}, u32[]{:S(2)}, u32[]{:S(2)}) %collective-permute-start.14) | collective-permute-done | bytes 524320 | tf_op jit(solution)/shard_map/ppermute | solution.py:58
  136.4 1.6 collective-permute-start.15
  138.2 11.3 %collective-permute-done.15.refs_6_ = bf16[128,2048]{1,0:T(8,128)(2,1)S(1)} collective-permute-done((bf16[128,2048]{1,0:T(8,128)(2,1)}, bf16[128,2048]{1,0:T(8,128)(2,1)S(1)}, u32[]{:S(2)}, u32[]{:S(2)}) %collective-permute-start.15) | collective-permute-done | bytes 524320 | tf_op jit(solution)/shard_map/ppermute | solution.py:58
  151.0 5.4 %all-to-all-start.2 = ((bf16[8,64,1024]{2,1,0:T(8,128)(2,1)}), bf16[8,64,1024]{2,1,0:T(8,128)(2,1)S(1)}, u32[]{:S(2)}, u32[]{:S(2)}) async-start(bf16[8,64,1024]{2,1,0:T(8,128)(2,1)} %get-tuple-element.285), calls=%async_computation.2 | async-start | bytes 2097152 | tf_op jit(solution)/shard_map/all_to_all | solution.py:101
  156.5 1.6 collective-permute-start.18
  158.1 2.0 collective-permute-start.17
  160.1 11.9 %shard_map.229 = (bf16[1024,1024]{1,0:T(8,128)(2,1)}, f32[1024,1024]{1,0:T(8,128)}) custom-call(bf16[1024,2048]{1,0:T(8,128)(2,1)} %get-tuple-element.286.mlp_ref.refs_0_, bf16[2048,1024]{1,0:T(8,128)(2,1)} %all-gather.6.cloned.1.call-done.w_ref.refs_13_, f32[1,1024]{1,0:T(1,128)} %constant_dynamic-slice_fusion.10.b_ref), custom_call_target="tpu_custom_call" | custom-call | flops 1 | bytes 1 | tf_op jit(solution)/shard_map/pallas_call | solution.py:124
  172.0 8.1 %collective-permute-done.18.refs_1_ = bf16[1024,512]{1,0:T(8,128)(2,1)S(1)} collective-permute-done((bf16[1024,512]{1,0:T(8,128)(2,1)S(1)}, bf16[1024,512]{1,0:T(8,128)(2,1)S(1)}, u32[]{:S(2)}, u32[]{:S(2)}) %collective-permute-start.18) | collective-permute-done | bytes 1048608 | tf_op jit(solution)/shard_map/ppermute | solution.py:58
  180.2 1.9 all-to-all-done.2
  183.6 6.3 %shard_map.230 = (bf16[1024,2048]{1,0:T(8,128)(2,1)}, bf16[1024,256]{1,0:T(8,128)(2,1)}) custom-call(bf16[128,2048]{1,0:T(8,128)(2,1)} %bitcast.150, bf16[128,2048]{1,0:T(8,128)(2,1)} %copy-done.23, bf16[128,2048]{1,0:T(8,128)(2,1)} %collective-permute-done.14.refs_2_, bf16[128,2048]{1,0:T(8,128)(2,1)} %collective-permute-done.16.refs_3_, ...), custom_call_target="tpu_custom_call" | custom-call | flops 1 | bytes 1 | tf_op jit(solution)/shard_map/pallas_call | solution.py:124
  189.9 7.3 %shard_map.231 = (bf16[512,1024]{1,0:T(8,128)(2,1)}, bf16[512,1024]{1,0:T(8,128)(2,1)}) custom-call(s32[2]{0:T(128)} %get-tuple-element.471.place_ref, bf16[1024,2048]{1,0:T(8,128)(2,1)} %get-tuple-element.307.lhs_ref.g_ref.refs_2_, bf16[1024,1024]{1,0:T(8,128)(2,1)} %get-tuple-element.301.rhs_ref.act_ref), custom_call_target="tpu_custom_call" | custom-call | flops 1 | bytes 1 | tf_op jit(solution)/shard_map/pallas_call | solution.py:302
  198.4 6.9 %shard_map.232 = (bf16[512,1024]{1,0:T(8,128)(2,1)}, bf16[512,1024]{1,0:T(8,128)(2,1)}) custom-call(s32[2]{0:T(128)} %pad_add_fusion.2.place_ref, bf16[1024,2048]{1,0:T(8,128)(2,1)} %get-tuple-element.307.lhs_ref.g_ref.refs_2_, bf16[1024,1024]{1,0:T(8,128)(2,1)} %get-tuple-element.301.rhs_ref.act_ref), custom_call_target="tpu_custom_call" | custom-call | flops 1 | bytes 1 | tf_op jit(solution)/shard_map/pallas_call | solution.py:302
  205.3 1.6 add_convert_fusion.1
  208.5 12.7 %shard_map.233 = (bf16[1024,256]{1,0:T(8,128)(2,1)}, bf16[1024,256]{1,0:T(8,128)(2,1)}, bf16[1024,512]{1,0:T(8,128)(2,1)}, bf16[1024,512]{1,0:T(8,128)(2,1)}) custom-call(s32[2]{0:T(128)} %get-tuple-element.470.place_ref, bf16[1024,256]{1,0:T(8,128)(2,1)} %get-tuple-element.259.q_ref, bf16[1024,256]{1,0:T(8,128)(2,1)} %get-tuple-element.314.g_ref, ...), custom_call_target="tpu_custom_call" | custom-call | flops 1 | bytes 1 | tf_op jit(solution)/shard_map/pallas_call | solution.py:124
  222.7 6.2 %shard_map.234 = (bf16[128,2048]{1,0:T(8,128)(2,1)}, bf16[128,2048]{1,0:T(8,128)(2,1)}, bf16[128,2048]{1,0:T(8,128)(2,1)}, bf16[128,2048]{1,0:T(8,128)(2,1)}) custom-call(bf16[1024,256]{1,0:T(8,128)(2,1)} %get-tuple-element.375.att_ref.refs_3_, bf16[1024,1024]{1,0:T(8,128)(2,1)} %get-tuple-element.301.rhs_ref.act_ref, ...), custom_call_target="tpu_custom_call" | custom-call | flops 1 | bytes 1 | tf_op jit(solution)/shard_map/pallas_call | solution.py:124
  228.9 6.9 %shard_map.235 = (f32[128,2048]{1,0:T(8,128)}, f32[128,2048]{1,0:T(8,128)}, f32[128,2048]{1,0:T(8,128)}, f32[128,2048]{1,0:T(8,128)}) custom-call(bf16[1024,256]{1,0:T(8,128)(2,1)} %get-tuple-element.375.att_ref.refs_3_, bf16[1024,1024]{1,0:T(8,128)(2,1)} %get-tuple-element.301.rhs_ref.act_ref, ...), custom_call_target="tpu_custom_call" | custom-call | flops 1 | bytes 1 | tf_op jit(solution)/shard_map/pallas_call | solution.py:124
  235.8 2.1 collective-permute-done.21
  237.9 1.6 add_convert_fusion
  239.5 5.5 %all-to-all-start.3 = ((bf16[8,64,1024]{2,1,0:T(8,128)(2,1)}), bf16[8,64,1024]{2,1,0:T(8,128)(2,1)S(1)}, u32[]{:S(2)}, u32[]{:S(2)}) async-start(bf16[8,64,1024]{2,1,0:T(8,128)(2,1)} %bitcast.26), calls=%async_computation.3 | async-start | bytes 2097152 | tf_op jit(solution)/shard_map/all_to_all | solution.py:115
  245.6 1.9 collective-permute-start.23
  247.6 9.3 %shard_map.236 = (bf16[1024,1024]{1,0:T(8,128)(2,1)}, f32[1,1024]{1,0:T(1,128)}) custom-call(bf16[1024,2048]{1,0:T(8,128)(2,1)} %get-tuple-element.307.lhs_ref.g_ref.refs_2_, bf16[2048,1024]{1,0:T(8,128)(2,1)} %all-gather.8.cloned.1.call-done.down_ref.w_ref, f32[1024,1024]{1,0:T(8,128)} %get-tuple-element.340.slope_ref), custom_call_target="tpu_custom_call" | custom-call | flops 1 | bytes 1 | tf_op jit(solution)/shard_map/pallas_call | solution.py:124
  256.9 8.5 %shard_map.237 = bf16[2048,1024]{1,0:T(8,128)(2,1)} custom-call(bf16[1024,2048]{1,0:T(8,128)(2,1)} %get-tuple-element.286.mlp_ref.refs_0_, bf16[1024,1024]{1,0:T(8,128)(2,1)} %get-tuple-element.349.refs_1_.refs_11_), custom_call_target="tpu_custom_call" | custom-call | flops 1 | bytes 1 | tf_op jit(solution)/shard_map/pallas_call | solution.py:124
  265.4 4.8 %collective-permute-done.22.refs_2_ = bf16[1024,512]{1,0:T(8,128)(2,1)S(1)} collective-permute-done((bf16[1024,512]{1,0:T(8,128)(2,1)}, bf16[1024,512]{1,0:T(8,128)(2,1)S(1)}, u32[]{:S(2)}, u32[]{:S(2)}) %collective-permute-start.22) | collective-permute-done | bytes 1048608 | tf_op jit(solution)/shard_map/ppermute | solution.py:58
  270.2 1.7 all-to-all-done.3
  276.2 4.5 %shard_map.238 = (bf16[1024,768]{1,0:T(8,128)(2,1)}, f32[1,768]{1,0:T(1,128)}) custom-call(bf16[1024,256]{1,0:T(8,128)(2,1)} %get-tuple-element.317.refs_0_, bf16[1024,512]{1,0:T(8,128)(2,1)} %get-tuple-element.318.refs_1_, bf16[1024,512]{1,0:T(8,128)(2,1)} %copy-done.21, f32[1024,128]{1,0:T(8,128)} %maximum_maximum_fusion.refs_11_.refs_3_, ...), custom_call_target="tpu_custom_call" | custom-call | flops 1 | bytes 1 | tf_op jit(solution)/shard_map/pallas_call | solution.py:124
  280.7 15.2 %shard_map.239 = (f32[128,2048]{1,0:T(8,128)}, f32[128,2048]{1,0:T(8,128)}, f32[128,2048]{1,0:T(8,128)}, f32[128,2048]{1,0:T(8,128)}, bf16[128,2048]{1,0:T(8,128...) custom-call(bf16[128,2048]{1,0:T(8,128)(2,1)} %bitcast.146, ...), custom_call_target="tpu_custom_call" | custom-call | flops 1 | bytes 1 | tf_op jit(solution)/shard_map/pallas_call | solution.py:124
  295.9 1.8 collective-permute-done.26
  304.5 9.2 %shard_map.240 = bf16[2048,1024]{1,0:T(8,128)(2,1)} custom-call(bf16[1024,2048]{1,0:T(8,128)(2,1)} %get-tuple-element.373.refs_0_, bf16[1024,768]{1,0:T(8,128)(2,1)} %get-tuple-element.374.refs_10_.refs_1_, bf16[1024,2048]{1,0:T(8,128)(2,1)} %get-tuple-element.307.lhs_ref.g_ref.refs_2_, bf16[1024,256]{1,0:T(8,128)(2,1)} %get-tuple-element.375.att_ref.refs_3_), custom_call_target="tpu_custom_call" | custom-call | flops 1 | bytes 1 | tf_op jit(solution)/shard_map/pallas_call | solution.py:124
  313.7 8.1 %collective-permute-done.27 = bf16[128,2048]{1,0:T(8,128)(2,1)} collective-permute-done((bf16[128,2048]{1,0:T(8,128)(2,1)}, bf16[128,2048]{1,0:T(8,128)(2,1)}, u32[]{:S(2)}, u32[]{:S(2)}) %collective-permute-start.27) | collective-permute-done | bytes 524320 | tf_op jit(solution)/shard_map/ppermute | solution.py:58
  321.9 2.6 collective-permute-done.30
  324.5 2.0 add_convert_fusion.4
  326.5 3.9 all-to-all-start.4
  331.4 2.1 collective-permute-start.31
  337.5 2.2 collective-permute-done.34
  339.8 2.7 fusion.7
  343.3 13.9 %collective-permute-done.31 = bf16[128,2048]{1,0:T(8,128)(2,1)S(1)} collective-permute-done((bf16[128,2048]{1,0:T(8,128)(2,1)}, bf16[128,2048]{1,0:T(8,128)(2,1)S(1)}, u32[]{:S(2)}, u32[]{:S(2)}) %collective-permute-start.31) | collective-permute-done | bytes 524320 | tf_op jit(solution)/shard_map/ppermute | solution.py:58
  358.8 5.1 %collective-permute-done.33 = bf16[128,2048]{1,0:T(8,128)(2,1)} collective-permute-done((bf16[128,2048]{1,0:T(8,128)(2,1)}, bf16[128,2048]{1,0:T(8,128)(2,1)}, u32[]{:S(2)}, u32[]{:S(2)}) %collective-permute-start.33) | collective-permute-done | bytes 524320 | tf_op jit(solution)/shard_map/ppermute | solution.py:58
  363.9 3.7 reduce-scatter.5.cloned.1.call-done
  367.5 5.7 %all-to-all-start.5 = ((bf16[8,64,1024]{2,1,0:T(8,128)(2,1)}), bf16[8,64,1024]{2,1,0:T(8,128)(2,1)S(1)}, u32[]{:S(2)}, u32[]{:S(2)}) async-start(bf16[8,64,1024]{2,1,0:T(8,128)(2,1)} %bitcast.162), calls=%async_computation.7 | async-start | bytes 2097152 | tf_op jit(solution)/shard_map/all_to_all | solution.py:115
  373.3 2.4 add_convert_fusion.2
  375.8 2.0 add_convert_fusion.3
  377.8 2.0 collective-permute-start.37
  381.4 2.4 collective-permute-start.39
  386.1 4.7 %collective-permute-done.38 = f32[2,12,64]{2,0,1:T(2,128)S(1)} collective-permute-done((f32[2,12,64]{2,0,1:T(2,128)S(1)}, f32[2,12,64]{2,0,1:T(2,128)S(1)}, u32[]{:S(2)}, u32[]{:S(2)}) %collective-permute-start.38) | collective-permute-done | bytes 6176 | tf_op jit(solution)/shard_map/ppermute | solution.py:58
  390.8 9.0 %collective-permute-done.39 = f32[2,12,64]{2,0,1:T(2,128)S(1)} collective-permute-done((f32[2,12,64]{2,0,1:T(2,128)S(1)}, f32[2,12,64]{2,0,1:T(2,128)S(1)}, u32[]{:S(2)}, u32[]{:S(2)}) %collective-permute-start.39) | collective-permute-done | bytes 6176 | tf_op jit(solution)/shard_map/ppermute | solution.py:58
  402.0 1.6 collective-permute-start.43
  406.0 2.6 reshape.275
  409.5 1.6 copy.76
  411.1 12.9 %collective-permute-done.41 = bf16[128,2048]{1,0:T(8,128)(2,1)} collective-permute-done((bf16[128,2048]{1,0:T(8,128)(2,1)}, bf16[128,2048]{1,0:T(8,128)(2,1)}, u32[]{:S(2)}, u32[]{:S(2)}) %collective-permute-start.41) | collective-permute-done | bytes 524320 | tf_op jit(solution)/shard_map/ppermute | solution.py:58
  424.6 1.9 fusion.24
  (248 shorter events, 67.8 us)
Async XLA Ops:
  7.2 26.3 %collective-permute-start = (bf16[128,2048]{1,0:T(8,128)(2,1)}, bf16[128,2048]{1,0:T(8,128)(2,1)S(1)}, u32[]{:S(2)}, u32[]{:S(2)}) collective-permute-start(bf16[128,2048]{1,0:T(8,128)(2,1)} %bitcast.142), channel_id=1, source_target_pairs={{0,1},{1,0},{2,3},{3,2},{4,5},{5,4},{6,7},{7,6},{8,9},{9,8},{10,11... | collective-permute-start | bytes 1572872 | tf_op jit(solution)/shard_map/ppermute | solution.py:58
  10.3 25.8 %collective-permute-start.1 = (bf16[128,2048]{1,0:T(8,128)(2,1)}, bf16[128,2048]{1,0:T(8,128)(2,1)S(1)}, u32[]{:S(2)}, u32[]{:S(2)}) collective-permute-start(bf16[128,2048]{1,0:T(8,128)(2,1)} %bitcast.143), channel_id=1, source_target_pairs={{0,2},{1,3},{2,0},{3,1},{4,6},{5,7},{6,4},{7,5},{8,10},{9,11},{10,... | collective-permute-start | bytes 1572872 | tf_op jit(solution)/shard_map/ppermute | solution.py:58
  12.9 23.2 %collective-permute-start.2 = (bf16[128,2048]{1,0:T(8,128)(2,1)}, bf16[128,2048]{1,0:T(8,128)(2,1)}, u32[]{:S(2)}, u32[]{:S(2)}) collective-permute-start(bf16[128,2048]{1,0:T(8,128)(2,1)} %bitcast.144), channel_id=1, source_target_pairs={{0,4},{4,0},{1,5},{5,1},{2,6},{6,2},{3,7},{7,3},{8,12},{12,8},{9,1... | collective-permute-start | bytes 1572872 | tf_op jit(solution)/shard_map/ppermute | solution.py:58
  14.3 23.2 %collective-permute-start.3 = (bf16[128,2048]{1,0:T(8,128)(2,1)}, bf16[128,2048]{1,0:T(8,128)(2,1)}, u32[]{:S(2)}, u32[]{:S(2)}) collective-permute-start(bf16[128,2048]{1,0:T(8,128)(2,1)} %bitcast.149), channel_id=1, source_target_pairs={{0,4},{4,0},{1,5},{5,1},{2,6},{6,2},{3,7},{7,3},{8,12},{12,8},{9,1... | collective-permute-start | bytes 1572872 | tf_op jit(solution)/shard_map/ppermute | solution.py:58
  33.5 13.1 %copy-start.6 = (bf16[128,2048]{1,0:T(8,128)(2,1)}, bf16[128,2048]{1,0:T(8,128)(2,1)S(1)}, u32[]{:S(2)}) copy-start(bf16[128,2048]{1,0:T(8,128)(2,1)S(1)} %collective-permute-done.refs_1_) | copy-start | bytes 1572868
  36.1 47.4 %copy-start.1 = (bf16[128,2048]{1,0:T(8,128)(2,1)}, bf16[128,2048]{1,0:T(8,128)(2,1)S(1)}, u32[]{:S(2)}) copy-start(bf16[128,2048]{1,0:T(8,128)(2,1)S(1)} %collective-permute-done.1.refs_2_) | copy-start | bytes 1572868
  37.5 34.9 %all-to-all-start = ((bf16[8,72,1024]{2,1,0:T(8,128)(2,1)}), bf16[8,72,1024]{2,1,0:T(8,128)(2,1)S(1)}, u32[]{:S(2)}, u32[]{:S(2)}) async-start(bf16[8,72,1024]{2,1,0:T(8,128)(2,1)} %pad_maximum_fusion), calls=%async_computation | async-start | bytes 2359296 | tf_op jit(solution)/shard_map/all_to_all | solution.py:590
  41.1 73.5 %all-gather.4.cloned.1.call-start = ((), (), s32[]{:S(2)}) async-start(), calls=%async_computation.8 | async-start | bytes 5242880 | tf_op jit(solution)/shard_map/all_gather | solution.py:106
  41.2 31.2 %collective-permute-start.4 = (bf16[128,2048]{1,0:T(8,128)(2,1)S(1)}, bf16[128,2048]{1,0:T(8,128)(2,1)S(1)}, u32[]{:S(2)}, u32[]{:S(2)}) collective-permute-start(bf16[128,2048]{1,0:T(8,128)(2,1)S(1)} %collective-permute-done.1.refs_2_), channel_id=1, source_target_pairs={{0,1},{1,0},{2,3},{3,2},{4,5},{5,4},{6,7},{7,6},{8,9},{9,8},{10,11... | collective-permute-start | bytes 1572872 | tf_op jit(solution)/shard_map/ppermute | solution.py:58
  43.1 29.3 %collective-permute-start.5 = (bf16[128,2048]{1,0:T(8,128)(2,1)S(1)}, bf16[128,2048]{1,0:T(8,128)(2,1)}, u32[]{:S(2)}, u32[]{:S(2)}) collective-permute-start(bf16[128,2048]{1,0:T(8,128)(2,1)S(1)} %collective-permute-done.refs_1_), channel_id=1, source_target_pairs={{0,4},{4,0},{1,5},{5,1},{2,6},{6,2},{3,7},{7,3},{8,12},{12,8},{9,1... | collective-permute-start | bytes 1572872 | tf_op jit(solution)/shard_map/ppermute | solution.py:58
  46.6 25.0 %collective-permute-start.6 = (bf16[64,2048]{1,0:T(8,128)(2,1)S(1)}, bf16[64,2048]{1,0:T(8,128)(2,1)S(1)}, u32[]{:S(2)}, u32[]{:S(2)}) collective-permute-start(bf16[64,2048]{1,0:T(8,128)(2,1)S(1)} %slice.63), channel_id=1, source_target_pairs={{0,4},{4,0},{1,5},{5,1},{2,6},{6,2},{3,7},{7,3},{8,12},{12,8},{9,1... | collective-permute-start | bytes 786440 | tf_op jit(solution)/shard_map/ppermute | solution.py:58
  74.2 35.4 %all-to-all-start.1 = ((bf16[8,64,1024]{2,1,0:T(8,128)(2,1)}), bf16[8,64,1024]{2,1,0:T(8,128)(2,1)}, u32[]{:S(2)}, u32[]{:S(2)}) async-start(bf16[8,64,1024]{2,1,0:T(8,128)(2,1)} %get-tuple-element.241), calls=%async_computation.1 | async-start | bytes 2097152 | tf_op jit(solution)/shard_map/all_to_all | solution.py:101
  79.0 81.1 %all-gather.6.cloned.1.call-start = ((), (), s32[]{:S(2)}) async-start(), calls=%async_computation.9 | async-start | bytes 5242880 | tf_op jit(solution)/shard_map/all_gather | solution.py:106
  79.3 4.3 collective-permute-start.12
  80.2 5.4 %collective-permute-start.11 = (bf16[8,768]{1,0:T(8,128)(2,1)S(1)}, bf16[8,768]{1,0:T(8,128)(2,1)S(1)}, u32[]{:S(2)}, u32[]{:S(2)}) collective-permute-start(bf16[8,768]{1,0:T(8,128)(2,1)S(1)} %bitcast.178), channel_id=1, source_target_pairs={{0,16},{8,24},{16,0},{24,8},{1,17},{9,25},{17,1},{25,9},{2,18},{10... | collective-permute-start | bytes 36872 | tf_op jit(solution)/shard_map/ppermute | solution.py:58
  81.0 4.6 %collective-permute-start.10 = (bf16[8,768]{1,0:T(8,128)(2,1)S(1)}, bf16[8,768]{1,0:T(8,128)(2,1)S(1)}, u32[]{:S(2)}, u32[]{:S(2)}) collective-permute-start(bf16[8,768]{1,0:T(8,128)(2,1)S(1)} %bitcast.179), channel_id=1, source_target_pairs={{0,8},{8,0},{16,24},{24,16},{1,9},{9,1},{17,25},{25,17},{2,10},{10... | collective-permute-start | bytes 36872 | tf_op jit(solution)/shard_map/ppermute | solution.py:58
  81.5 28.1 %collective-permute-start.7 = (bf16[128,2048]{1,0:T(8,128)(2,1)S(1)}, bf16[128,2048]{1,0:T(8,128)(2,1)S(1)}, u32[]{:S(2)}, u32[]{:S(2)}) collective-permute-start(bf16[128,2048]{1,0:T(8,128)(2,1)S(1)} %copy-done.8), channel_id=1, source_target_pairs={{0,4},{4,0},{1,5},{5,1},{2,6},{6,2},{3,7},{7,3},{8,12},{12,8},{9,1... | collective-permute-start | bytes 1572872 | tf_op jit(solution)/shard_map/ppermute | solution.py:58
  83.5 26.1 %collective-permute-start.8 = (bf16[64,2048]{1,0:T(8,128)(2,1)S(1)}, bf16[64,2048]{1,0:T(8,128)(2,1)S(1)}, u32[]{:S(2)}, u32[]{:S(2)}) collective-permute-start(bf16[64,2048]{1,0:T(8,128)(2,1)S(1)} %slice.64), channel_id=1, source_target_pairs={{0,4},{4,0},{1,5},{5,1},{2,6},{6,2},{3,7},{7,3},{8,12},{12,8},{9,1... | collective-permute-start | bytes 786440 | tf_op jit(solution)/shard_map/ppermute | solution.py:58
  83.6 26.0 %collective-permute-start.9 = (bf16[128,2048]{1,0:T(8,128)(2,1)S(1)}, bf16[128,2048]{1,0:T(8,128)(2,1)S(1)}, u32[]{:S(2)}, u32[]{:S(2)}) collective-permute-start(bf16[128,2048]{1,0:T(8,128)(2,1)S(1)} %bitcast.151), channel_id=1, source_target_pairs={{0,1},{1,0},{2,3},{3,2},{4,5},{5,4},{6,7},{7,6},{8,9},{9,8},{10,11... | collective-permute-start | bytes 1572872 | tf_op jit(solution)/shard_map/ppermute | solution.py:58
  109.6 19.2 %copy-start.23 = (bf16[128,2048]{1,0:T(8,128)(2,1)}, bf16[128,2048]{1,0:T(8,128)(2,1)S(1)}, u32[]{:S(2)}) copy-start(bf16[128,2048]{1,0:T(8,128)(2,1)S(1)} %collective-permute-done.9.refs_1_) | copy-start | bytes 1572868
  110.3 18.5 %collective-permute-start.13 = (bf16[128,2048]{1,0:T(8,128)(2,1)S(1)}, bf16[128,2048]{1,0:T(8,128)(2,1)S(1)}, u32[]{:S(2)}, u32[]{:S(2)}) collective-permute-start(bf16[128,2048]{1,0:T(8,128)(2,1)S(1)} %collective-permute-done.9.refs_1_), channel_id=1, source_target_pairs={{0,4},{4,0},{1,5},{5,1},{2,6},{6,2},{3,7},{7,3},{8,12},{12,8},{9,1... | collective-permute-start | bytes 1572872 | tf_op jit(solution)/shard_map/ppermute | solution.py:58
  111.2 25.2 %collective-permute-start.14 = (bf16[128,2048]{1,0:T(8,128)(2,1)S(1)}, bf16[128,2048]{1,0:T(8,128)(2,1)}, u32[]{:S(2)}, u32[]{:S(2)}) collective-permute-start(bf16[128,2048]{1,0:T(8,128)(2,1)S(1)} %bitcast.152), channel_id=1, source_target_pairs={{0,2},{1,3},{2,0},{3,1},{4,6},{5,7},{6,4},{7,5},{8,10},{9,11},{10,... | collective-permute-start | bytes 1572872 | tf_op jit(solution)/shard_map/ppermute | solution.py:58
  128.8 27.7 %copy-start.11 = (bf16[1024,512]{1,0:T(8,128)(2,1)S(1)}, bf16[1024,512]{1,0:T(8,128)(2,1)}, u32[]{:S(2)}) copy-start(bf16[1024,512]{1,0:T(8,128)(2,1)} %get-tuple-element.315.refs_0_) | copy-start | bytes 3145732
  128.8 27.6 %copy-start.26 = (bf16[128,2048]{1,0:T(8,128)(2,1)}, bf16[128,2048]{1,0:T(8,128)(2,1)S(1)}, u32[]{:S(2)}) copy-start(bf16[128,2048]{1,0:T(8,128)(2,1)S(1)} %collective-permute-done.13.refs_5_) | copy-start | bytes 1572868
  136.4 13.1 %collective-permute-start.15 = (bf16[128,2048]{1,0:T(8,128)(2,1)}, bf16[128,2048]{1,0:T(8,128)(2,1)S(1)}, u32[]{:S(2)}, u32[]{:S(2)}) collective-permute-start(bf16[128,2048]{1,0:T(8,128)(2,1)} %collective-permute-done.14.refs_2_), channel_id=1, source_target_pairs={{0,4},{4,0},{1,5},{5,1},{2,6},{6,2},{3,7},{7,3},{8,12},{12,8},{9,1... | collective-permute-start | bytes 1572872 | tf_op jit(solution)/shard_map/ppermute | solution.py:58
  138.0 13.0 %collective-permute-start.16 = (bf16[128,2048]{1,0:T(8,128)(2,1)}, bf16[128,2048]{1,0:T(8,128)(2,1)}, u32[]{:S(2)}, u32[]{:S(2)}) collective-permute-start(bf16[128,2048]{1,0:T(8,128)(2,1)} %collective-permute-done.14.refs_2_), channel_id=1, source_target_pairs={{0,1},{1,0},{2,3},{3,2},{4,5},{5,4},{6,7},{7,6},{8,9},{9,8},{10,11... | collective-permute-start | bytes 1572872 | tf_op jit(solution)/shard_map/ppermute | solution.py:58
  151.0 31.1 %all-to-all-start.2 = ((bf16[8,64,1024]{2,1,0:T(8,128)(2,1)}), bf16[8,64,1024]{2,1,0:T(8,128)(2,1)S(1)}, u32[]{:S(2)}, u32[]{:S(2)}) async-start(bf16[8,64,1024]{2,1,0:T(8,128)(2,1)} %get-tuple-element.285), calls=%async_computation.2 | async-start | bytes 2097152 | tf_op jit(solution)/shard_map/all_to_all | solution.py:101
  156.4 66.3 %all-gather.8.cloned.1.call-start = ((), (), s32[]{:S(2)}) async-start(), calls=%async_computation.10 | async-start | bytes 5242880 | tf_op jit(solution)/shard_map/all_gather | solution.py:106
  156.5 23.7 %collective-permute-start.18 = (bf16[1024,512]{1,0:T(8,128)(2,1)S(1)}, bf16[1024,512]{1,0:T(8,128)(2,1)S(1)}, u32[]{:S(2)}, u32[]{:S(2)}) collective-permute-start(bf16[1024,512]{1,0:T(8,128)(2,1)S(1)} %copy-done.11), channel_id=1, source_target_pairs={{0,8},{8,0},{1,9},{9,1},{2,10},{10,2},{3,11},{11,3},{4,12},{12,4},... | collective-permute-start | bytes 3145736 | tf_op jit(solution)/shard_map/ppermute | solution.py:58
  158.1 22.1 %collective-permute-start.17 = (bf16[128,2048]{1,0:T(8,128)(2,1)}, bf16[128,2048]{1,0:T(8,128)(2,1)}, u32[]{:S(2)}, u32[]{:S(2)}) collective-permute-start(bf16[128,2048]{1,0:T(8,128)(2,1)} %collective-permute-done.16.refs_3_), channel_id=1, source_target_pairs={{0,4},{4,0},{1,5},{5,1},{2,6},{6,2},{3,7},{7,3},{8,12},{12,8},{9,1... | collective-permute-start | bytes 1572872 | tf_op jit(solution)/shard_map/ppermute | solution.py:58
  180.2 17.1 %copy-start.15 = (bf16[1024,512]{1,0:T(8,128)(2,1)}, bf16[1024,512]{1,0:T(8,128)(2,1)S(1)}, u32[]{:S(2)}) copy-start(bf16[1024,512]{1,0:T(8,128)(2,1)S(1)} %collective-permute-done.18.refs_1_) | copy-start | bytes 3145732
  197.3 8.0 %collective-permute-start.19 = (bf16[512,1024]{1,0:T(8,128)(2,1)}, bf16[512,1024]{1,0:T(8,128)(2,1)S(1)}, u32[]{:S(2)}, u32[]{:S(2)}) collective-permute-start(bf16[512,1024]{1,0:T(8,128)(2,1)} %get-tuple-element.305), channel_id=1, source_target_pairs={{0,16},{16,0},{1,17},{17,1},{2,18},{18,2},{3,19},{19,3},{4,20},{20... | collective-permute-start | bytes 3145736 | tf_op jit(solution)/shard_map/ppermute | solution.py:58
  197.3 8.0 %collective-permute-start.20 = (bf16[512,1024]{1,0:T(8,128)(2,1)}, bf16[512,1024]{1,0:T(8,128)(2,1)S(1)}, u32[]{:S(2)}, u32[]{:S(2)}) collective-permute-start(bf16[512,1024]{1,0:T(8,128)(2,1)} %get-tuple-element.306), channel_id=1, source_target_pairs={{0,16},{16,0},{1,17},{17,1},{2,18},{18,2},{3,19},{19,3},{4,20},{20... | collective-permute-start | bytes 3145736 | tf_op jit(solution)/shard_map/ppermute | solution.py:58
  207.0 30.9 %collective-permute-start.21 = (bf16[512,1024]{1,0:T(8,128)(2,1)S(1)}, bf16[512,1024]{1,0:T(8,128)(2,1)S(1)}, u32[]{:S(2)}, u32[]{:S(2)}) collective-permute-start(bf16[512,1024]{1,0:T(8,128)(2,1)S(1)} %add_convert_fusion.1), channel_id=1, source_target_pairs={{0,8},{8,0},{1,9},{9,1},{2,10},{10,2},{3,11},{11,3},{4,12},{12,4},... | collective-permute-start | bytes 3145736 | tf_op jit(solution)/shard_map/ppermute | solution.py:58
  239.5 32.4 %all-to-all-start.3 = ((bf16[8,64,1024]{2,1,0:T(8,128)(2,1)}), bf16[8,64,1024]{2,1,0:T(8,128)(2,1)S(1)}, u32[]{:S(2)}, u32[]{:S(2)}) async-start(bf16[8,64,1024]{2,1,0:T(8,128)(2,1)} %bitcast.26), calls=%async_computation.3 | async-start | bytes 2097152 | tf_op jit(solution)/shard_map/all_to_all | solution.py:115
  245.0 79.5 %reduce-scatter.3.cloned.1.call-start = ((), (), s32[]{:S(2)}) async-start(), calls=%async_computation.11 | async-start | bytes 5242880 | tf_op jit(solution)/shard_map/reduce_scatter | solution.py:110
  245.0 25.2 %collective-permute-start.22 = (bf16[1024,512]{1,0:T(8,128)(2,1)}, bf16[1024,512]{1,0:T(8,128)(2,1)S(1)}, u32[]{:S(2)}, u32[]{:S(2)}) collective-permute-start(bf16[1024,512]{1,0:T(8,128)(2,1)} %get-tuple-element.332), channel_id=1, source_target_pairs={{0,8},{8,0},{1,9},{9,1},{2,10},{10,2},{3,11},{11,3},{4,12},{12,4},... | collective-permute-start | bytes 3145736 | tf_op jit(solution)/shard_map/ppermute | solution.py:58
  245.6 24.6 %collective-permute-start.23 = (bf16[128,2048]{1,0:T(8,128)(2,1)}, bf16[128,2048]{1,0:T(8,128)(2,1)}, u32[]{:S(2)}, u32[]{:S(2)}) collective-permute-start(bf16[128,2048]{1,0:T(8,128)(2,1)} %get-tuple-element.339), channel_id=1, source_target_pairs={{0,4},{4,0},{1,5},{5,1},{2,6},{6,2},{3,7},{7,3},{8,12},{12,8},{9,1... | collective-permute-start | bytes 1572872 | tf_op jit(solution)/shard_map/ppermute | solution.py:58
  271.9 95.6 %reduce-scatter.5.cloned.1.call-start = ((), (), s32[]{:S(2)}) async-start(), calls=%async_computation.12 | async-start | bytes 5242880 | tf_op jit(solution)/shard_map/reduce_scatter | solution.py:110
  273.2 22.6 %collective-permute-start.24 = (bf16[128,2048]{1,0:T(8,128)(2,1)S(1)}, bf16[128,2048]{1,0:T(8,128)(2,1)S(1)}, u32[]{:S(2)}, u32[]{:S(2)}) collective-permute-start(bf16[128,2048]{1,0:T(8,128)(2,1)S(1)} %add_convert_fusion.7), channel_id=1, source_target_pairs={{0,1},{1,0},{2,3},{3,2},{4,5},{5,4},{6,7},{7,6},{8,9},{9,8},{10,11... | collective-permute-start | bytes 1572872 | tf_op jit(solution)/shard_map/ppermute | solution.py:58
  274.1 21.7 %collective-permute-start.25 = (bf16[128,2048]{1,0:T(8,128)(2,1)S(1)}, bf16[128,2048]{1,0:T(8,128)(2,1)S(1)}, u32[]{:S(2)}, u32[]{:S(2)}) collective-permute-start(bf16[128,2048]{1,0:T(8,128)(2,1)S(1)} %copy-done.35), channel_id=1, source_target_pairs={{0,4},{4,0},{1,5},{5,1},{2,6},{6,2},{3,7},{7,3},{8,12},{12,8},{9,1... | collective-permute-start | bytes 1572872 | tf_op jit(solution)/shard_map/ppermute | solution.py:58
  275.6 22.1 %collective-permute-start.26 = (bf16[128,2048]{1,0:T(8,128)(2,1)S(1)}, bf16[128,2048]{1,0:T(8,128)(2,1)S(1)}, u32[]{:S(2)}, u32[]{:S(2)}) collective-permute-start(bf16[128,2048]{1,0:T(8,128)(2,1)S(1)} %copy-done.34), channel_id=1, source_target_pairs={{0,4},{4,0},{1,5},{5,1},{2,6},{6,2},{3,7},{7,3},{8,12},{12,8},{9,1... | collective-permute-start | bytes 1572872 | tf_op jit(solution)/shard_map/ppermute | solution.py:58
  280.7 17.0 %copy-start.14 = (f32[128,2048]{1,0:T(8,128)S(1)}, f32[128,2048]{1,0:T(8,128)}, u32[]{:S(2)}) copy-start(f32[128,2048]{1,0:T(8,128)} %get-tuple-element.362) | copy-start | bytes 3145732
  298.8 23.1 %collective-permute-start.27 = (bf16[128,2048]{1,0:T(8,128)(2,1)}, bf16[128,2048]{1,0:T(8,128)(2,1)}, u32[]{:S(2)}, u32[]{:S(2)}) collective-permute-start(bf16[128,2048]{1,0:T(8,128)(2,1)} %add_convert_fusion.5), channel_id=1, source_target_pairs={{0,1},{1,0},{2,3},{3,2},{4,5},{5,4},{6,7},{7,6},{8,9},{9,8},{10,11... | collective-permute-start | bytes 1572872 | tf_op jit(solution)/shard_map/ppermute | solution.py:58
  300.3 21.6 %collective-permute-start.28 = (bf16[128,2048]{1,0:T(8,128)(2,1)S(1)}, bf16[128,2048]{1,0:T(8,128)(2,1)}, u32[]{:S(2)}, u32[]{:S(2)}) collective-permute-start(bf16[128,2048]{1,0:T(8,128)(2,1)S(1)} %add_convert_fusion.6), channel_id=1, source_target_pairs={{0,2},{1,3},{2,0},{3,1},{4,6},{5,7},{6,4},{7,5},{8,10},{9,11},{10,... | collective-permute-start | bytes 1572872 | tf_op jit(solution)/shard_map/ppermute | solution.py:58
  301.8 20.1 %collective-permute-start.29 = (bf16[128,2048]{1,0:T(8,128)(2,1)}, bf16[128,2048]{1,0:T(8,128)(2,1)}, u32[]{:S(2)}, u32[]{:S(2)}) collective-permute-start(bf16[128,2048]{1,0:T(8,128)(2,1)} %get-tuple-element.371), channel_id=1, source_target_pairs={{0,4},{4,0},{1,5},{5,1},{2,6},{6,2},{3,7},{7,3},{8,12},{12,8},{9,1... | collective-permute-start | bytes 1572872 | tf_op jit(solution)/shard_map/ppermute | solution.py:58
  303.2 21.2 %collective-permute-start.30 = (bf16[128,2048]{1,0:T(8,128)(2,1)}, bf16[128,2048]{1,0:T(8,128)(2,1)}, u32[]{:S(2)}, u32[]{:S(2)}) collective-permute-start(bf16[128,2048]{1,0:T(8,128)(2,1)} %get-tuple-element.372), channel_id=1, source_target_pairs={{0,4},{4,0},{1,5},{5,1},{2,6},{6,2},{3,7},{7,3},{8,12},{12,8},{9,1... | collective-permute-start | bytes 1572872 | tf_op jit(solution)/shard_map/ppermute | solution.py:58
  313.7 10.7 %copy-start.12 = (f32[128,2048]{1,0:T(8,128)S(1)}, f32[128,2048]{1,0:T(8,128)}, u32[]{:S(2)}) copy-start(f32[128,2048]{1,0:T(8,128)} %get-tuple-element.350) | copy-start | bytes 3145732
  326.5 37.4 %all-to-all-start.4 = ((bf16[8,64,1024]{2,1,0:T(8,128)(2,1)}), bf16[8,64,1024]{2,1,0:T(8,128)(2,1)S(1)}, u32[]{:S(2)}, u32[]{:S(2)}) async-start(bf16[8,64,1024]{2,1,0:T(8,128)(2,1)} %bitcast.161), calls=%async_computation.5 | async-start | bytes 2097152 | tf_op jit(solution)/shard_map/all_to_all | solution.py:115
  331.4 25.8 %collective-permute-start.31 = (bf16[128,2048]{1,0:T(8,128)(2,1)}, bf16[128,2048]{1,0:T(8,128)(2,1)S(1)}, u32[]{:S(2)}, u32[]{:S(2)}) collective-permute-start(bf16[128,2048]{1,0:T(8,128)(2,1)} %add_convert_fusion.4), channel_id=1, source_target_pairs={{0,1},{1,0},{2,3},{3,2},{4,5},{5,4},{6,7},{7,6},{8,9},{9,8},{10,11... | collective-permute-start | bytes 1572872 | tf_op jit(solution)/shard_map/ppermute | solution.py:58
  333.5 23.7 %collective-permute-start.32 = (bf16[128,2048]{1,0:T(8,128)(2,1)}, bf16[128,2048]{1,0:T(8,128)(2,1)S(1)}, u32[]{:S(2)}, u32[]{:S(2)}) collective-permute-start(bf16[128,2048]{1,0:T(8,128)(2,1)} %get-tuple-element.390), channel_id=1, source_target_pairs={{0,4},{4,0},{1,5},{5,1},{2,6},{6,2},{3,7},{7,3},{8,12},{12,8},{9,1... | collective-permute-start | bytes 1572872 | tf_op jit(solution)/shard_map/ppermute | solution.py:58
  335.0 28.9 %collective-permute-start.33 = (bf16[128,2048]{1,0:T(8,128)(2,1)}, bf16[128,2048]{1,0:T(8,128)(2,1)}, u32[]{:S(2)}, u32[]{:S(2)}) collective-permute-start(bf16[128,2048]{1,0:T(8,128)(2,1)} %get-tuple-element.391), channel_id=1, source_target_pairs={{0,4},{4,0},{1,5},{5,1},{2,6},{6,2},{3,7},{7,3},{8,12},{12,8},{9,1... | collective-permute-start | bytes 1572872 | tf_op jit(solution)/shard_map/ppermute | solution.py:58
  335.6 4.2 collective-permute-start.34
  337.4 5.1 %collective-permute-start.35 = (f32[2,4,12,64]{3,1,2,0:T(4,128)S(1)}, f32[2,4,12,64]{3,1,2,0:T(4,128)S(1)}, u32[]{:S(2)}, u32[]{:S(2)}) collective-permute-start(f32[2,4,12,64]{3,1,2,0:T(4,128)S(1)} %bitcast.174), channel_id=1, source_target_pairs={{0,16},{8,24},{16,0},{24,8},{1,17},{9,25},{17,1},{25,9},{2,18},{10... | collective-permute-start | bytes 73736 | tf_op jit(solution)/shard_map/ppermute | solution.py:58
  339.8 3.5 collective-permute-start.36
  367.5 33.1 %all-to-all-start.5 = ((bf16[8,64,1024]{2,1,0:T(8,128)(2,1)}), bf16[8,64,1024]{2,1,0:T(8,128)(2,1)S(1)}, u32[]{:S(2)}, u32[]{:S(2)}) async-start(bf16[8,64,1024]{2,1,0:T(8,128)(2,1)} %bitcast.162), calls=%async_computation.7 | async-start | bytes 2097152 | tf_op jit(solution)/shard_map/all_to_all | solution.py:115
  377.8 22.1 %collective-permute-start.37 = (bf16[128,2048]{1,0:T(8,128)(2,1)S(1)}, bf16[128,2048]{1,0:T(8,128)(2,1)}, u32[]{:S(2)}, u32[]{:S(2)}) collective-permute-start(bf16[128,2048]{1,0:T(8,128)(2,1)S(1)} %copy-done.33), channel_id=1, source_target_pairs={{0,4},{4,0},{1,5},{5,1},{2,6},{6,2},{3,7},{7,3},{8,12},{12,8},{9,1... | collective-permute-start | bytes 1572872 | tf_op jit(solution)/shard_map/ppermute | solution.py:58
  379.9 10.9 %collective-permute-start.38 = (f32[2,12,64]{2,0,1:T(2,128)S(1)}, f32[2,12,64]{2,0,1:T(2,128)S(1)}, u32[]{:S(2)}, u32[]{:S(2)}) collective-permute-start(f32[2,12,64]{2,0,1:T(2,128)S(1)} %bitcast.192), channel_id=1, source_target_pairs={{0,1},{1,0},{2,3},{3,2},{4,5},{5,4},{6,7},{7,6},{8,9},{9,8},{10,11... | collective-permute-start | bytes 18440 | tf_op jit(solution)/shard_map/ppermute | solution.py:58
  381.4 18.4 %collective-permute-start.39 = (f32[2,12,64]{2,0,1:T(2,128)S(1)}, f32[2,12,64]{2,0,1:T(2,128)S(1)}, u32[]{:S(2)}, u32[]{:S(2)}) collective-permute-start(f32[2,12,64]{2,0,1:T(2,128)S(1)} %bitcast.193), channel_id=1, source_target_pairs={{0,2},{1,3},{2,0},{3,1},{4,6},{5,7},{6,4},{7,5},{8,10},{9,11},{10,... | collective-permute-start | bytes 18440 | tf_op jit(solution)/shard_map/ppermute | solution.py:58
  383.8 16.0 %collective-permute-start.40 = (f32[2,12,64]{2,0,1:T(2,128)S(1)}, f32[2,12,64]{2,0,1:T(2,128)S(1)}, u32[]{:S(2)}, u32[]{:S(2)}) collective-permute-start(f32[2,12,64]{2,0,1:T(2,128)S(1)} %bitcast.194), channel_id=1, source_target_pairs={{0,3},{1,2},{2,1},{3,0},{4,7},{5,6},{6,5},{7,4},{8,11},{9,10},{10,... | collective-permute-start | bytes 18440 | tf_op jit(solution)/shard_map/ppermute | solution.py:58
  400.6 23.4 %collective-permute-start.41 = (bf16[128,2048]{1,0:T(8,128)(2,1)}, bf16[128,2048]{1,0:T(8,128)(2,1)}, u32[]{:S(2)}, u32[]{:S(2)}) collective-permute-start(bf16[128,2048]{1,0:T(8,128)(2,1)} %add_convert_fusion.2), channel_id=1, source_target_pairs={{0,1},{1,0},{2,3},{3,2},{4,5},{5,4},{6,7},{7,6},{8,9},{9,8},{10,11... | collective-permute-start | bytes 1572872 | tf_op jit(solution)/shard_map/ppermute | solution.py:58
  400.6 23.4 %collective-permute-start.42 = (bf16[128,2048]{1,0:T(8,128)(2,1)}, bf16[128,2048]{1,0:T(8,128)(2,1)}, u32[]{:S(2)}, u32[]{:S(2)}) collective-permute-start(bf16[128,2048]{1,0:T(8,128)(2,1)} %add_convert_fusion.3), channel_id=1, source_target_pairs={{0,2},{1,3},{2,0},{3,1},{4,6},{5,7},{6,4},{7,5},{8,10},{9,11},{10,... | collective-permute-start | bytes 1572872 | tf_op jit(solution)/shard_map/ppermute | solution.py:58
  402.0 9.2 %collective-permute-start.43 = (f32[12,64]{1,0:T(8,128)S(1)}, f32[12,64]{1,0:T(8,128)S(1)}, u32[]{:S(2)}, u32[]{:S(2)}) collective-permute-start(f32[12,64]{1,0:T(8,128)S(1)} %bitcast.198), channel_id=1, source_target_pairs={{0,4},{4,0},{1,5},{5,1},{2,6},{6,2},{3,7},{7,3},{8,12},{12,8},{9,1... | collective-permute-start | bytes 9224 | tf_op jit(solution)/shard_map/ppermute | solution.py:58
  409.5 15.1 %copy-start.19 = (f32[128,2048]{1,0:T(8,128)S(1)}, f32[128,2048]{1,0:T(8,128)}, u32[]{:S(2)}) copy-start(f32[128,2048]{1,0:T(8,128)} %get-tuple-element.427) | copy-start | bytes 3145732
  (27 other events, 104.8 us)
Sparse Core Ops, SparseCore 0:
  74.4 34.5 all-gather.3
  110.5 34.6 all-gather.5
  183.2 39.4 all-gather.7
  272.0 42.9 reduce-scatter.2
  324.6 42.8 reduce-scatter.4

commit v5 on v4

--- a/solution.py
+++ b/solution.py
@@ -288,7 +288,7 @@
 def weight_half(lhs, rhs, other):
     bh = lax.axis_size("bh")
     part = D // (2 * bh)
-    tile = min(2 * TILE, part)
+    tile = min(TILE, part)
     per = part // tile
     place = jnp.stack([lax.axis_index("dp") ^ other, lax.axis_index("bh")]).astype(jnp.int32)
     count, cols = rhs.shape
@@ -778,10 +778,12 @@
 
     projected = total(out_own, received, out_near)
     output = (x_own.astype(f32) + projected + vectors[4:5]).astype(bf16)
-    in_near, received_in, small, dense_grad, qkv_grad, output, in_own = join(
-        in_near, received_in, small, dense_grad, qkv_grad, output, in_own
-    )
     small = sum(small[1:], small[0])
+    smalls = [small[i] for i in range(5)]
+    smalls += [small[5 : 5 + nq].reshape(-1), small[5 + nq :].reshape(-1)]
+    in_near, received_in, smalls, dense_grad, qkv_grad, output, in_own = join(
+        in_near, received_in, smalls, dense_grad, qkv_grad, output, in_own
+    )
     grad_normed = total(in_own, received_in, in_near)
     own = x_own.astype(f32)
     own_average, own_inverse = statistics(own)
@@ -794,17 +796,14 @@
     return (
         output.reshape(seq_count, sub_len, D),
         grad_hidden.reshape(seq_count, sub_len, D),
-        small[0],
-        small[1],
-        small[2],
-        small[3],
+        *smalls[:4],
         qkv_grad,
-        small[5 : 5 + nq].reshape(-1),
+        smalls[5],
         dense_grad,
         up_grad,
-        small[5 + nq :].reshape(-1),
+        smalls[6],
         down_grad,
-        small[4],
+        smalls[4],
     )
 
 

time: 441 us -> 439 us (level)
  transfers between devices with their start and end apart: 55 -> 55, of which waited for: 27 -> 26; matrix products, arithmetic and copies ran while one was open for 10% -> 11% of each run, Pallas kernels for 27% -> 28%
where the time goes in v5:
time: 439 us; the launch traced here: 433 us
  waiting for transfers between devices  159 us (36%)
  Pallas kernels  119 us (27%)
  starting transfers between devices  82.5 us (19%)
  local copies, waits for them, and re-layouts  31.6 us (7%)
  other arithmetic  25.8 us (6%)
  between operations  14.9 us (3%)
    ppermute x44, waiting for transfers between devices, swap(): return lax.ppermute(value, axis, [(i, i ^ distance) for i in range(size)])  152 us
    pallas_call x11, Pallas kernels, call(): pl.pallas_call(kernel, grid=grid, out_shape=[jax.ShapeDtypeStruct(shape,...  104 us
    ppermute x44, starting transfers between devices, swap(): return lax.ppermute(value, axis, [(i, i ^ distance) for i in range(size)])  53.6 us
    pallas_call x2, Pallas kernels, weight_half(): pl.pallas_call(functools.partial(weight_half_kernel, per), grid_spec=pltp...  15.1 us
    all_to_all x3, starting transfers between devices, collect_group(): return lax.all_to_all(mine, TP, split_axis=0, concat_axis=0, tiled=True)  14.8 us
    convert_element_type x8, other arithmetic, add(): sum((x.astype(f32) for x in arrays[1:]), arrays[0].astype(f32))  12 us
    all_to_all x2, starting transfers between devices, spread_group(): mine = lax.all_to_all(shard, TP, split_axis=0, concat_axis=0, tiled=True)  10.2 us
  transfers between devices with their start and end apart: 55, of which 26 were waited for; matrix products, arithmetic and copies ran while one was open for 11% of the time, Pallas kernels for 28%

profile of v5, /device:TPU:0, one launch (start us, length us, event | category | flops | bytes accessed | tf_op | source)
XLA Modules:
  0.0 433.3 jit_solution(2536769691062365339)
XLA Ops:
  7.2 3.1 collective-permute-start
  10.3 2.6 collective-permute-start.1
  24.3 9.2 %collective-permute-done.refs_1_ = bf16[128,2048]{1,0:T(8,128)(2,1)S(1)} collective-permute-done((bf16[128,2048]{1,0:T(8,128)(2,1)}, bf16[128,2048]{1,0:T(8,128)(2,1)S(1)}, u32[]{:S(2)}, u32[]{:S(2)}) %collective-permute-start) | collective-permute-done | bytes 524320 | tf_op jit(solution)/shard_map/ppermute | solution.py:58
  33.5 2.5 collective-permute-done.1.refs_2_
  37.5 3.6 all-to-all-start
  41.2 1.9 collective-permute-start.4
  44.6 1.9 multiply_sine_fusion
  49.7 22.0 %collective-permute-done.6 = bf16[64,2048]{1,0:T(8,128)(2,1)S(1)} collective-permute-done((bf16[64,2048]{1,0:T(8,128)(2,1)S(1)}, bf16[64,2048]{1,0:T(8,128)(2,1)S(1)}, u32[]{:S(2)}, u32[]{:S(2)}) %collective-permute-start.6) | collective-permute-done | bytes 262176 | tf_op jit(solution)/shard_map/ppermute | solution.py:58
  74.2 4.8 %all-to-all-start.1 = ((bf16[8,64,1024]{2,1,0:T(8,128)(2,1)}), bf16[8,64,1024]{2,1,0:T(8,128)(2,1)}, u32[]{:S(2)}, u32[]{:S(2)}) async-start(bf16[8,64,1024]{2,1,0:T(8,128)(2,1)} %get-tuple-element.246), calls=%async_computation.1 | async-start | bytes 2097152 | tf_op jit(solution)/shard_map/all_to_all | solution.py:101
  81.5 2.0 collective-permute-start.7
  83.6 2.0 collective-permute-start.9
  88.4 21.2 %collective-permute-done.8 = bf16[64,2048]{1,0:T(8,128)(2,1)S(1)} collective-permute-done((bf16[64,2048]{1,0:T(8,128)(2,1)S(1)}, bf16[64,2048]{1,0:T(8,128)(2,1)S(1)}, u32[]{:S(2)}, u32[]{:S(2)}) %collective-permute-start.8) | collective-permute-done | bytes 262176 | tf_op jit(solution)/shard_map/ppermute | solution.py:58
  111.2 2.4 collective-permute-start.14
  115.4 13.4 %shard_map.228 = (bf16[1024,2048]{1,0:T(8,128)(2,1)}, bf16[1024,2048]{1,0:T(8,128)(2,1)}, bf16[1024,256]{1,0:T(8,128)(2,1)}, bf16[1024,512]{1,0:T(8,128)(2,1)}, f32[1024,1]{1,0:T(8,128)}, /*index=5*/f32[1024,1]{1,0:T(8,128)}) custom-call(bf16[128,2048]{1,0:T(8,128)(2,1)} %bitcast.144, bf16[128,2048]{1,0:T(8,128)(2,1)} %copy-done.6, ...), custom_call_target="tpu_custom_call" | custom-call | flops 1 | bytes 1 | tf_op jit(solution)/shard_map/pallas_call | solution.py:124
  128.9 7.6 %collective-permute-done.14.refs_2_ = bf16[128,2048]{1,0:T(8,128)(2,1)} collective-permute-done((bf16[128,2048]{1,0:T(8,128)(2,1)S(1)}, bf16[128,2048]{1,0:T(8,128)(2,1)}, u32[]{:S(2)}, u32[]{:S(2)}) %collective-permute-start.14) | collective-permute-done | bytes 524320 | tf_op jit(solution)/shard_map/ppermute | solution.py:58
  138.2 11.3 %collective-permute-done.15.refs_6_ = bf16[128,2048]{1,0:T(8,128)(2,1)S(1)} collective-permute-done((bf16[128,2048]{1,0:T(8,128)(2,1)}, bf16[128,2048]{1,0:T(8,128)(2,1)S(1)}, u32[]{:S(2)}, u32[]{:S(2)}) %collective-permute-start.15) | collective-permute-done | bytes 524320 | tf_op jit(solution)/shard_map/ppermute | solution.py:58
  151.0 5.4 %all-to-all-start.2 = ((bf16[8,64,1024]{2,1,0:T(8,128)(2,1)}), bf16[8,64,1024]{2,1,0:T(8,128)(2,1)S(1)}, u32[]{:S(2)}, u32[]{:S(2)}) async-start(bf16[8,64,1024]{2,1,0:T(8,128)(2,1)} %get-tuple-element.290), calls=%async_computation.2 | async-start | bytes 2097152 | tf_op jit(solution)/shard_map/all_to_all | solution.py:101
  156.5 1.6 collective-permute-start.18
  158.1 2.0 collective-permute-start.17
  160.1 11.9 %shard_map.229 = (bf16[1024,1024]{1,0:T(8,128)(2,1)}, f32[1024,1024]{1,0:T(8,128)}) custom-call(bf16[1024,2048]{1,0:T(8,128)(2,1)} %get-tuple-element.291.mlp_ref.refs_0_, bf16[2048,1024]{1,0:T(8,128)(2,1)} %all-gather.6.cloned.1.call-done.w_ref.refs_13_, f32[1,1024]{1,0:T(1,128)} %constant_dynamic-slice_fusion.10.b_ref), custom_call_target="tpu_custom_call" | custom-call | flops 1 | bytes 1 | tf_op jit(solution)/shard_map/pallas_call | solution.py:124
  172.0 8.1 %collective-permute-done.18.refs_1_ = bf16[1024,512]{1,0:T(8,128)(2,1)S(1)} collective-permute-done((bf16[1024,512]{1,0:T(8,128)(2,1)S(1)}, bf16[1024,512]{1,0:T(8,128)(2,1)S(1)}, u32[]{:S(2)}, u32[]{:S(2)}) %collective-permute-start.18) | collective-permute-done | bytes 1048608 | tf_op jit(solution)/shard_map/ppermute | solution.py:58
  180.2 1.9 all-to-all-done.2
  183.6 6.3 %shard_map.230 = (bf16[1024,2048]{1,0:T(8,128)(2,1)}, bf16[1024,256]{1,0:T(8,128)(2,1)}) custom-call(bf16[128,2048]{1,0:T(8,128)(2,1)} %bitcast.149, bf16[128,2048]{1,0:T(8,128)(2,1)} %copy-done.23, bf16[128,2048]{1,0:T(8,128)(2,1)} %collective-permute-done.14.refs_2_, bf16[128,2048]{1,0:T(8,128)(2,1)} %collective-permute-done.16.refs_3_, ...), custom_call_target="tpu_custom_call" | custom-call | flops 1 | bytes 1 | tf_op jit(solution)/shard_map/pallas_call | solution.py:124
  189.9 7.7 %shard_map.231 = (bf16[512,1024]{1,0:T(8,128)(2,1)}, bf16[512,1024]{1,0:T(8,128)(2,1)}) custom-call(s32[2]{0:T(128)} %get-tuple-element.481.place_ref, bf16[1024,2048]{1,0:T(8,128)(2,1)} %get-tuple-element.312.lhs_ref.g_ref.refs_2_, bf16[1024,1024]{1,0:T(8,128)(2,1)} %get-tuple-element.306.rhs_ref.act_ref), custom_call_target="tpu_custom_call" | custom-call | flops 1 | bytes 1 | tf_op jit(solution)/shard_map/pallas_call | solution.py:302
  198.8 7.3 %shard_map.232 = (bf16[512,1024]{1,0:T(8,128)(2,1)}, bf16[512,1024]{1,0:T(8,128)(2,1)}) custom-call(s32[2]{0:T(128)} %pad_add_fusion.2.place_ref, bf16[1024,2048]{1,0:T(8,128)(2,1)} %get-tuple-element.312.lhs_ref.g_ref.refs_2_, bf16[1024,1024]{1,0:T(8,128)(2,1)} %get-tuple-element.306.rhs_ref.act_ref), custom_call_target="tpu_custom_call" | custom-call | flops 1 | bytes 1 | tf_op jit(solution)/shard_map/pallas_call | solution.py:302
  206.1 1.6 add_convert_fusion.1
  207.8 1.6 collective-permute-start.21
  209.3 12.7 %shard_map.233 = (bf16[1024,256]{1,0:T(8,128)(2,1)}, bf16[1024,256]{1,0:T(8,128)(2,1)}, bf16[1024,512]{1,0:T(8,128)(2,1)}, bf16[1024,512]{1,0:T(8,128)(2,1)}) custom-call(s32[2]{0:T(128)} %get-tuple-element.480.place_ref, bf16[1024,256]{1,0:T(8,128)(2,1)} %get-tuple-element.264.q_ref, bf16[1024,256]{1,0:T(8,128)(2,1)} %get-tuple-element.319.g_ref, ...), custom_call_target="tpu_custom_call" | custom-call | flops 1 | bytes 1 | tf_op jit(solution)/shard_map/pallas_call | solution.py:124
  222.0 6.2 %shard_map.234 = (bf16[128,2048]{1,0:T(8,128)(2,1)}, bf16[128,2048]{1,0:T(8,128)(2,1)}, bf16[128,2048]{1,0:T(8,128)(2,1)}, bf16[128,2048]{1,0:T(8,128)(2,1)}) custom-call(bf16[1024,256]{1,0:T(8,128)(2,1)} %get-tuple-element.380.att_ref.refs_3_, bf16[1024,1024]{1,0:T(8,128)(2,1)} %get-tuple-element.306.rhs_ref.act_ref, ...), custom_call_target="tpu_custom_call" | custom-call | flops 1 | bytes 1 | tf_op jit(solution)/shard_map/pallas_call | solution.py:124
  228.2 6.9 %shard_map.235 = (f32[128,2048]{1,0:T(8,128)}, f32[128,2048]{1,0:T(8,128)}, f32[128,2048]{1,0:T(8,128)}, f32[128,2048]{1,0:T(8,128)}) custom-call(bf16[1024,256]{1,0:T(8,128)(2,1)} %get-tuple-element.380.att_ref.refs_3_, bf16[1024,1024]{1,0:T(8,128)(2,1)} %get-tuple-element.306.rhs_ref.act_ref, ...), custom_call_target="tpu_custom_call" | custom-call | flops 1 | bytes 1 | tf_op jit(solution)/shard_map/pallas_call | solution.py:124
  235.1 2.7 collective-permute-done.21
  237.9 1.6 add_convert_fusion
  239.5 5.5 %all-to-all-start.3 = ((bf16[8,64,1024]{2,1,0:T(8,128)(2,1)}), bf16[8,64,1024]{2,1,0:T(8,128)(2,1)S(1)}, u32[]{:S(2)}, u32[]{:S(2)}) async-start(bf16[8,64,1024]{2,1,0:T(8,128)(2,1)} %bitcast.26), calls=%async_computation.3 | async-start | bytes 2097152 | tf_op jit(solution)/shard_map/all_to_all | solution.py:115
  245.6 1.9 collective-permute-start.23
  247.6 9.3 %shard_map.236 = (bf16[1024,1024]{1,0:T(8,128)(2,1)}, f32[1,1024]{1,0:T(1,128)}) custom-call(bf16[1024,2048]{1,0:T(8,128)(2,1)} %get-tuple-element.312.lhs_ref.g_ref.refs_2_, bf16[2048,1024]{1,0:T(8,128)(2,1)} %all-gather.8.cloned.1.call-done.down_ref.w_ref, f32[1024,1024]{1,0:T(8,128)} %get-tuple-element.345.slope_ref), custom_call_target="tpu_custom_call" | custom-call | flops 1 | bytes 1 | tf_op jit(solution)/shard_map/pallas_call | solution.py:124
  256.9 8.5 %shard_map.237 = bf16[2048,1024]{1,0:T(8,128)(2,1)} custom-call(bf16[1024,2048]{1,0:T(8,128)(2,1)} %get-tuple-element.291.mlp_ref.refs_0_, bf16[1024,1024]{1,0:T(8,128)(2,1)} %get-tuple-element.354.refs_1_.refs_11_), custom_call_target="tpu_custom_call" | custom-call | flops 1 | bytes 1 | tf_op jit(solution)/shard_map/pallas_call | solution.py:124
  265.4 4.5 %collective-permute-done.22.refs_2_ = bf16[1024,512]{1,0:T(8,128)(2,1)S(1)} collective-permute-done((bf16[1024,512]{1,0:T(8,128)(2,1)}, bf16[1024,512]{1,0:T(8,128)(2,1)S(1)}, u32[]{:S(2)}, u32[]{:S(2)}) %collective-permute-start.22) | collective-permute-done | bytes 1048608 | tf_op jit(solution)/shard_map/ppermute | solution.py:58
  269.9 1.7 all-to-all-done.3
  275.9 4.5 %shard_map.238 = (bf16[1024,768]{1,0:T(8,128)(2,1)}, f32[1,768]{1,0:T(1,128)}) custom-call(bf16[1024,256]{1,0:T(8,128)(2,1)} %get-tuple-element.322.refs_0_, bf16[1024,512]{1,0:T(8,128)(2,1)} %get-tuple-element.323.refs_1_, bf16[1024,512]{1,0:T(8,128)(2,1)} %copy-done.21, f32[1024,128]{1,0:T(8,128)} %maximum_maximum_fusion.refs_11_.refs_3_, ...), custom_call_target="tpu_custom_call" | custom-call | flops 1 | bytes 1 | tf_op jit(solution)/shard_map/pallas_call | solution.py:124
  280.4 15.2 %shard_map.239 = (f32[128,2048]{1,0:T(8,128)}, f32[128,2048]{1,0:T(8,128)}, f32[128,2048]{1,0:T(8,128)}, f32[128,2048]{1,0:T(8,128)}, bf16[128,2048]{1,0:T(8,128...) custom-call(bf16[128,2048]{1,0:T(8,128)(2,1)} %bitcast.145, ...), custom_call_target="tpu_custom_call" | custom-call | flops 1 | bytes 1 | tf_op jit(solution)/shard_map/pallas_call | solution.py:124
  299.3 2.1 collective-permute-start.28
  304.2 9.2 %shard_map.240 = bf16[2048,1024]{1,0:T(8,128)(2,1)} custom-call(bf16[1024,2048]{1,0:T(8,128)(2,1)} %get-tuple-element.378.refs_0_, bf16[1024,768]{1,0:T(8,128)(2,1)} %get-tuple-element.379.refs_10_.refs_1_, bf16[1024,2048]{1,0:T(8,128)(2,1)} %get-tuple-element.312.lhs_ref.g_ref.refs_2_, bf16[1024,256]{1,0:T(8,128)(2,1)} %get-tuple-element.380.att_ref.refs_3_), custom_call_target="tpu_custom_call" | custom-call | flops 1 | bytes 1 | tf_op jit(solution)/shard_map/pallas_call | solution.py:124
  313.4 7.5 %collective-permute-done.27 = bf16[128,2048]{1,0:T(8,128)(2,1)} collective-permute-done((bf16[128,2048]{1,0:T(8,128)(2,1)}, bf16[128,2048]{1,0:T(8,128)(2,1)}, u32[]{:S(2)}, u32[]{:S(2)}) %collective-permute-start.27) | collective-permute-done | bytes 524320 | tf_op jit(solution)/shard_map/ppermute | solution.py:58
  321.0 3.2 collective-permute-done.30
  324.2 2.0 add_convert_fusion.4
  326.2 3.6 all-to-all-start.4
  330.9 1.9 collective-permute-start.31
  337.4 1.7 collective-permute-done.34
  339.0 2.7 fusion.7
  342.5 14.4 %collective-permute-done.31 = bf16[128,2048]{1,0:T(8,128)(2,1)S(1)} collective-permute-done((bf16[128,2048]{1,0:T(8,128)(2,1)}, bf16[128,2048]{1,0:T(8,128)(2,1)S(1)}, u32[]{:S(2)}, u32[]{:S(2)}) %collective-permute-start.31) | collective-permute-done | bytes 524320 | tf_op jit(solution)/shard_map/ppermute | solution.py:58
  358.5 5.1 %collective-permute-done.33 = bf16[128,2048]{1,0:T(8,128)(2,1)} collective-permute-done((bf16[128,2048]{1,0:T(8,128)(2,1)}, bf16[128,2048]{1,0:T(8,128)(2,1)}, u32[]{:S(2)}, u32[]{:S(2)}) %collective-permute-start.33) | collective-permute-done | bytes 524320 | tf_op jit(solution)/shard_map/ppermute | solution.py:58
  363.6 3.2 reduce-scatter.5.cloned.1.call-done
  366.8 5.7 %all-to-all-start.5 = ((bf16[8,64,1024]{2,1,0:T(8,128)(2,1)}), bf16[8,64,1024]{2,1,0:T(8,128)(2,1)S(1)}, u32[]{:S(2)}, u32[]{:S(2)}) async-start(bf16[8,64,1024]{2,1,0:T(8,128)(2,1)} %bitcast.161), calls=%async_computation.7 | async-start | bytes 2097152 | tf_op jit(solution)/shard_map/all_to_all | solution.py:115
  372.5 2.4 add_convert_fusion.2
  375.0 2.0 add_convert_fusion.3
  377.0 2.0 collective-permute-start.37
  380.6 2.4 collective-permute-start.39
  385.3 4.7 %collective-permute-done.38 = f32[2,12,64]{2,0,1:T(2,128)S(1)} collective-permute-done((f32[2,12,64]{2,0,1:T(2,128)S(1)}, f32[2,12,64]{2,0,1:T(2,128)S(1)}, u32[]{:S(2)}, u32[]{:S(2)}) %collective-permute-start.38) | collective-permute-done | bytes 6176 | tf_op jit(solution)/shard_map/ppermute | solution.py:58
  390.0 9.0 %collective-permute-done.39 = f32[2,12,64]{2,0,1:T(2,128)S(1)} collective-permute-done((f32[2,12,64]{2,0,1:T(2,128)S(1)}, f32[2,12,64]{2,0,1:T(2,128)S(1)}, u32[]{:S(2)}, u32[]{:S(2)}) %collective-permute-start.39) | collective-permute-done | bytes 6176 | tf_op jit(solution)/shard_map/ppermute | solution.py:58
  401.2 1.6 collective-permute-start.43
  405.2 2.6 reshape.277
  408.7 1.6 copy.76
  412.2 11.1 %collective-permute-done.41 = bf16[128,2048]{1,0:T(8,128)(2,1)} collective-permute-done((bf16[128,2048]{1,0:T(8,128)(2,1)}, bf16[128,2048]{1,0:T(8,128)(2,1)}, u32[]{:S(2)}, u32[]{:S(2)}) %collective-permute-start.41) | collective-permute-done | bytes 524320 | tf_op jit(solution)/shard_map/ppermute | solution.py:58
  423.3 1.9 fusion.24
  (247 shorter events, 66.5 us)
Async XLA Ops:
  7.2 26.3 %collective-permute-start = (bf16[128,2048]{1,0:T(8,128)(2,1)}, bf16[128,2048]{1,0:T(8,128)(2,1)S(1)}, u32[]{:S(2)}, u32[]{:S(2)}) collective-permute-start(bf16[128,2048]{1,0:T(8,128)(2,1)} %bitcast.141), channel_id=1, source_target_pairs={{0,1},{1,0},{2,3},{3,2},{4,5},{5,4},{6,7},{7,6},{8,9},{9,8},{10,11... | collective-permute-start | bytes 1572872 | tf_op jit(solution)/shard_map/ppermute | solution.py:58
  10.3 25.8 %collective-permute-start.1 = (bf16[128,2048]{1,0:T(8,128)(2,1)}, bf16[128,2048]{1,0:T(8,128)(2,1)S(1)}, u32[]{:S(2)}, u32[]{:S(2)}) collective-permute-start(bf16[128,2048]{1,0:T(8,128)(2,1)} %bitcast.142), channel_id=1, source_target_pairs={{0,2},{1,3},{2,0},{3,1},{4,6},{5,7},{6,4},{7,5},{8,10},{9,11},{10,... | collective-permute-start | bytes 1572872 | tf_op jit(solution)/shard_map/ppermute | solution.py:58
  12.9 23.2 %collective-permute-start.2 = (bf16[128,2048]{1,0:T(8,128)(2,1)}, bf16[128,2048]{1,0:T(8,128)(2,1)}, u32[]{:S(2)}, u32[]{:S(2)}) collective-permute-start(bf16[128,2048]{1,0:T(8,128)(2,1)} %bitcast.143), channel_id=1, source_target_pairs={{0,4},{4,0},{1,5},{5,1},{2,6},{6,2},{3,7},{7,3},{8,12},{12,8},{9,1... | collective-permute-start | bytes 1572872 | tf_op jit(solution)/shard_map/ppermute | solution.py:58
  14.3 23.2 %collective-permute-start.3 = (bf16[128,2048]{1,0:T(8,128)(2,1)}, bf16[128,2048]{1,0:T(8,128)(2,1)}, u32[]{:S(2)}, u32[]{:S(2)}) collective-permute-start(bf16[128,2048]{1,0:T(8,128)(2,1)} %bitcast.148), channel_id=1, source_target_pairs={{0,4},{4,0},{1,5},{5,1},{2,6},{6,2},{3,7},{7,3},{8,12},{12,8},{9,1... | collective-permute-start | bytes 1572872 | tf_op jit(solution)/shard_map/ppermute | solution.py:58
  33.5 13.1 %copy-start.6 = (bf16[128,2048]{1,0:T(8,128)(2,1)}, bf16[128,2048]{1,0:T(8,128)(2,1)S(1)}, u32[]{:S(2)}) copy-start(bf16[128,2048]{1,0:T(8,128)(2,1)S(1)} %collective-permute-done.refs_1_) | copy-start | bytes 1572868
  36.1 47.4 %copy-start.1 = (bf16[128,2048]{1,0:T(8,128)(2,1)}, bf16[128,2048]{1,0:T(8,128)(2,1)S(1)}, u32[]{:S(2)}) copy-start(bf16[128,2048]{1,0:T(8,128)(2,1)S(1)} %collective-permute-done.1.refs_2_) | copy-start | bytes 1572868
  37.5 34.9 %all-to-all-start = ((bf16[8,72,1024]{2,1,0:T(8,128)(2,1)}), bf16[8,72,1024]{2,1,0:T(8,128)(2,1)S(1)}, u32[]{:S(2)}, u32[]{:S(2)}) async-start(bf16[8,72,1024]{2,1,0:T(8,128)(2,1)} %pad_maximum_fusion), calls=%async_computation | async-start | bytes 2359296 | tf_op jit(solution)/shard_map/all_to_all | solution.py:590
  41.1 73.5 %all-gather.4.cloned.1.call-start = ((), (), s32[]{:S(2)}) async-start(), calls=%async_computation.8 | async-start | bytes 5242880 | tf_op jit(solution)/shard_map/all_gather | solution.py:106
  41.2 31.2 %collective-permute-start.4 = (bf16[128,2048]{1,0:T(8,128)(2,1)S(1)}, bf16[128,2048]{1,0:T(8,128)(2,1)S(1)}, u32[]{:S(2)}, u32[]{:S(2)}) collective-permute-start(bf16[128,2048]{1,0:T(8,128)(2,1)S(1)} %collective-permute-done.1.refs_2_), channel_id=1, source_target_pairs={{0,1},{1,0},{2,3},{3,2},{4,5},{5,4},{6,7},{7,6},{8,9},{9,8},{10,11... | collective-permute-start | bytes 1572872 | tf_op jit(solution)/shard_map/ppermute | solution.py:58
  43.1 29.3 %collective-permute-start.5 = (bf16[128,2048]{1,0:T(8,128)(2,1)S(1)}, bf16[128,2048]{1,0:T(8,128)(2,1)}, u32[]{:S(2)}, u32[]{:S(2)}) collective-permute-start(bf16[128,2048]{1,0:T(8,128)(2,1)S(1)} %collective-permute-done.refs_1_), channel_id=1, source_target_pairs={{0,4},{4,0},{1,5},{5,1},{2,6},{6,2},{3,7},{7,3},{8,12},{12,8},{9,1... | collective-permute-start | bytes 1572872 | tf_op jit(solution)/shard_map/ppermute | solution.py:58
  46.6 25.0 %collective-permute-start.6 = (bf16[64,2048]{1,0:T(8,128)(2,1)S(1)}, bf16[64,2048]{1,0:T(8,128)(2,1)S(1)}, u32[]{:S(2)}, u32[]{:S(2)}) collective-permute-start(bf16[64,2048]{1,0:T(8,128)(2,1)S(1)} %slice.63), channel_id=1, source_target_pairs={{0,4},{4,0},{1,5},{5,1},{2,6},{6,2},{3,7},{7,3},{8,12},{12,8},{9,1... | collective-permute-start | bytes 786440 | tf_op jit(solution)/shard_map/ppermute | solution.py:58
  74.2 35.4 %all-to-all-start.1 = ((bf16[8,64,1024]{2,1,0:T(8,128)(2,1)}), bf16[8,64,1024]{2,1,0:T(8,128)(2,1)}, u32[]{:S(2)}, u32[]{:S(2)}) async-start(bf16[8,64,1024]{2,1,0:T(8,128)(2,1)} %get-tuple-element.246), calls=%async_computation.1 | async-start | bytes 2097152 | tf_op jit(solution)/shard_map/all_to_all | solution.py:101
  79.0 81.1 %all-gather.6.cloned.1.call-start = ((), (), s32[]{:S(2)}) async-start(), calls=%async_computation.9 | async-start | bytes 5242880 | tf_op jit(solution)/shard_map/all_gather | solution.py:106
  79.3 4.3 collective-permute-start.12
  80.2 5.4 %collective-permute-start.11 = (bf16[8,768]{1,0:T(8,128)(2,1)S(1)}, bf16[8,768]{1,0:T(8,128)(2,1)S(1)}, u32[]{:S(2)}, u32[]{:S(2)}) collective-permute-start(bf16[8,768]{1,0:T(8,128)(2,1)S(1)} %bitcast.177), channel_id=1, source_target_pairs={{0,16},{8,24},{16,0},{24,8},{1,17},{9,25},{17,1},{25,9},{2,18},{10... | collective-permute-start | bytes 36872 | tf_op jit(solution)/shard_map/ppermute | solution.py:58
  81.0 4.6 %collective-permute-start.10 = (bf16[8,768]{1,0:T(8,128)(2,1)S(1)}, bf16[8,768]{1,0:T(8,128)(2,1)S(1)}, u32[]{:S(2)}, u32[]{:S(2)}) collective-permute-start(bf16[8,768]{1,0:T(8,128)(2,1)S(1)} %bitcast.178), channel_id=1, source_target_pairs={{0,8},{8,0},{16,24},{24,16},{1,9},{9,1},{17,25},{25,17},{2,10},{10... | collective-permute-start | bytes 36872 | tf_op jit(solution)/shard_map/ppermute | solution.py:58
  81.5 28.1 %collective-permute-start.7 = (bf16[128,2048]{1,0:T(8,128)(2,1)S(1)}, bf16[128,2048]{1,0:T(8,128)(2,1)S(1)}, u32[]{:S(2)}, u32[]{:S(2)}) collective-permute-start(bf16[128,2048]{1,0:T(8,128)(2,1)S(1)} %copy-done.8), channel_id=1, source_target_pairs={{0,4},{4,0},{1,5},{5,1},{2,6},{6,2},{3,7},{7,3},{8,12},{12,8},{9,1... | collective-permute-start | bytes 1572872 | tf_op jit(solution)/shard_map/ppermute | solution.py:58
  83.5 26.1 %collective-permute-start.8 = (bf16[64,2048]{1,0:T(8,128)(2,1)S(1)}, bf16[64,2048]{1,0:T(8,128)(2,1)S(1)}, u32[]{:S(2)}, u32[]{:S(2)}) collective-permute-start(bf16[64,2048]{1,0:T(8,128)(2,1)S(1)} %slice.64), channel_id=1, source_target_pairs={{0,4},{4,0},{1,5},{5,1},{2,6},{6,2},{3,7},{7,3},{8,12},{12,8},{9,1... | collective-permute-start | bytes 786440 | tf_op jit(solution)/shard_map/ppermute | solution.py:58
  83.6 26.0 %collective-permute-start.9 = (bf16[128,2048]{1,0:T(8,128)(2,1)S(1)}, bf16[128,2048]{1,0:T(8,128)(2,1)S(1)}, u32[]{:S(2)}, u32[]{:S(2)}) collective-permute-start(bf16[128,2048]{1,0:T(8,128)(2,1)S(1)} %bitcast.150), channel_id=1, source_target_pairs={{0,1},{1,0},{2,3},{3,2},{4,5},{5,4},{6,7},{7,6},{8,9},{9,8},{10,11... | collective-permute-start | bytes 1572872 | tf_op jit(solution)/shard_map/ppermute | solution.py:58
  109.6 19.2 %copy-start.23 = (bf16[128,2048]{1,0:T(8,128)(2,1)}, bf16[128,2048]{1,0:T(8,128)(2,1)S(1)}, u32[]{:S(2)}) copy-start(bf16[128,2048]{1,0:T(8,128)(2,1)S(1)} %collective-permute-done.9.refs_1_) | copy-start | bytes 1572868
  110.3 18.5 %collective-permute-start.13 = (bf16[128,2048]{1,0:T(8,128)(2,1)S(1)}, bf16[128,2048]{1,0:T(8,128)(2,1)S(1)}, u32[]{:S(2)}, u32[]{:S(2)}) collective-permute-start(bf16[128,2048]{1,0:T(8,128)(2,1)S(1)} %collective-permute-done.9.refs_1_), channel_id=1, source_target_pairs={{0,4},{4,0},{1,5},{5,1},{2,6},{6,2},{3,7},{7,3},{8,12},{12,8},{9,1... | collective-permute-start | bytes 1572872 | tf_op jit(solution)/shard_map/ppermute | solution.py:58
  111.2 25.2 %collective-permute-start.14 = (bf16[128,2048]{1,0:T(8,128)(2,1)S(1)}, bf16[128,2048]{1,0:T(8,128)(2,1)}, u32[]{:S(2)}, u32[]{:S(2)}) collective-permute-start(bf16[128,2048]{1,0:T(8,128)(2,1)S(1)} %bitcast.151), channel_id=1, source_target_pairs={{0,2},{1,3},{2,0},{3,1},{4,6},{5,7},{6,4},{7,5},{8,10},{9,11},{10,... | collective-permute-start | bytes 1572872 | tf_op jit(solution)/shard_map/ppermute | solution.py:58
  128.8 27.7 %copy-start.11 = (bf16[1024,512]{1,0:T(8,128)(2,1)S(1)}, bf16[1024,512]{1,0:T(8,128)(2,1)}, u32[]{:S(2)}) copy-start(bf16[1024,512]{1,0:T(8,128)(2,1)} %get-tuple-element.320.refs_0_) | copy-start | bytes 3145732
  128.8 27.6 %copy-start.26 = (bf16[128,2048]{1,0:T(8,128)(2,1)}, bf16[128,2048]{1,0:T(8,128)(2,1)S(1)}, u32[]{:S(2)}) copy-start(bf16[128,2048]{1,0:T(8,128)(2,1)S(1)} %collective-permute-done.13.refs_5_) | copy-start | bytes 1572868
  136.4 13.1 %collective-permute-start.15 = (bf16[128,2048]{1,0:T(8,128)(2,1)}, bf16[128,2048]{1,0:T(8,128)(2,1)S(1)}, u32[]{:S(2)}, u32[]{:S(2)}) collective-permute-start(bf16[128,2048]{1,0:T(8,128)(2,1)} %collective-permute-done.14.refs_2_), channel_id=1, source_target_pairs={{0,4},{4,0},{1,5},{5,1},{2,6},{6,2},{3,7},{7,3},{8,12},{12,8},{9,1... | collective-permute-start | bytes 1572872 | tf_op jit(solution)/shard_map/ppermute | solution.py:58
  138.0 13.0 %collective-permute-start.16 = (bf16[128,2048]{1,0:T(8,128)(2,1)}, bf16[128,2048]{1,0:T(8,128)(2,1)}, u32[]{:S(2)}, u32[]{:S(2)}) collective-permute-start(bf16[128,2048]{1,0:T(8,128)(2,1)} %collective-permute-done.14.refs_2_), channel_id=1, source_target_pairs={{0,1},{1,0},{2,3},{3,2},{4,5},{5,4},{6,7},{7,6},{8,9},{9,8},{10,11... | collective-permute-start | bytes 1572872 | tf_op jit(solution)/shard_map/ppermute | solution.py:58
  151.0 31.1 %all-to-all-start.2 = ((bf16[8,64,1024]{2,1,0:T(8,128)(2,1)}), bf16[8,64,1024]{2,1,0:T(8,128)(2,1)S(1)}, u32[]{:S(2)}, u32[]{:S(2)}) async-start(bf16[8,64,1024]{2,1,0:T(8,128)(2,1)} %get-tuple-element.290), calls=%async_computation.2 | async-start | bytes 2097152 | tf_op jit(solution)/shard_map/all_to_all | solution.py:101
  156.4 65.6 %all-gather.8.cloned.1.call-start = ((), (), s32[]{:S(2)}) async-start(), calls=%async_computation.10 | async-start | bytes 5242880 | tf_op jit(solution)/shard_map/all_gather | solution.py:106
  156.5 23.7 %collective-permute-start.18 = (bf16[1024,512]{1,0:T(8,128)(2,1)S(1)}, bf16[1024,512]{1,0:T(8,128)(2,1)S(1)}, u32[]{:S(2)}, u32[]{:S(2)}) collective-permute-start(bf16[1024,512]{1,0:T(8,128)(2,1)S(1)} %copy-done.11), channel_id=1, source_target_pairs={{0,8},{8,0},{1,9},{9,1},{2,10},{10,2},{3,11},{11,3},{4,12},{12,4},... | collective-permute-start | bytes 3145736 | tf_op jit(solution)/shard_map/ppermute | solution.py:58
  158.1 22.1 %collective-permute-start.17 = (bf16[128,2048]{1,0:T(8,128)(2,1)}, bf16[128,2048]{1,0:T(8,128)(2,1)}, u32[]{:S(2)}, u32[]{:S(2)}) collective-permute-start(bf16[128,2048]{1,0:T(8,128)(2,1)} %collective-permute-done.16.refs_3_), channel_id=1, source_target_pairs={{0,4},{4,0},{1,5},{5,1},{2,6},{6,2},{3,7},{7,3},{8,12},{12,8},{9,1... | collective-permute-start | bytes 1572872 | tf_op jit(solution)/shard_map/ppermute | solution.py:58
  180.2 17.5 %copy-start.15 = (bf16[1024,512]{1,0:T(8,128)(2,1)}, bf16[1024,512]{1,0:T(8,128)(2,1)S(1)}, u32[]{:S(2)}) copy-start(bf16[1024,512]{1,0:T(8,128)(2,1)S(1)} %collective-permute-done.18.refs_1_) | copy-start | bytes 3145732
  197.7 8.4 %collective-permute-start.19 = (bf16[512,1024]{1,0:T(8,128)(2,1)}, bf16[512,1024]{1,0:T(8,128)(2,1)S(1)}, u32[]{:S(2)}, u32[]{:S(2)}) collective-permute-start(bf16[512,1024]{1,0:T(8,128)(2,1)} %get-tuple-element.310), channel_id=1, source_target_pairs={{0,16},{16,0},{1,17},{17,1},{2,18},{18,2},{3,19},{19,3},{4,20},{20... | collective-permute-start | bytes 3145736 | tf_op jit(solution)/shard_map/ppermute | solution.py:58
  197.7 8.4 %collective-permute-start.20 = (bf16[512,1024]{1,0:T(8,128)(2,1)}, bf16[512,1024]{1,0:T(8,128)(2,1)S(1)}, u32[]{:S(2)}, u32[]{:S(2)}) collective-permute-start(bf16[512,1024]{1,0:T(8,128)(2,1)} %get-tuple-element.311), channel_id=1, source_target_pairs={{0,16},{16,0},{1,17},{17,1},{2,18},{18,2},{3,19},{19,3},{4,20},{20... | collective-permute-start | bytes 3145736 | tf_op jit(solution)/shard_map/ppermute | solution.py:58
  207.8 30.1 %collective-permute-start.21 = (bf16[512,1024]{1,0:T(8,128)(2,1)S(1)}, bf16[512,1024]{1,0:T(8,128)(2,1)S(1)}, u32[]{:S(2)}, u32[]{:S(2)}) collective-permute-start(bf16[512,1024]{1,0:T(8,128)(2,1)S(1)} %add_convert_fusion.1), channel_id=1, source_target_pairs={{0,8},{8,0},{1,9},{9,1},{2,10},{10,2},{3,11},{11,3},{4,12},{12,4},... | collective-permute-start | bytes 3145736 | tf_op jit(solution)/shard_map/ppermute | solution.py:58
  239.5 32.1 %all-to-all-start.3 = ((bf16[8,64,1024]{2,1,0:T(8,128)(2,1)}), bf16[8,64,1024]{2,1,0:T(8,128)(2,1)S(1)}, u32[]{:S(2)}, u32[]{:S(2)}) async-start(bf16[8,64,1024]{2,1,0:T(8,128)(2,1)} %bitcast.26), calls=%async_computation.3 | async-start | bytes 2097152 | tf_op jit(solution)/shard_map/all_to_all | solution.py:115
  245.0 79.2 %reduce-scatter.3.cloned.1.call-start = ((), (), s32[]{:S(2)}) async-start(), calls=%async_computation.11 | async-start | bytes 5242880 | tf_op jit(solution)/shard_map/reduce_scatter | solution.py:110
  245.0 24.9 %collective-permute-start.22 = (bf16[1024,512]{1,0:T(8,128)(2,1)}, bf16[1024,512]{1,0:T(8,128)(2,1)S(1)}, u32[]{:S(2)}, u32[]{:S(2)}) collective-permute-start(bf16[1024,512]{1,0:T(8,128)(2,1)} %get-tuple-element.337), channel_id=1, source_target_pairs={{0,8},{8,0},{1,9},{9,1},{2,10},{10,2},{3,11},{11,3},{4,12},{12,4},... | collective-permute-start | bytes 3145736 | tf_op jit(solution)/shard_map/ppermute | solution.py:58
  245.6 24.3 %collective-permute-start.23 = (bf16[128,2048]{1,0:T(8,128)(2,1)}, bf16[128,2048]{1,0:T(8,128)(2,1)}, u32[]{:S(2)}, u32[]{:S(2)}) collective-permute-start(bf16[128,2048]{1,0:T(8,128)(2,1)} %get-tuple-element.344), channel_id=1, source_target_pairs={{0,4},{4,0},{1,5},{5,1},{2,6},{6,2},{3,7},{7,3},{8,12},{12,8},{9,1... | collective-permute-start | bytes 1572872 | tf_op jit(solution)/shard_map/ppermute | solution.py:58
  271.6 95.1 %reduce-scatter.5.cloned.1.call-start = ((), (), s32[]{:S(2)}) async-start(), calls=%async_computation.12 | async-start | bytes 5242880 | tf_op jit(solution)/shard_map/reduce_scatter | solution.py:110
  272.9 22.7 %collective-permute-start.24 = (bf16[128,2048]{1,0:T(8,128)(2,1)S(1)}, bf16[128,2048]{1,0:T(8,128)(2,1)S(1)}, u32[]{:S(2)}, u32[]{:S(2)}) collective-permute-start(bf16[128,2048]{1,0:T(8,128)(2,1)S(1)} %add_convert_fusion.7), channel_id=1, source_target_pairs={{0,1},{1,0},{2,3},{3,2},{4,5},{5,4},{6,7},{7,6},{8,9},{9,8},{10,11... | collective-permute-start | bytes 1572872 | tf_op jit(solution)/shard_map/ppermute | solution.py:58
  273.8 21.8 %collective-permute-start.25 = (bf16[128,2048]{1,0:T(8,128)(2,1)S(1)}, bf16[128,2048]{1,0:T(8,128)(2,1)S(1)}, u32[]{:S(2)}, u32[]{:S(2)}) collective-permute-start(bf16[128,2048]{1,0:T(8,128)(2,1)S(1)} %copy-done.35), channel_id=1, source_target_pairs={{0,4},{4,0},{1,5},{5,1},{2,6},{6,2},{3,7},{7,3},{8,12},{12,8},{9,1... | collective-permute-start | bytes 1572872 | tf_op jit(solution)/shard_map/ppermute | solution.py:58
  275.3 21.8 %collective-permute-start.26 = (bf16[128,2048]{1,0:T(8,128)(2,1)S(1)}, bf16[128,2048]{1,0:T(8,128)(2,1)S(1)}, u32[]{:S(2)}, u32[]{:S(2)}) collective-permute-start(bf16[128,2048]{1,0:T(8,128)(2,1)S(1)} %copy-done.34), channel_id=1, source_target_pairs={{0,4},{4,0},{1,5},{5,1},{2,6},{6,2},{3,7},{7,3},{8,12},{12,8},{9,1... | collective-permute-start | bytes 1572872 | tf_op jit(solution)/shard_map/ppermute | solution.py:58
  280.4 16.7 %copy-start.14 = (f32[128,2048]{1,0:T(8,128)S(1)}, f32[128,2048]{1,0:T(8,128)}, u32[]{:S(2)}) copy-start(f32[128,2048]{1,0:T(8,128)} %get-tuple-element.367) | copy-start | bytes 3145732
  298.2 22.8 %collective-permute-start.27 = (bf16[128,2048]{1,0:T(8,128)(2,1)}, bf16[128,2048]{1,0:T(8,128)(2,1)}, u32[]{:S(2)}, u32[]{:S(2)}) collective-permute-start(bf16[128,2048]{1,0:T(8,128)(2,1)} %add_convert_fusion.5), channel_id=1, source_target_pairs={{0,1},{1,0},{2,3},{3,2},{4,5},{5,4},{6,7},{7,6},{8,9},{9,8},{10,11... | collective-permute-start | bytes 1572872 | tf_op jit(solution)/shard_map/ppermute | solution.py:58
  299.3 21.7 %collective-permute-start.28 = (bf16[128,2048]{1,0:T(8,128)(2,1)S(1)}, bf16[128,2048]{1,0:T(8,128)(2,1)}, u32[]{:S(2)}, u32[]{:S(2)}) collective-permute-start(bf16[128,2048]{1,0:T(8,128)(2,1)S(1)} %add_convert_fusion.6), channel_id=1, source_target_pairs={{0,2},{1,3},{2,0},{3,1},{4,6},{5,7},{6,4},{7,5},{8,10},{9,11},{10,... | collective-permute-start | bytes 1572872 | tf_op jit(solution)/shard_map/ppermute | solution.py:58
  301.5 19.5 %collective-permute-start.29 = (bf16[128,2048]{1,0:T(8,128)(2,1)}, bf16[128,2048]{1,0:T(8,128)(2,1)}, u32[]{:S(2)}, u32[]{:S(2)}) collective-permute-start(bf16[128,2048]{1,0:T(8,128)(2,1)} %get-tuple-element.376), channel_id=1, source_target_pairs={{0,4},{4,0},{1,5},{5,1},{2,6},{6,2},{3,7},{7,3},{8,12},{12,8},{9,1... | collective-permute-start | bytes 1572872 | tf_op jit(solution)/shard_map/ppermute | solution.py:58
  302.7 21.5 %collective-permute-start.30 = (bf16[128,2048]{1,0:T(8,128)(2,1)}, bf16[128,2048]{1,0:T(8,128)(2,1)}, u32[]{:S(2)}, u32[]{:S(2)}) collective-permute-start(bf16[128,2048]{1,0:T(8,128)(2,1)} %get-tuple-element.377), channel_id=1, source_target_pairs={{0,4},{4,0},{1,5},{5,1},{2,6},{6,2},{3,7},{7,3},{8,12},{12,8},{9,1... | collective-permute-start | bytes 1572872 | tf_op jit(solution)/shard_map/ppermute | solution.py:58
  313.4 10.7 %copy-start.12 = (f32[128,2048]{1,0:T(8,128)S(1)}, f32[128,2048]{1,0:T(8,128)}, u32[]{:S(2)}) copy-start(f32[128,2048]{1,0:T(8,128)} %get-tuple-element.355) | copy-start | bytes 3145732
  326.2 37.4 %all-to-all-start.4 = ((bf16[8,64,1024]{2,1,0:T(8,128)(2,1)}), bf16[8,64,1024]{2,1,0:T(8,128)(2,1)S(1)}, u32[]{:S(2)}, u32[]{:S(2)}) async-start(bf16[8,64,1024]{2,1,0:T(8,128)(2,1)} %bitcast.160), calls=%async_computation.5 | async-start | bytes 2097152 | tf_op jit(solution)/shard_map/all_to_all | solution.py:115
  330.9 26.0 %collective-permute-start.31 = (bf16[128,2048]{1,0:T(8,128)(2,1)}, bf16[128,2048]{1,0:T(8,128)(2,1)S(1)}, u32[]{:S(2)}, u32[]{:S(2)}) collective-permute-start(bf16[128,2048]{1,0:T(8,128)(2,1)} %add_convert_fusion.4), channel_id=1, source_target_pairs={{0,1},{1,0},{2,3},{3,2},{4,5},{5,4},{6,7},{7,6},{8,9},{9,8},{10,11... | collective-permute-start | bytes 1572872 | tf_op jit(solution)/shard_map/ppermute | solution.py:58
  332.8 24.1 %collective-permute-start.32 = (bf16[128,2048]{1,0:T(8,128)(2,1)}, bf16[128,2048]{1,0:T(8,128)(2,1)S(1)}, u32[]{:S(2)}, u32[]{:S(2)}) collective-permute-start(bf16[128,2048]{1,0:T(8,128)(2,1)} %get-tuple-element.395), channel_id=1, source_target_pairs={{0,4},{4,0},{1,5},{5,1},{2,6},{6,2},{3,7},{7,3},{8,12},{12,8},{9,1... | collective-permute-start | bytes 1572872 | tf_op jit(solution)/shard_map/ppermute | solution.py:58
  334.3 29.3 %collective-permute-start.33 = (bf16[128,2048]{1,0:T(8,128)(2,1)}, bf16[128,2048]{1,0:T(8,128)(2,1)}, u32[]{:S(2)}, u32[]{:S(2)}) collective-permute-start(bf16[128,2048]{1,0:T(8,128)(2,1)} %get-tuple-element.396), channel_id=1, source_target_pairs={{0,4},{4,0},{1,5},{5,1},{2,6},{6,2},{3,7},{7,3},{8,12},{12,8},{9,1... | collective-permute-start | bytes 1572872 | tf_op jit(solution)/shard_map/ppermute | solution.py:58
  334.9 4.2 collective-permute-start.34
  337.3 4.5 %collective-permute-start.35 = (f32[2,4,12,64]{3,1,2,0:T(4,128)S(1)}, f32[2,4,12,64]{3,1,2,0:T(4,128)S(1)}, u32[]{:S(2)}, u32[]{:S(2)}) collective-permute-start(f32[2,4,12,64]{3,1,2,0:T(4,128)S(1)} %bitcast.173), channel_id=1, source_target_pairs={{0,16},{8,24},{16,0},{24,8},{1,17},{9,25},{17,1},{25,9},{2,18},{10... | collective-permute-start | bytes 73736 | tf_op jit(solution)/shard_map/ppermute | solution.py:58
  339.0 3.5 collective-permute-start.36
  366.8 33.1 %all-to-all-start.5 = ((bf16[8,64,1024]{2,1,0:T(8,128)(2,1)}), bf16[8,64,1024]{2,1,0:T(8,128)(2,1)S(1)}, u32[]{:S(2)}, u32[]{:S(2)}) async-start(bf16[8,64,1024]{2,1,0:T(8,128)(2,1)} %bitcast.161), calls=%async_computation.7 | async-start | bytes 2097152 | tf_op jit(solution)/shard_map/all_to_all | solution.py:115
  377.0 22.1 %collective-permute-start.37 = (bf16[128,2048]{1,0:T(8,128)(2,1)S(1)}, bf16[128,2048]{1,0:T(8,128)(2,1)}, u32[]{:S(2)}, u32[]{:S(2)}) collective-permute-start(bf16[128,2048]{1,0:T(8,128)(2,1)S(1)} %copy-done.33), channel_id=1, source_target_pairs={{0,4},{4,0},{1,5},{5,1},{2,6},{6,2},{3,7},{7,3},{8,12},{12,8},{9,1... | collective-permute-start | bytes 1572872 | tf_op jit(solution)/shard_map/ppermute | solution.py:58
  379.1 10.9 %collective-permute-start.38 = (f32[2,12,64]{2,0,1:T(2,128)S(1)}, f32[2,12,64]{2,0,1:T(2,128)S(1)}, u32[]{:S(2)}, u32[]{:S(2)}) collective-permute-start(f32[2,12,64]{2,0,1:T(2,128)S(1)} %bitcast.190), channel_id=1, source_target_pairs={{0,1},{1,0},{2,3},{3,2},{4,5},{5,4},{6,7},{7,6},{8,9},{9,8},{10,11... | collective-permute-start | bytes 18440 | tf_op jit(solution)/shard_map/ppermute | solution.py:58
  380.6 18.4 %collective-permute-start.39 = (f32[2,12,64]{2,0,1:T(2,128)S(1)}, f32[2,12,64]{2,0,1:T(2,128)S(1)}, u32[]{:S(2)}, u32[]{:S(2)}) collective-permute-start(f32[2,12,64]{2,0,1:T(2,128)S(1)} %bitcast.191), channel_id=1, source_target_pairs={{0,2},{1,3},{2,0},{3,1},{4,6},{5,7},{6,4},{7,5},{8,10},{9,11},{10,... | collective-permute-start | bytes 18440 | tf_op jit(solution)/shard_map/ppermute | solution.py:58
  383.0 16.0 %collective-permute-start.40 = (f32[2,12,64]{2,0,1:T(2,128)S(1)}, f32[2,12,64]{2,0,1:T(2,128)S(1)}, u32[]{:S(2)}, u32[]{:S(2)}) collective-permute-start(f32[2,12,64]{2,0,1:T(2,128)S(1)} %bitcast.192), channel_id=1, source_target_pairs={{0,3},{1,2},{2,1},{3,0},{4,7},{5,6},{6,5},{7,4},{8,11},{9,10},{10,... | collective-permute-start | bytes 18440 | tf_op jit(solution)/shard_map/ppermute | solution.py:58
  399.8 23.4 %collective-permute-start.41 = (bf16[128,2048]{1,0:T(8,128)(2,1)}, bf16[128,2048]{1,0:T(8,128)(2,1)}, u32[]{:S(2)}, u32[]{:S(2)}) collective-permute-start(bf16[128,2048]{1,0:T(8,128)(2,1)} %add_convert_fusion.2), channel_id=1, source_target_pairs={{0,1},{1,0},{2,3},{3,2},{4,5},{5,4},{6,7},{7,6},{8,9},{9,8},{10,11... | collective-permute-start | bytes 1572872 | tf_op jit(solution)/shard_map/ppermute | solution.py:58
  399.8 23.4 %collective-permute-start.42 = (bf16[128,2048]{1,0:T(8,128)(2,1)}, bf16[128,2048]{1,0:T(8,128)(2,1)}, u32[]{:S(2)}, u32[]{:S(2)}) collective-permute-start(bf16[128,2048]{1,0:T(8,128)(2,1)} %add_convert_fusion.3), channel_id=1, source_target_pairs={{0,2},{1,3},{2,0},{3,1},{4,6},{5,7},{6,4},{7,5},{8,10},{9,11},{10,... | collective-permute-start | bytes 1572872 | tf_op jit(solution)/shard_map/ppermute | solution.py:58
  401.2 9.1 %collective-permute-start.43 = (f32[12,64]{1,0:T(8,128)S(1)}, f32[12,64]{1,0:T(8,128)S(1)}, u32[]{:S(2)}, u32[]{:S(2)}) collective-permute-start(f32[12,64]{1,0:T(8,128)S(1)} %bitcast.196), channel_id=1, source_target_pairs={{0,4},{4,0},{1,5},{5,1},{2,6},{6,2},{3,7},{7,3},{8,12},{12,8},{9,1... | collective-permute-start | bytes 9224 | tf_op jit(solution)/shard_map/ppermute | solution.py:58
  408.7 14.5 %copy-start.19 = (f32[128,2048]{1,0:T(8,128)S(1)}, f32[128,2048]{1,0:T(8,128)}, u32[]{:S(2)}) copy-start(f32[128,2048]{1,0:T(8,128)} %get-tuple-element.432) | copy-start | bytes 3145732
  (27 other events, 105.1 us)
Sparse Core Ops, SparseCore 0:
  74.4 34.5 all-gather.3
  110.5 34.6 all-gather.5
  183.2 38.6 all-gather.7
  271.7 42.8 reduce-scatter.2
  324.3 42.4 reduce-scatter.4

commit v6 on v5

--- a/solution.py
+++ b/solution.py
@@ -193,10 +193,7 @@
     for i in range(count):
         g_ref[i * rows : (i + 1) * rows, :] = g_refs[i][...]
 
-    def step(at):
-        out_ref[at, :] = mm(g_ref[at, :], w_ref[...]).astype(bf16)
-
-    tiles(g_ref.shape[0], step)
+    out_ref[...] = mm(g_ref[...], w_ref[...]).astype(bf16)
 
 
 def forward_kernel(mlp_ref, w_ref, b_ref, act_ref, slope_ref):

time: 439 us -> 439 us (level)
  transfers between devices with their start and end apart: 55 -> 55, of which waited for: 26 -> 27; matrix products, arithmetic and copies ran while one was open for 11% -> 11% of each run, Pallas kernels for 28% -> 27%
where the time goes in v6:
time: 439 us; the launch traced here: 433 us
  waiting for transfers between devices  160 us (36%)
  Pallas kernels  119 us (27%)
  starting transfers between devices  82.3 us (19%)
  local copies, waits for them, and re-layouts  31.6 us (7%)
  other arithmetic  25.8 us (6%)
  between operations  14.9 us (3%)
    ppermute x44, waiting for transfers between devices, swap(): return lax.ppermute(value, axis, [(i, i ^ distance) for i in range(size)])  151 us
    pallas_call x11, Pallas kernels, call(): pl.pallas_call(kernel, grid=grid, out_shape=[jax.ShapeDtypeStruct(shape,...  104 us
    ppermute x44, starting transfers between devices, swap(): return lax.ppermute(value, axis, [(i, i ^ distance) for i in range(size)])  53.3 us
    pallas_call x2, Pallas kernels, weight_half(): pl.pallas_call(functools.partial(weight_half_kernel, per), grid_spec=pltp...  15 us
    all_to_all x3, starting transfers between devices, collect_group(): return lax.all_to_all(mine, TP, split_axis=0, concat_axis=0, tiled=True)  14.8 us
    convert_element_type x8, other arithmetic, add(): sum((x.astype(f32) for x in arrays[1:]), arrays[0].astype(f32))  12 us
    all_to_all x2, starting transfers between devices, spread_group(): mine = lax.all_to_all(shard, TP, split_axis=0, concat_axis=0, tiled=True)  10.2 us
  transfers between devices with their start and end apart: 55, of which 27 were waited for; matrix products, arithmetic and copies ran while one was open for 11% of the time, Pallas kernels for 27%

profile of v6, /device:TPU:0, one launch (start us, length us, event | category | flops | bytes accessed | tf_op | source)
XLA Modules:
  0.0 433.3 jit_solution(15465402105356657724)
XLA Ops:
  7.2 3.1 collective-permute-start
  10.3 2.6 collective-permute-start.1
  24.3 9.2 %collective-permute-done.refs_1_ = bf16[128,2048]{1,0:T(8,128)(2,1)S(1)} collective-permute-done((bf16[128,2048]{1,0:T(8,128)(2,1)}, bf16[128,2048]{1,0:T(8,128)(2,1)S(1)}, u32[]{:S(2)}, u32[]{:S(2)}) %collective-permute-start) | collective-permute-done | bytes 524320 | tf_op jit(solution)/shard_map/ppermute | solution.py:58
  33.5 2.5 collective-permute-done.1.refs_2_
  37.5 3.6 all-to-all-start
  41.2 1.9 collective-permute-start.4
  44.6 1.9 multiply_sine_fusion
  49.7 22.0 %collective-permute-done.6 = bf16[64,2048]{1,0:T(8,128)(2,1)S(1)} collective-permute-done((bf16[64,2048]{1,0:T(8,128)(2,1)S(1)}, bf16[64,2048]{1,0:T(8,128)(2,1)S(1)}, u32[]{:S(2)}, u32[]{:S(2)}) %collective-permute-start.6) | collective-permute-done | bytes 262176 | tf_op jit(solution)/shard_map/ppermute | solution.py:58
  74.2 4.8 %all-to-all-start.1 = ((bf16[8,64,1024]{2,1,0:T(8,128)(2,1)}), bf16[8,64,1024]{2,1,0:T(8,128)(2,1)}, u32[]{:S(2)}, u32[]{:S(2)}) async-start(bf16[8,64,1024]{2,1,0:T(8,128)(2,1)} %get-tuple-element.246), calls=%async_computation.1 | async-start | bytes 2097152 | tf_op jit(solution)/shard_map/all_to_all | solution.py:101
  81.5 2.0 collective-permute-start.7
  83.6 2.0 collective-permute-start.9
  88.4 21.2 %collective-permute-done.8 = bf16[64,2048]{1,0:T(8,128)(2,1)S(1)} collective-permute-done((bf16[64,2048]{1,0:T(8,128)(2,1)S(1)}, bf16[64,2048]{1,0:T(8,128)(2,1)S(1)}, u32[]{:S(2)}, u32[]{:S(2)}) %collective-permute-start.8) | collective-permute-done | bytes 262176 | tf_op jit(solution)/shard_map/ppermute | solution.py:58
  111.2 2.4 collective-permute-start.14
  115.4 13.4 %shard_map.228 = (bf16[1024,2048]{1,0:T(8,128)(2,1)}, bf16[1024,2048]{1,0:T(8,128)(2,1)}, bf16[1024,256]{1,0:T(8,128)(2,1)}, bf16[1024,512]{1,0:T(8,128)(2,1)}, f32[1024,1]{1,0:T(8,128)}, /*index=5*/f32[1024,1]{1,0:T(8,128)}) custom-call(bf16[128,2048]{1,0:T(8,128)(2,1)} %bitcast.144, bf16[128,2048]{1,0:T(8,128)(2,1)} %copy-done.6, ...), custom_call_target="tpu_custom_call" | custom-call | flops 1 | bytes 1 | tf_op jit(solution)/shard_map/pallas_call | solution.py:124
  128.9 7.6 %collective-permute-done.14.refs_2_ = bf16[128,2048]{1,0:T(8,128)(2,1)} collective-permute-done((bf16[128,2048]{1,0:T(8,128)(2,1)S(1)}, bf16[128,2048]{1,0:T(8,128)(2,1)}, u32[]{:S(2)}, u32[]{:S(2)}) %collective-permute-start.14) | collective-permute-done | bytes 524320 | tf_op jit(solution)/shard_map/ppermute | solution.py:58
  136.4 1.6 collective-permute-start.15
  138.2 11.3 %collective-permute-done.15.refs_6_ = bf16[128,2048]{1,0:T(8,128)(2,1)S(1)} collective-permute-done((bf16[128,2048]{1,0:T(8,128)(2,1)}, bf16[128,2048]{1,0:T(8,128)(2,1)S(1)}, u32[]{:S(2)}, u32[]{:S(2)}) %collective-permute-start.15) | collective-permute-done | bytes 524320 | tf_op jit(solution)/shard_map/ppermute | solution.py:58
  151.0 5.4 %all-to-all-start.2 = ((bf16[8,64,1024]{2,1,0:T(8,128)(2,1)}), bf16[8,64,1024]{2,1,0:T(8,128)(2,1)S(1)}, u32[]{:S(2)}, u32[]{:S(2)}) async-start(bf16[8,64,1024]{2,1,0:T(8,128)(2,1)} %get-tuple-element.290), calls=%async_computation.2 | async-start | bytes 2097152 | tf_op jit(solution)/shard_map/all_to_all | solution.py:101
  156.5 1.6 collective-permute-start.18
  158.1 2.0 collective-permute-start.17
  160.1 11.9 %shard_map.229 = (bf16[1024,1024]{1,0:T(8,128)(2,1)}, f32[1024,1024]{1,0:T(8,128)}) custom-call(bf16[1024,2048]{1,0:T(8,128)(2,1)} %get-tuple-element.291.mlp_ref.refs_0_, bf16[2048,1024]{1,0:T(8,128)(2,1)} %all-gather.6.cloned.1.call-done.w_ref.refs_13_, f32[1,1024]{1,0:T(1,128)} %constant_dynamic-slice_fusion.10.b_ref), custom_call_target="tpu_custom_call" | custom-call | flops 1 | bytes 1 | tf_op jit(solution)/shard_map/pallas_call | solution.py:124
  172.0 8.1 %collective-permute-done.18.refs_1_ = bf16[1024,512]{1,0:T(8,128)(2,1)S(1)} collective-permute-done((bf16[1024,512]{1,0:T(8,128)(2,1)S(1)}, bf16[1024,512]{1,0:T(8,128)(2,1)S(1)}, u32[]{:S(2)}, u32[]{:S(2)}) %collective-permute-start.18) | collective-permute-done | bytes 1048608 | tf_op jit(solution)/shard_map/ppermute | solution.py:58
  180.2 1.9 all-to-all-done.2
  183.6 5.8 %shard_map.230 = (bf16[1024,2048]{1,0:T(8,128)(2,1)}, bf16[1024,256]{1,0:T(8,128)(2,1)}) custom-call(bf16[128,2048]{1,0:T(8,128)(2,1)} %bitcast.149, bf16[128,2048]{1,0:T(8,128)(2,1)} %copy-done.23, bf16[128,2048]{1,0:T(8,128)(2,1)} %collective-permute-done.14.refs_2_, bf16[128,2048]{1,0:T(8,128)(2,1)} %collective-permute-done.16.refs_3_, ...), custom_call_target="tpu_custom_call" | custom-call | flops 1 | bytes 1 | tf_op jit(solution)/shard_map/pallas_call | solution.py:124
  189.4 7.6 %shard_map.231 = (bf16[512,1024]{1,0:T(8,128)(2,1)}, bf16[512,1024]{1,0:T(8,128)(2,1)}) custom-call(s32[2]{0:T(128)} %get-tuple-element.481.place_ref, bf16[1024,2048]{1,0:T(8,128)(2,1)} %get-tuple-element.312.lhs_ref.g_ref.refs_2_, bf16[1024,1024]{1,0:T(8,128)(2,1)} %get-tuple-element.306.rhs_ref.act_ref), custom_call_target="tpu_custom_call" | custom-call | flops 1 | bytes 1 | tf_op jit(solution)/shard_map/pallas_call | solution.py:299
  198.1 7.4 %shard_map.232 = (bf16[512,1024]{1,0:T(8,128)(2,1)}, bf16[512,1024]{1,0:T(8,128)(2,1)}) custom-call(s32[2]{0:T(128)} %pad_add_fusion.2.place_ref, bf16[1024,2048]{1,0:T(8,128)(2,1)} %get-tuple-element.312.lhs_ref.g_ref.refs_2_, bf16[1024,1024]{1,0:T(8,128)(2,1)} %get-tuple-element.306.rhs_ref.act_ref), custom_call_target="tpu_custom_call" | custom-call | flops 1 | bytes 1 | tf_op jit(solution)/shard_map/pallas_call | solution.py:299
  205.5 1.6 add_convert_fusion.1
  208.4 12.7 %shard_map.233 = (bf16[1024,256]{1,0:T(8,128)(2,1)}, bf16[1024,256]{1,0:T(8,128)(2,1)}, bf16[1024,512]{1,0:T(8,128)(2,1)}, bf16[1024,512]{1,0:T(8,128)(2,1)}) custom-call(s32[2]{0:T(128)} %get-tuple-element.480.place_ref, bf16[1024,256]{1,0:T(8,128)(2,1)} %get-tuple-element.264.q_ref, bf16[1024,256]{1,0:T(8,128)(2,1)} %get-tuple-element.319.g_ref, ...), custom_call_target="tpu_custom_call" | custom-call | flops 1 | bytes 1 | tf_op jit(solution)/shard_map/pallas_call | solution.py:124
  222.5 6.2 %shard_map.234 = (bf16[128,2048]{1,0:T(8,128)(2,1)}, bf16[128,2048]{1,0:T(8,128)(2,1)}, bf16[128,2048]{1,0:T(8,128)(2,1)}, bf16[128,2048]{1,0:T(8,128)(2,1)}) custom-call(bf16[1024,256]{1,0:T(8,128)(2,1)} %get-tuple-element.380.att_ref.refs_3_, bf16[1024,1024]{1,0:T(8,128)(2,1)} %get-tuple-element.306.rhs_ref.act_ref, ...), custom_call_target="tpu_custom_call" | custom-call | flops 1 | bytes 1 | tf_op jit(solution)/shard_map/pallas_call | solution.py:124
  228.7 6.9 %shard_map.235 = (f32[128,2048]{1,0:T(8,128)}, f32[128,2048]{1,0:T(8,128)}, f32[128,2048]{1,0:T(8,128)}, f32[128,2048]{1,0:T(8,128)}) custom-call(bf16[1024,256]{1,0:T(8,128)(2,1)} %get-tuple-element.380.att_ref.refs_3_, bf16[1024,1024]{1,0:T(8,128)(2,1)} %get-tuple-element.306.rhs_ref.act_ref, ...), custom_call_target="tpu_custom_call" | custom-call | flops 1 | bytes 1 | tf_op jit(solution)/shard_map/pallas_call | solution.py:124
  235.6 2.3 collective-permute-done.21
  237.9 1.6 add_convert_fusion
  239.5 5.5 %all-to-all-start.3 = ((bf16[8,64,1024]{2,1,0:T(8,128)(2,1)}), bf16[8,64,1024]{2,1,0:T(8,128)(2,1)S(1)}, u32[]{:S(2)}, u32[]{:S(2)}) async-start(bf16[8,64,1024]{2,1,0:T(8,128)(2,1)} %bitcast.26), calls=%async_computation.3 | async-start | bytes 2097152 | tf_op jit(solution)/shard_map/all_to_all | solution.py:115
  245.6 1.9 collective-permute-start.23
  247.5 9.3 %shard_map.236 = (bf16[1024,1024]{1,0:T(8,128)(2,1)}, f32[1,1024]{1,0:T(1,128)}) custom-call(bf16[1024,2048]{1,0:T(8,128)(2,1)} %get-tuple-element.312.lhs_ref.g_ref.refs_2_, bf16[2048,1024]{1,0:T(8,128)(2,1)} %all-gather.8.cloned.1.call-done.down_ref.w_ref, f32[1024,1024]{1,0:T(8,128)} %get-tuple-element.345.slope_ref), custom_call_target="tpu_custom_call" | custom-call | flops 1 | bytes 1 | tf_op jit(solution)/shard_map/pallas_call | solution.py:124
  256.9 8.5 %shard_map.237 = bf16[2048,1024]{1,0:T(8,128)(2,1)} custom-call(bf16[1024,2048]{1,0:T(8,128)(2,1)} %get-tuple-element.291.mlp_ref.refs_0_, bf16[1024,1024]{1,0:T(8,128)(2,1)} %get-tuple-element.354.refs_1_.refs_11_), custom_call_target="tpu_custom_call" | custom-call | flops 1 | bytes 1 | tf_op jit(solution)/shard_map/pallas_call | solution.py:124
  265.4 4.5 %collective-permute-done.22.refs_2_ = bf16[1024,512]{1,0:T(8,128)(2,1)S(1)} collective-permute-done((bf16[1024,512]{1,0:T(8,128)(2,1)}, bf16[1024,512]{1,0:T(8,128)(2,1)S(1)}, u32[]{:S(2)}, u32[]{:S(2)}) %collective-permute-start.22) | collective-permute-done | bytes 1048608 | tf_op jit(solution)/shard_map/ppermute | solution.py:58
  269.9 1.7 all-to-all-done.3
  275.9 4.5 %shard_map.238 = (bf16[1024,768]{1,0:T(8,128)(2,1)}, f32[1,768]{1,0:T(1,128)}) custom-call(bf16[1024,256]{1,0:T(8,128)(2,1)} %get-tuple-element.322.refs_0_, bf16[1024,512]{1,0:T(8,128)(2,1)} %get-tuple-element.323.refs_1_, bf16[1024,512]{1,0:T(8,128)(2,1)} %copy-done.21, f32[1024,128]{1,0:T(8,128)} %maximum_maximum_fusion.refs_11_.refs_3_, ...), custom_call_target="tpu_custom_call" | custom-call | flops 1 | bytes 1 | tf_op jit(solution)/shard_map/pallas_call | solution.py:124
  280.3 15.2 %shard_map.239 = (f32[128,2048]{1,0:T(8,128)}, f32[128,2048]{1,0:T(8,128)}, f32[128,2048]{1,0:T(8,128)}, f32[128,2048]{1,0:T(8,128)}, bf16[128,2048]{1,0:T(8,128...) custom-call(bf16[128,2048]{1,0:T(8,128)(2,1)} %bitcast.145, ...), custom_call_target="tpu_custom_call" | custom-call | flops 1 | bytes 1 | tf_op jit(solution)/shard_map/pallas_call | solution.py:124
  299.3 2.2 collective-permute-start.28
  304.2 9.2 %shard_map.240 = bf16[2048,1024]{1,0:T(8,128)(2,1)} custom-call(bf16[1024,2048]{1,0:T(8,128)(2,1)} %get-tuple-element.378.refs_0_, bf16[1024,768]{1,0:T(8,128)(2,1)} %get-tuple-element.379.refs_10_.refs_1_, bf16[1024,2048]{1,0:T(8,128)(2,1)} %get-tuple-element.312.lhs_ref.g_ref.refs_2_, bf16[1024,256]{1,0:T(8,128)(2,1)} %get-tuple-element.380.att_ref.refs_3_), custom_call_target="tpu_custom_call" | custom-call | flops 1 | bytes 1 | tf_op jit(solution)/shard_map/pallas_call | solution.py:124
  313.4 7.5 %collective-permute-done.27 = bf16[128,2048]{1,0:T(8,128)(2,1)} collective-permute-done((bf16[128,2048]{1,0:T(8,128)(2,1)}, bf16[128,2048]{1,0:T(8,128)(2,1)}, u32[]{:S(2)}, u32[]{:S(2)}) %collective-permute-start.27) | collective-permute-done | bytes 524320 | tf_op jit(solution)/shard_map/ppermute | solution.py:58
  320.9 3.2 collective-permute-done.30
  324.2 2.0 add_convert_fusion.4
  326.2 3.6 all-to-all-start.4
  330.9 1.9 collective-permute-start.31
  337.3 1.7 collective-permute-done.34
  339.0 2.7 fusion.7
  342.5 14.4 %collective-permute-done.31 = bf16[128,2048]{1,0:T(8,128)(2,1)S(1)} collective-permute-done((bf16[128,2048]{1,0:T(8,128)(2,1)}, bf16[128,2048]{1,0:T(8,128)(2,1)S(1)}, u32[]{:S(2)}, u32[]{:S(2)}) %collective-permute-start.31) | collective-permute-done | bytes 524320 | tf_op jit(solution)/shard_map/ppermute | solution.py:58
  358.5 5.1 %collective-permute-done.33 = bf16[128,2048]{1,0:T(8,128)(2,1)} collective-permute-done((bf16[128,2048]{1,0:T(8,128)(2,1)}, bf16[128,2048]{1,0:T(8,128)(2,1)}, u32[]{:S(2)}, u32[]{:S(2)}) %collective-permute-start.33) | collective-permute-done | bytes 524320 | tf_op jit(solution)/shard_map/ppermute | solution.py:58
  363.6 3.2 reduce-scatter.5.cloned.1.call-done
  366.7 5.7 %all-to-all-start.5 = ((bf16[8,64,1024]{2,1,0:T(8,128)(2,1)}), bf16[8,64,1024]{2,1,0:T(8,128)(2,1)S(1)}, u32[]{:S(2)}, u32[]{:S(2)}) async-start(bf16[8,64,1024]{2,1,0:T(8,128)(2,1)} %bitcast.161), calls=%async_computation.7 | async-start | bytes 2097152 | tf_op jit(solution)/shard_map/all_to_all | solution.py:115
  372.5 2.4 add_convert_fusion.2
  375.0 2.0 add_convert_fusion.3
  377.0 2.0 collective-permute-start.37
  380.6 2.4 collective-permute-start.39
  385.3 4.7 %collective-permute-done.38 = f32[2,12,64]{2,0,1:T(2,128)S(1)} collective-permute-done((f32[2,12,64]{2,0,1:T(2,128)S(1)}, f32[2,12,64]{2,0,1:T(2,128)S(1)}, u32[]{:S(2)}, u32[]{:S(2)}) %collective-permute-start.38) | collective-permute-done | bytes 6176 | tf_op jit(solution)/shard_map/ppermute | solution.py:58
  390.0 9.0 %collective-permute-done.39 = f32[2,12,64]{2,0,1:T(2,128)S(1)} collective-permute-done((f32[2,12,64]{2,0,1:T(2,128)S(1)}, f32[2,12,64]{2,0,1:T(2,128)S(1)}, u32[]{:S(2)}, u32[]{:S(2)}) %collective-permute-start.39) | collective-permute-done | bytes 6176 | tf_op jit(solution)/shard_map/ppermute | solution.py:58
  401.2 1.6 collective-permute-start.43
  405.2 2.6 reshape.277
  408.7 1.6 copy.76
  412.2 11.1 %collective-permute-done.41 = bf16[128,2048]{1,0:T(8,128)(2,1)} collective-permute-done((bf16[128,2048]{1,0:T(8,128)(2,1)}, bf16[128,2048]{1,0:T(8,128)(2,1)}, u32[]{:S(2)}, u32[]{:S(2)}) %collective-permute-start.41) | collective-permute-done | bytes 524320 | tf_op jit(solution)/shard_map/ppermute | solution.py:58
  423.3 1.9 fusion.24
  (247 shorter events, 67.6 us)
Async XLA Ops:
  7.2 26.3 %collective-permute-start = (bf16[128,2048]{1,0:T(8,128)(2,1)}, bf16[128,2048]{1,0:T(8,128)(2,1)S(1)}, u32[]{:S(2)}, u32[]{:S(2)}) collective-permute-start(bf16[128,2048]{1,0:T(8,128)(2,1)} %bitcast.141), channel_id=1, source_target_pairs={{0,1},{1,0},{2,3},{3,2},{4,5},{5,4},{6,7},{7,6},{8,9},{9,8},{10,11... | collective-permute-start | bytes 1572872 | tf_op jit(solution)/shard_map/ppermute | solution.py:58
  10.3 25.8 %collective-permute-start.1 = (bf16[128,2048]{1,0:T(8,128)(2,1)}, bf16[128,2048]{1,0:T(8,128)(2,1)S(1)}, u32[]{:S(2)}, u32[]{:S(2)}) collective-permute-start(bf16[128,2048]{1,0:T(8,128)(2,1)} %bitcast.142), channel_id=1, source_target_pairs={{0,2},{1,3},{2,0},{3,1},{4,6},{5,7},{6,4},{7,5},{8,10},{9,11},{10,... | collective-permute-start | bytes 1572872 | tf_op jit(solution)/shard_map/ppermute | solution.py:58
  12.9 23.2 %collective-permute-start.2 = (bf16[128,2048]{1,0:T(8,128)(2,1)}, bf16[128,2048]{1,0:T(8,128)(2,1)}, u32[]{:S(2)}, u32[]{:S(2)}) collective-permute-start(bf16[128,2048]{1,0:T(8,128)(2,1)} %bitcast.143), channel_id=1, source_target_pairs={{0,4},{4,0},{1,5},{5,1},{2,6},{6,2},{3,7},{7,3},{8,12},{12,8},{9,1... | collective-permute-start | bytes 1572872 | tf_op jit(solution)/shard_map/ppermute | solution.py:58
  14.3 23.2 %collective-permute-start.3 = (bf16[128,2048]{1,0:T(8,128)(2,1)}, bf16[128,2048]{1,0:T(8,128)(2,1)}, u32[]{:S(2)}, u32[]{:S(2)}) collective-permute-start(bf16[128,2048]{1,0:T(8,128)(2,1)} %bitcast.148), channel_id=1, source_target_pairs={{0,4},{4,0},{1,5},{5,1},{2,6},{6,2},{3,7},{7,3},{8,12},{12,8},{9,1... | collective-permute-start | bytes 1572872 | tf_op jit(solution)/shard_map/ppermute | solution.py:58
  33.5 13.1 %copy-start.6 = (bf16[128,2048]{1,0:T(8,128)(2,1)}, bf16[128,2048]{1,0:T(8,128)(2,1)S(1)}, u32[]{:S(2)}) copy-start(bf16[128,2048]{1,0:T(8,128)(2,1)S(1)} %collective-permute-done.refs_1_) | copy-start | bytes 1572868
  36.1 47.4 %copy-start.1 = (bf16[128,2048]{1,0:T(8,128)(2,1)}, bf16[128,2048]{1,0:T(8,128)(2,1)S(1)}, u32[]{:S(2)}) copy-start(bf16[128,2048]{1,0:T(8,128)(2,1)S(1)} %collective-permute-done.1.refs_2_) | copy-start | bytes 1572868
  37.5 34.9 %all-to-all-start = ((bf16[8,72,1024]{2,1,0:T(8,128)(2,1)}), bf16[8,72,1024]{2,1,0:T(8,128)(2,1)S(1)}, u32[]{:S(2)}, u32[]{:S(2)}) async-start(bf16[8,72,1024]{2,1,0:T(8,128)(2,1)} %pad_maximum_fusion), calls=%async_computation | async-start | bytes 2359296 | tf_op jit(solution)/shard_map/all_to_all | solution.py:587
  41.1 73.5 %all-gather.4.cloned.1.call-start = ((), (), s32[]{:S(2)}) async-start(), calls=%async_computation.8 | async-start | bytes 5242880 | tf_op jit(solution)/shard_map/all_gather | solution.py:106
  41.2 31.2 %collective-permute-start.4 = (bf16[128,2048]{1,0:T(8,128)(2,1)S(1)}, bf16[128,2048]{1,0:T(8,128)(2,1)S(1)}, u32[]{:S(2)}, u32[]{:S(2)}) collective-permute-start(bf16[128,2048]{1,0:T(8,128)(2,1)S(1)} %collective-permute-done.1.refs_2_), channel_id=1, source_target_pairs={{0,1},{1,0},{2,3},{3,2},{4,5},{5,4},{6,7},{7,6},{8,9},{9,8},{10,11... | collective-permute-start | bytes 1572872 | tf_op jit(solution)/shard_map/ppermute | solution.py:58
  43.1 29.3 %collective-permute-start.5 = (bf16[128,2048]{1,0:T(8,128)(2,1)S(1)}, bf16[128,2048]{1,0:T(8,128)(2,1)}, u32[]{:S(2)}, u32[]{:S(2)}) collective-permute-start(bf16[128,2048]{1,0:T(8,128)(2,1)S(1)} %collective-permute-done.refs_1_), channel_id=1, source_target_pairs={{0,4},{4,0},{1,5},{5,1},{2,6},{6,2},{3,7},{7,3},{8,12},{12,8},{9,1... | collective-permute-start | bytes 1572872 | tf_op jit(solution)/shard_map/ppermute | solution.py:58
  46.6 25.0 %collective-permute-start.6 = (bf16[64,2048]{1,0:T(8,128)(2,1)S(1)}, bf16[64,2048]{1,0:T(8,128)(2,1)S(1)}, u32[]{:S(2)}, u32[]{:S(2)}) collective-permute-start(bf16[64,2048]{1,0:T(8,128)(2,1)S(1)} %slice.63), channel_id=1, source_target_pairs={{0,4},{4,0},{1,5},{5,1},{2,6},{6,2},{3,7},{7,3},{8,12},{12,8},{9,1... | collective-permute-start | bytes 786440 | tf_op jit(solution)/shard_map/ppermute | solution.py:58
  74.2 35.4 %all-to-all-start.1 = ((bf16[8,64,1024]{2,1,0:T(8,128)(2,1)}), bf16[8,64,1024]{2,1,0:T(8,128)(2,1)}, u32[]{:S(2)}, u32[]{:S(2)}) async-start(bf16[8,64,1024]{2,1,0:T(8,128)(2,1)} %get-tuple-element.246), calls=%async_computation.1 | async-start | bytes 2097152 | tf_op jit(solution)/shard_map/all_to_all | solution.py:101
  79.0 81.1 %all-gather.6.cloned.1.call-start = ((), (), s32[]{:S(2)}) async-start(), calls=%async_computation.9 | async-start | bytes 5242880 | tf_op jit(solution)/shard_map/all_gather | solution.py:106
  79.3 4.3 collective-permute-start.12
  80.2 5.4 %collective-permute-start.11 = (bf16[8,768]{1,0:T(8,128)(2,1)S(1)}, bf16[8,768]{1,0:T(8,128)(2,1)S(1)}, u32[]{:S(2)}, u32[]{:S(2)}) collective-permute-start(bf16[8,768]{1,0:T(8,128)(2,1)S(1)} %bitcast.177), channel_id=1, source_target_pairs={{0,16},{8,24},{16,0},{24,8},{1,17},{9,25},{17,1},{25,9},{2,18},{10... | collective-permute-start | bytes 36872 | tf_op jit(solution)/shard_map/ppermute | solution.py:58
  81.0 4.6 %collective-permute-start.10 = (bf16[8,768]{1,0:T(8,128)(2,1)S(1)}, bf16[8,768]{1,0:T(8,128)(2,1)S(1)}, u32[]{:S(2)}, u32[]{:S(2)}) collective-permute-start(bf16[8,768]{1,0:T(8,128)(2,1)S(1)} %bitcast.178), channel_id=1, source_target_pairs={{0,8},{8,0},{16,24},{24,16},{1,9},{9,1},{17,25},{25,17},{2,10},{10... | collective-permute-start | bytes 36872 | tf_op jit(solution)/shard_map/ppermute | solution.py:58
  81.5 28.1 %collective-permute-start.7 = (bf16[128,2048]{1,0:T(8,128)(2,1)S(1)}, bf16[128,2048]{1,0:T(8,128)(2,1)S(1)}, u32[]{:S(2)}, u32[]{:S(2)}) collective-permute-start(bf16[128,2048]{1,0:T(8,128)(2,1)S(1)} %copy-done.8), channel_id=1, source_target_pairs={{0,4},{4,0},{1,5},{5,1},{2,6},{6,2},{3,7},{7,3},{8,12},{12,8},{9,1... | collective-permute-start | bytes 1572872 | tf_op jit(solution)/shard_map/ppermute | solution.py:58
  83.5 26.1 %collective-permute-start.8 = (bf16[64,2048]{1,0:T(8,128)(2,1)S(1)}, bf16[64,2048]{1,0:T(8,128)(2,1)S(1)}, u32[]{:S(2)}, u32[]{:S(2)}) collective-permute-start(bf16[64,2048]{1,0:T(8,128)(2,1)S(1)} %slice.64), channel_id=1, source_target_pairs={{0,4},{4,0},{1,5},{5,1},{2,6},{6,2},{3,7},{7,3},{8,12},{12,8},{9,1... | collective-permute-start | bytes 786440 | tf_op jit(solution)/shard_map/ppermute | solution.py:58
  83.6 26.0 %collective-permute-start.9 = (bf16[128,2048]{1,0:T(8,128)(2,1)S(1)}, bf16[128,2048]{1,0:T(8,128)(2,1)S(1)}, u32[]{:S(2)}, u32[]{:S(2)}) collective-permute-start(bf16[128,2048]{1,0:T(8,128)(2,1)S(1)} %bitcast.150), channel_id=1, source_target_pairs={{0,1},{1,0},{2,3},{3,2},{4,5},{5,4},{6,7},{7,6},{8,9},{9,8},{10,11... | collective-permute-start | bytes 1572872 | tf_op jit(solution)/shard_map/ppermute | solution.py:58
  109.6 19.2 %copy-start.23 = (bf16[128,2048]{1,0:T(8,128)(2,1)}, bf16[128,2048]{1,0:T(8,128)(2,1)S(1)}, u32[]{:S(2)}) copy-start(bf16[128,2048]{1,0:T(8,128)(2,1)S(1)} %collective-permute-done.9.refs_1_) | copy-start | bytes 1572868
  110.3 18.5 %collective-permute-start.13 = (bf16[128,2048]{1,0:T(8,128)(2,1)S(1)}, bf16[128,2048]{1,0:T(8,128)(2,1)S(1)}, u32[]{:S(2)}, u32[]{:S(2)}) collective-permute-start(bf16[128,2048]{1,0:T(8,128)(2,1)S(1)} %collective-permute-done.9.refs_1_), channel_id=1, source_target_pairs={{0,4},{4,0},{1,5},{5,1},{2,6},{6,2},{3,7},{7,3},{8,12},{12,8},{9,1... | collective-permute-start | bytes 1572872 | tf_op jit(solution)/shard_map/ppermute | solution.py:58
  111.2 25.2 %collective-permute-start.14 = (bf16[128,2048]{1,0:T(8,128)(2,1)S(1)}, bf16[128,2048]{1,0:T(8,128)(2,1)}, u32[]{:S(2)}, u32[]{:S(2)}) collective-permute-start(bf16[128,2048]{1,0:T(8,128)(2,1)S(1)} %bitcast.151), channel_id=1, source_target_pairs={{0,2},{1,3},{2,0},{3,1},{4,6},{5,7},{6,4},{7,5},{8,10},{9,11},{10,... | collective-permute-start | bytes 1572872 | tf_op jit(solution)/shard_map/ppermute | solution.py:58
  128.8 27.7 %copy-start.11 = (bf16[1024,512]{1,0:T(8,128)(2,1)S(1)}, bf16[1024,512]{1,0:T(8,128)(2,1)}, u32[]{:S(2)}) copy-start(bf16[1024,512]{1,0:T(8,128)(2,1)} %get-tuple-element.320.refs_0_) | copy-start | bytes 3145732
  128.8 27.6 %copy-start.26 = (bf16[128,2048]{1,0:T(8,128)(2,1)}, bf16[128,2048]{1,0:T(8,128)(2,1)S(1)}, u32[]{:S(2)}) copy-start(bf16[128,2048]{1,0:T(8,128)(2,1)S(1)} %collective-permute-done.13.refs_5_) | copy-start | bytes 1572868
  136.4 13.1 %collective-permute-start.15 = (bf16[128,2048]{1,0:T(8,128)(2,1)}, bf16[128,2048]{1,0:T(8,128)(2,1)S(1)}, u32[]{:S(2)}, u32[]{:S(2)}) collective-permute-start(bf16[128,2048]{1,0:T(8,128)(2,1)} %collective-permute-done.14.refs_2_), channel_id=1, source_target_pairs={{0,4},{4,0},{1,5},{5,1},{2,6},{6,2},{3,7},{7,3},{8,12},{12,8},{9,1... | collective-permute-start | bytes 1572872 | tf_op jit(solution)/shard_map/ppermute | solution.py:58
  138.0 13.0 %collective-permute-start.16 = (bf16[128,2048]{1,0:T(8,128)(2,1)}, bf16[128,2048]{1,0:T(8,128)(2,1)}, u32[]{:S(2)}, u32[]{:S(2)}) collective-permute-start(bf16[128,2048]{1,0:T(8,128)(2,1)} %collective-permute-done.14.refs_2_), channel_id=1, source_target_pairs={{0,1},{1,0},{2,3},{3,2},{4,5},{5,4},{6,7},{7,6},{8,9},{9,8},{10,11... | collective-permute-start | bytes 1572872 | tf_op jit(solution)/shard_map/ppermute | solution.py:58
  151.0 31.1 %all-to-all-start.2 = ((bf16[8,64,1024]{2,1,0:T(8,128)(2,1)}), bf16[8,64,1024]{2,1,0:T(8,128)(2,1)S(1)}, u32[]{:S(2)}, u32[]{:S(2)}) async-start(bf16[8,64,1024]{2,1,0:T(8,128)(2,1)} %get-tuple-element.290), calls=%async_computation.2 | async-start | bytes 2097152 | tf_op jit(solution)/shard_map/all_to_all | solution.py:101
  156.4 66.1 %all-gather.8.cloned.1.call-start = ((), (), s32[]{:S(2)}) async-start(), calls=%async_computation.10 | async-start | bytes 5242880 | tf_op jit(solution)/shard_map/all_gather | solution.py:106
  156.5 23.7 %collective-permute-start.18 = (bf16[1024,512]{1,0:T(8,128)(2,1)S(1)}, bf16[1024,512]{1,0:T(8,128)(2,1)S(1)}, u32[]{:S(2)}, u32[]{:S(2)}) collective-permute-start(bf16[1024,512]{1,0:T(8,128)(2,1)S(1)} %copy-done.11), channel_id=1, source_target_pairs={{0,8},{8,0},{1,9},{9,1},{2,10},{10,2},{3,11},{11,3},{4,12},{12,4},... | collective-permute-start | bytes 3145736 | tf_op jit(solution)/shard_map/ppermute | solution.py:58
  158.1 22.1 %collective-permute-start.17 = (bf16[128,2048]{1,0:T(8,128)(2,1)}, bf16[128,2048]{1,0:T(8,128)(2,1)}, u32[]{:S(2)}, u32[]{:S(2)}) collective-permute-start(bf16[128,2048]{1,0:T(8,128)(2,1)} %collective-permute-done.16.refs_3_), channel_id=1, source_target_pairs={{0,4},{4,0},{1,5},{5,1},{2,6},{6,2},{3,7},{7,3},{8,12},{12,8},{9,1... | collective-permute-start | bytes 1572872 | tf_op jit(solution)/shard_map/ppermute | solution.py:58
  180.2 16.8 %copy-start.15 = (bf16[1024,512]{1,0:T(8,128)(2,1)}, bf16[1024,512]{1,0:T(8,128)(2,1)S(1)}, u32[]{:S(2)}) copy-start(bf16[1024,512]{1,0:T(8,128)(2,1)S(1)} %collective-permute-done.18.refs_1_) | copy-start | bytes 3145732
  197.0 8.5 %collective-permute-start.19 = (bf16[512,1024]{1,0:T(8,128)(2,1)}, bf16[512,1024]{1,0:T(8,128)(2,1)S(1)}, u32[]{:S(2)}, u32[]{:S(2)}) collective-permute-start(bf16[512,1024]{1,0:T(8,128)(2,1)} %get-tuple-element.310), channel_id=1, source_target_pairs={{0,16},{16,0},{1,17},{17,1},{2,18},{18,2},{3,19},{19,3},{4,20},{20... | collective-permute-start | bytes 3145736 | tf_op jit(solution)/shard_map/ppermute | solution.py:58
  197.0 8.5 %collective-permute-start.20 = (bf16[512,1024]{1,0:T(8,128)(2,1)}, bf16[512,1024]{1,0:T(8,128)(2,1)S(1)}, u32[]{:S(2)}, u32[]{:S(2)}) collective-permute-start(bf16[512,1024]{1,0:T(8,128)(2,1)} %get-tuple-element.311), channel_id=1, source_target_pairs={{0,16},{16,0},{1,17},{17,1},{2,18},{18,2},{3,19},{19,3},{4,20},{20... | collective-permute-start | bytes 3145736 | tf_op jit(solution)/shard_map/ppermute | solution.py:58
  207.1 30.7 %collective-permute-start.21 = (bf16[512,1024]{1,0:T(8,128)(2,1)S(1)}, bf16[512,1024]{1,0:T(8,128)(2,1)S(1)}, u32[]{:S(2)}, u32[]{:S(2)}) collective-permute-start(bf16[512,1024]{1,0:T(8,128)(2,1)S(1)} %add_convert_fusion.1), channel_id=1, source_target_pairs={{0,8},{8,0},{1,9},{9,1},{2,10},{10,2},{3,11},{11,3},{4,12},{12,4},... | collective-permute-start | bytes 3145736 | tf_op jit(solution)/shard_map/ppermute | solution.py:58
  239.5 32.1 %all-to-all-start.3 = ((bf16[8,64,1024]{2,1,0:T(8,128)(2,1)}), bf16[8,64,1024]{2,1,0:T(8,128)(2,1)S(1)}, u32[]{:S(2)}, u32[]{:S(2)}) async-start(bf16[8,64,1024]{2,1,0:T(8,128)(2,1)} %bitcast.26), calls=%async_computation.3 | async-start | bytes 2097152 | tf_op jit(solution)/shard_map/all_to_all | solution.py:115
  245.0 79.2 %reduce-scatter.3.cloned.1.call-start = ((), (), s32[]{:S(2)}) async-start(), calls=%async_computation.11 | async-start | bytes 5242880 | tf_op jit(solution)/shard_map/reduce_scatter | solution.py:110
  245.0 24.9 %collective-permute-start.22 = (bf16[1024,512]{1,0:T(8,128)(2,1)}, bf16[1024,512]{1,0:T(8,128)(2,1)S(1)}, u32[]{:S(2)}, u32[]{:S(2)}) collective-permute-start(bf16[1024,512]{1,0:T(8,128)(2,1)} %get-tuple-element.337), channel_id=1, source_target_pairs={{0,8},{8,0},{1,9},{9,1},{2,10},{10,2},{3,11},{11,3},{4,12},{12,4},... | collective-permute-start | bytes 3145736 | tf_op jit(solution)/shard_map/ppermute | solution.py:58
  245.6 24.3 %collective-permute-start.23 = (bf16[128,2048]{1,0:T(8,128)(2,1)}, bf16[128,2048]{1,0:T(8,128)(2,1)}, u32[]{:S(2)}, u32[]{:S(2)}) collective-permute-start(bf16[128,2048]{1,0:T(8,128)(2,1)} %get-tuple-element.344), channel_id=1, source_target_pairs={{0,4},{4,0},{1,5},{5,1},{2,6},{6,2},{3,7},{7,3},{8,12},{12,8},{9,1... | collective-permute-start | bytes 1572872 | tf_op jit(solution)/shard_map/ppermute | solution.py:58
  271.6 95.1 %reduce-scatter.5.cloned.1.call-start = ((), (), s32[]{:S(2)}) async-start(), calls=%async_computation.12 | async-start | bytes 5242880 | tf_op jit(solution)/shard_map/reduce_scatter | solution.py:110
  272.9 22.7 %collective-permute-start.24 = (bf16[128,2048]{1,0:T(8,128)(2,1)S(1)}, bf16[128,2048]{1,0:T(8,128)(2,1)S(1)}, u32[]{:S(2)}, u32[]{:S(2)}) collective-permute-start(bf16[128,2048]{1,0:T(8,128)(2,1)S(1)} %add_convert_fusion.7), channel_id=1, source_target_pairs={{0,1},{1,0},{2,3},{3,2},{4,5},{5,4},{6,7},{7,6},{8,9},{9,8},{10,11... | collective-permute-start | bytes 1572872 | tf_op jit(solution)/shard_map/ppermute | solution.py:58
  273.8 21.8 %collective-permute-start.25 = (bf16[128,2048]{1,0:T(8,128)(2,1)S(1)}, bf16[128,2048]{1,0:T(8,128)(2,1)S(1)}, u32[]{:S(2)}, u32[]{:S(2)}) collective-permute-start(bf16[128,2048]{1,0:T(8,128)(2,1)S(1)} %copy-done.35), channel_id=1, source_target_pairs={{0,4},{4,0},{1,5},{5,1},{2,6},{6,2},{3,7},{7,3},{8,12},{12,8},{9,1... | collective-permute-start | bytes 1572872 | tf_op jit(solution)/shard_map/ppermute | solution.py:58
  275.3 21.8 %collective-permute-start.26 = (bf16[128,2048]{1,0:T(8,128)(2,1)S(1)}, bf16[128,2048]{1,0:T(8,128)(2,1)S(1)}, u32[]{:S(2)}, u32[]{:S(2)}) collective-permute-start(bf16[128,2048]{1,0:T(8,128)(2,1)S(1)} %copy-done.34), channel_id=1, source_target_pairs={{0,4},{4,0},{1,5},{5,1},{2,6},{6,2},{3,7},{7,3},{8,12},{12,8},{9,1... | collective-permute-start | bytes 1572872 | tf_op jit(solution)/shard_map/ppermute | solution.py:58
  280.3 16.7 %copy-start.14 = (f32[128,2048]{1,0:T(8,128)S(1)}, f32[128,2048]{1,0:T(8,128)}, u32[]{:S(2)}) copy-start(f32[128,2048]{1,0:T(8,128)} %get-tuple-element.367) | copy-start | bytes 3145732
  298.2 22.8 %collective-permute-start.27 = (bf16[128,2048]{1,0:T(8,128)(2,1)}, bf16[128,2048]{1,0:T(8,128)(2,1)}, u32[]{:S(2)}, u32[]{:S(2)}) collective-permute-start(bf16[128,2048]{1,0:T(8,128)(2,1)} %add_convert_fusion.5), channel_id=1, source_target_pairs={{0,1},{1,0},{2,3},{3,2},{4,5},{5,4},{6,7},{7,6},{8,9},{9,8},{10,11... | collective-permute-start | bytes 1572872 | tf_op jit(solution)/shard_map/ppermute | solution.py:58
  299.3 21.6 %collective-permute-start.28 = (bf16[128,2048]{1,0:T(8,128)(2,1)S(1)}, bf16[128,2048]{1,0:T(8,128)(2,1)}, u32[]{:S(2)}, u32[]{:S(2)}) collective-permute-start(bf16[128,2048]{1,0:T(8,128)(2,1)S(1)} %add_convert_fusion.6), channel_id=1, source_target_pairs={{0,2},{1,3},{2,0},{3,1},{4,6},{5,7},{6,4},{7,5},{8,10},{9,11},{10,... | collective-permute-start | bytes 1572872 | tf_op jit(solution)/shard_map/ppermute | solution.py:58
  301.5 19.5 %collective-permute-start.29 = (bf16[128,2048]{1,0:T(8,128)(2,1)}, bf16[128,2048]{1,0:T(8,128)(2,1)}, u32[]{:S(2)}, u32[]{:S(2)}) collective-permute-start(bf16[128,2048]{1,0:T(8,128)(2,1)} %get-tuple-element.376), channel_id=1, source_target_pairs={{0,4},{4,0},{1,5},{5,1},{2,6},{6,2},{3,7},{7,3},{8,12},{12,8},{9,1... | collective-permute-start | bytes 1572872 | tf_op jit(solution)/shard_map/ppermute | solution.py:58
  302.6 21.5 %collective-permute-start.30 = (bf16[128,2048]{1,0:T(8,128)(2,1)}, bf16[128,2048]{1,0:T(8,128)(2,1)}, u32[]{:S(2)}, u32[]{:S(2)}) collective-permute-start(bf16[128,2048]{1,0:T(8,128)(2,1)} %get-tuple-element.377), channel_id=1, source_target_pairs={{0,4},{4,0},{1,5},{5,1},{2,6},{6,2},{3,7},{7,3},{8,12},{12,8},{9,1... | collective-permute-start | bytes 1572872 | tf_op jit(solution)/shard_map/ppermute | solution.py:58
  313.4 10.7 %copy-start.12 = (f32[128,2048]{1,0:T(8,128)S(1)}, f32[128,2048]{1,0:T(8,128)}, u32[]{:S(2)}) copy-start(f32[128,2048]{1,0:T(8,128)} %get-tuple-element.355) | copy-start | bytes 3145732
  326.2 37.4 %all-to-all-start.4 = ((bf16[8,64,1024]{2,1,0:T(8,128)(2,1)}), bf16[8,64,1024]{2,1,0:T(8,128)(2,1)S(1)}, u32[]{:S(2)}, u32[]{:S(2)}) async-start(bf16[8,64,1024]{2,1,0:T(8,128)(2,1)} %bitcast.160), calls=%async_computation.5 | async-start | bytes 2097152 | tf_op jit(solution)/shard_map/all_to_all | solution.py:115
  330.9 26.0 %collective-permute-start.31 = (bf16[128,2048]{1,0:T(8,128)(2,1)}, bf16[128,2048]{1,0:T(8,128)(2,1)S(1)}, u32[]{:S(2)}, u32[]{:S(2)}) collective-permute-start(bf16[128,2048]{1,0:T(8,128)(2,1)} %add_convert_fusion.4), channel_id=1, source_target_pairs={{0,1},{1,0},{2,3},{3,2},{4,5},{5,4},{6,7},{7,6},{8,9},{9,8},{10,11... | collective-permute-start | bytes 1572872 | tf_op jit(solution)/shard_map/ppermute | solution.py:58
  332.8 24.1 %collective-permute-start.32 = (bf16[128,2048]{1,0:T(8,128)(2,1)}, bf16[128,2048]{1,0:T(8,128)(2,1)S(1)}, u32[]{:S(2)}, u32[]{:S(2)}) collective-permute-start(bf16[128,2048]{1,0:T(8,128)(2,1)} %get-tuple-element.395), channel_id=1, source_target_pairs={{0,4},{4,0},{1,5},{5,1},{2,6},{6,2},{3,7},{7,3},{8,12},{12,8},{9,1... | collective-permute-start | bytes 1572872 | tf_op jit(solution)/shard_map/ppermute | solution.py:58
  334.3 29.3 %collective-permute-start.33 = (bf16[128,2048]{1,0:T(8,128)(2,1)}, bf16[128,2048]{1,0:T(8,128)(2,1)}, u32[]{:S(2)}, u32[]{:S(2)}) collective-permute-start(bf16[128,2048]{1,0:T(8,128)(2,1)} %get-tuple-element.396), channel_id=1, source_target_pairs={{0,4},{4,0},{1,5},{5,1},{2,6},{6,2},{3,7},{7,3},{8,12},{12,8},{9,1... | collective-permute-start | bytes 1572872 | tf_op jit(solution)/shard_map/ppermute | solution.py:58
  334.9 4.2 collective-permute-start.34
  337.2 4.5 %collective-permute-start.35 = (f32[2,4,12,64]{3,1,2,0:T(4,128)S(1)}, f32[2,4,12,64]{3,1,2,0:T(4,128)S(1)}, u32[]{:S(2)}, u32[]{:S(2)}) collective-permute-start(f32[2,4,12,64]{3,1,2,0:T(4,128)S(1)} %bitcast.173), channel_id=1, source_target_pairs={{0,16},{8,24},{16,0},{24,8},{1,17},{9,25},{17,1},{25,9},{2,18},{10... | collective-permute-start | bytes 73736 | tf_op jit(solution)/shard_map/ppermute | solution.py:58
  339.0 3.5 collective-permute-start.36
  366.7 33.1 %all-to-all-start.5 = ((bf16[8,64,1024]{2,1,0:T(8,128)(2,1)}), bf16[8,64,1024]{2,1,0:T(8,128)(2,1)S(1)}, u32[]{:S(2)}, u32[]{:S(2)}) async-start(bf16[8,64,1024]{2,1,0:T(8,128)(2,1)} %bitcast.161), calls=%async_computation.7 | async-start | bytes 2097152 | tf_op jit(solution)/shard_map/all_to_all | solution.py:115
  377.0 22.1 %collective-permute-start.37 = (bf16[128,2048]{1,0:T(8,128)(2,1)S(1)}, bf16[128,2048]{1,0:T(8,128)(2,1)}, u32[]{:S(2)}, u32[]{:S(2)}) collective-permute-start(bf16[128,2048]{1,0:T(8,128)(2,1)S(1)} %copy-done.33), channel_id=1, source_target_pairs={{0,4},{4,0},{1,5},{5,1},{2,6},{6,2},{3,7},{7,3},{8,12},{12,8},{9,1... | collective-permute-start | bytes 1572872 | tf_op jit(solution)/shard_map/ppermute | solution.py:58
  379.1 10.9 %collective-permute-start.38 = (f32[2,12,64]{2,0,1:T(2,128)S(1)}, f32[2,12,64]{2,0,1:T(2,128)S(1)}, u32[]{:S(2)}, u32[]{:S(2)}) collective-permute-start(f32[2,12,64]{2,0,1:T(2,128)S(1)} %bitcast.190), channel_id=1, source_target_pairs={{0,1},{1,0},{2,3},{3,2},{4,5},{5,4},{6,7},{7,6},{8,9},{9,8},{10,11... | collective-permute-start | bytes 18440 | tf_op jit(solution)/shard_map/ppermute | solution.py:58
  380.6 18.4 %collective-permute-start.39 = (f32[2,12,64]{2,0,1:T(2,128)S(1)}, f32[2,12,64]{2,0,1:T(2,128)S(1)}, u32[]{:S(2)}, u32[]{:S(2)}) collective-permute-start(f32[2,12,64]{2,0,1:T(2,128)S(1)} %bitcast.191), channel_id=1, source_target_pairs={{0,2},{1,3},{2,0},{3,1},{4,6},{5,7},{6,4},{7,5},{8,10},{9,11},{10,... | collective-permute-start | bytes 18440 | tf_op jit(solution)/shard_map/ppermute | solution.py:58
  383.0 16.1 %collective-permute-start.40 = (f32[2,12,64]{2,0,1:T(2,128)S(1)}, f32[2,12,64]{2,0,1:T(2,128)S(1)}, u32[]{:S(2)}, u32[]{:S(2)}) collective-permute-start(f32[2,12,64]{2,0,1:T(2,128)S(1)} %bitcast.192), channel_id=1, source_target_pairs={{0,3},{1,2},{2,1},{3,0},{4,7},{5,6},{6,5},{7,4},{8,11},{9,10},{10,... | collective-permute-start | bytes 18440 | tf_op jit(solution)/shard_map/ppermute | solution.py:58
  399.8 23.5 %collective-permute-start.41 = (bf16[128,2048]{1,0:T(8,128)(2,1)}, bf16[128,2048]{1,0:T(8,128)(2,1)}, u32[]{:S(2)}, u32[]{:S(2)}) collective-permute-start(bf16[128,2048]{1,0:T(8,128)(2,1)} %add_convert_fusion.2), channel_id=1, source_target_pairs={{0,1},{1,0},{2,3},{3,2},{4,5},{5,4},{6,7},{7,6},{8,9},{9,8},{10,11... | collective-permute-start | bytes 1572872 | tf_op jit(solution)/shard_map/ppermute | solution.py:58
  399.8 23.5 %collective-permute-start.42 = (bf16[128,2048]{1,0:T(8,128)(2,1)}, bf16[128,2048]{1,0:T(8,128)(2,1)}, u32[]{:S(2)}, u32[]{:S(2)}) collective-permute-start(bf16[128,2048]{1,0:T(8,128)(2,1)} %add_convert_fusion.3), channel_id=1, source_target_pairs={{0,2},{1,3},{2,0},{3,1},{4,6},{5,7},{6,4},{7,5},{8,10},{9,11},{10,... | collective-permute-start | bytes 1572872 | tf_op jit(solution)/shard_map/ppermute | solution.py:58
  401.2 9.1 %collective-permute-start.43 = (f32[12,64]{1,0:T(8,128)S(1)}, f32[12,64]{1,0:T(8,128)S(1)}, u32[]{:S(2)}, u32[]{:S(2)}) collective-permute-start(f32[12,64]{1,0:T(8,128)S(1)} %bitcast.196), channel_id=1, source_target_pairs={{0,4},{4,0},{1,5},{5,1},{2,6},{6,2},{3,7},{7,3},{8,12},{12,8},{9,1... | collective-permute-start | bytes 9224 | tf_op jit(solution)/shard_map/ppermute | solution.py:58
  408.7 14.6 %copy-start.19 = (f32[128,2048]{1,0:T(8,128)S(1)}, f32[128,2048]{1,0:T(8,128)}, u32[]{:S(2)}) copy-start(f32[128,2048]{1,0:T(8,128)} %get-tuple-element.432) | copy-start | bytes 3145732
  (27 other events, 104.7 us)
Sparse Core Ops, SparseCore 0:
  74.4 34.5 all-gather.3
  110.5 34.6 all-gather.5
  183.2 39.2 all-gather.7
  271.7 42.9 reduce-scatter.2
  324.3 42.4 reduce-scatter.4
